TPU v7x, 512 devices: a whole 4x8x8 slice. The times are simulated.
512 devices in a mesh: loop: 32 (over y_hi, z), group: 16 (over x, y_lo, core).
Axes of the slice: x: 4, y: 8 (y_hi: 4, y_lo: 2; y = y_hi * 2 + y_lo), z: 8, core: 2. Of those that a mesh axis runs over, the one named last changes fastest.
Arguments:
- cand_query: bfloat16 [16, 4096, 2048], P('group', 'loop'), may hold values from -6 to 6
- cand_kv: bfloat16 [16, 4096, 4096], P('group', 'loop'), may hold values from -6 to 6
- cand_gate: bfloat16 [16, 4096, 2048], P('group', 'loop'), may hold values from -6 to 6
- cache_store: bfloat16 [256, 32, 4, 4096], P('group', 'loop'), may hold values from -6 to 6
- holders: int32 [256], replicated, may hold values from 0 to 255, as said below
- lengths: int32 [16], P('group'), may hold values from 256 to 2048, as said below
- buckets: int32 [16, 2048], P('group'), may hold values from 0 to 127
- time_bias: float32 [128, 16], replicated, may hold values from -3 to 3
- self_bias: float32 [16], replicated, may hold values from 2 to 4
- norm_gain: float32 [2048], replicated, may hold values from 0.5 to 1.5
Outputs:
- gated_output: bfloat16 [16, 4096, 2048], P('group', 'loop')
Inputs may be any that keep to these rules, and one draw needn't show every extreme that they name: `holders`: entry g * 16 + j names the cache slot of piece j of session g; every slot is named once; slot s lies in group s // 16; every group holds exactly 1 pieces of every session. `lengths`: some session has exactly 2048 positions in every draw.
All inputs are finite; a program needn't handle non-finite values.
Results may differ from a plain program's by a relative error of at most 0.005.
Values may be sent and summed in bfloat16 or wider, within the bound.
No kernel may reach another device: no remote copies, remote signals or barrier semaphores. Data moves between devices by JAX's collectives and lax.ppermute only.
A program may use at most 64 MiB of HBM per device.

v0:
```python
import math

import jax
import jax.numpy as jnp
from jax import lax
from jax.sharding import PartitionSpec as P

HEADS = 16


def shifted(value, axis, steps):
    count = lax.axis_size(axis)
    pairs = [(source, (source + steps) % count) for source in range(count)]
    return lax.ppermute(value, axis, pairs)


def attend_tile(running, query_heads, shard, bias_cols, valid_cols):
    row_count = query_heads.shape[0]
    positions = shard.shape[0]
    model_width = shard.shape[1] // 2
    head_dim = model_width // HEADS
    scaling = 1.0 / math.sqrt(head_dim)
    key_heads = shard[:, :model_width].reshape(positions, HEADS, head_dim)
    value_heads = shard[:, model_width:].reshape(positions, HEADS, head_dim)
    scores = (
        jnp.einsum("chd,khd->hck", query_heads, key_heads, preferred_element_type=jnp.float32)
        * scaling
    )
    scores = scores + bias_cols[:, None, :]
    weights = jnp.where(valid_cols[None, None, :], jax.nn.silu(scores), 0.0).astype(jnp.bfloat16)
    partial_value = jnp.einsum(
        "hck,khd->chd", weights, value_heads, preferred_element_type=jnp.float32
    )
    return running + partial_value.reshape(row_count, model_width)


def per_device(
    cand_query,
    cand_kv,
    cand_gate,
    cache_store,
    holders,
    lengths,
    buckets,
    time_bias,
    self_bias,
    norm_gain,
):
    group_count = lax.axis_size("group")
    cycle_size = lax.axis_size("loop")
    group_index = lax.axis_index("group")
    loop_index = lax.axis_index("loop")
    slot_count = cache_store.shape[0]
    piece_len = cache_store.shape[2]
    double_width = cache_store.shape[3]
    model_width = double_width // 2
    capacity = slot_count // group_count
    entries = holders.shape[0]
    positions = jnp.arange(entries, dtype=jnp.int32)
    source = holders // slot_count
    slot_of = holders % slot_count
    target = positions // slot_count
    earlier = (
        (source[:, None] == source[None, :])
        & (target[:, None] == target[None, :])
        & (positions[None, :] < positions[:, None])
    )
    rank_in = jnp.sum(earlier.astype(jnp.int32), axis=1)
    outlets = jnp.arange(group_count * capacity, dtype=jnp.int32)
    matches = (source == group_index)[None, :] & (
        (target * capacity + rank_in)[None, :] == outlets[:, None]
    )
    chosen = jnp.sum(jnp.where(matches, slot_of[None, :], 0), axis=1)
    filled = jnp.any(matches, axis=1)
    outgoing = jnp.where(filled[:, None, None], cache_store[chosen, 0], jnp.zeros((), jnp.bfloat16))
    outgoing = outgoing.reshape(group_count, capacity, piece_len, double_width)
    incoming = lax.all_to_all(outgoing, "group", split_axis=0, concat_axis=0, tiled=True)
    own_source = lax.dynamic_slice_in_dim(source, group_index * slot_count, slot_count)
    own_rank = lax.dynamic_slice_in_dim(rank_in, group_index * slot_count, slot_count)
    received = incoming.reshape(group_count * capacity, piece_len, double_width)
    history = received[own_source * capacity + own_rank].reshape(-1, double_width)
    hist_len = history.shape[0]
    bucket_row = buckets[0]
    table_size = time_bias.shape[0]
    one_hot = (bucket_row[:, None] == jnp.arange(table_size, dtype=jnp.int32)[None, :]).astype(
        jnp.float32
    )
    time_all = jnp.einsum("kn,nh->hk", one_hot, time_bias, precision=lax.Precision.HIGHEST)
    own_length = lengths[0]
    in_range_all = jnp.arange(bucket_row.shape[0], dtype=jnp.int32) < own_length
    queries = cand_query[0]
    own_pairs = cand_kv[0]
    row_count = queries.shape[0]
    head_dim = model_width // HEADS
    scaling = 1.0 / math.sqrt(head_dim)
    query_heads = queries.reshape(row_count, HEADS, head_dim)

    def contribute(totals, shard, start):
        bias_cols = lax.dynamic_slice_in_dim(time_all, start, shard.shape[0], 1)
        valid_cols = lax.dynamic_slice_in_dim(in_range_all, start, shard.shape[0], 0)
        return attend_tile(totals, query_heads, shard, bias_cols, valid_cols)

    key_heads = own_pairs[:, :model_width].reshape(row_count, HEADS, head_dim)
    value_heads = own_pairs[:, model_width:].reshape(row_count, HEADS, head_dim)
    own_scores = (
        jnp.einsum("chd,chd->ch", query_heads, key_heads, preferred_element_type=jnp.float32)
        * scaling
        + self_bias
    )
    own_weights = jax.nn.silu(own_scores).astype(jnp.bfloat16)
    running = (
        own_weights[:, :, None].astype(jnp.float32) * value_heads.astype(jnp.float32)
    ).reshape(row_count, model_width)

    def advance(step_index, state_now):
        shard, totals = state_now
        anchor = (loop_index - step_index) % cycle_size
        totals = contribute(totals, shard, anchor * hist_len)
        shard = shifted(shard, "loop", 1)
        return (shard, totals)

    shard, running = lax.fori_loop(0, cycle_size - 1, advance, (history, running))
    running = contribute(running, shard, (loop_index + 1) % cycle_size * hist_len)
    average = jnp.mean(running, axis=-1, keepdims=True)
    centered = running - average
    variance = jnp.mean(centered * centered, axis=-1, keepdims=True)
    normed = centered * lax.rsqrt(variance + 1e-05) * norm_gain * cand_gate[0].astype(jnp.float32)
    return normed.astype(jnp.bfloat16)[None]


def solution(mesh):
    return jax.shard_map(
        per_device,
        mesh=mesh,
        in_specs=(
            P("group", "loop", None),
            P("group", "loop", None),
            P("group", "loop", None),
            P("group", "loop", None, None),
            P(),
            P("group"),
            P("group", None),
            P(),
            P(),
            P(),
        ),
        out_specs=P("group", "loop", None),
        check_vma=False,
    )
```

profile of v0, /device:TPU:57, one launch (start us, length us, event | category | flops | bytes accessed | tf_op | source)
XLA Modules:
  0.0 909.7 jit_solution(6264826641852475644)
XLA Ops:
  21.2 881.0 %while.17 = (s32[]{:T(128)}, bf16[64,4096]{1,0:T(8,128)(2,1)}, f32[128,2048]{0,1:T(8,128)S(1)}, s32[]{:T(128)}, pred[2048]{0:T(1024)(128)(4,1)S(1)}, /*index=5*/...) while((s32[]{:T(128)}, bf16[64,4096]{1,0:T(8,128)(2,1)}, ...), condition=%wide.region_4.5_spmd, body=%wide.region_3.4_spmd.sunk | while | flops 68419600 | bytes 9466444 | solution.py:122
  29.6 28.6 %collective-permute-done = bf16[64,4096]{1,0:T(8,128)(2,1)} collective-permute-done((bf16[64,4096]{1,0:T(8,128)(2,1)S(1)}, bf16[64,4096]{1,0:T(8,128)(2,1)}, u32[]{:S(2)}, u32[]{:S(2)}) %collective-permute-start) | collective-permute-done | bytes 524320 | tf_op jit(solution)/shard_map/while/body/eval_jaxpr/ppermute | solution.py:14
  154.1 22.0 %collective-permute-done = bf16[64,4096]{1,0:T(8,128)(2,1)} collective-permute-done((bf16[64,4096]{1,0:T(8,128)(2,1)S(1)}, bf16[64,4096]{1,0:T(8,128)(2,1)}, u32[]{:S(2)}, u32[]{:S(2)}) %collective-permute-start) | collective-permute-done | bytes 524320 | tf_op jit(solution)/shard_map/while/body/eval_jaxpr/ppermute | solution.py:14
  206.7 23.8 %collective-permute-done = bf16[64,4096]{1,0:T(8,128)(2,1)} collective-permute-done((bf16[64,4096]{1,0:T(8,128)(2,1)S(1)}, bf16[64,4096]{1,0:T(8,128)(2,1)}, u32[]{:S(2)}, u32[]{:S(2)}) %collective-permute-start) | collective-permute-done | bytes 524320 | tf_op jit(solution)/shard_map/while/body/eval_jaxpr/ppermute | solution.py:14
  237.5 22.8 %collective-permute-done = bf16[64,4096]{1,0:T(8,128)(2,1)} collective-permute-done((bf16[64,4096]{1,0:T(8,128)(2,1)S(1)}, bf16[64,4096]{1,0:T(8,128)(2,1)}, u32[]{:S(2)}, u32[]{:S(2)}) %collective-permute-start) | collective-permute-done | bytes 524320 | tf_op jit(solution)/shard_map/while/body/eval_jaxpr/ppermute | solution.py:14
  267.4 23.8 %collective-permute-done = bf16[64,4096]{1,0:T(8,128)(2,1)} collective-permute-done((bf16[64,4096]{1,0:T(8,128)(2,1)S(1)}, bf16[64,4096]{1,0:T(8,128)(2,1)}, u32[]{:S(2)}, u32[]{:S(2)}) %collective-permute-start) | collective-permute-done | bytes 524320 | tf_op jit(solution)/shard_map/while/body/eval_jaxpr/ppermute | solution.py:14
  298.2 20.8 %collective-permute-done = bf16[64,4096]{1,0:T(8,128)(2,1)} collective-permute-done((bf16[64,4096]{1,0:T(8,128)(2,1)S(1)}, bf16[64,4096]{1,0:T(8,128)(2,1)}, u32[]{:S(2)}, u32[]{:S(2)}) %collective-permute-start) | collective-permute-done | bytes 524320 | tf_op jit(solution)/shard_map/while/body/eval_jaxpr/ppermute | solution.py:14
  374.6 23.6 %collective-permute-done = bf16[64,4096]{1,0:T(8,128)(2,1)} collective-permute-done((bf16[64,4096]{1,0:T(8,128)(2,1)S(1)}, bf16[64,4096]{1,0:T(8,128)(2,1)}, u32[]{:S(2)}, u32[]{:S(2)}) %collective-permute-start) | collective-permute-done | bytes 524320 | tf_op jit(solution)/shard_map/while/body/eval_jaxpr/ppermute | solution.py:14
  405.2 22.9 %collective-permute-done = bf16[64,4096]{1,0:T(8,128)(2,1)} collective-permute-done((bf16[64,4096]{1,0:T(8,128)(2,1)S(1)}, bf16[64,4096]{1,0:T(8,128)(2,1)}, u32[]{:S(2)}, u32[]{:S(2)}) %collective-permute-start) | collective-permute-done | bytes 524320 | tf_op jit(solution)/shard_map/while/body/eval_jaxpr/ppermute | solution.py:14
  435.2 23.8 %collective-permute-done = bf16[64,4096]{1,0:T(8,128)(2,1)} collective-permute-done((bf16[64,4096]{1,0:T(8,128)(2,1)S(1)}, bf16[64,4096]{1,0:T(8,128)(2,1)}, u32[]{:S(2)}, u32[]{:S(2)}) %collective-permute-start) | collective-permute-done | bytes 524320 | tf_op jit(solution)/shard_map/while/body/eval_jaxpr/ppermute | solution.py:14
  466.0 23.6 %collective-permute-done = bf16[64,4096]{1,0:T(8,128)(2,1)} collective-permute-done((bf16[64,4096]{1,0:T(8,128)(2,1)S(1)}, bf16[64,4096]{1,0:T(8,128)(2,1)}, u32[]{:S(2)}, u32[]{:S(2)}) %collective-permute-start) | collective-permute-done | bytes 524320 | tf_op jit(solution)/shard_map/while/body/eval_jaxpr/ppermute | solution.py:14
  496.7 24.0 %collective-permute-done = bf16[64,4096]{1,0:T(8,128)(2,1)} collective-permute-done((bf16[64,4096]{1,0:T(8,128)(2,1)S(1)}, bf16[64,4096]{1,0:T(8,128)(2,1)}, u32[]{:S(2)}, u32[]{:S(2)}) %collective-permute-start) | collective-permute-done | bytes 524320 | tf_op jit(solution)/shard_map/while/body/eval_jaxpr/ppermute | solution.py:14
  527.8 23.6 %collective-permute-done = bf16[64,4096]{1,0:T(8,128)(2,1)} collective-permute-done((bf16[64,4096]{1,0:T(8,128)(2,1)S(1)}, bf16[64,4096]{1,0:T(8,128)(2,1)}, u32[]{:S(2)}, u32[]{:S(2)}) %collective-permute-start) | collective-permute-done | bytes 524320 | tf_op jit(solution)/shard_map/while/body/eval_jaxpr/ppermute | solution.py:14
  558.4 22.2 %collective-permute-done = bf16[64,4096]{1,0:T(8,128)(2,1)} collective-permute-done((bf16[64,4096]{1,0:T(8,128)(2,1)S(1)}, bf16[64,4096]{1,0:T(8,128)(2,1)}, u32[]{:S(2)}, u32[]{:S(2)}) %collective-permute-start) | collective-permute-done | bytes 524320 | tf_op jit(solution)/shard_map/while/body/eval_jaxpr/ppermute | solution.py:14
  587.6 21.3 %collective-permute-done = bf16[64,4096]{1,0:T(8,128)(2,1)} collective-permute-done((bf16[64,4096]{1,0:T(8,128)(2,1)S(1)}, bf16[64,4096]{1,0:T(8,128)(2,1)}, u32[]{:S(2)}, u32[]{:S(2)}) %collective-permute-start) | collective-permute-done | bytes 524320 | tf_op jit(solution)/shard_map/while/body/eval_jaxpr/ppermute | solution.py:14
  616.0 21.5 %collective-permute-done = bf16[64,4096]{1,0:T(8,128)(2,1)} collective-permute-done((bf16[64,4096]{1,0:T(8,128)(2,1)S(1)}, bf16[64,4096]{1,0:T(8,128)(2,1)}, u32[]{:S(2)}, u32[]{:S(2)}) %collective-permute-start) | collective-permute-done | bytes 524320 | tf_op jit(solution)/shard_map/while/body/eval_jaxpr/ppermute | solution.py:14
  644.5 20.8 %collective-permute-done = bf16[64,4096]{1,0:T(8,128)(2,1)} collective-permute-done((bf16[64,4096]{1,0:T(8,128)(2,1)S(1)}, bf16[64,4096]{1,0:T(8,128)(2,1)}, u32[]{:S(2)}, u32[]{:S(2)}) %collective-permute-start) | collective-permute-done | bytes 524320 | tf_op jit(solution)/shard_map/while/body/eval_jaxpr/ppermute | solution.py:14
  672.4 20.9 %collective-permute-done = bf16[64,4096]{1,0:T(8,128)(2,1)} collective-permute-done((bf16[64,4096]{1,0:T(8,128)(2,1)S(1)}, bf16[64,4096]{1,0:T(8,128)(2,1)}, u32[]{:S(2)}, u32[]{:S(2)}) %collective-permute-start) | collective-permute-done | bytes 524320 | tf_op jit(solution)/shard_map/while/body/eval_jaxpr/ppermute | solution.py:14
  700.3 21.1 %collective-permute-done = bf16[64,4096]{1,0:T(8,128)(2,1)} collective-permute-done((bf16[64,4096]{1,0:T(8,128)(2,1)S(1)}, bf16[64,4096]{1,0:T(8,128)(2,1)}, u32[]{:S(2)}, u32[]{:S(2)}) %collective-permute-start) | collective-permute-done | bytes 524320 | tf_op jit(solution)/shard_map/while/body/eval_jaxpr/ppermute | solution.py:14
  728.4 21.5 %collective-permute-done = bf16[64,4096]{1,0:T(8,128)(2,1)} collective-permute-done((bf16[64,4096]{1,0:T(8,128)(2,1)S(1)}, bf16[64,4096]{1,0:T(8,128)(2,1)}, u32[]{:S(2)}, u32[]{:S(2)}) %collective-permute-start) | collective-permute-done | bytes 524320 | tf_op jit(solution)/shard_map/while/body/eval_jaxpr/ppermute | solution.py:14
  757.0 22.3 %collective-permute-done = bf16[64,4096]{1,0:T(8,128)(2,1)} collective-permute-done((bf16[64,4096]{1,0:T(8,128)(2,1)S(1)}, bf16[64,4096]{1,0:T(8,128)(2,1)}, u32[]{:S(2)}, u32[]{:S(2)}) %collective-permute-start) | collective-permute-done | bytes 524320 | tf_op jit(solution)/shard_map/while/body/eval_jaxpr/ppermute | solution.py:14
  786.3 22.5 %collective-permute-done = bf16[64,4096]{1,0:T(8,128)(2,1)} collective-permute-done((bf16[64,4096]{1,0:T(8,128)(2,1)S(1)}, bf16[64,4096]{1,0:T(8,128)(2,1)}, u32[]{:S(2)}, u32[]{:S(2)}) %collective-permute-start) | collective-permute-done | bytes 524320 | tf_op jit(solution)/shard_map/while/body/eval_jaxpr/ppermute | solution.py:14
  815.8 23.4 %collective-permute-done = bf16[64,4096]{1,0:T(8,128)(2,1)} collective-permute-done((bf16[64,4096]{1,0:T(8,128)(2,1)S(1)}, bf16[64,4096]{1,0:T(8,128)(2,1)}, u32[]{:S(2)}, u32[]{:S(2)}) %collective-permute-start) | collective-permute-done | bytes 524320 | tf_op jit(solution)/shard_map/while/body/eval_jaxpr/ppermute | solution.py:14
  873.4 28.2 %collective-permute-done = bf16[64,4096]{1,0:T(8,128)(2,1)} collective-permute-done((bf16[64,4096]{1,0:T(8,128)(2,1)S(1)}, bf16[64,4096]{1,0:T(8,128)(2,1)}, u32[]{:S(2)}, u32[]{:S(2)}) %collective-permute-start) | collective-permute-done | bytes 524320 | tf_op jit(solution)/shard_map/while/body/eval_jaxpr/ppermute | solution.py:14
  (405 shorter events, 379.2 us)
Async XLA Ops:
  22.2 36.0 %collective-permute-start = (bf16[64,4096]{1,0:T(8,128)(2,1)S(1)}, bf16[64,4096]{1,0:T(8,128)(2,1)}, u32[]{:S(2)}, u32[]{:S(2)}) collective-permute-start(bf16[64,4096]{1,0:T(8,128)(2,1)S(1)} %copy.81), channel_id=1, source_target_pairs={{0,16},{16,32},{32,48},{48,64},{64,80},{80,96},{96,112},{112,128},... | collective-permute-start | bytes 1572872 | tf_op jit(solution)/shard_map/while/body/eval_jaxpr/ppermute | solution.py:14
  148.7 27.3 %collective-permute-start = (bf16[64,4096]{1,0:T(8,128)(2,1)S(1)}, bf16[64,4096]{1,0:T(8,128)(2,1)}, u32[]{:S(2)}, u32[]{:S(2)}) collective-permute-start(bf16[64,4096]{1,0:T(8,128)(2,1)S(1)} %copy.81), channel_id=1, source_target_pairs={{0,16},{16,32},{32,48},{48,64},{64,80},{80,96},{96,112},{112,128},... | collective-permute-start | bytes 1572872 | tf_op jit(solution)/shard_map/while/body/eval_jaxpr/ppermute | solution.py:14
  201.4 29.1 %collective-permute-start = (bf16[64,4096]{1,0:T(8,128)(2,1)S(1)}, bf16[64,4096]{1,0:T(8,128)(2,1)}, u32[]{:S(2)}, u32[]{:S(2)}) collective-permute-start(bf16[64,4096]{1,0:T(8,128)(2,1)S(1)} %copy.81), channel_id=1, source_target_pairs={{0,16},{16,32},{32,48},{48,64},{64,80},{80,96},{96,112},{112,128},... | collective-permute-start | bytes 1572872 | tf_op jit(solution)/shard_map/while/body/eval_jaxpr/ppermute | solution.py:14
  232.2 28.1 %collective-permute-start = (bf16[64,4096]{1,0:T(8,128)(2,1)S(1)}, bf16[64,4096]{1,0:T(8,128)(2,1)}, u32[]{:S(2)}, u32[]{:S(2)}) collective-permute-start(bf16[64,4096]{1,0:T(8,128)(2,1)S(1)} %copy.81), channel_id=1, source_target_pairs={{0,16},{16,32},{32,48},{48,64},{64,80},{80,96},{96,112},{112,128},... | collective-permute-start | bytes 1572872 | tf_op jit(solution)/shard_map/while/body/eval_jaxpr/ppermute | solution.py:14
  262.1 29.1 %collective-permute-start = (bf16[64,4096]{1,0:T(8,128)(2,1)S(1)}, bf16[64,4096]{1,0:T(8,128)(2,1)}, u32[]{:S(2)}, u32[]{:S(2)}) collective-permute-start(bf16[64,4096]{1,0:T(8,128)(2,1)S(1)} %copy.81), channel_id=1, source_target_pairs={{0,16},{16,32},{32,48},{48,64},{64,80},{80,96},{96,112},{112,128},... | collective-permute-start | bytes 1572872 | tf_op jit(solution)/shard_map/while/body/eval_jaxpr/ppermute | solution.py:14
  292.9 26.1 %collective-permute-start = (bf16[64,4096]{1,0:T(8,128)(2,1)S(1)}, bf16[64,4096]{1,0:T(8,128)(2,1)}, u32[]{:S(2)}, u32[]{:S(2)}) collective-permute-start(bf16[64,4096]{1,0:T(8,128)(2,1)S(1)} %copy.81), channel_id=1, source_target_pairs={{0,16},{16,32},{32,48},{48,64},{64,80},{80,96},{96,112},{112,128},... | collective-permute-start | bytes 1572872 | tf_op jit(solution)/shard_map/while/body/eval_jaxpr/ppermute | solution.py:14
  369.3 28.9 %collective-permute-start = (bf16[64,4096]{1,0:T(8,128)(2,1)S(1)}, bf16[64,4096]{1,0:T(8,128)(2,1)}, u32[]{:S(2)}, u32[]{:S(2)}) collective-permute-start(bf16[64,4096]{1,0:T(8,128)(2,1)S(1)} %copy.81), channel_id=1, source_target_pairs={{0,16},{16,32},{32,48},{48,64},{64,80},{80,96},{96,112},{112,128},... | collective-permute-start | bytes 1572872 | tf_op jit(solution)/shard_map/while/body/eval_jaxpr/ppermute | solution.py:14
  399.9 28.2 %collective-permute-start = (bf16[64,4096]{1,0:T(8,128)(2,1)S(1)}, bf16[64,4096]{1,0:T(8,128)(2,1)}, u32[]{:S(2)}, u32[]{:S(2)}) collective-permute-start(bf16[64,4096]{1,0:T(8,128)(2,1)S(1)} %copy.81), channel_id=1, source_target_pairs={{0,16},{16,32},{32,48},{48,64},{64,80},{80,96},{96,112},{112,128},... | collective-permute-start | bytes 1572872 | tf_op jit(solution)/shard_map/while/body/eval_jaxpr/ppermute | solution.py:14
  429.9 29.1 %collective-permute-start = (bf16[64,4096]{1,0:T(8,128)(2,1)S(1)}, bf16[64,4096]{1,0:T(8,128)(2,1)}, u32[]{:S(2)}, u32[]{:S(2)}) collective-permute-start(bf16[64,4096]{1,0:T(8,128)(2,1)S(1)} %copy.81), channel_id=1, source_target_pairs={{0,16},{16,32},{32,48},{48,64},{64,80},{80,96},{96,112},{112,128},... | collective-permute-start | bytes 1572872 | tf_op jit(solution)/shard_map/while/body/eval_jaxpr/ppermute | solution.py:14
  460.7 28.9 %collective-permute-start = (bf16[64,4096]{1,0:T(8,128)(2,1)S(1)}, bf16[64,4096]{1,0:T(8,128)(2,1)}, u32[]{:S(2)}, u32[]{:S(2)}) collective-permute-start(bf16[64,4096]{1,0:T(8,128)(2,1)S(1)} %copy.81), channel_id=1, source_target_pairs={{0,16},{16,32},{32,48},{48,64},{64,80},{80,96},{96,112},{112,128},... | collective-permute-start | bytes 1572872 | tf_op jit(solution)/shard_map/while/body/eval_jaxpr/ppermute | solution.py:14
  491.4 29.3 %collective-permute-start = (bf16[64,4096]{1,0:T(8,128)(2,1)S(1)}, bf16[64,4096]{1,0:T(8,128)(2,1)}, u32[]{:S(2)}, u32[]{:S(2)}) collective-permute-start(bf16[64,4096]{1,0:T(8,128)(2,1)S(1)} %copy.81), channel_id=1, source_target_pairs={{0,16},{16,32},{32,48},{48,64},{64,80},{80,96},{96,112},{112,128},... | collective-permute-start | bytes 1572872 | tf_op jit(solution)/shard_map/while/body/eval_jaxpr/ppermute | solution.py:14
  522.4 28.9 %collective-permute-start = (bf16[64,4096]{1,0:T(8,128)(2,1)S(1)}, bf16[64,4096]{1,0:T(8,128)(2,1)}, u32[]{:S(2)}, u32[]{:S(2)}) collective-permute-start(bf16[64,4096]{1,0:T(8,128)(2,1)S(1)} %copy.81), channel_id=1, source_target_pairs={{0,16},{16,32},{32,48},{48,64},{64,80},{80,96},{96,112},{112,128},... | collective-permute-start | bytes 1572872 | tf_op jit(solution)/shard_map/while/body/eval_jaxpr/ppermute | solution.py:14
  553.1 27.5 %collective-permute-start = (bf16[64,4096]{1,0:T(8,128)(2,1)S(1)}, bf16[64,4096]{1,0:T(8,128)(2,1)}, u32[]{:S(2)}, u32[]{:S(2)}) collective-permute-start(bf16[64,4096]{1,0:T(8,128)(2,1)S(1)} %copy.81), channel_id=1, source_target_pairs={{0,16},{16,32},{32,48},{48,64},{64,80},{80,96},{96,112},{112,128},... | collective-permute-start | bytes 1572872 | tf_op jit(solution)/shard_map/while/body/eval_jaxpr/ppermute | solution.py:14
  582.3 26.6 %collective-permute-start = (bf16[64,4096]{1,0:T(8,128)(2,1)S(1)}, bf16[64,4096]{1,0:T(8,128)(2,1)}, u32[]{:S(2)}, u32[]{:S(2)}) collective-permute-start(bf16[64,4096]{1,0:T(8,128)(2,1)S(1)} %copy.81), channel_id=1, source_target_pairs={{0,16},{16,32},{32,48},{48,64},{64,80},{80,96},{96,112},{112,128},... | collective-permute-start | bytes 1572872 | tf_op jit(solution)/shard_map/while/body/eval_jaxpr/ppermute | solution.py:14
  610.7 26.8 %collective-permute-start = (bf16[64,4096]{1,0:T(8,128)(2,1)S(1)}, bf16[64,4096]{1,0:T(8,128)(2,1)}, u32[]{:S(2)}, u32[]{:S(2)}) collective-permute-start(bf16[64,4096]{1,0:T(8,128)(2,1)S(1)} %copy.81), channel_id=1, source_target_pairs={{0,16},{16,32},{32,48},{48,64},{64,80},{80,96},{96,112},{112,128},... | collective-permute-start | bytes 1572872 | tf_op jit(solution)/shard_map/while/body/eval_jaxpr/ppermute | solution.py:14
  639.2 26.1 %collective-permute-start = (bf16[64,4096]{1,0:T(8,128)(2,1)S(1)}, bf16[64,4096]{1,0:T(8,128)(2,1)}, u32[]{:S(2)}, u32[]{:S(2)}) collective-permute-start(bf16[64,4096]{1,0:T(8,128)(2,1)S(1)} %copy.81), channel_id=1, source_target_pairs={{0,16},{16,32},{32,48},{48,64},{64,80},{80,96},{96,112},{112,128},... | collective-permute-start | bytes 1572872 | tf_op jit(solution)/shard_map/while/body/eval_jaxpr/ppermute | solution.py:14
  667.1 26.2 %collective-permute-start = (bf16[64,4096]{1,0:T(8,128)(2,1)S(1)}, bf16[64,4096]{1,0:T(8,128)(2,1)}, u32[]{:S(2)}, u32[]{:S(2)}) collective-permute-start(bf16[64,4096]{1,0:T(8,128)(2,1)S(1)} %copy.81), channel_id=1, source_target_pairs={{0,16},{16,32},{32,48},{48,64},{64,80},{80,96},{96,112},{112,128},... | collective-permute-start | bytes 1572872 | tf_op jit(solution)/shard_map/while/body/eval_jaxpr/ppermute | solution.py:14
  695.0 26.4 %collective-permute-start = (bf16[64,4096]{1,0:T(8,128)(2,1)S(1)}, bf16[64,4096]{1,0:T(8,128)(2,1)}, u32[]{:S(2)}, u32[]{:S(2)}) collective-permute-start(bf16[64,4096]{1,0:T(8,128)(2,1)S(1)} %copy.81), channel_id=1, source_target_pairs={{0,16},{16,32},{32,48},{48,64},{64,80},{80,96},{96,112},{112,128},... | collective-permute-start | bytes 1572872 | tf_op jit(solution)/shard_map/while/body/eval_jaxpr/ppermute | solution.py:14
  723.1 26.8 %collective-permute-start = (bf16[64,4096]{1,0:T(8,128)(2,1)S(1)}, bf16[64,4096]{1,0:T(8,128)(2,1)}, u32[]{:S(2)}, u32[]{:S(2)}) collective-permute-start(bf16[64,4096]{1,0:T(8,128)(2,1)S(1)} %copy.81), channel_id=1, source_target_pairs={{0,16},{16,32},{32,48},{48,64},{64,80},{80,96},{96,112},{112,128},... | collective-permute-start | bytes 1572872 | tf_op jit(solution)/shard_map/while/body/eval_jaxpr/ppermute | solution.py:14
  751.6 27.6 %collective-permute-start = (bf16[64,4096]{1,0:T(8,128)(2,1)S(1)}, bf16[64,4096]{1,0:T(8,128)(2,1)}, u32[]{:S(2)}, u32[]{:S(2)}) collective-permute-start(bf16[64,4096]{1,0:T(8,128)(2,1)S(1)} %copy.81), channel_id=1, source_target_pairs={{0,16},{16,32},{32,48},{48,64},{64,80},{80,96},{96,112},{112,128},... | collective-permute-start | bytes 1572872 | tf_op jit(solution)/shard_map/while/body/eval_jaxpr/ppermute | solution.py:14
  781.0 27.8 %collective-permute-start = (bf16[64,4096]{1,0:T(8,128)(2,1)S(1)}, bf16[64,4096]{1,0:T(8,128)(2,1)}, u32[]{:S(2)}, u32[]{:S(2)}) collective-permute-start(bf16[64,4096]{1,0:T(8,128)(2,1)S(1)} %copy.81), channel_id=1, source_target_pairs={{0,16},{16,32},{32,48},{48,64},{64,80},{80,96},{96,112},{112,128},... | collective-permute-start | bytes 1572872 | tf_op jit(solution)/shard_map/while/body/eval_jaxpr/ppermute | solution.py:14
  810.5 28.7 %collective-permute-start = (bf16[64,4096]{1,0:T(8,128)(2,1)S(1)}, bf16[64,4096]{1,0:T(8,128)(2,1)}, u32[]{:S(2)}, u32[]{:S(2)}) collective-permute-start(bf16[64,4096]{1,0:T(8,128)(2,1)S(1)} %copy.81), channel_id=1, source_target_pairs={{0,16},{16,32},{32,48},{48,64},{64,80},{80,96},{96,112},{112,128},... | collective-permute-start | bytes 1572872 | tf_op jit(solution)/shard_map/while/body/eval_jaxpr/ppermute | solution.py:14
  840.9 25.4 %collective-permute-start = (bf16[64,4096]{1,0:T(8,128)(2,1)S(1)}, bf16[64,4096]{1,0:T(8,128)(2,1)}, u32[]{:S(2)}, u32[]{:S(2)}) collective-permute-start(bf16[64,4096]{1,0:T(8,128)(2,1)S(1)} %copy.81), channel_id=1, source_target_pairs={{0,16},{16,32},{32,48},{48,64},{64,80},{80,96},{96,112},{112,128},... | collective-permute-start | bytes 1572872 | tf_op jit(solution)/shard_map/while/body/eval_jaxpr/ppermute | solution.py:14
  868.0 33.5 %collective-permute-start = (bf16[64,4096]{1,0:T(8,128)(2,1)S(1)}, bf16[64,4096]{1,0:T(8,128)(2,1)}, u32[]{:S(2)}, u32[]{:S(2)}) collective-permute-start(bf16[64,4096]{1,0:T(8,128)(2,1)S(1)} %copy.81), channel_id=1, source_target_pairs={{0,16},{16,32},{32,48},{48,64},{64,80},{80,96},{96,112},{112,128},... | collective-permute-start | bytes 1572872 | tf_op jit(solution)/shard_map/while/body/eval_jaxpr/ppermute | solution.py:14
  (81 other events, 320.5 us)
where the time goes:
time: 914 us; the launch traced here: 910 us
  waiting for transfers between devices  663 us (73%)
  local copies, waits for them, and re-layouts  112 us (12%)
  starting transfers between devices  67.5 us (7%)
  matrix products  57 us (6%)
    ppermute x31, waiting for transfers between devices, shifted(): return lax.ppermute(value, axis, pairs)  661 us
    ppermute x31, starting transfers between devices, shifted(): return lax.ppermute(value, axis, pairs)  61.3 us
    dot_general x32, matrix products, attend_tile(): jnp.einsum('hck,khd->chd', weights, value_heads, preferred_element_type=j...  56 us
    while x155, local copies, waits for them, and re-layouts  44.4 us
    another operation x31, local copies, waits for them, and re-layouts  32.4 us
    dynamic_slice x32, local copies, waits for them, and re-layouts, contribute(): lax.dynamic_slice_in_dim(in_range_all, start, shard.shape[0], 0)  20.9 us
  transfers between devices with their start and end apart: 32, of which 32 were waited for; matrix products, arithmetic and copies ran while one was open for 12% of the time, Pallas kernels for 0%

commit v1 on v0

v1 whole, which is shorter than its diff:
```python
import math

import jax
import jax.numpy as jnp
from jax import lax
from jax.experimental import pallas as pl
from jax.experimental.pallas import tpu as pltpu
from jax.sharding import Mesh
from jax.sharding import PartitionSpec as P

HEADS = 16
HEAD_DIM = 128
GROUP = ("x", "ylo", "core")
LOOP = ("yhi", "z")


def shifted(value, axis, steps):
    count = lax.axis_size(axis)
    return lax.ppermute(value, axis, [(i, (i + steps) % count) for i in range(count)])


def gathered(value, axis):
    count = lax.axis_size(axis)
    index = lax.axis_index(axis)
    parts = [value] + [shifted(value, axis, s) for s in range(1, count)]
    stacked = jnp.stack(parts)
    order = (index - jnp.arange(count)) % count
    return stacked[order]


def attend_kernel(q_ref, k_ref, v_ref, bias_ref, valid_ref, out_ref):
    scale = 0.5 / math.sqrt(HEAD_DIM)
    keys = k_ref[...]
    values = v_ref[...] * valid_ref[...]
    bias = bias_ref[0] * 0.5
    for block in range(q_ref.shape[0]):
        scores = lax.dot_general(
            q_ref[block], keys, (((1,), (1,)), ((), ())), preferred_element_type=jnp.float32
        )
        half = scores * scale + bias
        weights = (half + half * jnp.tanh(half)).astype(jnp.bfloat16)
        out_ref[block] = jnp.dot(
            weights, values, preferred_element_type=jnp.float32
        ).astype(out_ref.dtype)


def attend(queries, history, bias, valid):
    blocks, rows, width = queries.shape
    positions = history.shape[0]
    heads = width // HEAD_DIM
    return pl.pallas_call(
        attend_kernel,
        grid=(heads,),
        in_specs=[
            pl.BlockSpec((blocks, rows, HEAD_DIM), lambda h: (0, 0, h)),
            pl.BlockSpec((positions, HEAD_DIM), lambda h: (0, h)),
            pl.BlockSpec((positions, HEAD_DIM), lambda h: (0, h + heads)),
            pl.BlockSpec((1, 1, positions), lambda h: (h, 0, 0)),
            pl.BlockSpec((positions, HEAD_DIM), lambda h: (0, 0)),
        ],
        out_specs=pl.BlockSpec((blocks, rows, HEAD_DIM), lambda h: (0, 0, h)),
        out_shape=jax.ShapeDtypeStruct((blocks, rows, width), jnp.bfloat16),
        compiler_params=pltpu.CompilerParams(vmem_limit_bytes=32 * 1024 * 1024),
        cost_estimate=pl.CostEstimate(
            flops=4 * blocks * rows * positions * width,
            bytes_accessed=4 * blocks * rows * width + 4 * positions * width,
            transcendentals=blocks * rows * positions * heads,
        ),
    )(queries, history, history, bias, valid)


def finish_kernel(part_ref, q_ref, own_ref, gate_ref, self_bias_ref, gain_ref, out_ref):
    width = q_ref.shape[1]
    scale = 0.5 / math.sqrt(HEAD_DIM)
    pieces = []
    for head in range(width // HEAD_DIM):
        cols = slice(head * HEAD_DIM, (head + 1) * HEAD_DIM)
        value_cols = slice(width + head * HEAD_DIM, width + (head + 1) * HEAD_DIM)
        product = q_ref[:, cols].astype(jnp.float32) * own_ref[:, cols].astype(jnp.float32)
        half = jnp.sum(product, axis=-1, keepdims=True) * scale + 0.5 * self_bias_ref[0, head]
        weight = (half + half * jnp.tanh(half)).astype(jnp.bfloat16).astype(jnp.float32)
        pieces.append(
            part_ref[:, cols].astype(jnp.float32)
            + weight * own_ref[:, value_cols].astype(jnp.float32)
        )
    total = jnp.concatenate(pieces, axis=-1)
    average = jnp.mean(total, axis=-1, keepdims=True)
    centered = total - average
    variance = jnp.mean(centered * centered, axis=-1, keepdims=True)
    normed = centered * lax.rsqrt(variance + 1e-05) * gain_ref[...]
    out_ref[...] = (normed * gate_ref[...].astype(jnp.float32)).astype(out_ref.dtype)


def finish(partial, queries, own, gate, self_bias, gain):
    rows, width = queries.shape
    block = 32
    row_spec = lambda cols: pl.BlockSpec((block, cols), lambda i: (i, 0))
    return pl.pallas_call(
        finish_kernel,
        grid=(rows // block,),
        in_specs=[
            row_spec(width),
            row_spec(width),
            row_spec(2 * width),
            row_spec(width),
            pl.BlockSpec(memory_space=pltpu.SMEM),
            pl.BlockSpec((1, width), lambda i: (0, 0)),
        ],
        out_specs=row_spec(width),
        out_shape=jax.ShapeDtypeStruct((rows, width), jnp.bfloat16),
        compiler_params=pltpu.CompilerParams(vmem_limit_bytes=32 * 1024 * 1024),
    )(partial, queries, own, gate, self_bias[None], gain[None])


def per_device(
    cand_query,
    cand_kv,
    cand_gate,
    cache_store,
    holders,
    lengths,
    buckets,
    time_bias,
    self_bias,
    norm_gain,
):
    group_index = lax.axis_index(GROUP)
    y_index = lax.axis_index("yhi")
    y_size = lax.axis_size("yhi")
    z_size = lax.axis_size("z")
    groups = lax.axis_size(GROUP)
    slots, _, piece_len, double_width = cache_store.shape
    holding = (holders // slots).reshape(groups, slots)
    slot_of = (holders % slots).reshape(groups, slots)
    mine = holding == group_index
    chosen = jnp.sum(jnp.where(mine, slot_of, 0), axis=1)
    outgoing = cache_store[chosen, 0]
    incoming = lax.all_to_all(outgoing, GROUP, 0, 0, tiled=True)
    pieces = incoming.reshape(slots * piece_len, double_width)
    history = lax.all_gather(pieces, "z", tiled=True)

    own_holding = lax.dynamic_index_in_dim(holding, group_index, 0, keepdims=False)
    arrived = own_holding[None, :] == jnp.arange(groups, dtype=jnp.int32)[:, None]
    piece_of = jnp.sum(jnp.where(arrived, jnp.arange(slots, dtype=jnp.int32)[None, :], 0), axis=1)
    per_y = z_size * slots * piece_len
    bucket_rows = lax.dynamic_slice_in_dim(buckets[0], y_index * per_y, per_y)
    bucket_rows = bucket_rows.reshape(z_size, slots, piece_len)[:, piece_of].reshape(per_y)
    place = (
        y_index * per_y
        + (jnp.arange(z_size, dtype=jnp.int32) * slots * piece_len)[:, None, None]
        + (piece_of * piece_len)[None, :, None]
        + jnp.arange(piece_len, dtype=jnp.int32)[None, None, :]
    ).reshape(per_y)
    one_hot = (
        bucket_rows[:, None] == jnp.arange(time_bias.shape[0], dtype=jnp.int32)[None, :]
    ).astype(jnp.float32)
    bias = jnp.einsum("kn,nh->hk", one_hot, time_bias, precision=lax.Precision.HIGHEST)
    valid = jnp.broadcast_to(
        (place < lengths[0]).astype(jnp.bfloat16)[:, None], (per_y, HEAD_DIM)
    )

    queries = cand_query[0]
    all_queries = gathered(queries, "yhi")
    partial = attend(all_queries, history, bias[:, None, :], valid)
    summed = lax.psum_scatter(partial, "yhi", scatter_dimension=0, tiled=False)
    return finish(summed, queries, cand_kv[0], cand_gate[0], self_bias, norm_gain)[None]


def solution(mesh):
    split = Mesh(mesh.devices.reshape(4, 8, 4, 2, 2), LOOP + GROUP)
    rows = P(GROUP, LOOP, None)
    return jax.shard_map(
        per_device,
        mesh=split,
        in_specs=(
            rows,
            rows,
            rows,
            P(GROUP, LOOP, None, None),
            P(),
            P(GROUP),
            P(GROUP, None),
            P(),
            P(),
            P(),
        ),
        out_specs=rows,
        check_vma=False,
    )
```

time: 914 us -> 171 us (0.19)
  the two profiles are of different devices: /device:TPU:57 before, /device:TPU:1 now
where the time goes in v1:
time: 171 us
  waiting for transfers between devices  94 us (55%)
  Pallas kernels  20.3 us (12%)
  blocking collectives  19.2 us (11%)
  between operations  14.2 us (8%)
  starting transfers between devices  10 us (6%)
  local copies, waits for them, and re-layouts  9.74 us (6%)
  other arithmetic  2.78 us (2%)
    reduce_scatter x1, waiting for transfers between devices, per_device(): summed = lax.psum_scatter(partial, 'yhi', scatter_dimension=0, tiled=False)  53.4 us
    ppermute x3, waiting for transfers between devices, shifted(): lax.ppermute(value, axis, [(i, (i + steps) % count) for i in range(count)])  31.1 us
    all_to_all x1, blocking collectives, per_device(): incoming = lax.all_to_all(outgoing, GROUP, 0, 0, tiled=True)  19.2 us
    pallas_call x1, Pallas kernels, attend(): pl.pallas_call(attend_kernel, grid=(heads,), in_specs=[pl.BlockSpec((bloc...  17.2 us
    ppermute x3, starting transfers between devices, shifted(): lax.ppermute(value, axis, [(i, (i + steps) % count) for i in range(count)])  9.96 us
    all_gather x1, waiting for transfers between devices, per_device(): history = lax.all_gather(pieces, 'z', tiled=True)  9.49 us
  transfers between devices with their start and end apart: 5, of which 5 were waited for; matrix products, arithmetic and copies ran while one was open for 4% of the time, Pallas kernels for 0%

profile of v1, /device:TPU:1, one launch (start us, length us, event | category | flops | bytes accessed | tf_op | source)
XLA Modules:
  0.0 170.6 jit_solution(13841397539878560142)
XLA Ops:
  6.5 0.8 and_select_fusion.1
  7.8 1.0 gather_fusion.1
  8.8 19.2 %all_to_all.5 = bf16[16,4,4096]{2,1,0:T(4,128)(2,1)S(1)} all-to-all(bf16[16,4,4096]{2,1,0:T(4,128)(2,1)S(1)} %gather_fusion.1), channel_id=1, replica_groups=mesh['yhi'=4,'z'=8,'x'=4,'ylo'=2,'core'=2] {'x','ylo','core'}, dimensions={0} | all-to-all | bytes 1048576 | tf_op jit(solution)/shard_map/all_to_all | solution.py:138
  28.0 0.9 reshape.152
  29.0 2.2 %collective-permute-start.2 = (bf16[128,2048]{1,0:T(8,128)(2,1)S(1)}, bf16[128,2048]{1,0:T(8,128)(2,1)S(1)}, u32[]{:S(2)}, u32[]{:S(2)}) collective-permute-start(bf16[128,2048]{1,0:T(8,128)(2,1)S(1)} %bitcast.28), channel_id=1, source_target_pairs={{0,384},{128,0},{256,128},{384,256},{1,385},{129,1},{257,129},{385... | collective-permute-start | bytes 1572872 | tf_op jit(solution)/shard_map/ppermute | solution.py:19
  31.2 4.4 %collective-permute-start.1 = (bf16[128,2048]{1,0:T(8,128)(2,1)S(1)}, bf16[128,2048]{1,0:T(8,128)(2,1)S(1)}, u32[]{:S(2)}, u32[]{:S(2)}) collective-permute-start(bf16[128,2048]{1,0:T(8,128)(2,1)S(1)} %bitcast.29), channel_id=1, source_target_pairs={{0,256},{128,384},{256,0},{384,128},{1,257},{129,385},{257,1},{385... | collective-permute-start | bytes 1572872 | tf_op jit(solution)/shard_map/ppermute | solution.py:19
  35.6 3.3 %collective-permute-start = (bf16[128,2048]{1,0:T(8,128)(2,1)S(1)}, bf16[128,2048]{1,0:T(8,128)(2,1)S(1)}, u32[]{:S(2)}, u32[]{:S(2)}) collective-permute-start(bf16[128,2048]{1,0:T(8,128)(2,1)S(1)} %bitcast.30), channel_id=1, source_target_pairs={{0,128},{128,256},{256,384},{384,0},{1,129},{129,257},{257,385},{3... | collective-permute-start | bytes 1572872 | tf_op jit(solution)/shard_map/ppermute | solution.py:19
  38.9 0.7 dynamic-slice_reduce_fusion
  39.8 0.2 copy.11
  39.9 0.6 gather_fusion.2
  40.5 0.2 copy.12
  40.9 0.3 convolution_bitcast_fusion
  42.2 6.6 %collective-permute-done.2 = bf16[128,2048]{1,0:T(8,128)(2,1)S(1)} collective-permute-done((bf16[128,2048]{1,0:T(8,128)(2,1)S(1)}, bf16[128,2048]{1,0:T(8,128)(2,1)S(1)}, u32[]{:S(2)}, u32[]{:S(2)}) %collective-permute-start.2) | collective-permute-done | bytes 524320 | tf_op jit(solution)/shard_map/ppermute | solution.py:19
  48.7 2.4 %collective-permute-done.1 = bf16[128,2048]{1,0:T(8,128)(2,1)S(1)} collective-permute-done((bf16[128,2048]{1,0:T(8,128)(2,1)S(1)}, bf16[128,2048]{1,0:T(8,128)(2,1)S(1)}, u32[]{:S(2)}, u32[]{:S(2)}) %collective-permute-start.1) | collective-permute-done | bytes 524320 | tf_op jit(solution)/shard_map/ppermute | solution.py:19
  51.1 22.1 %collective-permute-done = bf16[128,2048]{1,0:T(8,128)(2,1)S(1)} collective-permute-done((bf16[128,2048]{1,0:T(8,128)(2,1)S(1)}, bf16[128,2048]{1,0:T(8,128)(2,1)S(1)}, u32[]{:S(2)}, u32[]{:S(2)}) %collective-permute-start) | collective-permute-done | bytes 524320 | tf_op jit(solution)/shard_map/ppermute | solution.py:19
  73.2 1.6 pad_maximum_fusion
  74.8 2.3 %gather_fusion = bf16[4,128,2048]{2,1,0:T(8,128)(2,1)S(1)} fusion(bf16[4,128,2048]{2,1,0:T(8,128)(2,1)} %pad_maximum_fusion, s32[1024]{0:T(1024)S(1)} %pad_clamp_fusion.1), kind=kCustom, calls=%fused_computation | custom fusion | bytes 4194320 | tf_op jit(solution)/shard_map/gather | solution.py:28
  77.1 9.5 %all-gather.2.cloned.1.call-done.k_ref.v_ref = bf16[512,4096]{1,0:T(8,128)(2,1)} async-done(((bf16[64,4096]{1,0:T(8,128)(2,1)}), bf16[512,4096]{1,0:T(8,128)(2,1)}) %all-gather.2.cloned.1.call-update) | async-done | bytes 4194320 | tf_op jit(solution)/shard_map/all_gather | solution.py:140
  86.6 0.1 broadcast_in_dim.27.valid_ref
  86.8 2.2 %copy-done.1 = bf16[512,4096]{1,0:T(8,128)(2,1)S(1)} copy-done((bf16[512,4096]{1,0:T(8,128)(2,1)S(1)}, bf16[512,4096]{1,0:T(8,128)(2,1)}, u32[]{:S(2)}) %copy-start.1) | copy-done | bytes 4194328
  88.9 17.2 %shard_map.100 = bf16[4,128,2048]{2,1,0:T(8,128)(2,1)} custom-call(bf16[4,128,2048]{2,1,0:T(8,128)(2,1)S(1)} %gather_fusion, bf16[512,4096]{1,0:T(8,128)(2,1)S(1)} %copy-done.1, bf16[512,4096]{1,0:T(8,128)(2,1)S(1)} %copy-done.1, f32[16,1,512]{2,1,0:T(1,128)S(1)} %broadcast_in_dim.26.bias_ref, bf16[512,128]{1,0:T(8,128)(2,1)S(1)} %broadcast_in_dim.27.valid_ref), custom_call_target="tpu_custom_call" | custom-call | flops 2147483648 | bytes 8388608 | tf_op jit(solution)/shard_map/pallas_call | solution.py:51
  106.2 53.4 %reduce-scatter.2.cloned.1.call-done = bf16[1,128,2048]{2,1,0:T(8,128)(2,1)} async-done(((bf16[4,128,2048]{2,1,0:T(8,128)(2,1)}), bf16[1,128,2048]{2,1,0:T(8,128)(2,1)}) %reduce-scatter.2.cloned.1.call-update) | async-done | bytes 524304 | tf_op jit(solution)/shard_map/reduce_scatter | solution.py:165
  159.7 1.0 copy-done.5
  160.7 3.1 %shard_map.101 = bf16[128,2048]{1,0:T(8,128)(2,1)} custom-call(bf16[128,2048]{1,0:T(8,128)(2,1)S(1)} %bitcast.34, bf16[128,2048]{1,0:T(8,128)(2,1)S(1)} %bitcast.31, bf16[128,4096]{1,0:T(8,128)(2,1)S(1)} %bitcast.32, bf16[128,2048]{1,0:T(8,128)(2,1)S(1)} %bitcast.33, f32[1,16]{1,0:T(1,128)S(1)} %bitcast.36, f32[1,2048]{1,0:T(1,128)S(1)} %bitcast.35), custom_call_target="tpu_custom_call" | custom-call | tf_op jit(solution)/shard_map/pallas_call | solution.py:98
  (37 shorter events, 1.1 us)
Async XLA Ops:
  6.5 1.2 copy-start
  6.5 22.4 %copy-start.2 = (bf16[1,128,2048]{2,1,0:T(8,128)(2,1)S(1)}, bf16[1,128,2048]{2,1,0:T(8,128)(2,1)}, u32[]{:S(2)}) copy-start(bf16[1,128,2048]{2,1,0:T(8,128)(2,1)} %param.10) | copy-start | bytes 1572868
  6.5 80.1 %all-gather.2.cloned.1.call-start = ((), (), s32[]{:S(2)}) async-start(), calls=%async_computation.2 | async-start | bytes 4718592 | tf_op jit(solution)/shard_map/all_gather | solution.py:140
  7.6 33.2 %copy-start.8 = (f32[128,16]{0,1:T(8,128)S(1)}, f32[128,16]{0,1:T(8,128)}, u32[]{:S(2)}) copy-start(f32[128,16]{0,1:T(8,128)} %param.17) | copy-start | bytes 24580
  28.9 130.7 %reduce-scatter.2.cloned.1.call-start = ((), (), s32[]{:S(2)}) async-start(), calls=%async_computation.3 | async-start | bytes 2621440 | tf_op jit(solution)/shard_map/reduce_scatter | solution.py:165
  29.0 19.8 %collective-permute-start.2 = (bf16[128,2048]{1,0:T(8,128)(2,1)S(1)}, bf16[128,2048]{1,0:T(8,128)(2,1)S(1)}, u32[]{:S(2)}, u32[]{:S(2)}) collective-permute-start(bf16[128,2048]{1,0:T(8,128)(2,1)S(1)} %bitcast.28), channel_id=1, source_target_pairs={{0,384},{128,0},{256,128},{384,256},{1,385},{129,1},{257,129},{385... | collective-permute-start | bytes 1572872 | tf_op jit(solution)/shard_map/ppermute | solution.py:19
  31.2 19.9 %collective-permute-start.1 = (bf16[128,2048]{1,0:T(8,128)(2,1)S(1)}, bf16[128,2048]{1,0:T(8,128)(2,1)S(1)}, u32[]{:S(2)}, u32[]{:S(2)}) collective-permute-start(bf16[128,2048]{1,0:T(8,128)(2,1)S(1)} %bitcast.29), channel_id=1, source_target_pairs={{0,256},{128,384},{256,0},{384,128},{1,257},{129,385},{257,1},{385... | collective-permute-start | bytes 1572872 | tf_op jit(solution)/shard_map/ppermute | solution.py:19
  35.6 37.6 %collective-permute-start = (bf16[128,2048]{1,0:T(8,128)(2,1)S(1)}, bf16[128,2048]{1,0:T(8,128)(2,1)S(1)}, u32[]{:S(2)}, u32[]{:S(2)}) collective-permute-start(bf16[128,2048]{1,0:T(8,128)(2,1)S(1)} %bitcast.30), channel_id=1, source_target_pairs={{0,128},{128,256},{256,384},{384,0},{1,129},{129,257},{257,385},{3... | collective-permute-start | bytes 1572872 | tf_op jit(solution)/shard_map/ppermute | solution.py:19
  86.7 2.2 %copy-start.1 = (bf16[512,4096]{1,0:T(8,128)(2,1)S(1)}, bf16[512,4096]{1,0:T(8,128)(2,1)}, u32[]{:S(2)}) copy-start(bf16[512,4096]{1,0:T(8,128)(2,1)} %all-gather.2.cloned.1.call-done.k_ref.v_ref) | copy-start | bytes 12582916
  106.2 53.5 %copy-start.3 = (bf16[1,128,4096]{2,1,0:T(8,128)(2,1)S(1)}, bf16[1,128,4096]{2,1,0:T(8,128)(2,1)}, u32[]{:S(2)}) copy-start(bf16[1,128,4096]{2,1,0:T(8,128)(2,1)} %param.11) | copy-start | bytes 3145732
  106.2 53.5 %copy-start.4 = (bf16[1,128,2048]{2,1,0:T(8,128)(2,1)S(1)}, bf16[1,128,2048]{2,1,0:T(8,128)(2,1)}, u32[]{:S(2)}) copy-start(bf16[1,128,2048]{2,1,0:T(8,128)(2,1)} %param.12) | copy-start | bytes 1572868
  106.2 53.5 %copy-start.6 = (f32[2048]{0:T(1024)S(1)}, f32[2048]{0:T(1024)}, u32[]{:S(2)}) copy-start(f32[2048]{0:T(1024)} %param.19) | copy-start | bytes 24580
  106.2 53.5 %copy-start.7 = (f32[16]{0:T(128)S(1)}, f32[16]{0:T(128)}, u32[]{:S(2)}) copy-start(f32[16]{0:T(128)} %param.18) | copy-start | bytes 196
  159.7 1.0 copy-start.5
Sparse Core Ops, SparseCore 0:
  29.0 57.5 all-gather.1
  106.3 53.2 reduce-scatter.1

commit v2 on v1

v2 whole, which is shorter than its diff:
```python
import math

import jax
import jax.numpy as jnp
from jax import lax
from jax.experimental import pallas as pl
from jax.experimental.pallas import tpu as pltpu
from jax.sharding import Mesh
from jax.sharding import PartitionSpec as P

HEADS = 16
HEAD_DIM = 128
GROUP = ("x", "ylo", "core")
LOOP = ("yhi", "z")


def shifted(value, axis, steps):
    count = lax.axis_size(axis)
    return lax.ppermute(value, axis, [(i, (i + steps) % count) for i in range(count)])


def make_attend_kernel(count, with_base):
    def kernel(*refs):
        q_refs = refs[:count]
        k_ref, v_ref, bias_ref, valid_ref = refs[count : count + 4]
        base_ref = refs[count + 4] if with_base else None
        out_refs = refs[count + 4 + with_base :]
        rows = q_refs[0].shape[0]
        scale = 0.5 / math.sqrt(HEAD_DIM)
        valid = valid_ref[...]
        for head in range(k_ref.shape[1] // HEAD_DIM):
            cols = slice(head * HEAD_DIM, (head + 1) * HEAD_DIM)
            queries = jnp.concatenate([q_ref[:, cols] for q_ref in q_refs], axis=0)
            scores = lax.dot_general(
                queries,
                k_ref[:, cols],
                (((1,), (1,)), ((), ())),
                preferred_element_type=jnp.float32,
            )
            half = scores * scale + bias_ref[head] * 0.5
            weights = (half + half * jnp.tanh(half)).astype(jnp.bfloat16)
            sums = jnp.dot(weights, v_ref[:, cols] * valid, preferred_element_type=jnp.float32)
            for i, out_ref in enumerate(out_refs):
                block = sums[i * rows : (i + 1) * rows]
                if with_base:
                    block = block + base_ref[:, cols]
                out_ref[:, cols] = block.astype(out_ref.dtype)

    return kernel


def attend(queries, history, bias, valid, types, first, heads, per_step, base=None):
    rows = queries[0].shape[0]
    positions = history.shape[0]
    width = per_step * HEAD_DIM
    steps = heads // per_step
    skip = first // per_step
    all_steps = HEADS // per_step
    count = len(queries)
    out_spec = pl.BlockSpec((rows, width), lambda i: (0, i))
    return pl.pallas_call(
        make_attend_kernel(count, base is not None),
        grid=(steps,),
        in_specs=[pl.BlockSpec((rows, width), lambda i: (0, i + skip))] * count
        + [
            pl.BlockSpec((positions, width), lambda i: (0, i + skip)),
            pl.BlockSpec((positions, width), lambda i: (0, i + skip + all_steps)),
            pl.BlockSpec((per_step, 1, positions), lambda i: (i + skip, 0, 0)),
            pl.BlockSpec((positions, HEAD_DIM), lambda i: (0, 0)),
        ]
        + ([] if base is None else [out_spec]),
        out_specs=[out_spec] * count,
        out_shape=[jax.ShapeDtypeStruct((rows, heads * HEAD_DIM), t) for t in types],
        compiler_params=pltpu.CompilerParams(vmem_limit_bytes=60 * 1024 * 1024),
        cost_estimate=pl.CostEstimate(
            flops=4 * count * rows * positions * heads * HEAD_DIM,
            bytes_accessed=4 * positions * heads * HEAD_DIM,
            transcendentals=count * rows * positions * heads,
        ),
    )(*queries, history, history, bias, valid, *([] if base is None else [base]))


def own_kernel(q_ref, own_ref, self_bias_ref, out_ref):
    width = q_ref.shape[1]
    scale = 0.5 / math.sqrt(HEAD_DIM)
    for head in range(width // HEAD_DIM):
        cols = slice(head * HEAD_DIM, (head + 1) * HEAD_DIM)
        value_cols = slice(width + head * HEAD_DIM, width + (head + 1) * HEAD_DIM)
        product = q_ref[:, cols].astype(jnp.float32) * own_ref[:, cols].astype(jnp.float32)
        half = jnp.sum(product, axis=-1, keepdims=True) * scale + 0.5 * self_bias_ref[0, head]
        weight = (half + half * jnp.tanh(half)).astype(jnp.bfloat16).astype(jnp.float32)
        out_ref[:, cols] = weight * own_ref[:, value_cols].astype(jnp.float32)


def own_term(queries, own, self_bias):
    rows, width = queries.shape
    block = 32
    return pl.pallas_call(
        own_kernel,
        grid=(rows // block,),
        in_specs=[
            pl.BlockSpec((block, width), lambda i: (i, 0)),
            pl.BlockSpec((block, 2 * width), lambda i: (i, 0)),
            pl.BlockSpec(memory_space=pltpu.SMEM),
        ],
        out_specs=pl.BlockSpec((block, width), lambda i: (i, 0)),
        out_shape=jax.ShapeDtypeStruct((rows, width), jnp.float32),
    )(queries, own, self_bias[None])


def finish_kernel(base_ref, a1_ref, a2_ref, b1_ref, b2_ref, gate_ref, gain_ref, out_ref):
    low = a1_ref[...].astype(jnp.float32) + a2_ref[...].astype(jnp.float32)
    high = b1_ref[...].astype(jnp.float32) + b2_ref[...].astype(jnp.float32)
    total = base_ref[...] + jnp.concatenate([low, high], axis=-1)
    average = jnp.mean(total, axis=-1, keepdims=True)
    centered = total - average
    variance = jnp.mean(centered * centered, axis=-1, keepdims=True)
    normed = centered * lax.rsqrt(variance + 1e-05) * gain_ref[...]
    out_ref[...] = (normed * gate_ref[...].astype(jnp.float32)).astype(out_ref.dtype)


def finish(base, low_parts, high_parts, gate, gain):
    rows, width = base.shape
    block = 64
    row_spec = lambda cols: pl.BlockSpec((block, cols), lambda i: (i, 0))
    return pl.pallas_call(
        finish_kernel,
        grid=(rows // block,),
        in_specs=[row_spec(width)]
        + [row_spec(width // 2)] * 4
        + [row_spec(width), pl.BlockSpec((1, width), lambda i: (0, 0))],
        out_specs=row_spec(width),
        out_shape=jax.ShapeDtypeStruct((rows, width), jnp.bfloat16),
    )(base, *low_parts, *high_parts, gate, gain[None])


def per_device(
    cand_query,
    cand_kv,
    cand_gate,
    cache_store,
    holders,
    lengths,
    buckets,
    time_bias,
    self_bias,
    norm_gain,
):
    group_index = lax.axis_index(GROUP)
    y_index = lax.axis_index("yhi")
    y_size = lax.axis_size("yhi")
    z_size = lax.axis_size("z")
    groups = lax.axis_size(GROUP)
    slots, _, piece_len, double_width = cache_store.shape
    holding = (holders // slots).reshape(groups, slots)
    slot_of = (holders % slots).reshape(groups, slots)
    mine = holding == group_index
    chosen = jnp.sum(jnp.where(mine, slot_of, 0), axis=1)
    outgoing = cache_store[chosen, 0]
    incoming = lax.all_to_all(outgoing, GROUP, 0, 0, tiled=True)
    pieces = incoming.reshape(slots * piece_len, double_width)
    history = lax.all_gather(pieces, "z", tiled=True)

    own_holding = lax.dynamic_index_in_dim(holding, group_index, 0, keepdims=False)
    arrived = own_holding[None, :] == jnp.arange(groups, dtype=jnp.int32)[:, None]
    piece_of = jnp.sum(jnp.where(arrived, jnp.arange(slots, dtype=jnp.int32)[None, :], 0), axis=1)
    per_y = z_size * slots * piece_len
    bucket_rows = lax.dynamic_slice_in_dim(buckets[0], y_index * per_y, per_y)
    bucket_rows = bucket_rows.reshape(z_size, slots, piece_len)[:, piece_of].reshape(per_y)
    place = (
        y_index * per_y
        + (jnp.arange(z_size, dtype=jnp.int32) * slots * piece_len)[:, None, None]
        + (piece_of * piece_len)[None, :, None]
        + jnp.arange(piece_len, dtype=jnp.int32)[None, None, :]
    ).reshape(per_y)
    one_hot = (
        bucket_rows[:, None] == jnp.arange(time_bias.shape[0], dtype=jnp.int32)[None, :]
    ).astype(jnp.float32)
    bias = jnp.einsum("kn,nh->hk", one_hot, time_bias, precision=lax.Precision.HIGHEST)
    valid = jnp.broadcast_to(
        (place < lengths[0]).astype(jnp.bfloat16)[:, None], (per_y, HEAD_DIM)
    )

    queries = cand_query[0]
    bias = bias[:, None, :]
    base = own_term(queries, cand_kv[0], self_bias)
    lower, upper, across = (shifted(queries, "yhi", s) for s in (1, -1, 2))
    half = HEADS // 2
    f32, bf16 = jnp.float32, jnp.bfloat16
    (far_low,) = attend([across], history, bias, valid, [bf16], 0, half, 8)
    from_lower = shifted(far_low, "yhi", 1)
    (far_high,) = attend([across], history, bias, valid, [bf16], half, half, 8)
    from_upper = shifted(far_high, "yhi", -1)
    lower_low, upper_low = attend([lower, upper], history, bias, valid, [bf16, f32], 0, half, 8)
    lower_high, upper_high = attend([lower, upper], history, bias, valid, [f32, bf16], half, half, 8)
    low_1 = shifted(lower_low, "yhi", -1)
    high_1 = shifted(upper_high, "yhi", 1)
    low_2 = shifted((upper_low + from_lower.astype(f32)).astype(bf16), "yhi", 1)
    high_2 = shifted((lower_high + from_upper.astype(f32)).astype(bf16), "yhi", -1)
    (total,) = attend([queries], history, bias, valid, [f32], 0, HEADS, 8, base)
    return finish(total, (low_1, low_2), (high_1, high_2), cand_gate[0], norm_gain)[None]


def solution(mesh):
    split = Mesh(mesh.devices.reshape(4, 8, 4, 2, 2), LOOP + GROUP)
    rows = P(GROUP, LOOP, None)
    return jax.shard_map(
        per_device,
        mesh=split,
        in_specs=(
            rows,
            rows,
            rows,
            P(GROUP, LOOP, None, None),
            P(),
            P(GROUP),
            P(GROUP, None),
            P(),
            P(),
            P(),
        ),
        out_specs=rows,
        check_vma=False,
    )
```

time: 171 us -> 158 us (0.924)
  waiting for transfers between devices: 94 us -> 50.1 us
  starting transfers between devices: 10 us -> 32.2 us
  Pallas kernels: 20.3 us -> 30.7 us
  local copies, waits for them, and re-layouts: 9.74 us -> 7.88 us
    reduce_scatter x1 -> x0, waiting for transfers between devices: 53.4 us -> none  [per_device(): summed = lax.psum_scatter(partial, 'yhi', scatter_dimension=0, tiled=False)]
    ppermute x3 -> x9, starting transfers between devices: 9.96 us -> 32.2 us  [shifted(): lax.ppermute(value, axis, [(i, (i + steps) % count) for i in range(count)])]
    all_gather x1, waiting for transfers between devices: 9.49 us -> 29.3 us  [per_device(): history = lax.all_gather(pieces, 'z', tiled=True)]
    pallas_call x1 -> x6, Pallas kernels: 17.2 us -> 27.9 us  [the longest x5 24.1 us: attend(): pl.pallas_call(make_attend_kernel(count, base is not None), grid=(steps,)...]
    ppermute x3 -> x9, waiting for transfers between devices: 31.1 us -> 20.8 us  [shifted(): lax.ppermute(value, axis, [(i, (i + steps) % count) for i in range(count)])]
    gather x1 -> x0, local copies, waits for them, and re-layouts: 2.29 us -> none  [gathered(): return stacked[order]]
  transfers between devices with their start and end apart: 5 -> 10, of which waited for: 5 -> 3; matrix products, arithmetic and copies ran while one was open for 4% -> 3% of each run, Pallas kernels for 0% -> 18%
where the time goes in v2:
time: 158 us; the launch traced here: 157 us
  waiting for transfers between devices  50.1 us (32%)
  starting transfers between devices  32.2 us (20%)
  Pallas kernels  30.7 us (19%)
  blocking collectives  19.2 us (12%)
  between operations  14.3 us (9%)
  local copies, waits for them, and re-layouts  7.88 us (5%)
  other arithmetic  2.31 us (1%)
    ppermute x9, starting transfers between devices, shifted(): lax.ppermute(value, axis, [(i, (i + steps) % count) for i in range(count)])  32.2 us
    all_gather x1, waiting for transfers between devices, per_device(): history = lax.all_gather(pieces, 'z', tiled=True)  29.3 us
    pallas_call x5, Pallas kernels, attend(): pl.pallas_call(make_attend_kernel(count, base is not None), grid=(steps,)...  24.1 us
    ppermute x9, waiting for transfers between devices, shifted(): lax.ppermute(value, axis, [(i, (i + steps) % count) for i in range(count)])  20.8 us
    all_to_all x1, blocking collectives, per_device(): incoming = lax.all_to_all(outgoing, GROUP, 0, 0, tiled=True)  19.2 us
    pallas_call x1, Pallas kernels, own_term(): pl.pallas_call(own_kernel, grid=(rows // block,), in_specs=[pl.BlockSpec(...  3.86 us
  transfers between devices with their start and end apart: 10, of which 3 were waited for; matrix products, arithmetic and copies ran while one was open for 3% of the time, Pallas kernels for 18%

profile of v2, /device:TPU:1, one launch (start us, length us, event | category | flops | bytes accessed | tf_op | source)
XLA Modules:
  0.0 157.0 jit_solution(8010257048510123833)
XLA Ops:
  7.7 1.0 gather_fusion
  8.7 19.2 %all_to_all.5 = bf16[16,4,4096]{2,1,0:T(4,128)(2,1)S(1)} all-to-all(bf16[16,4,4096]{2,1,0:T(4,128)(2,1)S(1)} %gather_fusion), channel_id=1, replica_groups=mesh['yhi'=4,'z'=8,'x'=4,'ylo'=2,'core'=2] {'x','ylo','core'}, dimensions={0} | all-to-all | bytes 1048576 | tf_op jit(solution)/shard_map/all_to_all | solution.py:160
  27.9 0.9 reshape.103
  28.9 1.9 %collective-permute-start = (bf16[128,2048]{1,0:T(8,128)(2,1)}, bf16[128,2048]{1,0:T(8,128)(2,1)S(1)}, u32[]{:S(2)}, u32[]{:S(2)}) collective-permute-start(bf16[128,2048]{1,0:T(8,128)(2,1)} %bitcast.22), channel_id=1, source_target_pairs={{0,128},{128,256},{256,384},{384,0},{1,129},{129,257},{257,385},{3... | collective-permute-start | bytes 1572872 | tf_op jit(solution)/shard_map/ppermute | solution.py:19
  30.8 5.5 %collective-permute-start.1 = (bf16[128,2048]{1,0:T(8,128)(2,1)}, bf16[128,2048]{1,0:T(8,128)(2,1)S(1)}, u32[]{:S(2)}, u32[]{:S(2)}) collective-permute-start(bf16[128,2048]{1,0:T(8,128)(2,1)} %bitcast.23), channel_id=1, source_target_pairs={{0,384},{128,0},{256,128},{384,256},{1,385},{129,1},{257,129},{385... | collective-permute-start | bytes 1572872 | tf_op jit(solution)/shard_map/ppermute | solution.py:19
  36.3 3.8 %collective-permute-start.3 = (bf16[128,2048]{1,0:T(8,128)(2,1)}, bf16[128,2048]{1,0:T(8,128)(2,1)S(1)}, u32[]{:S(2)}, u32[]{:S(2)}) collective-permute-start(bf16[128,2048]{1,0:T(8,128)(2,1)} %bitcast.24), channel_id=1, source_target_pairs={{0,256},{128,384},{256,0},{384,128},{1,257},{129,385},{257,1},{385... | collective-permute-start | bytes 1572872 | tf_op jit(solution)/shard_map/ppermute | solution.py:19
  43.9 13.4 %collective-permute-done.3.refs_0_ = bf16[128,2048]{1,0:T(8,128)(2,1)S(1)} collective-permute-done((bf16[128,2048]{1,0:T(8,128)(2,1)}, bf16[128,2048]{1,0:T(8,128)(2,1)S(1)}, u32[]{:S(2)}, u32[]{:S(2)}) %collective-permute-start.3) | collective-permute-done | bytes 524320 | tf_op jit(solution)/shard_map/ppermute | solution.py:19
  57.2 29.3 %all-gather.2.cloned.1.call-done.refs_1_.refs_2_.refs_3_ = bf16[512,4096]{1,0:T(8,128)(2,1)} async-done(((bf16[64,4096]{1,0:T(8,128)(2,1)}), bf16[512,4096]{1,0:T(8,128)(2,1)}) %all-gather.2.cloned.1.call-update) | async-done | bytes 4194320 | tf_op jit(solution)/shard_map/all_gather | solution.py:162
  87.4 4.1 %shard_map.103 = bf16[128,1024]{1,0:T(8,128)(2,1)} custom-call(bf16[128,2048]{1,0:T(8,128)(2,1)} %copy-done.3, bf16[512,4096]{1,0:T(8,128)(2,1)} %all-gather.2.cloned.1.call-done.refs_1_.refs_2_.refs_3_, bf16[512,4096]{1,0:T(8,128)(2,1)} %all-gather.2.cloned.1.call-done.refs_1_.refs_2_.refs_3_, f32[16,1,512]{2,1,0:T(1,128)} %broadcast_in_dim.26.refs_3_.refs_4_, ...), custom_call_target="tpu_custom_call" | custom-call | flops 268435456 | bytes 2097152 | tf_op jit(solution)/shard_map/pallas_call | solution.py:61
  91.4 4.0 %collective-permute-start.4 = (bf16[128,1024]{1,0:T(8,128)(2,1)}, bf16[128,1024]{1,0:T(8,128)(2,1)S(1)}, u32[]{:S(2)}, u32[]{:S(2)}) collective-permute-start(bf16[128,1024]{1,0:T(8,128)(2,1)} %shard_map.103), channel_id=1, source_target_pairs={{0,128},{128,256},{256,384},{384,0},{1,129},{129,257},{257,385},{3... | collective-permute-start | bytes 786440 | tf_op jit(solution)/shard_map/ppermute | solution.py:19
  95.4 4.1 %shard_map.105 = bf16[128,1024]{1,0:T(8,128)(2,1)} custom-call(bf16[128,2048]{1,0:T(8,128)(2,1)} %copy-done.3, bf16[512,4096]{1,0:T(8,128)(2,1)} %all-gather.2.cloned.1.call-done.refs_1_.refs_2_.refs_3_, bf16[512,4096]{1,0:T(8,128)(2,1)} %all-gather.2.cloned.1.call-done.refs_1_.refs_2_.refs_3_, f32[16,1,512]{2,1,0:T(1,128)} %broadcast_in_dim.26.refs_3_.refs_4_, ...), custom_call_target="tpu_custom_call" | custom-call | flops 268435456 | bytes 2097152 | tf_op jit(solution)/shard_map/pallas_call | solution.py:61
  99.5 3.4 %collective-permute-start.7 = (bf16[128,1024]{1,0:T(8,128)(2,1)}, bf16[128,1024]{1,0:T(8,128)(2,1)S(1)}, u32[]{:S(2)}, u32[]{:S(2)}) collective-permute-start(bf16[128,1024]{1,0:T(8,128)(2,1)} %shard_map.105), channel_id=1, source_target_pairs={{0,384},{128,0},{256,128},{384,256},{1,385},{129,1},{257,129},{385... | collective-permute-start | bytes 786440 | tf_op jit(solution)/shard_map/ppermute | solution.py:19
  103.7 0.8 copy-done.2
  104.5 4.7 %shard_map.102 = (bf16[128,1024]{1,0:T(8,128)(2,1)}, f32[128,1024]{1,0:T(8,128)}) custom-call(bf16[128,2048]{1,0:T(8,128)(2,1)} %copy-done.1, bf16[128,2048]{1,0:T(8,128)(2,1)} %copy-done.2, bf16[512,4096]{1,0:T(8,128)(2,1)} %all-gather.2.cloned.1.call-done.refs_1_.refs_2_.refs_3_, bf16[512,4096]{1,0:T(8,128)(2,1)} %all-gather.2.cloned.1.call-done.refs_1_.refs_2_.refs_3_, ...), custom_call_target="tpu_custom_call" | custom-call | flops 536870912 | bytes 2097152 | tf_op jit(solution)/shard_map/pallas_call | solution.py:61
  109.2 4.3 %collective-permute-start.2 = (bf16[128,1024]{1,0:T(8,128)(2,1)}, bf16[128,1024]{1,0:T(8,128)(2,1)S(1)}, u32[]{:S(2)}, u32[]{:S(2)}) collective-permute-start(bf16[128,1024]{1,0:T(8,128)(2,1)} %get-tuple-element.9), channel_id=1, source_target_pairs={{0,384},{128,0},{256,128},{384,256},{1,385},{129,1},{257,129},{385... | collective-permute-start | bytes 786440 | tf_op jit(solution)/shard_map/ppermute | solution.py:19
  113.5 4.7 %shard_map.104 = (f32[128,1024]{1,0:T(8,128)}, bf16[128,1024]{1,0:T(8,128)(2,1)}) custom-call(bf16[128,2048]{1,0:T(8,128)(2,1)} %copy-done.1, bf16[128,2048]{1,0:T(8,128)(2,1)} %copy-done.2, bf16[512,4096]{1,0:T(8,128)(2,1)} %all-gather.2.cloned.1.call-done.refs_1_.refs_2_.refs_3_, bf16[512,4096]{1,0:T(8,128)(2,1)} %all-gather.2.cloned.1.call-done.refs_1_.refs_2_.refs_3_, ...), custom_call_target="tpu_custom_call" | custom-call | flops 536870912 | bytes 2097152 | tf_op jit(solution)/shard_map/pallas_call | solution.py:61
  118.2 2.0 %collective-permute-start.6 = (bf16[128,1024]{1,0:T(8,128)(2,1)}, bf16[128,1024]{1,0:T(8,128)(2,1)S(1)}, u32[]{:S(2)}, u32[]{:S(2)}) collective-permute-start(bf16[128,1024]{1,0:T(8,128)(2,1)} %get-tuple-element.11), channel_id=1, source_target_pairs={{0,128},{128,256},{256,384},{384,0},{1,129},{129,257},{257,385},{3... | collective-permute-start | bytes 786440 | tf_op jit(solution)/shard_map/ppermute | solution.py:19
  120.3 5.0 %collective-permute-start.5 = (bf16[128,1024]{1,0:T(8,128)(2,1)S(1)}, bf16[128,1024]{1,0:T(8,128)(2,1)S(1)}, u32[]{:S(2)}, u32[]{:S(2)}) collective-permute-start(bf16[128,1024]{1,0:T(8,128)(2,1)S(1)} %add_convert_fusion.1), channel_id=1, source_target_pairs={{0,128},{128,256},{256,384},{384,0},{1,129},{129,257},{257,385},{3... | collective-permute-start | bytes 786440 | tf_op jit(solution)/shard_map/ppermute | solution.py:19
  125.4 1.1 add_convert_fusion
  126.5 2.4 %collective-permute-start.8 = (bf16[128,1024]{1,0:T(8,128)(2,1)S(1)}, bf16[128,1024]{1,0:T(8,128)(2,1)S(1)}, u32[]{:S(2)}, u32[]{:S(2)}) collective-permute-start(bf16[128,1024]{1,0:T(8,128)(2,1)S(1)} %add_convert_fusion), channel_id=1, source_target_pairs={{0,384},{128,0},{256,128},{384,256},{1,385},{129,1},{257,129},{385... | collective-permute-start | bytes 786440 | tf_op jit(solution)/shard_map/ppermute | solution.py:19
  128.8 3.9 %shard_map.100.refs_5_ = f32[128,2048]{1,0:T(8,128)} custom-call(bf16[128,2048]{1,0:T(8,128)(2,1)} %bitcast.25, bf16[128,4096]{1,0:T(8,128)(2,1)} %bitcast.27, f32[1,16]{1,0:T(1,128)} %bitcast.31), custom_call_target="tpu_custom_call" | custom-call | tf_op jit(solution)/shard_map/pallas_call | solution.py:98
  132.7 6.5 %shard_map.101.base_ref = f32[128,2048]{1,0:T(8,128)} custom-call(bf16[128,2048]{1,0:T(8,128)(2,1)} %bitcast.26, bf16[512,4096]{1,0:T(8,128)(2,1)} %all-gather.2.cloned.1.call-done.refs_1_.refs_2_.refs_3_, bf16[512,4096]{1,0:T(8,128)(2,1)} %all-gather.2.cloned.1.call-done.refs_1_.refs_2_.refs_3_, f32[16,1,512]{2,1,0:T(1,128)} %broadcast_in_dim.26.refs_3_.refs_4_, ...), custom_call_target="tpu_custom_call" | custom-call | flops 536870912 | bytes 4194304 | tf_op jit(solution)/shard_map/pallas_call | solution.py:61
  139.3 7.4 %collective-permute-done.5.a2_ref = bf16[128,1024]{1,0:T(8,128)(2,1)S(1)} collective-permute-done((bf16[128,1024]{1,0:T(8,128)(2,1)S(1)}, bf16[128,1024]{1,0:T(8,128)(2,1)S(1)}, u32[]{:S(2)}, u32[]{:S(2)}) %collective-permute-start.5) | collective-permute-done | bytes 262176 | tf_op jit(solution)/shard_map/ppermute | solution.py:19
  147.4 2.7 %shard_map.106 = bf16[128,2048]{1,0:T(8,128)(2,1)} custom-call(f32[128,2048]{1,0:T(8,128)} %shard_map.101.base_ref, bf16[128,1024]{1,0:T(8,128)(2,1)} %copy-done.5, bf16[128,1024]{1,0:T(8,128)(2,1)} %copy-done.7, bf16[128,1024]{1,0:T(8,128)(2,1)} %copy-done.6, bf16[128,1024]{1,0:T(8,128)(2,1)} %copy-done.8, bf16[128,2048]{1,0:T(8,128)(2,1)} %bitcast.28, ...), custom_call_target="tpu_custom_call" | custom-call | tf_op jit(solution)/shard_map/pallas_call | solution.py:126
  (51 shorter events, 6.7 us)
Async XLA Ops:
  6.5 1.2 copy-start
  6.5 35.4 %copy-start.9 = (f32[128,16]{0,1:T(8,128)S(1)}, f32[128,16]{0,1:T(8,128)}, u32[]{:S(2)}) copy-start(f32[128,16]{0,1:T(8,128)} %param.17) | copy-start | bytes 24580
  6.5 80.0 %all-gather.2.cloned.1.call-start = ((), (), s32[]{:S(2)}) async-start(), calls=%async_computation.1 | async-start | bytes 4718592 | tf_op jit(solution)/shard_map/all_gather | solution.py:162
  28.9 74.0 %collective-permute-start = (bf16[128,2048]{1,0:T(8,128)(2,1)}, bf16[128,2048]{1,0:T(8,128)(2,1)S(1)}, u32[]{:S(2)}, u32[]{:S(2)}) collective-permute-start(bf16[128,2048]{1,0:T(8,128)(2,1)} %bitcast.22), channel_id=1, source_target_pairs={{0,128},{128,256},{256,384},{384,0},{1,129},{129,257},{257,385},{3... | collective-permute-start | bytes 1572872 | tf_op jit(solution)/shard_map/ppermute | solution.py:19
  30.8 72.1 %collective-permute-start.1 = (bf16[128,2048]{1,0:T(8,128)(2,1)}, bf16[128,2048]{1,0:T(8,128)(2,1)S(1)}, u32[]{:S(2)}, u32[]{:S(2)}) collective-permute-start(bf16[128,2048]{1,0:T(8,128)(2,1)} %bitcast.23), channel_id=1, source_target_pairs={{0,384},{128,0},{256,128},{384,256},{1,385},{129,1},{257,129},{385... | collective-permute-start | bytes 1572872 | tf_op jit(solution)/shard_map/ppermute | solution.py:19
  36.3 21.0 %collective-permute-start.3 = (bf16[128,2048]{1,0:T(8,128)(2,1)}, bf16[128,2048]{1,0:T(8,128)(2,1)S(1)}, u32[]{:S(2)}, u32[]{:S(2)}) collective-permute-start(bf16[128,2048]{1,0:T(8,128)(2,1)} %bitcast.24), channel_id=1, source_target_pairs={{0,256},{128,384},{256,0},{384,128},{1,257},{129,385},{257,1},{385... | collective-permute-start | bytes 1572872 | tf_op jit(solution)/shard_map/ppermute | solution.py:19
  57.2 30.1 %copy-start.3 = (bf16[128,2048]{1,0:T(8,128)(2,1)}, bf16[128,2048]{1,0:T(8,128)(2,1)S(1)}, u32[]{:S(2)}) copy-start(bf16[128,2048]{1,0:T(8,128)(2,1)S(1)} %collective-permute-done.3.refs_0_) | copy-start | bytes 1572868
  91.4 28.8 %collective-permute-start.4 = (bf16[128,1024]{1,0:T(8,128)(2,1)}, bf16[128,1024]{1,0:T(8,128)(2,1)S(1)}, u32[]{:S(2)}, u32[]{:S(2)}) collective-permute-start(bf16[128,1024]{1,0:T(8,128)(2,1)} %shard_map.103), channel_id=1, source_target_pairs={{0,128},{128,256},{256,384},{384,0},{1,129},{129,257},{257,385},{3... | collective-permute-start | bytes 786440 | tf_op jit(solution)/shard_map/ppermute | solution.py:19
  99.5 25.8 %collective-permute-start.7 = (bf16[128,1024]{1,0:T(8,128)(2,1)}, bf16[128,1024]{1,0:T(8,128)(2,1)S(1)}, u32[]{:S(2)}, u32[]{:S(2)}) collective-permute-start(bf16[128,1024]{1,0:T(8,128)(2,1)} %shard_map.105), channel_id=1, source_target_pairs={{0,384},{128,0},{256,128},{384,256},{1,385},{129,1},{257,129},{385... | collective-permute-start | bytes 786440 | tf_op jit(solution)/shard_map/ppermute | solution.py:19
  102.9 0.8 copy-start.1
  103.7 0.8 copy-start.2
  109.2 11.0 %copy-start.4 = (f32[128,1024]{1,0:T(8,128)S(1)}, f32[128,1024]{1,0:T(8,128)}, u32[]{:S(2)}) copy-start(f32[128,1024]{1,0:T(8,128)} %get-tuple-element.10) | copy-start | bytes 1572868
  109.2 30.0 %collective-permute-start.2 = (bf16[128,1024]{1,0:T(8,128)(2,1)}, bf16[128,1024]{1,0:T(8,128)(2,1)S(1)}, u32[]{:S(2)}, u32[]{:S(2)}) collective-permute-start(bf16[128,1024]{1,0:T(8,128)(2,1)} %get-tuple-element.9), channel_id=1, source_target_pairs={{0,384},{128,0},{256,128},{384,256},{1,385},{129,1},{257,129},{385... | collective-permute-start | bytes 786440 | tf_op jit(solution)/shard_map/ppermute | solution.py:19
  118.2 21.1 %collective-permute-start.6 = (bf16[128,1024]{1,0:T(8,128)(2,1)}, bf16[128,1024]{1,0:T(8,128)(2,1)S(1)}, u32[]{:S(2)}, u32[]{:S(2)}) collective-permute-start(bf16[128,1024]{1,0:T(8,128)(2,1)} %get-tuple-element.11), channel_id=1, source_target_pairs={{0,128},{128,256},{256,384},{384,0},{1,129},{129,257},{257,385},{3... | collective-permute-start | bytes 786440 | tf_op jit(solution)/shard_map/ppermute | solution.py:19
  120.3 26.3 %collective-permute-start.5 = (bf16[128,1024]{1,0:T(8,128)(2,1)S(1)}, bf16[128,1024]{1,0:T(8,128)(2,1)S(1)}, u32[]{:S(2)}, u32[]{:S(2)}) collective-permute-start(bf16[128,1024]{1,0:T(8,128)(2,1)S(1)} %add_convert_fusion.1), channel_id=1, source_target_pairs={{0,128},{128,256},{256,384},{384,0},{1,129},{129,257},{257,385},{3... | collective-permute-start | bytes 786440 | tf_op jit(solution)/shard_map/ppermute | solution.py:19
  126.5 20.2 %collective-permute-start.8 = (bf16[128,1024]{1,0:T(8,128)(2,1)S(1)}, bf16[128,1024]{1,0:T(8,128)(2,1)S(1)}, u32[]{:S(2)}, u32[]{:S(2)}) collective-permute-start(bf16[128,1024]{1,0:T(8,128)(2,1)S(1)} %add_convert_fusion), channel_id=1, source_target_pairs={{0,384},{128,0},{256,128},{384,256},{1,385},{129,1},{257,129},{385... | collective-permute-start | bytes 786440 | tf_op jit(solution)/shard_map/ppermute | solution.py:19
  139.2 7.4 %copy-start.5 = (bf16[128,1024]{1,0:T(8,128)(2,1)}, bf16[128,1024]{1,0:T(8,128)(2,1)S(1)}, u32[]{:S(2)}) copy-start(bf16[128,1024]{1,0:T(8,128)(2,1)S(1)} %collective-permute-done.2.a1_ref) | copy-start | bytes 786436
  139.2 7.4 %copy-start.6 = (bf16[128,1024]{1,0:T(8,128)(2,1)}, bf16[128,1024]{1,0:T(8,128)(2,1)S(1)}, u32[]{:S(2)}) copy-start(bf16[128,1024]{1,0:T(8,128)(2,1)S(1)} %collective-permute-done.6.b1_ref) | copy-start | bytes 786436
  146.6 0.7 copy-start.7
  146.6 0.8 copy-start.8
Sparse Core Ops, SparseCore 0:
  29.0 57.5 all-gather.1

commit v3 on v2

v3 whole, which is shorter than its diff:
```python
import math

import jax
import jax.numpy as jnp
from jax import lax
from jax.experimental import pallas as pl
from jax.experimental.pallas import tpu as pltpu
from jax.sharding import Mesh
from jax.sharding import PartitionSpec as P

HEADS = 16
HEAD_DIM = 128
GROUP = ("x", "ylo", "core")
LOOP = ("yhi", "z")


def shifted(value, axis, steps):
    count = lax.axis_size(axis)
    return lax.ppermute(value, axis, [(i, (i + steps) % count) for i in range(count)])


def make_attend_kernel(blocks, pieces):
    def kernel(*refs):
        q_refs = refs[:blocks]
        k_refs = refs[blocks : blocks + pieces]
        v_refs = refs[blocks + pieces : blocks + 2 * pieces]
        bias_ref, valid_ref, base_ref = refs[blocks + 2 * pieces : blocks + 2 * pieces + 3]
        out_refs = refs[blocks + 2 * pieces + 3 :]
        rows = q_refs[0].shape[0]
        scale = 0.5 / math.sqrt(HEAD_DIM)
        valid = valid_ref[...]
        for head in range(bias_ref.shape[0]):
            cols = slice(head * HEAD_DIM, (head + 1) * HEAD_DIM)
            queries = jnp.concatenate([q_ref[:, cols] for q_ref in q_refs], axis=0)
            keys = jnp.concatenate([k_ref[:, cols] for k_ref in k_refs], axis=0)
            values = jnp.concatenate([v_ref[:, cols] for v_ref in v_refs], axis=0)
            scores = lax.dot_general(
                queries, keys, (((1,), (1,)), ((), ())), preferred_element_type=jnp.float32
            )
            half = scores * scale + bias_ref[head] * 0.5
            weights = (half + half * jnp.tanh(half)).astype(jnp.bfloat16)
            sums = jnp.dot(weights, values * valid, preferred_element_type=jnp.float32)
            for i, out_ref in enumerate(out_refs):
                block = sums[i * rows : (i + 1) * rows]
                if i == 0:
                    block = block + base_ref[:, cols]
                out_ref[:, cols] = block.astype(out_ref.dtype)

    return kernel


def attend(queries, history, bias, valid, base, types, part, parts, per_step):
    rows = queries[0].shape[0]
    positions = valid.shape[0]
    width = per_step * HEAD_DIM
    steps = HEADS // parts // per_step
    skip = part * steps
    out_spec = pl.BlockSpec((rows, width), lambda i: (0, i))
    full_spec = pl.BlockSpec((rows, width), lambda i: (0, i + skip))
    heads = HEADS // parts
    return pl.pallas_call(
        make_attend_kernel(len(queries), len(history)),
        grid=(steps,),
        in_specs=[full_spec] * len(queries)
        + [pl.BlockSpec((h.shape[0], width), lambda i: (0, i)) for h in history]
        + [pl.BlockSpec((h.shape[0], width), lambda i: (0, i + steps)) for h in history]
        + [
            pl.BlockSpec((per_step, 1, positions), lambda i: (i + skip, 0, 0)),
            pl.BlockSpec((positions, HEAD_DIM), lambda i: (0, 0)),
            full_spec,
        ],
        out_specs=[out_spec] * len(queries),
        out_shape=[jax.ShapeDtypeStruct((rows, heads * HEAD_DIM), t) for t in types],
        compiler_params=pltpu.CompilerParams(vmem_limit_bytes=56 * 1024 * 1024),
        cost_estimate=pl.CostEstimate(
            flops=4 * len(queries) * rows * positions * heads * HEAD_DIM,
            bytes_accessed=4 * positions * heads * HEAD_DIM,
            transcendentals=len(queries) * rows * positions * heads,
        ),
    )(*queries, *history, *history, bias, valid, base)


def ring_step(blocks, rows=None):
    up, down = blocks
    if rows is not None:
        up, down = up[:rows], down[rows:]
    return shifted(up, "z", 1), shifted(down, "z", -1)


def own_kernel(q_ref, own_ref, self_bias_ref, out_ref):
    width = q_ref.shape[1]
    scale = 0.5 / math.sqrt(HEAD_DIM)
    for head in range(width // HEAD_DIM):
        cols = slice(head * HEAD_DIM, (head + 1) * HEAD_DIM)
        value_cols = slice(width + head * HEAD_DIM, width + (head + 1) * HEAD_DIM)
        product = q_ref[:, cols].astype(jnp.float32) * own_ref[:, cols].astype(jnp.float32)
        half = jnp.sum(product, axis=-1, keepdims=True) * scale + 0.5 * self_bias_ref[0, head]
        weight = (half + half * jnp.tanh(half)).astype(jnp.bfloat16).astype(jnp.float32)
        out_ref[:, cols] = weight * own_ref[:, value_cols].astype(jnp.float32)


def own_term(queries, own, self_bias):
    rows, width = queries.shape
    block = 32
    return pl.pallas_call(
        own_kernel,
        grid=(rows // block,),
        in_specs=[
            pl.BlockSpec((block, width), lambda i: (i, 0)),
            pl.BlockSpec((block, 2 * width), lambda i: (i, 0)),
            pl.BlockSpec(memory_space=pltpu.SMEM),
        ],
        out_specs=pl.BlockSpec((block, width), lambda i: (i, 0)),
        out_shape=jax.ShapeDtypeStruct((rows, width), jnp.float32),
    )(queries, own, self_bias[None])


def finish_kernel(a0_ref, a1_ref, a2_ref, b0_ref, b1_ref, b2_ref, gate_ref, gain_ref, out_ref):
    low = a0_ref[...] + a1_ref[...].astype(jnp.float32) + a2_ref[...].astype(jnp.float32)
    high = b0_ref[...] + b1_ref[...].astype(jnp.float32) + b2_ref[...].astype(jnp.float32)
    total = jnp.concatenate([low, high], axis=-1)
    average = jnp.mean(total, axis=-1, keepdims=True)
    centered = total - average
    variance = jnp.mean(centered * centered, axis=-1, keepdims=True)
    normed = centered * lax.rsqrt(variance + 1e-05) * gain_ref[...]
    out_ref[...] = (normed * gate_ref[...].astype(jnp.float32)).astype(out_ref.dtype)


def finish(low_parts, high_parts, gate, gain):
    rows, width = gate.shape
    block = 64
    row_spec = lambda cols: pl.BlockSpec((block, cols), lambda i: (i, 0))
    return pl.pallas_call(
        finish_kernel,
        grid=(rows // block,),
        in_specs=[row_spec(width // 2)] * 6
        + [row_spec(width), pl.BlockSpec((1, width), lambda i: (0, 0))],
        out_specs=row_spec(width),
        out_shape=jax.ShapeDtypeStruct((rows, width), jnp.bfloat16),
    )(*low_parts, *high_parts, gate, gain[None])


def per_device(
    cand_query,
    cand_kv,
    cand_gate,
    cache_store,
    holders,
    lengths,
    buckets,
    time_bias,
    self_bias,
    norm_gain,
):
    group_index = lax.axis_index(GROUP)
    y_index = lax.axis_index("yhi")
    y_size = lax.axis_size("yhi")
    z_size = lax.axis_size("z")
    groups = lax.axis_size(GROUP)
    slots, _, piece_len, double_width = cache_store.shape
    holding = (holders // slots).reshape(groups, slots)
    slot_of = (holders % slots).reshape(groups, slots)
    mine = holding == group_index
    chosen = jnp.sum(jnp.where(mine, slot_of, 0), axis=1)
    outgoing = cache_store[chosen, 0]
    incoming = lax.all_to_all(outgoing, GROUP, 0, 0, tiled=True)
    pieces = incoming.reshape(slots * piece_len, double_width)
    quarter = double_width // 4
    first, second = (
        jnp.concatenate(
            [pieces[:, i * quarter : (i + 1) * quarter], pieces[:, (i + 2) * quarter : (i + 3) * quarter]],
            axis=1,
        )
        for i in range(2)
    )
    low_history, high_history = [first], [second]
    low_pair, high_pair = (first, first), (second, second)
    for rows in (None, None, None, slots * piece_len // 2):
        low_pair = ring_step(low_pair, rows)
        high_pair = ring_step(high_pair, rows)
        low_history += low_pair
        high_history += high_pair

    own_holding = lax.dynamic_index_in_dim(holding, group_index, 0, keepdims=False)
    arrived = own_holding[None, :] == jnp.arange(groups, dtype=jnp.int32)[:, None]
    piece_of = jnp.sum(jnp.where(arrived, jnp.arange(slots, dtype=jnp.int32)[None, :], 0), axis=1)
    per_y = z_size * slots * piece_len
    bucket_rows = lax.dynamic_slice_in_dim(buckets[0], y_index * per_y, per_y)
    near = (lax.axis_index("z") - jnp.array([0, 1, -1, 2, -2, 3, -3, 4], jnp.int32)) % z_size
    bucket_rows = bucket_rows.reshape(z_size, slots, piece_len)[near[:, None], piece_of[None, :]]
    bucket_rows = bucket_rows.reshape(per_y)
    place = (
        y_index * per_y
        + (near * slots * piece_len)[:, None, None]
        + (piece_of * piece_len)[None, :, None]
        + jnp.arange(piece_len, dtype=jnp.int32)[None, None, :]
    ).reshape(per_y)
    one_hot = (
        bucket_rows[:, None] == jnp.arange(time_bias.shape[0], dtype=jnp.int32)[None, :]
    ).astype(jnp.float32)
    bias = jnp.einsum("kn,nh->hk", one_hot, time_bias, precision=lax.Precision.HIGHEST)
    valid = jnp.broadcast_to(
        (place < lengths[0]).astype(jnp.bfloat16)[:, None], (per_y, HEAD_DIM)
    )

    queries = cand_query[0]
    bias = bias[:, None, :]
    base = own_term(queries, cand_kv[0], self_bias)
    lower, upper, across = (shifted(queries, "yhi", s) for s in (1, -1, 2))
    f32, bf16 = jnp.float32, jnp.bfloat16
    blocks = [queries, lower, upper, across]
    own_low, lower_low, upper_low, far_low = attend(
        blocks, low_history, bias, valid, base, [f32, bf16, f32, bf16], 0, 2, 4
    )
    from_lower = shifted(far_low, "yhi", 1)
    low_1 = shifted(lower_low, "yhi", -1)
    own_high, lower_high, upper_high, far_high = attend(
        blocks, high_history, bias, valid, base, [f32, f32, bf16, bf16], 1, 2, 4
    )
    from_upper = shifted(far_high, "yhi", -1)
    high_1 = shifted(upper_high, "yhi", 1)
    low_2 = shifted((upper_low + from_lower.astype(f32)).astype(bf16), "yhi", 1)
    high_2 = shifted((lower_high + from_upper.astype(f32)).astype(bf16), "yhi", -1)
    return finish(
        (own_low, low_1, low_2), (own_high, high_1, high_2), cand_gate[0], norm_gain
    )[None]


def solution(mesh):
    split = Mesh(mesh.devices.reshape(4, 8, 4, 2, 2), LOOP + GROUP)
    rows = P(GROUP, LOOP, None)
    return jax.shard_map(
        per_device,
        mesh=split,
        in_specs=(
            rows,
            rows,
            rows,
            P(GROUP, LOOP, None, None),
            P(),
            P(GROUP),
            P(GROUP, None),
            P(),
            P(),
            P(),
        ),
        out_specs=rows,
        check_vma=False,
    )
```

time: 158 us -> 176 us (1.11)
  the two profiles are of different devices: /device:TPU:1 before, /device:TPU:6 now
where the time goes in v3:
time: 176 us; the launch traced here: 175 us
  starting transfers between devices  110 us (62%)
  waiting for transfers between devices  35.5 us (20%)
  Pallas kernels  17.2 us (10%)
  local copies, waits for them, and re-layouts  9.55 us (5%)
    ppermute x25, starting transfers between devices, shifted(): lax.ppermute(value, axis, [(i, (i + steps) % count) for i in range(count)])  101 us
    ppermute x25, waiting for transfers between devices, shifted(): lax.ppermute(value, axis, [(i, (i + steps) % count) for i in range(count)])  19.5 us
    all_to_all x1, waiting for transfers between devices, per_device(): incoming = lax.all_to_all(outgoing, GROUP, 0, 0, tiled=True)  16.1 us
    pallas_call x2, Pallas kernels, attend(): pl.pallas_call(make_attend_kernel(len(queries), len(history)), grid=(step...  10.6 us
    all_to_all x1, starting transfers between devices, per_device(): incoming = lax.all_to_all(outgoing, GROUP, 0, 0, tiled=True)  9.42 us
    pallas_call x1, Pallas kernels, own_term(): pl.pallas_call(own_kernel, grid=(rows // block,), in_specs=[pl.BlockSpec(...  3.82 us
  transfers between devices with their start and end apart: 26, of which 10 were waited for; matrix products, arithmetic and copies ran while one was open for 4% of the time, Pallas kernels for 8%

profile of v3, /device:TPU:6, one launch (start us, length us, event | category | flops | bytes accessed | tf_op | source)
XLA Modules:
  0.0 174.9 jit_solution(4197377741427327288)
XLA Ops:
  2.8 9.4 %all-to-all-start = ((bf16[16,4,4096]{2,1,0:T(4,128)(2,1)}), bf16[16,4,4096]{2,1,0:T(4,128)(2,1)S(1)}, u32[]{:S(2)}, u32[]{:S(2)}) async-start(bf16[16,4,4096]{2,1,0:T(4,128)(2,1)} %gather_fusion), calls=%async_computation | async-start | bytes 1048576 | tf_op jit(solution)/shard_map/all_to_all | solution.py:166
  14.2 16.1 %all-to-all-done = bf16[16,4,4096]{2,1,0:T(4,128)(2,1)S(1)} async-done(((bf16[16,4,4096]{2,1,0:T(4,128)(2,1)}), bf16[16,4,4096]{2,1,0:T(4,128)(2,1)S(1)}, u32[]{:S(2)}, u32[]{:S(2)}) %all-to-all-start) | async-done | bytes 524320 | tf_op jit(solution)/shard_map/all_to_all | solution.py:166
  32.5 7.6 %collective-permute-start.15 = (bf16[64,2048]{1,0:T(8,128)(2,1)S(1)}, bf16[64,2048]{1,0:T(8,128)(2,1)}, u32[]{:S(2)}, u32[]{:S(2)}) collective-permute-start(bf16[64,2048]{1,0:T(8,128)(2,1)S(1)} %pad_maximum_fusion.1.refs_4_.refs_13_), channel_id=1, source_target_pairs={{0,112},{16,0},{32,16},{48,32},{64,48},{80,64},{96,80},{112,96},{1... | collective-permute-start | bytes 786440 | tf_op jit(solution)/shard_map/ppermute | solution.py:19
  40.2 3.9 %collective-permute-start.4 = (bf16[64,2048]{1,0:T(8,128)(2,1)S(1)}, bf16[64,2048]{1,0:T(8,128)(2,1)S(1)}, u32[]{:S(2)}, u32[]{:S(2)}) collective-permute-start(bf16[64,2048]{1,0:T(8,128)(2,1)S(1)} %pad_maximum_fusion.refs_4_.refs_13_), channel_id=1, source_target_pairs={{0,112},{16,0},{32,16},{48,32},{64,48},{80,64},{96,80},{112,96},{1... | collective-permute-start | bytes 786440 | tf_op jit(solution)/shard_map/ppermute | solution.py:19
  49.1 5.1 %collective-permute-start.17 = (bf16[64,2048]{1,0:T(8,128)(2,1)}, bf16[64,2048]{1,0:T(8,128)(2,1)}, u32[]{:S(2)}, u32[]{:S(2)}) collective-permute-start(bf16[64,2048]{1,0:T(8,128)(2,1)} %collective-permute-done.15.refs_6_.refs_15_), channel_id=1, source_target_pairs={{0,112},{16,0},{32,16},{48,32},{64,48},{80,64},{96,80},{112,96},{1... | collective-permute-start | bytes 786440 | tf_op jit(solution)/shard_map/ppermute | solution.py:19
  54.3 3.9 %collective-permute-start.6 = (bf16[64,2048]{1,0:T(8,128)(2,1)S(1)}, bf16[64,2048]{1,0:T(8,128)(2,1)}, u32[]{:S(2)}, u32[]{:S(2)}) collective-permute-start(bf16[64,2048]{1,0:T(8,128)(2,1)S(1)} %collective-permute-done.4.refs_6_.refs_15_), channel_id=1, source_target_pairs={{0,112},{16,0},{32,16},{48,32},{64,48},{80,64},{96,80},{112,96},{1... | collective-permute-start | bytes 786440 | tf_op jit(solution)/shard_map/ppermute | solution.py:19
  60.2 4.4 %collective-permute-start.1 = (bf16[128,2048]{1,0:T(8,128)(2,1)S(1)}, bf16[128,2048]{1,0:T(8,128)(2,1)S(1)}, u32[]{:S(2)}, u32[]{:S(2)}) collective-permute-start(bf16[128,2048]{1,0:T(8,128)(2,1)S(1)} %bitcast.23), channel_id=1, source_target_pairs={{0,384},{128,0},{256,128},{384,256},{1,385},{129,1},{257,129},{385... | collective-permute-start | bytes 1572872 | tf_op jit(solution)/shard_map/ppermute | solution.py:19
  67.0 4.7 %collective-permute-start.2 = (bf16[128,2048]{1,0:T(8,128)(2,1)S(1)}, bf16[128,2048]{1,0:T(8,128)(2,1)S(1)}, u32[]{:S(2)}, u32[]{:S(2)}) collective-permute-start(bf16[128,2048]{1,0:T(8,128)(2,1)S(1)} %bitcast.24), channel_id=1, source_target_pairs={{0,256},{128,384},{256,0},{384,128},{1,257},{129,385},{257,1},{385... | collective-permute-start | bytes 1572872 | tf_op jit(solution)/shard_map/ppermute | solution.py:19
  73.7 5.1 %collective-permute-start.19 = (bf16[64,2048]{1,0:T(8,128)(2,1)}, bf16[64,2048]{1,0:T(8,128)(2,1)S(1)}, u32[]{:S(2)}, u32[]{:S(2)}) collective-permute-start(bf16[64,2048]{1,0:T(8,128)(2,1)} %collective-permute-done.17.refs_8_.refs_17_), channel_id=1, source_target_pairs={{0,112},{16,0},{32,16},{48,32},{64,48},{80,64},{96,80},{112,96},{1... | collective-permute-start | bytes 786440 | tf_op jit(solution)/shard_map/ppermute | solution.py:19
  81.3 3.7 %collective-permute-start.8 = (bf16[64,2048]{1,0:T(8,128)(2,1)}, bf16[64,2048]{1,0:T(8,128)(2,1)S(1)}, u32[]{:S(2)}, u32[]{:S(2)}) collective-permute-start(bf16[64,2048]{1,0:T(8,128)(2,1)} %collective-permute-done.6.refs_8_.refs_17_), channel_id=1, source_target_pairs={{0,112},{16,0},{32,16},{48,32},{64,48},{80,64},{96,80},{112,96},{1... | collective-permute-start | bytes 786440 | tf_op jit(solution)/shard_map/ppermute | solution.py:19
  85.0 3.8 %collective-permute-start.7 = (bf16[64,2048]{1,0:T(8,128)(2,1)}, bf16[64,2048]{1,0:T(8,128)(2,1)S(1)}, u32[]{:S(2)}, u32[]{:S(2)}) collective-permute-start(bf16[64,2048]{1,0:T(8,128)(2,1)} %collective-permute-done.5.refs_7_.refs_16_), channel_id=1, source_target_pairs={{0,16},{16,32},{32,48},{48,64},{64,80},{80,96},{96,112},{112,0},{1... | collective-permute-start | bytes 786440 | tf_op jit(solution)/shard_map/ppermute | solution.py:19
  89.5 3.3 %collective-permute-start.20 = (bf16[32,2048]{1,0:T(8,128)(2,1)}, bf16[32,2048]{1,0:T(8,128)(2,1)S(1)}, u32[]{:S(2)}, u32[]{:S(2)}) collective-permute-start(bf16[32,2048]{1,0:T(8,128)(2,1)} %slice.42), channel_id=1, source_target_pairs={{0,16},{16,32},{32,48},{48,64},{64,80},{80,96},{96,112},{112,0},{1... | collective-permute-start | bytes 393224 | tf_op jit(solution)/shard_map/ppermute | solution.py:19
  92.8 3.8 %collective-permute-start.21 = (bf16[32,2048]{1,0:T(8,128)(2,1)}, bf16[32,2048]{1,0:T(8,128)(2,1)S(1)}, u32[]{:S(2)}, u32[]{:S(2)}) collective-permute-start(bf16[32,2048]{1,0:T(8,128)(2,1)} %slice.43), channel_id=1, source_target_pairs={{0,112},{16,0},{32,16},{48,32},{64,48},{80,64},{96,80},{112,96},{1... | collective-permute-start | bytes 393224 | tf_op jit(solution)/shard_map/ppermute | solution.py:19
  96.8 3.8 %shard_map.109.refs_24_ = f32[128,2048]{1,0:T(8,128)} custom-call(bf16[128,2048]{1,0:T(8,128)(2,1)} %bitcast.19, bf16[128,4096]{1,0:T(8,128)(2,1)} %bitcast.25, f32[1,16]{1,0:T(1,128)} %bitcast.28), custom_call_target="tpu_custom_call" | custom-call | tf_op jit(solution)/shard_map/pallas_call | solution.py:105
  101.6 5.3 %shard_map.111 = (f32[128,1024]{1,0:T(8,128)}, f32[128,1024]{1,0:T(8,128)}, bf16[128,1024]{1,0:T(8,128)(2,1)}, bf16[128,1024]{1,0:T(8,128)(2,1)}) custom-call(bf16[128,2048]{1,0:T(8,128)(2,1)} %bitcast.20, bf16[128,2048]{1,0:T(8,128)(2,1)} %copy-done.4, bf16[128,2048]{1,0:T(8,128)(2,1)} %copy-done.5, bf16[128,2048]{1,0:T(8,128)(2,1)} %copy-done.6, ...), custom_call_target="tpu_custom_call" | custom-call | flops 1073741824 | bytes 2097152 | tf_op jit(solution)/shard_map/pallas_call | solution.py:61
  106.9 15.5 %collective-permute-start.23 = (bf16[128,1024]{1,0:T(8,128)(2,1)}, bf16[128,1024]{1,0:T(8,128)(2,1)S(1)}, u32[]{:S(2)}, u32[]{:S(2)}) collective-permute-start(bf16[128,1024]{1,0:T(8,128)(2,1)} %get-tuple-element.20), channel_id=1, source_target_pairs={{0,384},{128,0},{256,128},{384,256},{1,385},{129,1},{257,129},{385... | collective-permute-start | bytes 786440 | tf_op jit(solution)/shard_map/ppermute | solution.py:19
  122.4 4.6 %collective-permute-start.10 = (bf16[32,2048]{1,0:T(8,128)(2,1)S(1)}, bf16[32,2048]{1,0:T(8,128)(2,1)S(1)}, u32[]{:S(2)}, u32[]{:S(2)}) collective-permute-start(bf16[32,2048]{1,0:T(8,128)(2,1)S(1)} %slice.39), channel_id=1, source_target_pairs={{0,112},{16,0},{32,16},{48,32},{64,48},{80,64},{96,80},{112,96},{1... | collective-permute-start | bytes 393224 | tf_op jit(solution)/shard_map/ppermute | solution.py:19
  129.6 5.8 %collective-permute-done.9.refs_11_.refs_20_ = bf16[32,2048]{1,0:T(8,128)(2,1)S(1)} collective-permute-done((bf16[32,2048]{1,0:T(8,128)(2,1)S(1)}, bf16[32,2048]{1,0:T(8,128)(2,1)S(1)}, u32[]{:S(2)}, u32[]{:S(2)}) %collective-permute-start.9) | collective-permute-done | bytes 131104 | tf_op jit(solution)/shard_map/ppermute | solution.py:19
  136.0 5.3 %shard_map.110 = (f32[128,1024]{1,0:T(8,128)}, bf16[128,1024]{1,0:T(8,128)(2,1)}, f32[128,1024]{1,0:T(8,128)}, bf16[128,1024]{1,0:T(8,128)(2,1)}) custom-call(bf16[128,2048]{1,0:T(8,128)(2,1)} %bitcast.21, bf16[128,2048]{1,0:T(8,128)(2,1)} %copy-done.4, bf16[128,2048]{1,0:T(8,128)(2,1)} %copy-done.5, bf16[128,2048]{1,0:T(8,128)(2,1)} %copy-done.6, ...), custom_call_target="tpu_custom_call" | custom-call | flops 1073741824 | bytes 2097152 | tf_op jit(solution)/shard_map/pallas_call | solution.py:61
  143.3 4.4 %collective-permute-start.22 = (bf16[128,1024]{1,0:T(8,128)(2,1)S(1)}, bf16[128,1024]{1,0:T(8,128)(2,1)S(1)}, u32[]{:S(2)}, u32[]{:S(2)}) collective-permute-start(bf16[128,1024]{1,0:T(8,128)(2,1)S(1)} %copy-done.26), channel_id=1, source_target_pairs={{0,128},{128,256},{256,384},{384,0},{1,129},{129,257},{257,385},{3... | collective-permute-start | bytes 786440 | tf_op jit(solution)/shard_map/ppermute | solution.py:19
  147.7 3.5 %collective-permute-start.11 = (bf16[128,1024]{1,0:T(8,128)(2,1)}, bf16[128,1024]{1,0:T(8,128)(2,1)S(1)}, u32[]{:S(2)}, u32[]{:S(2)}) collective-permute-start(bf16[128,1024]{1,0:T(8,128)(2,1)} %get-tuple-element.14), channel_id=1, source_target_pairs={{0,384},{128,0},{256,128},{384,256},{1,385},{129,1},{257,129},{385... | collective-permute-start | bytes 786440 | tf_op jit(solution)/shard_map/ppermute | solution.py:19
  151.3 5.0 %collective-permute-start.24 = (bf16[128,1024]{1,0:T(8,128)(2,1)S(1)}, bf16[128,1024]{1,0:T(8,128)(2,1)S(1)}, u32[]{:S(2)}, u32[]{:S(2)}) collective-permute-start(bf16[128,1024]{1,0:T(8,128)(2,1)S(1)} %add_convert_fusion), channel_id=1, source_target_pairs={{0,384},{128,0},{256,128},{384,256},{1,385},{129,1},{257,129},{385... | collective-permute-start | bytes 786440 | tf_op jit(solution)/shard_map/ppermute | solution.py:19
  156.3 3.8 %collective-permute-done.12 = bf16[128,1024]{1,0:T(8,128)(2,1)S(1)} collective-permute-done((bf16[128,1024]{1,0:T(8,128)(2,1)}, bf16[128,1024]{1,0:T(8,128)(2,1)S(1)}, u32[]{:S(2)}, u32[]{:S(2)}) %collective-permute-start.12) | collective-permute-done | bytes 262176 | tf_op jit(solution)/shard_map/ppermute | solution.py:19
  168.1 3.4 %collective-permute-done.13.a2_ref = bf16[128,1024]{1,0:T(8,128)(2,1)S(1)} collective-permute-done((bf16[128,1024]{1,0:T(8,128)(2,1)S(1)}, bf16[128,1024]{1,0:T(8,128)(2,1)S(1)}, u32[]{:S(2)}, u32[]{:S(2)}) %collective-permute-start.13) | collective-permute-done | bytes 262176 | tf_op jit(solution)/shard_map/ppermute | solution.py:19
  (121 shorter events, 38.3 us)
Async XLA Ops:
  2.8 27.4 %all-to-all-start = ((bf16[16,4,4096]{2,1,0:T(4,128)(2,1)}), bf16[16,4,4096]{2,1,0:T(4,128)(2,1)S(1)}, u32[]{:S(2)}, u32[]{:S(2)}) async-start(bf16[16,4,4096]{2,1,0:T(4,128)(2,1)} %gather_fusion), calls=%async_computation | async-start | bytes 1048576 | tf_op jit(solution)/shard_map/all_to_all | solution.py:166
  12.2 77.2 %collective-permute-start = (bf16[128,2048]{1,0:T(8,128)(2,1)S(1)}, bf16[128,2048]{1,0:T(8,128)(2,1)S(1)}, u32[]{:S(2)}, u32[]{:S(2)}) collective-permute-start(bf16[128,2048]{1,0:T(8,128)(2,1)S(1)} %bitcast.22), channel_id=1, source_target_pairs={{0,128},{128,256},{256,384},{384,0},{1,129},{129,257},{257,385},{3... | collective-permute-start | bytes 1572872 | tf_op jit(solution)/shard_map/ppermute | solution.py:19
  30.5 14.8 %collective-permute-start.14 = (bf16[64,2048]{1,0:T(8,128)(2,1)S(1)}, bf16[64,2048]{1,0:T(8,128)(2,1)S(1)}, u32[]{:S(2)}, u32[]{:S(2)}) collective-permute-start(bf16[64,2048]{1,0:T(8,128)(2,1)S(1)} %pad_maximum_fusion.1.refs_4_.refs_13_), channel_id=1, source_target_pairs={{0,16},{16,32},{32,48},{48,64},{64,80},{80,96},{96,112},{112,0},{1... | collective-permute-start | bytes 786440 | tf_op jit(solution)/shard_map/ppermute | solution.py:19
  32.5 16.6 %collective-permute-start.15 = (bf16[64,2048]{1,0:T(8,128)(2,1)S(1)}, bf16[64,2048]{1,0:T(8,128)(2,1)}, u32[]{:S(2)}, u32[]{:S(2)}) collective-permute-start(bf16[64,2048]{1,0:T(8,128)(2,1)S(1)} %pad_maximum_fusion.1.refs_4_.refs_13_), channel_id=1, source_target_pairs={{0,112},{16,0},{32,16},{48,32},{64,48},{80,64},{96,80},{112,96},{1... | collective-permute-start | bytes 786440 | tf_op jit(solution)/shard_map/ppermute | solution.py:19
  40.2 14.1 %collective-permute-start.4 = (bf16[64,2048]{1,0:T(8,128)(2,1)S(1)}, bf16[64,2048]{1,0:T(8,128)(2,1)S(1)}, u32[]{:S(2)}, u32[]{:S(2)}) collective-permute-start(bf16[64,2048]{1,0:T(8,128)(2,1)S(1)} %pad_maximum_fusion.refs_4_.refs_13_), channel_id=1, source_target_pairs={{0,112},{16,0},{32,16},{48,32},{64,48},{80,64},{96,80},{112,96},{1... | collective-permute-start | bytes 786440 | tf_op jit(solution)/shard_map/ppermute | solution.py:19
  45.2 13.0 %collective-permute-start.16 = (bf16[64,2048]{1,0:T(8,128)(2,1)S(1)}, bf16[64,2048]{1,0:T(8,128)(2,1)}, u32[]{:S(2)}, u32[]{:S(2)}) collective-permute-start(bf16[64,2048]{1,0:T(8,128)(2,1)S(1)} %collective-permute-done.14.refs_5_.refs_14_), channel_id=1, source_target_pairs={{0,16},{16,32},{32,48},{48,64},{64,80},{80,96},{96,112},{112,0},{1... | collective-permute-start | bytes 786440 | tf_op jit(solution)/shard_map/ppermute | solution.py:19
  47.2 13.0 %collective-permute-start.3 = (bf16[64,2048]{1,0:T(8,128)(2,1)S(1)}, bf16[64,2048]{1,0:T(8,128)(2,1)S(1)}, u32[]{:S(2)}, u32[]{:S(2)}) collective-permute-start(bf16[64,2048]{1,0:T(8,128)(2,1)S(1)} %pad_maximum_fusion.refs_4_.refs_13_), channel_id=1, source_target_pairs={{0,16},{16,32},{32,48},{48,64},{64,80},{80,96},{96,112},{112,0},{1... | collective-permute-start | bytes 786440 | tf_op jit(solution)/shard_map/ppermute | solution.py:19
  49.1 17.9 %collective-permute-start.17 = (bf16[64,2048]{1,0:T(8,128)(2,1)}, bf16[64,2048]{1,0:T(8,128)(2,1)}, u32[]{:S(2)}, u32[]{:S(2)}) collective-permute-start(bf16[64,2048]{1,0:T(8,128)(2,1)} %collective-permute-done.15.refs_6_.refs_15_), channel_id=1, source_target_pairs={{0,112},{16,0},{32,16},{48,32},{64,48},{80,64},{96,80},{112,96},{1... | collective-permute-start | bytes 786440 | tf_op jit(solution)/shard_map/ppermute | solution.py:19
  54.3 17.4 %collective-permute-start.6 = (bf16[64,2048]{1,0:T(8,128)(2,1)S(1)}, bf16[64,2048]{1,0:T(8,128)(2,1)}, u32[]{:S(2)}, u32[]{:S(2)}) collective-permute-start(bf16[64,2048]{1,0:T(8,128)(2,1)S(1)} %collective-permute-done.4.refs_6_.refs_15_), channel_id=1, source_target_pairs={{0,112},{16,0},{32,16},{48,32},{64,48},{80,64},{96,80},{112,96},{1... | collective-permute-start | bytes 786440 | tf_op jit(solution)/shard_map/ppermute | solution.py:19
  58.2 15.4 %collective-permute-start.18 = (bf16[64,2048]{1,0:T(8,128)(2,1)}, bf16[64,2048]{1,0:T(8,128)(2,1)S(1)}, u32[]{:S(2)}, u32[]{:S(2)}) collective-permute-start(bf16[64,2048]{1,0:T(8,128)(2,1)} %collective-permute-done.16.refs_7_.refs_16_), channel_id=1, source_target_pairs={{0,16},{16,32},{32,48},{48,64},{64,80},{80,96},{96,112},{112,0},{1... | collective-permute-start | bytes 786440 | tf_op jit(solution)/shard_map/ppermute | solution.py:19
  60.2 32.6 %collective-permute-start.1 = (bf16[128,2048]{1,0:T(8,128)(2,1)S(1)}, bf16[128,2048]{1,0:T(8,128)(2,1)S(1)}, u32[]{:S(2)}, u32[]{:S(2)}) collective-permute-start(bf16[128,2048]{1,0:T(8,128)(2,1)S(1)} %bitcast.23), channel_id=1, source_target_pairs={{0,384},{128,0},{256,128},{384,256},{1,385},{129,1},{257,129},{385... | collective-permute-start | bytes 1572872 | tf_op jit(solution)/shard_map/ppermute | solution.py:19
  67.0 33.6 %collective-permute-start.2 = (bf16[128,2048]{1,0:T(8,128)(2,1)S(1)}, bf16[128,2048]{1,0:T(8,128)(2,1)S(1)}, u32[]{:S(2)}, u32[]{:S(2)}) collective-permute-start(bf16[128,2048]{1,0:T(8,128)(2,1)S(1)} %bitcast.24), channel_id=1, source_target_pairs={{0,256},{128,384},{256,0},{384,128},{1,257},{129,385},{257,1},{385... | collective-permute-start | bytes 1572872 | tf_op jit(solution)/shard_map/ppermute | solution.py:19
  71.7 9.6 %collective-permute-start.5 = (bf16[64,2048]{1,0:T(8,128)(2,1)S(1)}, bf16[64,2048]{1,0:T(8,128)(2,1)}, u32[]{:S(2)}, u32[]{:S(2)}) collective-permute-start(bf16[64,2048]{1,0:T(8,128)(2,1)S(1)} %collective-permute-done.3.refs_5_.refs_14_), channel_id=1, source_target_pairs={{0,16},{16,32},{32,48},{48,64},{64,80},{80,96},{96,112},{112,0},{1... | collective-permute-start | bytes 786440 | tf_op jit(solution)/shard_map/ppermute | solution.py:19
  73.7 11.3 %collective-permute-start.19 = (bf16[64,2048]{1,0:T(8,128)(2,1)}, bf16[64,2048]{1,0:T(8,128)(2,1)S(1)}, u32[]{:S(2)}, u32[]{:S(2)}) collective-permute-start(bf16[64,2048]{1,0:T(8,128)(2,1)} %collective-permute-done.17.refs_8_.refs_17_), channel_id=1, source_target_pairs={{0,112},{16,0},{32,16},{48,32},{64,48},{80,64},{96,80},{112,96},{1... | collective-permute-start | bytes 786440 | tf_op jit(solution)/shard_map/ppermute | solution.py:19
  81.3 41.1 %collective-permute-start.8 = (bf16[64,2048]{1,0:T(8,128)(2,1)}, bf16[64,2048]{1,0:T(8,128)(2,1)S(1)}, u32[]{:S(2)}, u32[]{:S(2)}) collective-permute-start(bf16[64,2048]{1,0:T(8,128)(2,1)} %collective-permute-done.6.refs_8_.refs_17_), channel_id=1, source_target_pairs={{0,112},{16,0},{32,16},{48,32},{64,48},{80,64},{96,80},{112,96},{1... | collective-permute-start | bytes 786440 | tf_op jit(solution)/shard_map/ppermute | solution.py:19
  85.0 42.1 %collective-permute-start.7 = (bf16[64,2048]{1,0:T(8,128)(2,1)}, bf16[64,2048]{1,0:T(8,128)(2,1)S(1)}, u32[]{:S(2)}, u32[]{:S(2)}) collective-permute-start(bf16[64,2048]{1,0:T(8,128)(2,1)} %collective-permute-done.5.refs_7_.refs_16_), channel_id=1, source_target_pairs={{0,16},{16,32},{32,48},{48,64},{64,80},{80,96},{96,112},{112,0},{1... | collective-permute-start | bytes 786440 | tf_op jit(solution)/shard_map/ppermute | solution.py:19
  89.5 11.2 %collective-permute-start.20 = (bf16[32,2048]{1,0:T(8,128)(2,1)}, bf16[32,2048]{1,0:T(8,128)(2,1)S(1)}, u32[]{:S(2)}, u32[]{:S(2)}) collective-permute-start(bf16[32,2048]{1,0:T(8,128)(2,1)} %slice.42), channel_id=1, source_target_pairs={{0,16},{16,32},{32,48},{48,64},{64,80},{80,96},{96,112},{112,0},{1... | collective-permute-start | bytes 393224 | tf_op jit(solution)/shard_map/ppermute | solution.py:19
  106.9 44.3 %collective-permute-start.23 = (bf16[128,1024]{1,0:T(8,128)(2,1)}, bf16[128,1024]{1,0:T(8,128)(2,1)S(1)}, u32[]{:S(2)}, u32[]{:S(2)}) collective-permute-start(bf16[128,1024]{1,0:T(8,128)(2,1)} %get-tuple-element.20), channel_id=1, source_target_pairs={{0,384},{128,0},{256,128},{384,256},{1,385},{129,1},{257,129},{385... | collective-permute-start | bytes 786440 | tf_op jit(solution)/shard_map/ppermute | solution.py:19
  127.2 8.2 %collective-permute-start.9 = (bf16[32,2048]{1,0:T(8,128)(2,1)S(1)}, bf16[32,2048]{1,0:T(8,128)(2,1)S(1)}, u32[]{:S(2)}, u32[]{:S(2)}) collective-permute-start(bf16[32,2048]{1,0:T(8,128)(2,1)S(1)} %slice.38), channel_id=1, source_target_pairs={{0,16},{16,32},{32,48},{48,64},{64,80},{80,96},{96,112},{112,0},{1... | collective-permute-start | bytes 393224 | tf_op jit(solution)/shard_map/ppermute | solution.py:19
  141.3 18.8 %collective-permute-start.12 = (bf16[128,1024]{1,0:T(8,128)(2,1)}, bf16[128,1024]{1,0:T(8,128)(2,1)S(1)}, u32[]{:S(2)}, u32[]{:S(2)}) collective-permute-start(bf16[128,1024]{1,0:T(8,128)(2,1)} %get-tuple-element.16), channel_id=1, source_target_pairs={{0,128},{128,256},{256,384},{384,0},{1,129},{129,257},{257,385},{3... | collective-permute-start | bytes 786440 | tf_op jit(solution)/shard_map/ppermute | solution.py:19
  143.3 20.8 %collective-permute-start.22 = (bf16[128,1024]{1,0:T(8,128)(2,1)S(1)}, bf16[128,1024]{1,0:T(8,128)(2,1)S(1)}, u32[]{:S(2)}, u32[]{:S(2)}) collective-permute-start(bf16[128,1024]{1,0:T(8,128)(2,1)S(1)} %copy-done.26), channel_id=1, source_target_pairs={{0,128},{128,256},{256,384},{384,0},{1,129},{129,257},{257,385},{3... | collective-permute-start | bytes 786440 | tf_op jit(solution)/shard_map/ppermute | solution.py:19
  147.7 17.5 %collective-permute-start.11 = (bf16[128,1024]{1,0:T(8,128)(2,1)}, bf16[128,1024]{1,0:T(8,128)(2,1)S(1)}, u32[]{:S(2)}, u32[]{:S(2)}) collective-permute-start(bf16[128,1024]{1,0:T(8,128)(2,1)} %get-tuple-element.14), channel_id=1, source_target_pairs={{0,384},{128,0},{256,128},{384,256},{1,385},{129,1},{257,129},{385... | collective-permute-start | bytes 786440 | tf_op jit(solution)/shard_map/ppermute | solution.py:19
  151.3 16.7 %collective-permute-start.24 = (bf16[128,1024]{1,0:T(8,128)(2,1)S(1)}, bf16[128,1024]{1,0:T(8,128)(2,1)S(1)}, u32[]{:S(2)}, u32[]{:S(2)}) collective-permute-start(bf16[128,1024]{1,0:T(8,128)(2,1)S(1)} %add_convert_fusion), channel_id=1, source_target_pairs={{0,384},{128,0},{256,128},{384,256},{1,385},{129,1},{257,129},{385... | collective-permute-start | bytes 786440 | tf_op jit(solution)/shard_map/ppermute | solution.py:19
  160.2 11.3 %collective-permute-start.13 = (bf16[128,1024]{1,0:T(8,128)(2,1)S(1)}, bf16[128,1024]{1,0:T(8,128)(2,1)S(1)}, u32[]{:S(2)}, u32[]{:S(2)}) collective-permute-start(bf16[128,1024]{1,0:T(8,128)(2,1)S(1)} %add_convert_fusion.1), channel_id=1, source_target_pairs={{0,128},{128,256},{256,384},{384,0},{1,129},{129,257},{257,385},{3... | collective-permute-start | bytes 786440 | tf_op jit(solution)/shard_map/ppermute | solution.py:19
  (30 other events, 247.0 us)

commit v4 on v3

--- a/solution.py
+++ b/solution.py
@@ -19,27 +19,26 @@
     return lax.ppermute(value, axis, [(i, (i + steps) % count) for i in range(count)])
 
 
-def make_attend_kernel(blocks, pieces):
+def make_attend_kernel(blocks):
     def kernel(*refs):
         q_refs = refs[:blocks]
-        k_refs = refs[blocks : blocks + pieces]
-        v_refs = refs[blocks + pieces : blocks + 2 * pieces]
-        bias_ref, valid_ref, base_ref = refs[blocks + 2 * pieces : blocks + 2 * pieces + 3]
-        out_refs = refs[blocks + 2 * pieces + 3 :]
+        k_ref, v_ref, bias_ref, valid_ref, base_ref = refs[blocks : blocks + 5]
+        out_refs = refs[blocks + 5 :]
         rows = q_refs[0].shape[0]
         scale = 0.5 / math.sqrt(HEAD_DIM)
         valid = valid_ref[...]
         for head in range(bias_ref.shape[0]):
             cols = slice(head * HEAD_DIM, (head + 1) * HEAD_DIM)
             queries = jnp.concatenate([q_ref[:, cols] for q_ref in q_refs], axis=0)
-            keys = jnp.concatenate([k_ref[:, cols] for k_ref in k_refs], axis=0)
-            values = jnp.concatenate([v_ref[:, cols] for v_ref in v_refs], axis=0)
             scores = lax.dot_general(
-                queries, keys, (((1,), (1,)), ((), ())), preferred_element_type=jnp.float32
+                queries,
+                k_ref[:, cols],
+                (((1,), (1,)), ((), ())),
+                preferred_element_type=jnp.float32,
             )
             half = scores * scale + bias_ref[head] * 0.5
             weights = (half + half * jnp.tanh(half)).astype(jnp.bfloat16)
-            sums = jnp.dot(weights, values * valid, preferred_element_type=jnp.float32)
+            sums = jnp.dot(weights, v_ref[:, cols] * valid, preferred_element_type=jnp.float32)
             for i, out_ref in enumerate(out_refs):
                 block = sums[i * rows : (i + 1) * rows]
                 if i == 0:
@@ -53,18 +52,19 @@
     rows = queries[0].shape[0]
     positions = valid.shape[0]
     width = per_step * HEAD_DIM
-    steps = HEADS // parts // per_step
+    heads = HEADS // parts
+    steps = heads // per_step
     skip = part * steps
+    all_steps = HEADS // per_step
     out_spec = pl.BlockSpec((rows, width), lambda i: (0, i))
     full_spec = pl.BlockSpec((rows, width), lambda i: (0, i + skip))
-    heads = HEADS // parts
     return pl.pallas_call(
-        make_attend_kernel(len(queries), len(history)),
+        make_attend_kernel(len(queries)),
         grid=(steps,),
         in_specs=[full_spec] * len(queries)
-        + [pl.BlockSpec((h.shape[0], width), lambda i: (0, i)) for h in history]
-        + [pl.BlockSpec((h.shape[0], width), lambda i: (0, i + steps)) for h in history]
         + [
+            pl.BlockSpec((positions, width), lambda i: (0, i + skip)),
+            pl.BlockSpec((positions, width), lambda i: (0, i + skip + all_steps)),
             pl.BlockSpec((per_step, 1, positions), lambda i: (i + skip, 0, 0)),
             pl.BlockSpec((positions, HEAD_DIM), lambda i: (0, 0)),
             full_spec,
@@ -77,14 +77,7 @@
             bytes_accessed=4 * positions * heads * HEAD_DIM,
             transcendentals=len(queries) * rows * positions * heads,
         ),
-    )(*queries, *history, *history, bias, valid, base)
-
-
-def ring_step(blocks, rows=None):
-    up, down = blocks
-    if rows is not None:
-        up, down = up[:rows], down[rows:]
-    return shifted(up, "z", 1), shifted(down, "z", -1)
+    )(*queries, history, history, bias, valid, base)
 
 
 def own_kernel(q_ref, own_ref, self_bias_ref, out_ref):
@@ -165,33 +158,17 @@
     outgoing = cache_store[chosen, 0]
     incoming = lax.all_to_all(outgoing, GROUP, 0, 0, tiled=True)
     pieces = incoming.reshape(slots * piece_len, double_width)
-    quarter = double_width // 4
-    first, second = (
-        jnp.concatenate(
-            [pieces[:, i * quarter : (i + 1) * quarter], pieces[:, (i + 2) * quarter : (i + 3) * quarter]],
-            axis=1,
-        )
-        for i in range(2)
-    )
-    low_history, high_history = [first], [second]
-    low_pair, high_pair = (first, first), (second, second)
-    for rows in (None, None, None, slots * piece_len // 2):
-        low_pair = ring_step(low_pair, rows)
-        high_pair = ring_step(high_pair, rows)
-        low_history += low_pair
-        high_history += high_pair
+    history = lax.all_gather(pieces, "z", tiled=True)
 
     own_holding = lax.dynamic_index_in_dim(holding, group_index, 0, keepdims=False)
     arrived = own_holding[None, :] == jnp.arange(groups, dtype=jnp.int32)[:, None]
     piece_of = jnp.sum(jnp.where(arrived, jnp.arange(slots, dtype=jnp.int32)[None, :], 0), axis=1)
     per_y = z_size * slots * piece_len
     bucket_rows = lax.dynamic_slice_in_dim(buckets[0], y_index * per_y, per_y)
-    near = (lax.axis_index("z") - jnp.array([0, 1, -1, 2, -2, 3, -3, 4], jnp.int32)) % z_size
-    bucket_rows = bucket_rows.reshape(z_size, slots, piece_len)[near[:, None], piece_of[None, :]]
-    bucket_rows = bucket_rows.reshape(per_y)
+    bucket_rows = bucket_rows.reshape(z_size, slots, piece_len)[:, piece_of].reshape(per_y)
     place = (
         y_index * per_y
-        + (near * slots * piece_len)[:, None, None]
+        + (jnp.arange(z_size, dtype=jnp.int32) * slots * piece_len)[:, None, None]
         + (piece_of * piece_len)[None, :, None]
         + jnp.arange(piece_len, dtype=jnp.int32)[None, None, :]
     ).reshape(per_y)
@@ -210,12 +187,12 @@
     f32, bf16 = jnp.float32, jnp.bfloat16
     blocks = [queries, lower, upper, across]
     own_low, lower_low, upper_low, far_low = attend(
-        blocks, low_history, bias, valid, base, [f32, bf16, f32, bf16], 0, 2, 4
+        blocks, history, bias, valid, base, [f32, bf16, f32, bf16], 0, 2, 4
     )
     from_lower = shifted(far_low, "yhi", 1)
     low_1 = shifted(lower_low, "yhi", -1)
     own_high, lower_high, upper_high, far_high = attend(
-        blocks, high_history, bias, valid, base, [f32, f32, bf16, bf16], 1, 2, 4
+        blocks, history, bias, valid, base, [f32, f32, bf16, bf16], 1, 2, 4
     )
     from_upper = shifted(far_high, "yhi", -1)
     high_1 = shifted(upper_high, "yhi", 1)

time: 176 us -> 156 us (0.89)
  the two profiles are of different devices: /device:TPU:6 before, /device:TPU:20 now
where the time goes in v4:
time: 156 us; the launch traced here: 155 us
  waiting for transfers between devices  65.6 us (42%)
  starting transfers between devices  34.6 us (22%)
  Pallas kernels  17.6 us (11%)
  between operations  14.3 us (9%)
  blocking collectives  13.9 us (9%)
  local copies, waits for them, and re-layouts  6.25 us (4%)
  other arithmetic  2.3 us (1%)
    ppermute x9, waiting for transfers between devices, shifted(): lax.ppermute(value, axis, [(i, (i + steps) % count) for i in range(count)])  59.8 us
    ppermute x9, starting transfers between devices, shifted(): lax.ppermute(value, axis, [(i, (i + steps) % count) for i in range(count)])  34.6 us
    all_to_all x1, blocking collectives, per_device(): incoming = lax.all_to_all(outgoing, GROUP, 0, 0, tiled=True)  13.9 us
    pallas_call x2, Pallas kernels, attend(): pl.pallas_call(make_attend_kernel(len(queries)), grid=(steps,), in_specs=...  11 us
    all_gather x1, waiting for transfers between devices, per_device(): history = lax.all_gather(pieces, 'z', tiled=True)  5.83 us
    pallas_call x1, Pallas kernels, own_term(): pl.pallas_call(own_kernel, grid=(rows // block,), in_specs=[pl.BlockSpec(...  3.83 us
  transfers between devices with their start and end apart: 10, of which 6 were waited for; matrix products, arithmetic and copies ran while one was open for 3% of the time, Pallas kernels for 6%

profile of v4, /device:TPU:20, one launch (start us, length us, event | category | flops | bytes accessed | tf_op | source)
XLA Modules:
  0.0 154.9 jit_solution(12352008136419715786)
XLA Ops:
  7.7 1.0 gather_fusion
  8.7 13.9 %all_to_all.5 = bf16[16,4,4096]{2,1,0:T(4,128)(2,1)S(1)} all-to-all(bf16[16,4,4096]{2,1,0:T(4,128)(2,1)S(1)} %gather_fusion), channel_id=1, replica_groups=mesh['yhi'=4,'z'=8,'x'=4,'ylo'=2,'core'=2] {'x','ylo','core'}, dimensions={0} | all-to-all | bytes 1048576 | tf_op jit(solution)/shard_map/all_to_all | solution.py:159
  22.6 0.9 reshape.103
  23.6 4.8 %collective-permute-start = (bf16[128,2048]{1,0:T(8,128)(2,1)}, bf16[128,2048]{1,0:T(8,128)(2,1)S(1)}, u32[]{:S(2)}, u32[]{:S(2)}) collective-permute-start(bf16[128,2048]{1,0:T(8,128)(2,1)} %bitcast.22), channel_id=1, source_target_pairs={{0,128},{128,256},{256,384},{384,0},{1,129},{129,257},{257,385},{3... | collective-permute-start | bytes 1572872 | tf_op jit(solution)/shard_map/ppermute | solution.py:19
  28.4 2.1 %collective-permute-start.1 = (bf16[128,2048]{1,0:T(8,128)(2,1)}, bf16[128,2048]{1,0:T(8,128)(2,1)S(1)}, u32[]{:S(2)}, u32[]{:S(2)}) collective-permute-start(bf16[128,2048]{1,0:T(8,128)(2,1)} %bitcast.23), channel_id=1, source_target_pairs={{0,384},{128,0},{256,128},{384,256},{1,385},{129,1},{257,129},{385... | collective-permute-start | bytes 1572872 | tf_op jit(solution)/shard_map/ppermute | solution.py:19
  30.5 5.5 %collective-permute-start.2 = (bf16[128,2048]{1,0:T(8,128)(2,1)}, bf16[128,2048]{1,0:T(8,128)(2,1)S(1)}, u32[]{:S(2)}, u32[]{:S(2)}) collective-permute-start(bf16[128,2048]{1,0:T(8,128)(2,1)} %bitcast.24), channel_id=1, source_target_pairs={{0,256},{128,384},{256,0},{384,128},{1,257},{129,385},{257,1},{385... | collective-permute-start | bytes 1572872 | tf_op jit(solution)/shard_map/ppermute | solution.py:19
  39.8 3.8 %shard_map.100.refs_8_ = f32[128,2048]{1,0:T(8,128)} custom-call(bf16[128,2048]{1,0:T(8,128)(2,1)} %bitcast.25, bf16[128,4096]{1,0:T(8,128)(2,1)} %bitcast.28, f32[1,16]{1,0:T(1,128)} %bitcast.32), custom_call_target="tpu_custom_call" | custom-call | tf_op jit(solution)/shard_map/pallas_call | solution.py:98
  43.7 19.5 %collective-permute-done.refs_1_ = bf16[128,2048]{1,0:T(8,128)(2,1)S(1)} collective-permute-done((bf16[128,2048]{1,0:T(8,128)(2,1)}, bf16[128,2048]{1,0:T(8,128)(2,1)S(1)}, u32[]{:S(2)}, u32[]{:S(2)}) %collective-permute-start) | collective-permute-done | bytes 524320 | tf_op jit(solution)/shard_map/ppermute | solution.py:19
  63.1 16.6 %collective-permute-done.1.refs_2_ = bf16[128,2048]{1,0:T(8,128)(2,1)S(1)} collective-permute-done((bf16[128,2048]{1,0:T(8,128)(2,1)}, bf16[128,2048]{1,0:T(8,128)(2,1)S(1)}, u32[]{:S(2)}, u32[]{:S(2)}) %collective-permute-start.1) | collective-permute-done | bytes 524320 | tf_op jit(solution)/shard_map/ppermute | solution.py:19
  79.7 5.8 %all-gather.2.cloned.1.call-done.refs_4_.refs_5_ = bf16[512,4096]{1,0:T(8,128)(2,1)} async-done(((bf16[64,4096]{1,0:T(8,128)(2,1)}), bf16[512,4096]{1,0:T(8,128)(2,1)}) %all-gather.2.cloned.1.call-update) | async-done | bytes 4194320 | tf_op jit(solution)/shard_map/all_gather | solution.py:161
  85.5 0.8 broadcast_in_dim.44.refs_7_
  86.3 5.5 %shard_map.101 = (f32[128,1024]{1,0:T(8,128)}, bf16[128,1024]{1,0:T(8,128)(2,1)}, f32[128,1024]{1,0:T(8,128)}, bf16[128,1024]{1,0:T(8,128)(2,1)}) custom-call(bf16[128,2048]{1,0:T(8,128)(2,1)} %bitcast.26, bf16[128,2048]{1,0:T(8,128)(2,1)} %copy-done.1, bf16[128,2048]{1,0:T(8,128)(2,1)} %copy-done.2, bf16[128,2048]{1,0:T(8,128)(2,1)} %copy-done.3, ...), custom_call_target="tpu_custom_call" | custom-call | flops 1073741824 | bytes 2097152 | tf_op jit(solution)/shard_map/pallas_call | solution.py:61
  91.9 5.7 %collective-permute-start.4 = (bf16[128,1024]{1,0:T(8,128)(2,1)}, bf16[128,1024]{1,0:T(8,128)(2,1)S(1)}, u32[]{:S(2)}, u32[]{:S(2)}) collective-permute-start(bf16[128,1024]{1,0:T(8,128)(2,1)} %get-tuple-element.16), channel_id=1, source_target_pairs={{0,128},{128,256},{256,384},{384,0},{1,129},{129,257},{257,385},{3... | collective-permute-start | bytes 786440 | tf_op jit(solution)/shard_map/ppermute | solution.py:19
  97.5 5.5 %shard_map.102 = (f32[128,1024]{1,0:T(8,128)}, f32[128,1024]{1,0:T(8,128)}, bf16[128,1024]{1,0:T(8,128)(2,1)}, bf16[128,1024]{1,0:T(8,128)(2,1)}) custom-call(bf16[128,2048]{1,0:T(8,128)(2,1)} %bitcast.27, bf16[128,2048]{1,0:T(8,128)(2,1)} %copy-done.1, bf16[128,2048]{1,0:T(8,128)(2,1)} %copy-done.2, bf16[128,2048]{1,0:T(8,128)(2,1)} %copy-done.3, ...), custom_call_target="tpu_custom_call" | custom-call | flops 1073741824 | bytes 2097152 | tf_op jit(solution)/shard_map/pallas_call | solution.py:61
  103.0 1.9 %collective-permute-start.7 = (bf16[128,1024]{1,0:T(8,128)(2,1)}, bf16[128,1024]{1,0:T(8,128)(2,1)S(1)}, u32[]{:S(2)}, u32[]{:S(2)}) collective-permute-start(bf16[128,1024]{1,0:T(8,128)(2,1)} %get-tuple-element.20), channel_id=1, source_target_pairs={{0,384},{128,0},{256,128},{384,256},{1,385},{129,1},{257,129},{385... | collective-permute-start | bytes 786440 | tf_op jit(solution)/shard_map/ppermute | solution.py:19
  105.0 2.9 %collective-permute-start.3 = (bf16[128,1024]{1,0:T(8,128)(2,1)S(1)}, bf16[128,1024]{1,0:T(8,128)(2,1)S(1)}, u32[]{:S(2)}, u32[]{:S(2)}) collective-permute-start(bf16[128,1024]{1,0:T(8,128)(2,1)S(1)} %copy-done.9), channel_id=1, source_target_pairs={{0,384},{128,0},{256,128},{384,256},{1,385},{129,1},{257,129},{385... | collective-permute-start | bytes 786440 | tf_op jit(solution)/shard_map/ppermute | solution.py:19
  107.9 5.0 %collective-permute-start.6 = (bf16[128,1024]{1,0:T(8,128)(2,1)}, bf16[128,1024]{1,0:T(8,128)(2,1)S(1)}, u32[]{:S(2)}, u32[]{:S(2)}) collective-permute-start(bf16[128,1024]{1,0:T(8,128)(2,1)} %get-tuple-element.18), channel_id=1, source_target_pairs={{0,128},{128,256},{256,384},{384,0},{1,129},{129,257},{257,385},{3... | collective-permute-start | bytes 786440 | tf_op jit(solution)/shard_map/ppermute | solution.py:19
  113.0 4.8 %collective-permute-start.5 = (bf16[128,1024]{1,0:T(8,128)(2,1)S(1)}, bf16[128,1024]{1,0:T(8,128)(2,1)S(1)}, u32[]{:S(2)}, u32[]{:S(2)}) collective-permute-start(bf16[128,1024]{1,0:T(8,128)(2,1)S(1)} %add_convert_fusion.1), channel_id=1, source_target_pairs={{0,128},{128,256},{256,384},{384,0},{1,129},{129,257},{257,385},{3... | collective-permute-start | bytes 786440 | tf_op jit(solution)/shard_map/ppermute | solution.py:19
  117.9 14.3 %collective-permute-done.7 = bf16[128,1024]{1,0:T(8,128)(2,1)S(1)} collective-permute-done((bf16[128,1024]{1,0:T(8,128)(2,1)}, bf16[128,1024]{1,0:T(8,128)(2,1)S(1)}, u32[]{:S(2)}, u32[]{:S(2)}) %collective-permute-start.7) | collective-permute-done | bytes 262176 | tf_op jit(solution)/shard_map/ppermute | solution.py:19
  132.2 1.1 add_convert_fusion
  133.3 1.9 %collective-permute-start.8 = (bf16[128,1024]{1,0:T(8,128)(2,1)S(1)}, bf16[128,1024]{1,0:T(8,128)(2,1)S(1)}, u32[]{:S(2)}, u32[]{:S(2)}) collective-permute-start(bf16[128,1024]{1,0:T(8,128)(2,1)S(1)} %add_convert_fusion), channel_id=1, source_target_pairs={{0,384},{128,0},{256,128},{384,256},{1,385},{129,1},{257,129},{385... | collective-permute-start | bytes 786440 | tf_op jit(solution)/shard_map/ppermute | solution.py:19
  135.2 2.6 %collective-permute-done.3.a1_ref = bf16[128,1024]{1,0:T(8,128)(2,1)S(1)} collective-permute-done((bf16[128,1024]{1,0:T(8,128)(2,1)S(1)}, bf16[128,1024]{1,0:T(8,128)(2,1)S(1)}, u32[]{:S(2)}, u32[]{:S(2)}) %collective-permute-start.3) | collective-permute-done | bytes 262176 | tf_op jit(solution)/shard_map/ppermute | solution.py:19
  137.8 6.8 %collective-permute-done.8.b2_ref = bf16[128,1024]{1,0:T(8,128)(2,1)S(1)} collective-permute-done((bf16[128,1024]{1,0:T(8,128)(2,1)S(1)}, bf16[128,1024]{1,0:T(8,128)(2,1)S(1)}, u32[]{:S(2)}, u32[]{:S(2)}) %collective-permute-start.8) | collective-permute-done | bytes 262176 | tf_op jit(solution)/shard_map/ppermute | solution.py:19
  145.3 2.7 %shard_map.103 = bf16[128,2048]{1,0:T(8,128)(2,1)} custom-call(f32[128,1024]{1,0:T(8,128)} %get-tuple-element.13.a0_ref, bf16[128,1024]{1,0:T(8,128)(2,1)} %copy-done.5, bf16[128,1024]{1,0:T(8,128)(2,1)} %copy-done.7, f32[128,1024]{1,0:T(8,128)} %get-tuple-element.17.b0_ref, bf16[128,1024]{1,0:T(8,128)(2,1)} %copy-done.6, bf16[128,1024]{1,0:T(8,128)(2,1)} %copy-done.8, ...), custom_call_target="tpu_custom_call" | custom-call | tf_op jit(solution)/shard_map/pallas_call | solution.py:126
  (50 shorter events, 5.1 us)
Async XLA Ops:
  6.5 1.2 copy-start
  6.5 31.3 %copy-start.10 = (f32[128,16]{0,1:T(8,128)S(1)}, f32[128,16]{0,1:T(8,128)}, u32[]{:S(2)}) copy-start(f32[128,16]{0,1:T(8,128)} %param.17) | copy-start | bytes 24580
  6.5 79.0 %all-gather.2.cloned.1.call-start = ((), (), s32[]{:S(2)}) async-start(), calls=%async_computation.1 | async-start | bytes 4718592 | tf_op jit(solution)/shard_map/all_gather | solution.py:161
  23.6 39.5 %collective-permute-start = (bf16[128,2048]{1,0:T(8,128)(2,1)}, bf16[128,2048]{1,0:T(8,128)(2,1)S(1)}, u32[]{:S(2)}, u32[]{:S(2)}) collective-permute-start(bf16[128,2048]{1,0:T(8,128)(2,1)} %bitcast.22), channel_id=1, source_target_pairs={{0,128},{128,256},{256,384},{384,0},{1,129},{129,257},{257,385},{3... | collective-permute-start | bytes 1572872 | tf_op jit(solution)/shard_map/ppermute | solution.py:19
  28.4 51.3 %collective-permute-start.1 = (bf16[128,2048]{1,0:T(8,128)(2,1)}, bf16[128,2048]{1,0:T(8,128)(2,1)S(1)}, u32[]{:S(2)}, u32[]{:S(2)}) collective-permute-start(bf16[128,2048]{1,0:T(8,128)(2,1)} %bitcast.23), channel_id=1, source_target_pairs={{0,384},{128,0},{256,128},{384,256},{1,385},{129,1},{257,129},{385... | collective-permute-start | bytes 1572872 | tf_op jit(solution)/shard_map/ppermute | solution.py:19
  30.5 49.2 %collective-permute-start.2 = (bf16[128,2048]{1,0:T(8,128)(2,1)}, bf16[128,2048]{1,0:T(8,128)(2,1)S(1)}, u32[]{:S(2)}, u32[]{:S(2)}) collective-permute-start(bf16[128,2048]{1,0:T(8,128)(2,1)} %bitcast.24), channel_id=1, source_target_pairs={{0,256},{128,384},{256,0},{384,128},{1,257},{129,385},{257,1},{385... | collective-permute-start | bytes 1572872 | tf_op jit(solution)/shard_map/ppermute | solution.py:19
  63.1 23.2 %copy-start.1 = (bf16[128,2048]{1,0:T(8,128)(2,1)}, bf16[128,2048]{1,0:T(8,128)(2,1)S(1)}, u32[]{:S(2)}) copy-start(bf16[128,2048]{1,0:T(8,128)(2,1)S(1)} %collective-permute-done.refs_1_) | copy-start | bytes 1572868
  79.7 6.6 %copy-start.2 = (bf16[128,2048]{1,0:T(8,128)(2,1)}, bf16[128,2048]{1,0:T(8,128)(2,1)S(1)}, u32[]{:S(2)}) copy-start(bf16[128,2048]{1,0:T(8,128)(2,1)S(1)} %collective-permute-done.1.refs_2_) | copy-start | bytes 1572868
  79.7 6.6 %copy-start.3 = (bf16[128,2048]{1,0:T(8,128)(2,1)}, bf16[128,2048]{1,0:T(8,128)(2,1)S(1)}, u32[]{:S(2)}) copy-start(bf16[128,2048]{1,0:T(8,128)(2,1)S(1)} %collective-permute-done.2.refs_3_) | copy-start | bytes 1572868
  91.9 13.1 %copy-start.9 = (bf16[128,1024]{1,0:T(8,128)(2,1)S(1)}, bf16[128,1024]{1,0:T(8,128)(2,1)}, u32[]{:S(2)}) copy-start(bf16[128,1024]{1,0:T(8,128)(2,1)} %get-tuple-element.14) | copy-start | bytes 786436
  91.9 21.1 %copy-start.4 = (f32[128,1024]{1,0:T(8,128)S(1)}, f32[128,1024]{1,0:T(8,128)}, u32[]{:S(2)}) copy-start(f32[128,1024]{1,0:T(8,128)} %get-tuple-element.15) | copy-start | bytes 1572868
  91.9 21.1 %collective-permute-start.4 = (bf16[128,1024]{1,0:T(8,128)(2,1)}, bf16[128,1024]{1,0:T(8,128)(2,1)S(1)}, u32[]{:S(2)}, u32[]{:S(2)}) collective-permute-start(bf16[128,1024]{1,0:T(8,128)(2,1)} %get-tuple-element.16), channel_id=1, source_target_pairs={{0,128},{128,256},{256,384},{384,0},{1,129},{129,257},{257,385},{3... | collective-permute-start | bytes 786440 | tf_op jit(solution)/shard_map/ppermute | solution.py:19
  103.0 29.1 %collective-permute-start.7 = (bf16[128,1024]{1,0:T(8,128)(2,1)}, bf16[128,1024]{1,0:T(8,128)(2,1)S(1)}, u32[]{:S(2)}, u32[]{:S(2)}) collective-permute-start(bf16[128,1024]{1,0:T(8,128)(2,1)} %get-tuple-element.20), channel_id=1, source_target_pairs={{0,384},{128,0},{256,128},{384,256},{1,385},{129,1},{257,129},{385... | collective-permute-start | bytes 786440 | tf_op jit(solution)/shard_map/ppermute | solution.py:19
  105.0 32.8 %collective-permute-start.3 = (bf16[128,1024]{1,0:T(8,128)(2,1)S(1)}, bf16[128,1024]{1,0:T(8,128)(2,1)S(1)}, u32[]{:S(2)}, u32[]{:S(2)}) collective-permute-start(bf16[128,1024]{1,0:T(8,128)(2,1)S(1)} %copy-done.9), channel_id=1, source_target_pairs={{0,384},{128,0},{256,128},{384,256},{1,385},{129,1},{257,129},{385... | collective-permute-start | bytes 786440 | tf_op jit(solution)/shard_map/ppermute | solution.py:19
  107.9 29.9 %collective-permute-start.6 = (bf16[128,1024]{1,0:T(8,128)(2,1)}, bf16[128,1024]{1,0:T(8,128)(2,1)S(1)}, u32[]{:S(2)}, u32[]{:S(2)}) collective-permute-start(bf16[128,1024]{1,0:T(8,128)(2,1)} %get-tuple-element.18), channel_id=1, source_target_pairs={{0,128},{128,256},{256,384},{384,0},{1,129},{129,257},{257,385},{3... | collective-permute-start | bytes 786440 | tf_op jit(solution)/shard_map/ppermute | solution.py:19
  113.0 24.8 %collective-permute-start.5 = (bf16[128,1024]{1,0:T(8,128)(2,1)S(1)}, bf16[128,1024]{1,0:T(8,128)(2,1)S(1)}, u32[]{:S(2)}, u32[]{:S(2)}) collective-permute-start(bf16[128,1024]{1,0:T(8,128)(2,1)S(1)} %add_convert_fusion.1), channel_id=1, source_target_pairs={{0,128},{128,256},{256,384},{384,0},{1,129},{129,257},{257,385},{3... | collective-permute-start | bytes 786440 | tf_op jit(solution)/shard_map/ppermute | solution.py:19
  133.3 11.4 %collective-permute-start.8 = (bf16[128,1024]{1,0:T(8,128)(2,1)S(1)}, bf16[128,1024]{1,0:T(8,128)(2,1)S(1)}, u32[]{:S(2)}, u32[]{:S(2)}) collective-permute-start(bf16[128,1024]{1,0:T(8,128)(2,1)S(1)} %add_convert_fusion), channel_id=1, source_target_pairs={{0,384},{128,0},{256,128},{384,256},{1,385},{129,1},{257,129},{385... | collective-permute-start | bytes 786440 | tf_op jit(solution)/shard_map/ppermute | solution.py:19
  137.8 6.9 %copy-start.5 = (bf16[128,1024]{1,0:T(8,128)(2,1)}, bf16[128,1024]{1,0:T(8,128)(2,1)S(1)}, u32[]{:S(2)}) copy-start(bf16[128,1024]{1,0:T(8,128)(2,1)S(1)} %collective-permute-done.3.a1_ref) | copy-start | bytes 786436
  137.8 6.9 %copy-start.6 = (bf16[128,1024]{1,0:T(8,128)(2,1)}, bf16[128,1024]{1,0:T(8,128)(2,1)S(1)}, u32[]{:S(2)}) copy-start(bf16[128,1024]{1,0:T(8,128)(2,1)S(1)} %collective-permute-done.6.b1_ref) | copy-start | bytes 786436
  137.8 6.9 %copy-start.7 = (bf16[128,1024]{1,0:T(8,128)(2,1)}, bf16[128,1024]{1,0:T(8,128)(2,1)S(1)}, u32[]{:S(2)}) copy-start(bf16[128,1024]{1,0:T(8,128)(2,1)S(1)} %collective-permute-done.5.a2_ref) | copy-start | bytes 786436
  144.6 0.7 copy-start.8
Sparse Core Ops, SparseCore 0:
  23.7 61.7 all-gather.1

commit v5 on v4

v5 whole, which is shorter than its diff:
```python
import math

import jax
import jax.numpy as jnp
from jax import lax
from jax.experimental import pallas as pl
from jax.experimental.pallas import tpu as pltpu
from jax.sharding import Mesh
from jax.sharding import PartitionSpec as P

HEADS = 16
HEAD_DIM = 128
GROUP = ("x", "ylo", "core")
LOOP = ("yh1", "yh0", "z")
Y = ("yh1", "yh0")


def attend_kernel(q_ref, k_ref, v_ref, bias_ref, mask_ref, out_ref):
    blocks, rows, width = q_ref.shape
    scale = 0.5 / math.sqrt(HEAD_DIM)
    inside = mask_ref[...] > 0.0
    for head in range(width // HEAD_DIM):
        cols = slice(head * HEAD_DIM, (head + 1) * HEAD_DIM)
        queries = q_ref[:, :, cols].reshape(blocks * rows, HEAD_DIM)
        scores = lax.dot_general(
            queries, k_ref[:, cols], (((1,), (1,)), ((), ())), preferred_element_type=jnp.float32
        )
        half = scores * scale + bias_ref[head]
        weights = jnp.where(inside, half + half * jnp.tanh(half), 0.0).astype(jnp.bfloat16)
        sums = jnp.dot(weights, v_ref[:, cols], preferred_element_type=jnp.float32)
        out_ref[:, :, cols] = sums.reshape(blocks, rows, HEAD_DIM).astype(out_ref.dtype)


def attend(queries, history, bias, mask, per_step):
    blocks, rows, full = queries.shape
    positions = history.shape[0]
    width = per_step * HEAD_DIM
    steps = full // width
    return pl.pallas_call(
        attend_kernel,
        grid=(steps,),
        in_specs=[
            pl.BlockSpec((blocks, rows, width), lambda i: (0, 0, i)),
            pl.BlockSpec((positions, width), lambda i: (0, i)),
            pl.BlockSpec((positions, width), lambda i: (0, i + steps)),
            pl.BlockSpec((per_step, 1, positions), lambda i: (i, 0, 0)),
            pl.BlockSpec((1, positions), lambda i: (0, 0)),
        ],
        out_specs=pl.BlockSpec((blocks, rows, width), lambda i: (0, 0, i)),
        out_shape=jax.ShapeDtypeStruct((blocks, rows, full), jnp.bfloat16),
        compiler_params=pltpu.CompilerParams(vmem_limit_bytes=56 * 1024 * 1024),
        cost_estimate=pl.CostEstimate(
            flops=4 * blocks * rows * positions * full,
            bytes_accessed=4 * positions * full + 4 * blocks * rows * full,
            transcendentals=blocks * rows * positions * full // HEAD_DIM,
        ),
    )(queries, history, history, bias, mask)


def own_kernel(q_ref, own_ref, self_bias_ref, out_ref):
    width = q_ref.shape[1]
    scale = 0.5 / math.sqrt(HEAD_DIM)
    for head in range(width // HEAD_DIM):
        cols = slice(head * HEAD_DIM, (head + 1) * HEAD_DIM)
        value_cols = slice(width + head * HEAD_DIM, width + (head + 1) * HEAD_DIM)
        product = q_ref[:, cols].astype(jnp.float32) * own_ref[:, cols].astype(jnp.float32)
        half = jnp.sum(product, axis=-1, keepdims=True) * scale + 0.5 * self_bias_ref[0, head]
        weight = (half + half * jnp.tanh(half)).astype(jnp.bfloat16).astype(jnp.float32)
        out_ref[:, cols] = weight * own_ref[:, value_cols].astype(jnp.float32)


def own_term(queries, own, self_bias):
    rows, width = queries.shape
    block = 32
    return pl.pallas_call(
        own_kernel,
        grid=(rows // block,),
        in_specs=[
            pl.BlockSpec((block, width), lambda i: (i, 0)),
            pl.BlockSpec((block, 2 * width), lambda i: (i, 0)),
            pl.BlockSpec(memory_space=pltpu.SMEM),
        ],
        out_specs=pl.BlockSpec((block, width), lambda i: (i, 0)),
        out_shape=jax.ShapeDtypeStruct((rows, width), jnp.float32),
    )(queries, own, self_bias[None])


def finish_kernel(core_ref, parts_ref, other_ref, base_ref, gate_ref, gain_ref, out_ref):
    first_core = core_ref[0] == 0
    a, b, c, d = (parts_ref[i].astype(jnp.float32) for i in range(4))
    mine = jnp.where(first_core, a + b, c + d)
    other = other_ref[...].astype(jnp.float32)
    low = jnp.where(first_core, mine, other)
    high = jnp.where(first_core, other, mine)
    total = base_ref[...] + jnp.concatenate([low, high], axis=-1)
    average = jnp.mean(total, axis=-1, keepdims=True)
    centered = total - average
    variance = jnp.mean(centered * centered, axis=-1, keepdims=True)
    normed = centered * lax.rsqrt(variance + 1e-05) * gain_ref[...]
    out_ref[...] = (normed * gate_ref[...].astype(jnp.float32)).astype(out_ref.dtype)


def finish(core, parts, other, base, gate, gain):
    rows, width = gate.shape
    block = 64
    row_spec = lambda cols: pl.BlockSpec((block, cols), lambda i: (i, 0))
    return pl.pallas_call(
        finish_kernel,
        grid=(rows // block,),
        in_specs=[
            pl.BlockSpec(memory_space=pltpu.SMEM),
            pl.BlockSpec((4, block, width // 2), lambda i: (0, i, 0)),
            row_spec(width // 2),
            row_spec(width),
            row_spec(width),
            pl.BlockSpec((1, width), lambda i: (0, 0)),
        ],
        out_specs=row_spec(width),
        out_shape=jax.ShapeDtypeStruct((rows, width), jnp.bfloat16),
    )(core[None], parts, other, base, gate, gain[None])


def swapped(value):
    return lax.ppermute(value, "core", [(0, 1), (1, 0)])


def per_device(
    cand_query,
    cand_kv,
    cand_gate,
    cache_store,
    holders,
    lengths,
    buckets,
    time_bias,
    self_bias,
    norm_gain,
):
    core = lax.axis_index("core")
    side = lax.axis_index("yh1")
    half_y = lax.axis_index("yh0")
    group_index = lax.axis_index(GROUP)
    groups = lax.axis_size(GROUP)
    z_size = lax.axis_size("z")
    slots, _, piece_len, double_width = cache_store.shape
    width = double_width // 2
    half_width = width // 2

    holding = (holders // slots).reshape(groups, slots)
    slot_of = (holders % slots).reshape(groups, slots)
    chosen = jnp.sum(jnp.where(holding == group_index, slot_of, 0), axis=1)
    by_half = jnp.stack(
        [
            jnp.concatenate(
                [
                    cache_store[:, 0, :, h * half_width : (h + 1) * half_width],
                    cache_store[:, 0, :, width + h * half_width : width + (h + 1) * half_width],
                ],
                axis=-1,
            )
            for h in range(2)
        ]
    ).reshape(2 * slots, piece_len, width)
    places = chosen.reshape(groups // 2, 2).T[:, :, None] + slots * jnp.arange(2, dtype=jnp.int32)
    outgoing = by_half[places.reshape(-1)]
    incoming = lax.all_to_all(outgoing, ("yh1",) + GROUP, 0, 0, tiled=True)
    pieces = incoming.reshape(2 * groups * piece_len, width)
    history = lax.all_gather(pieces, "z", tiled=True)

    queries = cand_query[0]
    own_half = lax.dynamic_slice_in_dim(queries, core * half_width, half_width, 1)
    other_half = lax.dynamic_slice_in_dim(queries, (1 - core) * half_width, half_width, 1)
    partner_half = swapped(other_half)
    first = jnp.where(core == 0, own_half, partner_half)
    second = jnp.where(core == 0, partner_half, own_half)
    spread = lax.all_to_all(jnp.stack([first, first, second, second]), Y, 0, 0, tiled=True)

    about = jnp.concatenate([buckets[0], lengths])
    about = jnp.where(core == side, about, swapped(about))
    session = (group_index // 2) * 2 + side
    own_holding = lax.dynamic_index_in_dim(holding, session, 0, keepdims=False)
    arrived = own_holding[None, :] == jnp.arange(groups, dtype=jnp.int32)[:, None]
    piece_of = jnp.sum(jnp.where(arrived, jnp.arange(slots, dtype=jnp.int32)[None, :], 0), axis=1)
    order = jnp.arange(z_size, dtype=jnp.int32)[:, None, None, None]
    order = order + (2 * jnp.arange(2, dtype=jnp.int32)[None, :, None, None] + half_y) * z_size
    place = (
        (order * slots + piece_of[None, None, :, None]) * piece_len
        + jnp.arange(piece_len, dtype=jnp.int32)[None, None, None, :]
    ).reshape(-1)
    mask = (place < about[-1]).astype(jnp.float32)[None, :]
    one_hot = (
        about[place][:, None] == jnp.arange(time_bias.shape[0], dtype=jnp.int32)[None, :]
    ).astype(jnp.float32)
    own_bias = lax.dynamic_slice_in_dim(time_bias, core * (HEADS // 2), HEADS // 2, 1)
    bias = 0.5 * jnp.einsum("kn,nh->hk", one_hot, own_bias, precision=lax.Precision.HIGHEST)

    base = own_term(queries, cand_kv[0], self_bias)
    partial = attend(spread, history, bias[:, None, :], mask, 2)
    parts = lax.all_to_all(partial, Y, 0, 0, tiled=True)
    pair = lax.dynamic_slice_in_dim(parts, 2 * (1 - core), 2).astype(jnp.float32)
    other = swapped((pair[0] + pair[1]).astype(jnp.bfloat16))
    return finish(core, parts, other, base, cand_gate[0], norm_gain)[None]


def solution(mesh):
    split = Mesh(mesh.devices.reshape(2, 2, 8, 4, 2, 2), LOOP + GROUP)
    rows = P(GROUP, LOOP, None)
    return jax.shard_map(
        per_device,
        mesh=split,
        in_specs=(
            rows,
            rows,
            rows,
            P(GROUP, LOOP, None, None),
            P(),
            P(GROUP),
            P(GROUP, None),
            P(),
            P(),
            P(),
        ),
        out_specs=rows,
        check_vma=False,
    )
```

time: 156 us -> 158 us (1.013)
  the two profiles are of different devices: /device:TPU:20 before, /device:TPU:1 now
where the time goes in v5:
time: 158 us; the launch traced here: 157 us
  waiting for transfers between devices  64.2 us (41%)
  blocking collectives  29.2 us (18%)
  starting transfers between devices  16.7 us (11%)
  Pallas kernels  14.3 us (9%)
  between operations  14.3 us (9%)
  local copies, waits for them, and re-layouts  13.4 us (8%)
  other arithmetic  4.06 us (3%)
    all_to_all x1, blocking collectives, per_device(): incoming = lax.all_to_all(outgoing, ('yh1',) + GROUP, 0, 0, tiled=True)  29.2 us
    all_gather x1, waiting for transfers between devices, per_device(): history = lax.all_gather(pieces, 'z', tiled=True)  28.4 us
    all_to_all x1, waiting for transfers between devices, per_device(): parts = lax.all_to_all(partial, Y, 0, 0, tiled=True)  26.2 us
    all_to_all x1, waiting for transfers between devices, per_device(): lax.all_to_all(jnp.stack([first, first, second, second]), Y, 0, 0, tiled=...  9.68 us
    pallas_call x1, Pallas kernels, attend(): pl.pallas_call(attend_kernel, grid=(steps,), in_specs=[pl.BlockSpec((bloc...  7.69 us
    ppermute x3, starting transfers between devices, swapped(): return lax.ppermute(value, 'core', [(0, 1), (1, 0)])  6.76 us
    all_to_all x1, starting transfers between devices, per_device(): parts = lax.all_to_all(partial, Y, 0, 0, tiled=True)  6.45 us
    gather x1, local copies, waits for them, and re-layouts, per_device(): about[place][:, None]  6.14 us
  transfers between devices with their start and end apart: 6, of which 3 were waited for; matrix products, arithmetic and copies ran while one was open for 7% of the time, Pallas kernels for 2%

profile of v5, /device:TPU:1, one launch (start us, length us, event | category | flops | bytes accessed | tf_op | source)
XLA Modules:
  0.0 156.8 jit_solution(16524062241366457620)
XLA Ops:
  6.6 0.7 and_select_fusion.1
  8.0 1.0 slice_bitcast_fusion.3
  8.9 1.2 slice_bitcast_fusion.2
  10.8 1.0 gather_fusion
  11.8 29.2 %all_to_all.15 = bf16[32,4,2048]{2,1,0:T(4,128)(2,1)S(1)} all-to-all(bf16[32,4,2048]{2,1,0:T(4,128)(2,1)S(1)} %gather_fusion), channel_id=1, replica_groups=mesh['yh1'=2,'yh0'=2,'z'=8,'x'=4,'ylo'=2,'core'=2] {'yh1','x','ylo','core'}, dimensions={0} | all-to-all | bytes 1048576 | tf_op jit(solution)/shard_map/all_to_all | solution.py:166
  41.1 0.9 reshape.160
  42.0 2.2 %collective-permute-start = (bf16[128,1024]{1,0:T(8,128)(2,1)S(1)}, bf16[128,1024]{1,0:T(8,128)(2,1)S(1)}, u32[]{:S(2)}, u32[]{:S(2)}) collective-permute-start(bf16[128,1024]{1,0:T(8,128)(2,1)S(1)} %dynamic-slice_bitcast_fusion), channel_id=1, source_target_pairs={{0,1},{1,0},{2,3},{3,2},{4,5},{5,4},{6,7},{7,6},{8,9},{9,8},{10,11... | collective-permute-start | bytes 786440 | tf_op jit(solution)/shard_map/ppermute | solution.py:124
  44.9 2.2 %collective-permute-start.1 = (s32[2049]{0:T(1024)S(1)}, s32[2049]{0:T(1024)S(1)}, u32[]{:S(2)}, u32[]{:S(2)}) collective-permute-start(s32[2049]{0:T(1024)S(1)} %pad_add_fusion), channel_id=1, source_target_pairs={{0,1},{1,0},{2,3},{3,2},{4,5},{5,4},{6,7},{7,6},{8,9},{9,8},{10,11... | collective-permute-start | bytes 24596 | tf_op jit(solution)/shard_map/ppermute | solution.py:124
  47.4 1.1 pad_maximum_fusion
  48.5 3.5 %all-to-all-start = ((bf16[4,128,1024]{2,1,0:T(8,128)(2,1)}), bf16[4,128,1024]{2,1,0:T(8,128)(2,1)S(1)}, u32[]{:S(2)}, u32[]{:S(2)}) async-start(bf16[4,128,1024]{2,1,0:T(8,128)(2,1)} %pad_maximum_fusion), calls=%async_computation | async-start | bytes 2097152 | tf_op jit(solution)/shard_map/all_to_all | solution.py:176
  52.4 0.6 slice.35
  52.9 6.1 %gather_fusion.1 = s32[1024]{0:T(1024)S(1)} fusion(s32[2049]{0:T(1024)S(1)} %broadcast_select_fusion, s32[1024]{0:T(1024)S(1)} %broadcast_clamp_fusion), kind=kCustom, calls=%fused_computation.1 | custom fusion | bytes 12288 | tf_op jit(solution)/shard_map/gather | solution.py:192
  59.5 0.6 broadcast_in_dim.27.bias_ref
  60.2 0.7 compare_convert_fusion
  60.9 0.7 reshape.161.mask_ref
  61.6 9.7 %all-to-all-done.q_ref = bf16[4,128,1024]{2,1,0:T(8,128)(2,1)S(1)} async-done(((bf16[4,128,1024]{2,1,0:T(8,128)(2,1)}), bf16[4,128,1024]{2,1,0:T(8,128)(2,1)S(1)}, u32[]{:S(2)}, u32[]{:S(2)}) %all-to-all-start) | async-done | bytes 1048608 | tf_op jit(solution)/shard_map/all_to_all | solution.py:176
  71.3 28.4 %all-gather.2.cloned.1.call-done.k_ref.v_ref = bf16[1024,2048]{1,0:T(8,128)(2,1)} async-done(((bf16[128,2048]{1,0:T(8,128)(2,1)}), bf16[1024,2048]{1,0:T(8,128)(2,1)}) %all-gather.2.cloned.1.call-update) | async-done | bytes 4194320 | tf_op jit(solution)/shard_map/all_gather | solution.py:168
  99.7 7.7 %shard_map.100 = bf16[4,128,1024]{2,1,0:T(8,128)(2,1)} custom-call(bf16[4,128,1024]{2,1,0:T(8,128)(2,1)} %copy-done.2, bf16[1024,2048]{1,0:T(8,128)(2,1)} %all-gather.2.cloned.1.call-done.k_ref.v_ref, bf16[1024,2048]{1,0:T(8,128)(2,1)} %all-gather.2.cloned.1.call-done.k_ref.v_ref, f32[8,1,1024]{2,1,0:T(1,128)} %broadcast_in_dim.27.bias_ref, ...), custom_call_target="tpu_custom_call" | custom-call | flops 2147483648 | bytes 6291456 | tf_op jit(solution)/shard_map/pallas_call | solution.py:39
  107.3 6.5 %all-to-all-start.2 = ((bf16[4,128,1024]{2,1,0:T(8,128)(2,1)}), bf16[4,128,1024]{2,1,0:T(8,128)(2,1)S(1)}, u32[]{:S(2)}, u32[]{:S(2)}) async-start(bf16[4,128,1024]{2,1,0:T(8,128)(2,1)} %shard_map.100), calls=%async_computation.2 | async-start | bytes 2097152 | tf_op jit(solution)/shard_map/all_to_all | solution.py:199
  113.8 26.2 %all-to-all-done.2.parts_ref = bf16[4,128,1024]{2,1,0:T(8,128)(2,1)S(1)} async-done(((bf16[4,128,1024]{2,1,0:T(8,128)(2,1)}), bf16[4,128,1024]{2,1,0:T(8,128)(2,1)S(1)}, u32[]{:S(2)}, u32[]{:S(2)}) %all-to-all-start.2) | async-done | bytes 1048608 | tf_op jit(solution)/shard_map/all_to_all | solution.py:199
  140.1 2.4 %collective-permute-start.2 = (bf16[128,1024]{1,0:T(8,128)(2,1)S(1)}, bf16[128,1024]{1,0:T(8,128)(2,1)S(1)}, u32[]{:S(2)}, u32[]{:S(2)}) collective-permute-start(bf16[128,1024]{1,0:T(8,128)(2,1)S(1)} %fusion.1), channel_id=1, source_target_pairs={{0,1},{1,0},{2,3},{3,2},{4,5},{5,4},{6,7},{7,6},{8,9},{9,8},{10,11... | collective-permute-start | bytes 786440 | tf_op jit(solution)/shard_map/ppermute | solution.py:124
  142.6 3.9 %shard_map.101.base_ref = f32[128,2048]{1,0:T(8,128)} custom-call(bf16[128,2048]{1,0:T(8,128)(2,1)} %bitcast.50, bf16[128,4096]{1,0:T(8,128)(2,1)} %bitcast.52, f32[1,16]{1,0:T(1,128)} %bitcast.60), custom_call_target="tpu_custom_call" | custom-call | tf_op jit(solution)/shard_map/pallas_call | solution.py:75
  146.4 0.7 copy-done.4
  147.1 2.8 %shard_map.102 = bf16[128,2048]{1,0:T(8,128)(2,1)} custom-call(s32[1]{0:T(128)} %bitcast.core_ref, bf16[4,128,1024]{2,1,0:T(8,128)(2,1)} %copy-done.1, bf16[128,1024]{1,0:T(8,128)(2,1)} %copy-done.4, f32[128,2048]{1,0:T(8,128)} %shard_map.101.base_ref, bf16[128,2048]{1,0:T(8,128)(2,1)} %bitcast.54, f32[1,2048]{1,0:T(1,128)} %bitcast.59), custom_call_target="tpu_custom_call" | custom-call | tf_op jit(solution)/shard_map/pallas_call | solution.py:107
  (44 shorter events, 2.6 us)
Async XLA Ops:
  6.5 52.5 %copy-start = (f32[128,16]{0,1:T(8,128)S(1)}, f32[128,16]{0,1:T(8,128)}, u32[]{:S(2)}) copy-start(f32[128,16]{0,1:T(8,128)} %param.17) | copy-start | bytes 24580
  6.5 35.5 %copy-start.3 = (bf16[1,128,2048]{2,1,0:T(8,128)(2,1)S(1)}, bf16[1,128,2048]{2,1,0:T(8,128)(2,1)}, u32[]{:S(2)}) copy-start(bf16[1,128,2048]{2,1,0:T(8,128)(2,1)} %param.10) | copy-start | bytes 1572868
  6.5 38.3 %copy-start.5 = (s32[1,2048]{1,0:T(1,128)S(1)}, s32[1,2048]{1,0:T(1,128)}, u32[]{:S(2)}) copy-start(s32[1,2048]{1,0:T(1,128)} %param.16) | copy-start | bytes 24580
  6.5 93.1 %all-gather.2.cloned.1.call-start = ((), (), s32[]{:S(2)}) async-start(), calls=%async_computation.3 | async-start | bytes 4718592 | tf_op jit(solution)/shard_map/all_gather | solution.py:168
  42.0 5.2 %collective-permute-start = (bf16[128,1024]{1,0:T(8,128)(2,1)S(1)}, bf16[128,1024]{1,0:T(8,128)(2,1)S(1)}, u32[]{:S(2)}, u32[]{:S(2)}) collective-permute-start(bf16[128,1024]{1,0:T(8,128)(2,1)S(1)} %dynamic-slice_bitcast_fusion), channel_id=1, source_target_pairs={{0,1},{1,0},{2,3},{3,2},{4,5},{5,4},{6,7},{7,6},{8,9},{9,8},{10,11... | collective-permute-start | bytes 786440 | tf_op jit(solution)/shard_map/ppermute | solution.py:124
  44.9 7.5 %collective-permute-start.1 = (s32[2049]{0:T(1024)S(1)}, s32[2049]{0:T(1024)S(1)}, u32[]{:S(2)}, u32[]{:S(2)}) collective-permute-start(s32[2049]{0:T(1024)S(1)} %pad_add_fusion), channel_id=1, source_target_pairs={{0,1},{1,0},{2,3},{3,2},{4,5},{5,4},{6,7},{7,6},{8,9},{9,8},{10,11... | collective-permute-start | bytes 24596 | tf_op jit(solution)/shard_map/ppermute | solution.py:124
  48.5 22.8 %all-to-all-start = ((bf16[4,128,1024]{2,1,0:T(8,128)(2,1)}), bf16[4,128,1024]{2,1,0:T(8,128)(2,1)S(1)}, u32[]{:S(2)}, u32[]{:S(2)}) async-start(bf16[4,128,1024]{2,1,0:T(8,128)(2,1)} %pad_maximum_fusion), calls=%async_computation | async-start | bytes 2097152 | tf_op jit(solution)/shard_map/all_to_all | solution.py:176
  71.3 28.4 %copy-start.2 = (bf16[4,128,1024]{2,1,0:T(8,128)(2,1)}, bf16[4,128,1024]{2,1,0:T(8,128)(2,1)S(1)}, u32[]{:S(2)}) copy-start(bf16[4,128,1024]{2,1,0:T(8,128)(2,1)S(1)} %all-to-all-done.q_ref) | copy-start | bytes 3145732
  107.3 32.6 %all-to-all-start.2 = ((bf16[4,128,1024]{2,1,0:T(8,128)(2,1)}), bf16[4,128,1024]{2,1,0:T(8,128)(2,1)S(1)}, u32[]{:S(2)}, u32[]{:S(2)}) async-start(bf16[4,128,1024]{2,1,0:T(8,128)(2,1)} %shard_map.100), calls=%async_computation.2 | async-start | bytes 2097152 | tf_op jit(solution)/shard_map/all_to_all | solution.py:199
  140.0 6.5 %copy-start.1 = (bf16[4,128,1024]{2,1,0:T(8,128)(2,1)}, bf16[4,128,1024]{2,1,0:T(8,128)(2,1)S(1)}, u32[]{:S(2)}) copy-start(bf16[4,128,1024]{2,1,0:T(8,128)(2,1)S(1)} %all-to-all-done.2.parts_ref) | copy-start | bytes 3145732
  140.1 6.3 %collective-permute-start.2 = (bf16[128,1024]{1,0:T(8,128)(2,1)S(1)}, bf16[128,1024]{1,0:T(8,128)(2,1)S(1)}, u32[]{:S(2)}, u32[]{:S(2)}) collective-permute-start(bf16[128,1024]{1,0:T(8,128)(2,1)S(1)} %fusion.1), channel_id=1, source_target_pairs={{0,1},{1,0},{2,3},{3,2},{4,5},{5,4},{6,7},{7,6},{8,9},{9,8},{10,11... | collective-permute-start | bytes 786440 | tf_op jit(solution)/shard_map/ppermute | solution.py:124
  146.4 0.7 copy-start.4
Sparse Core Ops, SparseCore 0:
  42.1 57.4 all-gather.1

commit v6 on v5

--- a/solution.py
+++ b/solution.py
@@ -31,19 +31,22 @@
         out_ref[:, :, cols] = sums.reshape(blocks, rows, HEAD_DIM).astype(out_ref.dtype)
 
 
-def attend(queries, history, bias, mask, per_step):
+def attend(queries, history, bias, mask, part, parts, per_step):
     blocks, rows, full = queries.shape
     positions = history.shape[0]
     width = per_step * HEAD_DIM
+    all_steps = full // width
+    full = full // parts
     steps = full // width
+    skip = part * steps
     return pl.pallas_call(
         attend_kernel,
         grid=(steps,),
         in_specs=[
-            pl.BlockSpec((blocks, rows, width), lambda i: (0, 0, i)),
-            pl.BlockSpec((positions, width), lambda i: (0, i)),
-            pl.BlockSpec((positions, width), lambda i: (0, i + steps)),
-            pl.BlockSpec((per_step, 1, positions), lambda i: (i, 0, 0)),
+            pl.BlockSpec((blocks, rows, width), lambda i: (0, 0, i + skip)),
+            pl.BlockSpec((positions, width), lambda i: (0, i + skip)),
+            pl.BlockSpec((positions, width), lambda i: (0, i + skip + all_steps)),
+            pl.BlockSpec((per_step, 1, positions), lambda i: (i + skip, 0, 0)),
             pl.BlockSpec((1, positions), lambda i: (0, 0)),
         ],
         out_specs=pl.BlockSpec((blocks, rows, width), lambda i: (0, 0, i)),
@@ -85,11 +88,14 @@
     )(queries, own, self_bias[None])
 
 
-def finish_kernel(core_ref, parts_ref, other_ref, base_ref, gate_ref, gain_ref, out_ref):
+def finish_kernel(core_ref, low_ref, high_ref, other_low_ref, other_high_ref, base_ref, gate_ref, gain_ref, out_ref):
     first_core = core_ref[0] == 0
-    a, b, c, d = (parts_ref[i].astype(jnp.float32) for i in range(4))
-    mine = jnp.where(first_core, a + b, c + d)
-    other = other_ref[...].astype(jnp.float32)
+    halves = []
+    for parts_ref in (low_ref, high_ref):
+        a, b, c, d = (parts_ref[i].astype(jnp.float32) for i in range(4))
+        halves.append(jnp.where(first_core, a + d, b + c))
+    mine = jnp.concatenate(halves, axis=-1)
+    other = jnp.concatenate([other_low_ref[...], other_high_ref[...]], axis=-1).astype(jnp.float32)
     low = jnp.where(first_core, mine, other)
     high = jnp.where(first_core, other, mine)
     total = base_ref[...] + jnp.concatenate([low, high], axis=-1)
@@ -100,24 +106,20 @@
     out_ref[...] = (normed * gate_ref[...].astype(jnp.float32)).astype(out_ref.dtype)
 
 
-def finish(core, parts, other, base, gate, gain):
+def finish(core, parts, others, base, gate, gain):
     rows, width = gate.shape
     block = 64
     row_spec = lambda cols: pl.BlockSpec((block, cols), lambda i: (i, 0))
     return pl.pallas_call(
         finish_kernel,
         grid=(rows // block,),
-        in_specs=[
-            pl.BlockSpec(memory_space=pltpu.SMEM),
-            pl.BlockSpec((4, block, width // 2), lambda i: (0, i, 0)),
-            row_spec(width // 2),
-            row_spec(width),
-            row_spec(width),
-            pl.BlockSpec((1, width), lambda i: (0, 0)),
-        ],
+        in_specs=[pl.BlockSpec(memory_space=pltpu.SMEM)]
+        + [pl.BlockSpec((4, block, width // 4), lambda i: (0, i, 0))] * 2
+        + [row_spec(width // 4)] * 2
+        + [row_spec(width), row_spec(width), pl.BlockSpec((1, width), lambda i: (0, 0))],
         out_specs=row_spec(width),
         out_shape=jax.ShapeDtypeStruct((rows, width), jnp.bfloat16),
-    )(core[None], parts, other, base, gate, gain[None])
+    )(core[None], *parts, *others, base, gate, gain[None])
 
 
 def swapped(value):
@@ -137,8 +139,8 @@
     norm_gain,
 ):
     core = lax.axis_index("core")
-    side = lax.axis_index("yh1")
-    half_y = lax.axis_index("yh0")
+    upper_y = lax.axis_index("yh1")
+    side = upper_y ^ lax.axis_index("yh0")
     group_index = lax.axis_index(GROUP)
     groups = lax.axis_size(GROUP)
     z_size = lax.axis_size("z")
@@ -148,22 +150,23 @@
 
     holding = (holders // slots).reshape(groups, slots)
     slot_of = (holders % slots).reshape(groups, slots)
-    chosen = jnp.sum(jnp.where(holding == group_index, slot_of, 0), axis=1)
-    by_half = jnp.stack(
+    chosen = jnp.sum(jnp.where(holding == group_index, slot_of, 0), axis=1).reshape(groups // 2, 2).T
+    chosen = jnp.where(upper_y == 0, chosen, chosen[::-1]).reshape(-1)
+    picked = cache_store[chosen, 0].reshape(groups, 1, piece_len, double_width)
+    outgoing = jnp.concatenate(
         [
             jnp.concatenate(
                 [
-                    cache_store[:, 0, :, h * half_width : (h + 1) * half_width],
-                    cache_store[:, 0, :, width + h * half_width : width + (h + 1) * half_width],
+                    picked[..., h * half_width : (h + 1) * half_width],
+                    picked[..., width + h * half_width : width + (h + 1) * half_width],
                 ],
                 axis=-1,
             )
             for h in range(2)
-        ]
-    ).reshape(2 * slots, piece_len, width)
-    places = chosen.reshape(groups // 2, 2).T[:, :, None] + slots * jnp.arange(2, dtype=jnp.int32)
-    outgoing = by_half[places.reshape(-1)]
-    incoming = lax.all_to_all(outgoing, ("yh1",) + GROUP, 0, 0, tiled=True)
+        ],
+        axis=1,
+    ).reshape(2 * groups, piece_len, width)
+    incoming = lax.all_to_all(outgoing, ("yh0",) + GROUP, 0, 0, tiled=True)
     pieces = incoming.reshape(2 * groups * piece_len, width)
     history = lax.all_gather(pieces, "z", tiled=True)
 
@@ -173,7 +176,7 @@
     partner_half = swapped(other_half)
     first = jnp.where(core == 0, own_half, partner_half)
     second = jnp.where(core == 0, partner_half, own_half)
-    spread = lax.all_to_all(jnp.stack([first, first, second, second]), Y, 0, 0, tiled=True)
+    spread = lax.all_to_all(jnp.stack([first, second, second, first]), Y, 0, 0, tiled=True)
 
     about = jnp.concatenate([buckets[0], lengths])
     about = jnp.where(core == side, about, swapped(about))
@@ -182,7 +185,7 @@
     arrived = own_holding[None, :] == jnp.arange(groups, dtype=jnp.int32)[:, None]
     piece_of = jnp.sum(jnp.where(arrived, jnp.arange(slots, dtype=jnp.int32)[None, :], 0), axis=1)
     order = jnp.arange(z_size, dtype=jnp.int32)[:, None, None, None]
-    order = order + (2 * jnp.arange(2, dtype=jnp.int32)[None, :, None, None] + half_y) * z_size
+    order = order + (jnp.arange(2, dtype=jnp.int32)[None, :, None, None] + 2 * upper_y) * z_size
     place = (
         (order * slots + piece_of[None, None, :, None]) * piece_len
         + jnp.arange(piece_len, dtype=jnp.int32)[None, None, None, :]
@@ -195,11 +198,15 @@
     bias = 0.5 * jnp.einsum("kn,nh->hk", one_hot, own_bias, precision=lax.Precision.HIGHEST)
 
     base = own_term(queries, cand_kv[0], self_bias)
-    partial = attend(spread, history, bias[:, None, :], mask, 2)
-    parts = lax.all_to_all(partial, Y, 0, 0, tiled=True)
-    pair = lax.dynamic_slice_in_dim(parts, 2 * (1 - core), 2).astype(jnp.float32)
-    other = swapped((pair[0] + pair[1]).astype(jnp.bfloat16))
-    return finish(core, parts, other, base, cand_gate[0], norm_gain)[None]
+    bias, mask, base = lax.optimization_barrier((bias[:, None, :], mask, base))
+    parts, others = [], []
+    for part in range(2):
+        partial = attend(spread, history, bias, mask, part, 2, 2)
+        came = lax.all_to_all(partial, Y, 0, 0, tiled=True)
+        a, b, c, d = (came[i].astype(jnp.float32) for i in range(4))
+        parts.append(came)
+        others.append(swapped(jnp.where(core == 0, b + c, a + d).astype(jnp.bfloat16)))
+    return finish(core, parts, others, base, cand_gate[0], norm_gain)[None]
 
 
 def solution(mesh):

time: 158 us -> 153 us (0.968)
  waiting for transfers between devices: 64.2 us -> 53.6 us
  starting transfers between devices: 16.7 us -> 26.6 us
  blocking collectives: 29.2 us -> 25.8 us
  Pallas kernels: 14.3 us -> 16.4 us
  local copies, waits for them, and re-layouts: 13.4 us -> 11.7 us
    all_gather x1, waiting for transfers between devices: 28.4 us -> 20.8 us  [per_device(): history = lax.all_gather(pieces, 'z', tiled=True)]
    ppermute x3 -> x4, starting transfers between devices: 6.76 us -> 12 us  [swapped(): return lax.ppermute(value, 'core', [(0, 1), (1, 0)])]
    all_to_all x2 -> x3, waiting for transfers between devices: 35.8 us -> 30.6 us  [the longest x2 18.9 us: per_device(): came = lax.all_to_all(partial, Y, 0, 0, tiled=True)]
    all_to_all x2 -> x3, starting transfers between devices: 9.97 us -> 14.6 us  [the longest x2 11.1 us: per_device(): came = lax.all_to_all(partial, Y, 0, 0, tiled=True)]
    all_to_all x1, blocking collectives: 29.2 us -> 25.8 us  [per_device(): incoming = lax.all_to_all(outgoing, ('yh0',) + GROUP, 0, 0, tiled=True)]
    ppermute x3 -> x4, waiting for transfers between devices: 0.01 us -> 2.27 us  [swapped(): return lax.ppermute(value, 'core', [(0, 1), (1, 0)])]
    squeeze x2 -> x0, local copies, waits for them, and re-layouts: 2.14 us -> none  [the longest x1 1.19 us: per_device(): cache_store[:, 0, :, h * half_width:(h + 1) * half_width]]
    pallas_call x1 -> x2, Pallas kernels: 7.69 us -> 9.72 us  [attend(): pl.pallas_call(attend_kernel, grid=(steps,), in_specs=[pl.BlockSpec((bloc...]
  transfers between devices with their start and end apart: 6 -> 8, of which waited for: 3 -> 6; matrix products, arithmetic and copies ran while one was open for 7% -> 7% of each run, Pallas kernels for 2% -> 6%
where the time goes in v6:
time: 153 us
  waiting for transfers between devices  53.6 us (35%)
  starting transfers between devices  26.6 us (17%)
  blocking collectives  25.8 us (17%)
  Pallas kernels  16.4 us (11%)
  between operations  14.3 us (9%)
  local copies, waits for them, and re-layouts  11.7 us (8%)
  other arithmetic  3.66 us (2%)
    all_to_all x1, blocking collectives, per_device(): incoming = lax.all_to_all(outgoing, ('yh0',) + GROUP, 0, 0, tiled=True)  25.8 us
    all_gather x1, waiting for transfers between devices, per_device(): history = lax.all_gather(pieces, 'z', tiled=True)  20.8 us
    all_to_all x2, waiting for transfers between devices, per_device(): came = lax.all_to_all(partial, Y, 0, 0, tiled=True)  18.9 us
    ppermute x4, starting transfers between devices, swapped(): return lax.ppermute(value, 'core', [(0, 1), (1, 0)])  12 us
    all_to_all x1, waiting for transfers between devices, per_device(): lax.all_to_all(jnp.stack([first, second, second, first]), Y, 0, 0, tiled=...  11.7 us
    all_to_all x2, starting transfers between devices, per_device(): came = lax.all_to_all(partial, Y, 0, 0, tiled=True)  11.1 us
    pallas_call x2, Pallas kernels, attend(): pl.pallas_call(attend_kernel, grid=(steps,), in_specs=[pl.BlockSpec((bloc...  9.72 us
    gather x1, local copies, waits for them, and re-layouts, per_device(): about[place][:, None]  6.14 us
  transfers between devices with their start and end apart: 8, of which 6 were waited for; matrix products, arithmetic and copies ran while one was open for 7% of the time, Pallas kernels for 6%

profile of v6, /device:TPU:1, one launch (start us, length us, event | category | flops | bytes accessed | tf_op | source)
XLA Modules:
  0.0 152.5 jit_solution(14113019010398350080)
XLA Ops:
  6.6 0.8 and_select_fusion.1
  8.0 1.0 gather_fusion
  9.7 25.8 %all_to_all.20 = bf16[32,4,2048]{2,1,0:T(4,128)(2,1)S(1)} all-to-all(bf16[32,4,2048]{2,1,0:T(4,128)(2,1)S(1)} %bitcast.41), channel_id=1, replica_groups=mesh['yh1'=2,'yh0'=2,'z'=8,'x'=4,'ylo'=2,'core'=2] {'yh0','x','ylo','core'}, dimensions={0} | all-to-all | bytes 1048576 | tf_op jit(solution)/shard_map/all_to_all | solution.py:169
  35.5 0.9 reshape.175
  37.1 3.1 %collective-permute-start.1 = (s32[2049]{0:T(1024)S(1)}, s32[2049]{0:T(1024)S(1)}, u32[]{:S(2)}, u32[]{:S(2)}) collective-permute-start(s32[2049]{0:T(1024)S(1)} %pad_add_fusion), channel_id=1, source_target_pairs={{0,1},{1,0},{2,3},{3,2},{4,5},{5,4},{6,7},{7,6},{8,9},{9,8},{10,11... | collective-permute-start | bytes 24596 | tf_op jit(solution)/shard_map/ppermute | solution.py:126
  40.3 1.9 %collective-permute-start = (bf16[128,1024]{1,0:T(8,128)(2,1)S(1)}, bf16[128,1024]{1,0:T(8,128)(2,1)S(1)}, u32[]{:S(2)}, u32[]{:S(2)}) collective-permute-start(bf16[128,1024]{1,0:T(8,128)(2,1)S(1)} %dynamic-slice_bitcast_fusion), channel_id=1, source_target_pairs={{0,1},{1,0},{2,3},{3,2},{4,5},{5,4},{6,7},{7,6},{8,9},{9,8},{10,11... | collective-permute-start | bytes 786440 | tf_op jit(solution)/shard_map/ppermute | solution.py:126
  42.4 1.3 collective-permute-done
  43.9 1.1 pad_maximum_fusion
  45.0 3.5 %all-to-all-start = ((bf16[4,128,1024]{2,1,0:T(8,128)(2,1)}), bf16[4,128,1024]{2,1,0:T(8,128)(2,1)S(1)}, u32[]{:S(2)}, u32[]{:S(2)}) async-start(bf16[4,128,1024]{2,1,0:T(8,128)(2,1)} %pad_maximum_fusion), calls=%async_computation | async-start | bytes 2097152 | tf_op jit(solution)/shard_map/all_to_all | solution.py:179
  48.9 3.8 %shard_map.100.base_ref = f32[128,2048]{1,0:T(8,128)} custom-call(bf16[128,2048]{1,0:T(8,128)(2,1)} %bitcast.39, bf16[128,4096]{1,0:T(8,128)(2,1)} %bitcast.42, f32[1,16]{1,0:T(1,128)} %bitcast.49), custom_call_target="tpu_custom_call" | custom-call | tf_op jit(solution)/shard_map/pallas_call | solution.py:78
  53.2 0.7 compare_convert_fusion
  54.7 6.1 %gather_fusion.1 = s32[1024]{0:T(1024)S(1)} fusion(s32[2049]{0:T(1024)S(1)} %broadcast_select_fusion, s32[1024]{0:T(1024)S(1)} %broadcast_clamp_fusion), kind=kCustom, calls=%fused_computation.1 | custom fusion | bytes 12288 | tf_op jit(solution)/shard_map/gather | solution.py:195
  61.9 11.7 %all-to-all-done.q_ref = bf16[4,128,1024]{2,1,0:T(8,128)(2,1)S(1)} async-done(((bf16[4,128,1024]{2,1,0:T(8,128)(2,1)}), bf16[4,128,1024]{2,1,0:T(8,128)(2,1)S(1)}, u32[]{:S(2)}, u32[]{:S(2)}) %all-to-all-start) | async-done | bytes 1048608 | tf_op jit(solution)/shard_map/all_to_all | solution.py:179
  73.7 20.8 %all-gather.2.cloned.1.call-done.k_ref.v_ref = bf16[1024,2048]{1,0:T(8,128)(2,1)} async-done(((bf16[128,2048]{1,0:T(8,128)(2,1)}), bf16[1024,2048]{1,0:T(8,128)(2,1)}) %all-gather.2.cloned.1.call-update) | async-done | bytes 4194320 | tf_op jit(solution)/shard_map/all_gather | solution.py:171
  94.4 4.9 %shard_map.101 = bf16[4,128,512]{2,1,0:T(8,128)(2,1)} custom-call(bf16[4,128,1024]{2,1,0:T(8,128)(2,1)} %copy-done.1, bf16[1024,2048]{1,0:T(8,128)(2,1)} %all-gather.2.cloned.1.call-done.k_ref.v_ref, bf16[1024,2048]{1,0:T(8,128)(2,1)} %all-gather.2.cloned.1.call-done.k_ref.v_ref, f32[8,1,1024]{2,1,0:T(1,128)} %broadcast_in_dim.44.bias_ref, ...), custom_call_target="tpu_custom_call" | custom-call | flops 1073741824 | bytes 3145728 | tf_op jit(solution)/shard_map/pallas_call | solution.py:42
  99.3 6.5 %all-to-all-start.2 = ((bf16[4,128,512]{2,1,0:T(8,128)(2,1)}), bf16[4,128,512]{2,1,0:T(8,128)(2,1)S(1)}, u32[]{:S(2)}, u32[]{:S(2)}) async-start(bf16[4,128,512]{2,1,0:T(8,128)(2,1)} %shard_map.101), calls=%async_computation.2 | async-start | bytes 1048576 | tf_op jit(solution)/shard_map/all_to_all | solution.py:205
  105.8 4.8 %shard_map.102 = bf16[4,128,512]{2,1,0:T(8,128)(2,1)} custom-call(bf16[4,128,1024]{2,1,0:T(8,128)(2,1)} %copy-done.1, bf16[1024,2048]{1,0:T(8,128)(2,1)} %all-gather.2.cloned.1.call-done.k_ref.v_ref, bf16[1024,2048]{1,0:T(8,128)(2,1)} %all-gather.2.cloned.1.call-done.k_ref.v_ref, f32[8,1,1024]{2,1,0:T(1,128)} %broadcast_in_dim.44.bias_ref, ...), custom_call_target="tpu_custom_call" | custom-call | flops 1073741824 | bytes 3145728 | tf_op jit(solution)/shard_map/pallas_call | solution.py:42
  110.6 9.9 %all-to-all-done.2.low_ref = bf16[4,128,512]{2,1,0:T(8,128)(2,1)S(1)} async-done(((bf16[4,128,512]{2,1,0:T(8,128)(2,1)}), bf16[4,128,512]{2,1,0:T(8,128)(2,1)S(1)}, u32[]{:S(2)}, u32[]{:S(2)}) %all-to-all-start.2) | async-done | bytes 524320 | tf_op jit(solution)/shard_map/all_to_all | solution.py:205
  120.4 4.6 %all-to-all-start.3 = ((bf16[4,128,512]{2,1,0:T(8,128)(2,1)}), bf16[4,128,512]{2,1,0:T(8,128)(2,1)S(1)}, u32[]{:S(2)}, u32[]{:S(2)}) async-start(bf16[4,128,512]{2,1,0:T(8,128)(2,1)} %shard_map.102), calls=%async_computation.3 | async-start | bytes 1048576 | tf_op jit(solution)/shard_map/all_to_all | solution.py:205
  125.1 2.9 %collective-permute-start.2 = (bf16[128,512]{1,0:T(8,128)(2,1)S(1)}, bf16[128,512]{1,0:T(8,128)(2,1)S(1)}, u32[]{:S(2)}, u32[]{:S(2)}) collective-permute-start(bf16[128,512]{1,0:T(8,128)(2,1)S(1)} %fusion.3), channel_id=1, source_target_pairs={{0,1},{1,0},{2,3},{3,2},{4,5},{5,4},{6,7},{7,6},{8,9},{9,8},{10,11... | collective-permute-start | bytes 393224 | tf_op jit(solution)/shard_map/ppermute | solution.py:126
  128.0 9.0 %all-to-all-done.3.high_ref = bf16[4,128,512]{2,1,0:T(8,128)(2,1)S(1)} async-done(((bf16[4,128,512]{2,1,0:T(8,128)(2,1)}), bf16[4,128,512]{2,1,0:T(8,128)(2,1)S(1)}, u32[]{:S(2)}, u32[]{:S(2)}) %all-to-all-start.3) | async-done | bytes 524320 | tf_op jit(solution)/shard_map/all_to_all | solution.py:205
  137.1 4.1 %collective-permute-start.3 = (bf16[128,512]{1,0:T(8,128)(2,1)S(1)}, bf16[128,512]{1,0:T(8,128)(2,1)S(1)}, u32[]{:S(2)}, u32[]{:S(2)}) collective-permute-start(bf16[128,512]{1,0:T(8,128)(2,1)S(1)} %fusion.4), channel_id=1, source_target_pairs={{0,1},{1,0},{2,3},{3,2},{4,5},{5,4},{6,7},{7,6},{8,9},{9,8},{10,11... | collective-permute-start | bytes 393224 | tf_op jit(solution)/shard_map/ppermute | solution.py:126
  141.2 0.9 collective-permute-done.3.other_high_ref
  142.8 2.8 %shard_map.103 = bf16[128,2048]{1,0:T(8,128)(2,1)} custom-call(s32[1]{0:T(128)} %bitcast.core_ref, bf16[4,128,512]{2,1,0:T(8,128)(2,1)} %copy-done.2, bf16[4,128,512]{2,1,0:T(8,128)(2,1)} %copy-done.3, bf16[128,512]{1,0:T(8,128)(2,1)} %copy-done.5, bf16[128,512]{1,0:T(8,128)(2,1)} %copy-done.6, f32[128,2048]{1,0:T(8,128)} %shard_map.100.base_ref, ...), custom_call_target="tpu_custom_call" | custom-call | tf_op jit(solution)/shard_map/pallas_call | solution.py:113
  (53 shorter events, 5.1 us)
Async XLA Ops:
  6.5 1.4 copy-start
  6.5 30.6 %copy-start.7 = (s32[1,2048]{1,0:T(1,128)S(1)}, s32[1,2048]{1,0:T(1,128)}, u32[]{:S(2)}) copy-start(s32[1,2048]{1,0:T(1,128)} %param.16) | copy-start | bytes 24580
  6.5 33.7 %copy-start.4 = (bf16[1,128,2048]{2,1,0:T(8,128)(2,1)S(1)}, bf16[1,128,2048]{2,1,0:T(8,128)(2,1)}, u32[]{:S(2)}) copy-start(bf16[1,128,2048]{2,1,0:T(8,128)(2,1)} %param.10) | copy-start | bytes 1572868
  6.5 87.9 %all-gather.2.cloned.1.call-start = ((), (), s32[]{:S(2)}) async-start(), calls=%async_computation.4 | async-start | bytes 4718592 | tf_op jit(solution)/shard_map/all_gather | solution.py:171
  37.1 15.6 %collective-permute-start.1 = (s32[2049]{0:T(1024)S(1)}, s32[2049]{0:T(1024)S(1)}, u32[]{:S(2)}, u32[]{:S(2)}) collective-permute-start(s32[2049]{0:T(1024)S(1)} %pad_add_fusion), channel_id=1, source_target_pairs={{0,1},{1,0},{2,3},{3,2},{4,5},{5,4},{6,7},{7,6},{8,9},{9,8},{10,11... | collective-permute-start | bytes 24596 | tf_op jit(solution)/shard_map/ppermute | solution.py:126
  40.3 3.4 %collective-permute-start = (bf16[128,1024]{1,0:T(8,128)(2,1)S(1)}, bf16[128,1024]{1,0:T(8,128)(2,1)S(1)}, u32[]{:S(2)}, u32[]{:S(2)}) collective-permute-start(bf16[128,1024]{1,0:T(8,128)(2,1)S(1)} %dynamic-slice_bitcast_fusion), channel_id=1, source_target_pairs={{0,1},{1,0},{2,3},{3,2},{4,5},{5,4},{6,7},{7,6},{8,9},{9,8},{10,11... | collective-permute-start | bytes 786440 | tf_op jit(solution)/shard_map/ppermute | solution.py:126
  45.0 28.7 %all-to-all-start = ((bf16[4,128,1024]{2,1,0:T(8,128)(2,1)}), bf16[4,128,1024]{2,1,0:T(8,128)(2,1)S(1)}, u32[]{:S(2)}, u32[]{:S(2)}) async-start(bf16[4,128,1024]{2,1,0:T(8,128)(2,1)} %pad_maximum_fusion), calls=%async_computation | async-start | bytes 2097152 | tf_op jit(solution)/shard_map/all_to_all | solution.py:179
  48.5 12.3 %copy-start.8 = (f32[128,16]{0,1:T(8,128)S(1)}, f32[128,16]{0,1:T(8,128)}, u32[]{:S(2)}) copy-start(f32[128,16]{0,1:T(8,128)} %param.17) | copy-start | bytes 24580
  73.7 20.8 %copy-start.1 = (bf16[4,128,1024]{2,1,0:T(8,128)(2,1)}, bf16[4,128,1024]{2,1,0:T(8,128)(2,1)S(1)}, u32[]{:S(2)}) copy-start(bf16[4,128,1024]{2,1,0:T(8,128)(2,1)S(1)} %all-to-all-done.q_ref) | copy-start | bytes 3145732
  99.3 21.1 %all-to-all-start.2 = ((bf16[4,128,512]{2,1,0:T(8,128)(2,1)}), bf16[4,128,512]{2,1,0:T(8,128)(2,1)S(1)}, u32[]{:S(2)}, u32[]{:S(2)}) async-start(bf16[4,128,512]{2,1,0:T(8,128)(2,1)} %shard_map.101), calls=%async_computation.2 | async-start | bytes 1048576 | tf_op jit(solution)/shard_map/all_to_all | solution.py:205
  120.4 21.7 %copy-start.2 = (bf16[4,128,512]{2,1,0:T(8,128)(2,1)}, bf16[4,128,512]{2,1,0:T(8,128)(2,1)S(1)}, u32[]{:S(2)}) copy-start(bf16[4,128,512]{2,1,0:T(8,128)(2,1)S(1)} %all-to-all-done.2.low_ref) | copy-start | bytes 1572868
  120.4 16.6 %all-to-all-start.3 = ((bf16[4,128,512]{2,1,0:T(8,128)(2,1)}), bf16[4,128,512]{2,1,0:T(8,128)(2,1)S(1)}, u32[]{:S(2)}, u32[]{:S(2)}) async-start(bf16[4,128,512]{2,1,0:T(8,128)(2,1)} %shard_map.102), calls=%async_computation.3 | async-start | bytes 1048576 | tf_op jit(solution)/shard_map/all_to_all | solution.py:205
  125.1 16.1 %collective-permute-start.2 = (bf16[128,512]{1,0:T(8,128)(2,1)S(1)}, bf16[128,512]{1,0:T(8,128)(2,1)S(1)}, u32[]{:S(2)}, u32[]{:S(2)}) collective-permute-start(bf16[128,512]{1,0:T(8,128)(2,1)S(1)} %fusion.3), channel_id=1, source_target_pairs={{0,1},{1,0},{2,3},{3,2},{4,5},{5,4},{6,7},{7,6},{8,9},{9,8},{10,11... | collective-permute-start | bytes 393224 | tf_op jit(solution)/shard_map/ppermute | solution.py:126
  137.0 5.2 %copy-start.3 = (bf16[4,128,512]{2,1,0:T(8,128)(2,1)}, bf16[4,128,512]{2,1,0:T(8,128)(2,1)S(1)}, u32[]{:S(2)}) copy-start(bf16[4,128,512]{2,1,0:T(8,128)(2,1)S(1)} %all-to-all-done.3.high_ref) | copy-start | bytes 1572868
  137.1 5.1 %collective-permute-start.3 = (bf16[128,512]{1,0:T(8,128)(2,1)S(1)}, bf16[128,512]{1,0:T(8,128)(2,1)S(1)}, u32[]{:S(2)}, u32[]{:S(2)}) collective-permute-start(bf16[128,512]{1,0:T(8,128)(2,1)S(1)} %fusion.4), channel_id=1, source_target_pairs={{0,1},{1,0},{2,3},{3,2},{4,5},{5,4},{6,7},{7,6},{8,9},{9,8},{10,11... | collective-permute-start | bytes 393224 | tf_op jit(solution)/shard_map/ppermute | solution.py:126
  141.2 1.0 copy-start.5
  142.2 0.6 copy-start.6
Sparse Core Ops, SparseCore 0:
  36.6 57.8 all-gather.1

commit v7 on v6

--- a/solution.py
+++ b/solution.py
@@ -15,49 +15,67 @@
 Y = ("yh1", "yh0")
 
 
-def attend_kernel(q_ref, k_ref, v_ref, bias_ref, mask_ref, out_ref):
+HOMES = {(0, 0): (1, 3, 2, 0), (0, 1): (0, 1, 3, 2), (3, 0): (2, 0, 1, 3), (3, 1): (3, 2, 0, 1)}
+
+
+def send_pairs(step):
+    pairs = []
+    for (yhi, core), homes in HOMES.items():
+        pairs.append((yhi * 2 + core, homes[step] * 2))
+        pairs.append(((yhi + 2) % 4 * 2 + 1 - core, (homes[step] + 2) % 4 * 2 + 1))
+    return pairs
+
+
+def send_order():
+    order = [None] * 8
+    for (yhi, core), homes in HOMES.items():
+        order[yhi * 2 + core] = list(homes)
+        order[(yhi + 2) % 4 * 2 + 1 - core] = [(home + 2) % 4 for home in homes]
+    return jnp.array(order, jnp.int32)
+
+
+def attend_kernel(order_ref, q_ref, k_ref, v_ref, bias_ref, mask_ref, *out_refs):
     blocks, rows, width = q_ref.shape
     scale = 0.5 / math.sqrt(HEAD_DIM)
     inside = mask_ref[...] > 0.0
     for head in range(width // HEAD_DIM):
         cols = slice(head * HEAD_DIM, (head + 1) * HEAD_DIM)
-        queries = q_ref[:, :, cols].reshape(blocks * rows, HEAD_DIM)
+        queries = jnp.concatenate([q_ref[order_ref[i], :, cols] for i in range(blocks)], axis=0)
         scores = lax.dot_general(
             queries, k_ref[:, cols], (((1,), (1,)), ((), ())), preferred_element_type=jnp.float32
         )
         half = scores * scale + bias_ref[head]
         weights = jnp.where(inside, half + half * jnp.tanh(half), 0.0).astype(jnp.bfloat16)
         sums = jnp.dot(weights, v_ref[:, cols], preferred_element_type=jnp.float32)
-        out_ref[:, :, cols] = sums.reshape(blocks, rows, HEAD_DIM).astype(out_ref.dtype)
-
-
-def attend(queries, history, bias, mask, part, parts, per_step):
+        for i, out_ref in enumerate(out_refs):
+            out_ref[:, cols] = sums[i * rows : (i + 1) * rows].astype(out_ref.dtype)
+
+
+def attend(order, queries, history, bias, mask, per_step):
     blocks, rows, full = queries.shape
     positions = history.shape[0]
     width = per_step * HEAD_DIM
-    all_steps = full // width
-    full = full // parts
     steps = full // width
-    skip = part * steps
     return pl.pallas_call(
         attend_kernel,
         grid=(steps,),
         in_specs=[
-            pl.BlockSpec((blocks, rows, width), lambda i: (0, 0, i + skip)),
-            pl.BlockSpec((positions, width), lambda i: (0, i + skip)),
-            pl.BlockSpec((positions, width), lambda i: (0, i + skip + all_steps)),
-            pl.BlockSpec((per_step, 1, positions), lambda i: (i + skip, 0, 0)),
+            pl.BlockSpec(memory_space=pltpu.SMEM),
+            pl.BlockSpec((blocks, rows, width), lambda i: (0, 0, i)),
+            pl.BlockSpec((positions, width), lambda i: (0, i)),
+            pl.BlockSpec((positions, width), lambda i: (0, i + steps)),
+            pl.BlockSpec((per_step, 1, positions), lambda i: (i, 0, 0)),
             pl.BlockSpec((1, positions), lambda i: (0, 0)),
         ],
-        out_specs=pl.BlockSpec((blocks, rows, width), lambda i: (0, 0, i)),
-        out_shape=jax.ShapeDtypeStruct((blocks, rows, full), jnp.bfloat16),
+        out_specs=[pl.BlockSpec((rows, width), lambda i: (0, i))] * blocks,
+        out_shape=[jax.ShapeDtypeStruct((rows, full), jnp.bfloat16)] * blocks,
         compiler_params=pltpu.CompilerParams(vmem_limit_bytes=56 * 1024 * 1024),
         cost_estimate=pl.CostEstimate(
             flops=4 * blocks * rows * positions * full,
             bytes_accessed=4 * positions * full + 4 * blocks * rows * full,
             transcendentals=blocks * rows * positions * full // HEAD_DIM,
         ),
-    )(queries, history, history, bias, mask)
+    )(order, queries, history, history, bias, mask)
 
 
 def own_kernel(q_ref, own_ref, self_bias_ref, out_ref):
@@ -88,16 +106,12 @@
     )(queries, own, self_bias[None])
 
 
-def finish_kernel(core_ref, low_ref, high_ref, other_low_ref, other_high_ref, base_ref, gate_ref, gain_ref, out_ref):
-    first_core = core_ref[0] == 0
-    halves = []
-    for parts_ref in (low_ref, high_ref):
-        a, b, c, d = (parts_ref[i].astype(jnp.float32) for i in range(4))
-        halves.append(jnp.where(first_core, a + d, b + c))
-    mine = jnp.concatenate(halves, axis=-1)
-    other = jnp.concatenate([other_low_ref[...], other_high_ref[...]], axis=-1).astype(jnp.float32)
-    low = jnp.where(first_core, mine, other)
-    high = jnp.where(first_core, other, mine)
+def finish_kernel(flag_ref, a_ref, b_ref, c_ref, d_ref, base_ref, gate_ref, gain_ref, out_ref):
+    a, b, c, d = (ref[...].astype(jnp.float32) for ref in (a_ref, b_ref, c_ref, d_ref))
+    odd, even = a + c, b + d
+    even_low = flag_ref[0] == 1
+    low = jnp.where(even_low, even, odd)
+    high = jnp.where(even_low, odd, even)
     total = base_ref[...] + jnp.concatenate([low, high], axis=-1)
     average = jnp.mean(total, axis=-1, keepdims=True)
     centered = total - average
@@ -106,7 +120,7 @@
     out_ref[...] = (normed * gate_ref[...].astype(jnp.float32)).astype(out_ref.dtype)
 
 
-def finish(core, parts, others, base, gate, gain):
+def finish(flag, parts, base, gate, gain):
     rows, width = gate.shape
     block = 64
     row_spec = lambda cols: pl.BlockSpec((block, cols), lambda i: (i, 0))
@@ -114,12 +128,11 @@
         finish_kernel,
         grid=(rows // block,),
         in_specs=[pl.BlockSpec(memory_space=pltpu.SMEM)]
-        + [pl.BlockSpec((4, block, width // 4), lambda i: (0, i, 0))] * 2
-        + [row_spec(width // 4)] * 2
+        + [row_spec(width // 2)] * 4
         + [row_spec(width), row_spec(width), pl.BlockSpec((1, width), lambda i: (0, 0))],
         out_specs=row_spec(width),
         out_shape=jax.ShapeDtypeStruct((rows, width), jnp.bfloat16),
-    )(core[None], *parts, *others, base, gate, gain[None])
+    )(flag[None], *parts, base, gate, gain[None])
 
 
 def swapped(value):
@@ -199,14 +212,13 @@
 
     base = own_term(queries, cand_kv[0], self_bias)
     bias, mask, base = lax.optimization_barrier((bias[:, None, :], mask, base))
-    parts, others = [], []
-    for part in range(2):
-        partial = attend(spread, history, bias, mask, part, 2, 2)
-        came = lax.all_to_all(partial, Y, 0, 0, tiled=True)
-        a, b, c, d = (came[i].astype(jnp.float32) for i in range(4))
-        parts.append(came)
-        others.append(swapped(jnp.where(core == 0, b + c, a + d).astype(jnp.bfloat16)))
-    return finish(core, parts, others, base, cand_gate[0], norm_gain)[None]
+    order = send_order()[lax.axis_index(Y + ("core",))]
+    partial = attend(order, spread, history, bias, mask, 2)
+    parts = [None] * 4
+    for step in (3, 2, 1, 0):
+        parts[step] = lax.ppermute(partial[step], Y + ("core",), send_pairs(step))
+    flag = ((core == 0) == (core == side)).astype(jnp.int32)
+    return finish(flag, parts, base, cand_gate[0], norm_gain)[None]
 
 
 def solution(mesh):

time: 153 us -> 147 us (0.961)
  waiting for transfers between devices: 53.6 us -> 49.5 us
  Pallas kernels: 16.4 us -> 14.4 us
    all_to_all x2 -> x0, waiting for transfers between devices: 18.9 us -> none  [per_device(): came = lax.all_to_all(partial, Y, 0, 0, tiled=True)]
    ppermute x0 -> x4, starting transfers between devices: none -> 17 us  [per_device(): parts[step] = lax.ppermute(partial[step], Y + ('core',), send_pairs(step))]
    ppermute x0 -> x4, waiting for transfers between devices: none -> 16.9 us  [per_device(): parts[step] = lax.ppermute(partial[step], Y + ('core',), send_pairs(step))]
    all_to_all x2 -> x0, starting transfers between devices: 11.1 us -> none  [per_device(): came = lax.all_to_all(partial, Y, 0, 0, tiled=True)]
    ppermute x4 -> x2, starting transfers between devices: 12 us -> 5.06 us  [swapped(): return lax.ppermute(value, 'core', [(0, 1), (1, 0)])]
    pallas_call x2 -> x1, Pallas kernels: 9.72 us -> 7.74 us  [attend(): pl.pallas_call(attend_kernel, grid=(steps,), in_specs=[pl.BlockSpec(memor...]
  transfers between devices with their start and end apart: 8 -> 8, of which waited for: 6 -> 5; matrix products, arithmetic and copies ran while one was open for 7% -> 8% of each run, Pallas kernels for 6% -> 3%
where the time goes in v7:
time: 147 us
  waiting for transfers between devices  49.5 us (34%)
  blocking collectives  25.8 us (18%)
  starting transfers between devices  25.6 us (17%)
  Pallas kernels  14.4 us (10%)
  between operations  14.3 us (10%)
  local copies, waits for them, and re-layouts  13.1 us (9%)
  other arithmetic  3.55 us (2%)
    all_to_all x1, blocking collectives, per_device(): incoming = lax.all_to_all(outgoing, ('yh0',) + GROUP, 0, 0, tiled=True)  25.8 us
    all_gather x1, waiting for transfers between devices, per_device(): history = lax.all_gather(pieces, 'z', tiled=True)  20.7 us
    ppermute x4, starting transfers between devices, per_device(): parts[step] = lax.ppermute(partial[step], Y + ('core',), send_pairs(step))  17 us
    ppermute x4, waiting for transfers between devices, per_device(): parts[step] = lax.ppermute(partial[step], Y + ('core',), send_pairs(step))  16.9 us
    all_to_all x1, waiting for transfers between devices, per_device(): lax.all_to_all(jnp.stack([first, second, second, first]), Y, 0, 0, tiled=...  10.5 us
    pallas_call x1, Pallas kernels, attend(): pl.pallas_call(attend_kernel, grid=(steps,), in_specs=[pl.BlockSpec(memor...  7.74 us
    gather x1, local copies, waits for them, and re-layouts, per_device(): about[place][:, None]  6.14 us
    ppermute x2, starting transfers between devices, swapped(): return lax.ppermute(value, 'core', [(0, 1), (1, 0)])  5.06 us
  transfers between devices with their start and end apart: 8, of which 5 were waited for; matrix products, arithmetic and copies ran while one was open for 8% of the time, Pallas kernels for 3%

profile of v7, /device:TPU:1, one launch (start us, length us, event | category | flops | bytes accessed | tf_op | source)
XLA Modules:
  0.0 146.6 jit_solution(5969614240432981936)
XLA Ops:
  6.6 0.8 and_select_fusion.1
  8.0 1.0 gather_fusion
  9.7 25.8 %all_to_all.10 = bf16[32,4,2048]{2,1,0:T(4,128)(2,1)S(1)} all-to-all(bf16[32,4,2048]{2,1,0:T(4,128)(2,1)S(1)} %bitcast.39), channel_id=1, replica_groups=mesh['yh1'=2,'yh0'=2,'z'=8,'x'=4,'ylo'=2,'core'=2] {'yh0','x','ylo','core'}, dimensions={0} | all-to-all | bytes 1048576 | tf_op jit(solution)/shard_map/all_to_all | solution.py:182
  35.5 0.9 reshape.157
  37.1 3.1 %collective-permute-start.1 = (s32[2049]{0:T(1024)S(1)}, s32[2049]{0:T(1024)S(1)}, u32[]{:S(2)}, u32[]{:S(2)}) collective-permute-start(s32[2049]{0:T(1024)S(1)} %pad_add_fusion), channel_id=1, source_target_pairs={{0,1},{1,0},{2,3},{3,2},{4,5},{5,4},{6,7},{7,6},{8,9},{9,8},{10,11... | collective-permute-start | bytes 24596 | tf_op jit(solution)/shard_map/ppermute | solution.py:139
  40.3 1.9 %collective-permute-start = (bf16[128,1024]{1,0:T(8,128)(2,1)S(1)}, bf16[128,1024]{1,0:T(8,128)(2,1)S(1)}, u32[]{:S(2)}, u32[]{:S(2)}) collective-permute-start(bf16[128,1024]{1,0:T(8,128)(2,1)S(1)} %dynamic-slice_bitcast_fusion), channel_id=1, source_target_pairs={{0,1},{1,0},{2,3},{3,2},{4,5},{5,4},{6,7},{7,6},{8,9},{9,8},{10,11... | collective-permute-start | bytes 786440 | tf_op jit(solution)/shard_map/ppermute | solution.py:139
  42.4 1.3 collective-permute-done
  43.9 1.2 pad_maximum_fusion
  45.0 3.5 %all-to-all-start = ((bf16[4,128,1024]{2,1,0:T(8,128)(2,1)}), bf16[4,128,1024]{2,1,0:T(8,128)(2,1)S(1)}, u32[]{:S(2)}, u32[]{:S(2)}) async-start(bf16[4,128,1024]{2,1,0:T(8,128)(2,1)} %pad_maximum_fusion), calls=%async_computation | async-start | bytes 2097152 | tf_op jit(solution)/shard_map/all_to_all | solution.py:192
  48.9 1.2 fusion.5.order_ref
  50.1 3.9 %shard_map.109.base_ref = f32[128,2048]{1,0:T(8,128)} custom-call(bf16[128,2048]{1,0:T(8,128)(2,1)} %bitcast.37, bf16[128,4096]{1,0:T(8,128)(2,1)} %bitcast.40, f32[1,16]{1,0:T(1,128)} %bitcast.47), custom_call_target="tpu_custom_call" | custom-call | tf_op jit(solution)/shard_map/pallas_call | solution.py:96
  54.5 0.7 compare_convert_fusion
  55.2 0.7 reshape.159.mask_ref
  55.9 6.1 %gather_fusion.1 = s32[1024]{0:T(1024)S(1)} fusion(s32[2049]{0:T(1024)S(1)} %broadcast_select_fusion, s32[1024]{0:T(1024)S(1)} %broadcast_clamp_fusion), kind=kCustom, calls=%fused_computation.1 | custom fusion | bytes 12288 | tf_op jit(solution)/shard_map/gather | solution.py:208
  63.2 10.5 %all-to-all-done.q_ref = bf16[4,128,1024]{2,1,0:T(8,128)(2,1)S(1)} async-done(((bf16[4,128,1024]{2,1,0:T(8,128)(2,1)}), bf16[4,128,1024]{2,1,0:T(8,128)(2,1)S(1)}, u32[]{:S(2)}, u32[]{:S(2)}) %all-to-all-start) | async-done | bytes 1048608 | tf_op jit(solution)/shard_map/all_to_all | solution.py:192
  73.7 20.7 %all-gather.2.cloned.1.call-done.k_ref.v_ref = bf16[1024,2048]{1,0:T(8,128)(2,1)} async-done(((bf16[128,2048]{1,0:T(8,128)(2,1)}), bf16[1024,2048]{1,0:T(8,128)(2,1)}) %all-gather.2.cloned.1.call-update) | async-done | bytes 4194320 | tf_op jit(solution)/shard_map/all_gather | solution.py:184
  94.4 7.7 %shard_map.110 = (bf16[128,1024]{1,0:T(8,128)(2,1)}, bf16[128,1024]{1,0:T(8,128)(2,1)}, bf16[128,1024]{1,0:T(8,128)(2,1)}, bf16[128,1024]{1,0:T(8,128)(2,1)}) custom-call(s32[4]{0:T(128)} %fusion.5.order_ref, bf16[4,128,1024]{2,1,0:T(8,128)(2,1)} %copy-done.1, bf16[1024,2048]{1,0:T(8,128)(2,1)} %all-gather.2.cloned.1.call-done.k_ref.v_ref, ...), custom_call_target="tpu_custom_call" | custom-call | flops 2147483648 | bytes 6291456 | tf_op jit(solution)/shard_map/pallas_call | solution.py:59
  102.2 2.6 %collective-permute-start.2 = (bf16[128,1024]{1,0:T(8,128)(2,1)}, bf16[128,1024]{1,0:T(8,128)(2,1)S(1)}, u32[]{:S(2)}, u32[]{:S(2)}) collective-permute-start(bf16[128,1024]{1,0:T(8,128)(2,1)} %get-tuple-element.14), channel_id=1, source_target_pairs={{0,128},{257,385},{1,0},{256,257},{384,256},{129,1},{385,384},{128... | collective-permute-start | bytes 786440 | tf_op jit(solution)/shard_map/ppermute | solution.py:219
  104.7 3.9 %collective-permute-start.3 = (bf16[128,1024]{1,0:T(8,128)(2,1)}, bf16[128,1024]{1,0:T(8,128)(2,1)S(1)}, u32[]{:S(2)}, u32[]{:S(2)}) collective-permute-start(bf16[128,1024]{1,0:T(8,128)(2,1)} %get-tuple-element.15), channel_id=1, source_target_pairs={{0,384},{257,129},{1,128},{256,385},{384,0},{129,257},{385,256},{1... | collective-permute-start | bytes 786440 | tf_op jit(solution)/shard_map/ppermute | solution.py:219
  108.7 6.0 %collective-permute-start.4 = (bf16[128,1024]{1,0:T(8,128)(2,1)}, bf16[128,1024]{1,0:T(8,128)(2,1)S(1)}, u32[]{:S(2)}, u32[]{:S(2)}) collective-permute-start(bf16[128,1024]{1,0:T(8,128)(2,1)} %get-tuple-element.16), channel_id=1, source_target_pairs={{0,256},{257,1},{1,384},{256,129},{384,128},{129,385},{385,0},{128... | collective-permute-start | bytes 786440 | tf_op jit(solution)/shard_map/ppermute | solution.py:219
  114.7 4.5 %collective-permute-start.5 = (bf16[128,1024]{1,0:T(8,128)(2,1)}, bf16[128,1024]{1,0:T(8,128)(2,1)S(1)}, u32[]{:S(2)}, u32[]{:S(2)}) collective-permute-start(bf16[128,1024]{1,0:T(8,128)(2,1)} %get-tuple-element.17), channel_id=1, source_target_pairs={{0,0},{257,257},{1,256},{256,1},{384,384},{129,129},{385,128},{128... | collective-permute-start | bytes 786440 | tf_op jit(solution)/shard_map/ppermute | solution.py:219
  119.2 2.5 %collective-permute-done.3.b_ref = bf16[128,1024]{1,0:T(8,128)(2,1)S(1)} collective-permute-done((bf16[128,1024]{1,0:T(8,128)(2,1)}, bf16[128,1024]{1,0:T(8,128)(2,1)S(1)}, u32[]{:S(2)}, u32[]{:S(2)}) %collective-permute-start.3) | collective-permute-done | bytes 262176 | tf_op jit(solution)/shard_map/ppermute | solution.py:219
  121.7 14.4 %collective-permute-done.4.c_ref = bf16[128,1024]{1,0:T(8,128)(2,1)S(1)} collective-permute-done((bf16[128,1024]{1,0:T(8,128)(2,1)}, bf16[128,1024]{1,0:T(8,128)(2,1)S(1)}, u32[]{:S(2)}, u32[]{:S(2)}) %collective-permute-start.4) | collective-permute-done | bytes 262176 | tf_op jit(solution)/shard_map/ppermute | solution.py:219
  136.9 2.8 %shard_map.111 = bf16[128,2048]{1,0:T(8,128)(2,1)} custom-call(s32[1]{0:T(128)} %bitcast.flag_ref, bf16[128,1024]{1,0:T(8,128)(2,1)} %copy-done.3, bf16[128,1024]{1,0:T(8,128)(2,1)} %copy-done.4, bf16[128,1024]{1,0:T(8,128)(2,1)} %copy-done.5, bf16[128,1024]{1,0:T(8,128)(2,1)} %copy-done.6, f32[128,2048]{1,0:T(8,128)} %shard_map.109.base_ref, ...), custom_call_target="tpu_custom_call" | custom-call | tf_op jit(solution)/shard_map/pallas_call | solution.py:127
  (51 shorter events, 4.5 us)
Async XLA Ops:
  6.5 1.4 copy-start
  6.5 30.5 %copy-start.7 = (s32[1,2048]{1,0:T(1,128)S(1)}, s32[1,2048]{1,0:T(1,128)}, u32[]{:S(2)}) copy-start(s32[1,2048]{1,0:T(1,128)} %param.17) | copy-start | bytes 24580
  6.5 33.7 %copy-start.2 = (bf16[1,128,2048]{2,1,0:T(8,128)(2,1)S(1)}, bf16[1,128,2048]{2,1,0:T(8,128)(2,1)}, u32[]{:S(2)}) copy-start(bf16[1,128,2048]{2,1,0:T(8,128)(2,1)} %param.11) | copy-start | bytes 1572868
  6.5 87.9 %all-gather.2.cloned.1.call-start = ((), (), s32[]{:S(2)}) async-start(), calls=%async_computation.2 | async-start | bytes 4718592 | tf_op jit(solution)/shard_map/all_gather | solution.py:184
  37.1 16.8 %collective-permute-start.1 = (s32[2049]{0:T(1024)S(1)}, s32[2049]{0:T(1024)S(1)}, u32[]{:S(2)}, u32[]{:S(2)}) collective-permute-start(s32[2049]{0:T(1024)S(1)} %pad_add_fusion), channel_id=1, source_target_pairs={{0,1},{1,0},{2,3},{3,2},{4,5},{5,4},{6,7},{7,6},{8,9},{9,8},{10,11... | collective-permute-start | bytes 24596 | tf_op jit(solution)/shard_map/ppermute | solution.py:139
  40.3 3.4 %collective-permute-start = (bf16[128,1024]{1,0:T(8,128)(2,1)S(1)}, bf16[128,1024]{1,0:T(8,128)(2,1)S(1)}, u32[]{:S(2)}, u32[]{:S(2)}) collective-permute-start(bf16[128,1024]{1,0:T(8,128)(2,1)S(1)} %dynamic-slice_bitcast_fusion), channel_id=1, source_target_pairs={{0,1},{1,0},{2,3},{3,2},{4,5},{5,4},{6,7},{7,6},{8,9},{9,8},{10,11... | collective-permute-start | bytes 786440 | tf_op jit(solution)/shard_map/ppermute | solution.py:139
  45.0 28.7 %all-to-all-start = ((bf16[4,128,1024]{2,1,0:T(8,128)(2,1)}), bf16[4,128,1024]{2,1,0:T(8,128)(2,1)S(1)}, u32[]{:S(2)}, u32[]{:S(2)}) async-start(bf16[4,128,1024]{2,1,0:T(8,128)(2,1)} %pad_maximum_fusion), calls=%async_computation | async-start | bytes 2097152 | tf_op jit(solution)/shard_map/all_to_all | solution.py:192
  48.5 13.6 %copy-start.8 = (f32[128,16]{0,1:T(8,128)S(1)}, f32[128,16]{0,1:T(8,128)}, u32[]{:S(2)}) copy-start(f32[128,16]{0,1:T(8,128)} %param.18) | copy-start | bytes 24580
  73.7 20.7 %copy-start.1 = (bf16[4,128,1024]{2,1,0:T(8,128)(2,1)}, bf16[4,128,1024]{2,1,0:T(8,128)(2,1)S(1)}, u32[]{:S(2)}) copy-start(bf16[4,128,1024]{2,1,0:T(8,128)(2,1)S(1)} %all-to-all-done.q_ref) | copy-start | bytes 3145732
  102.2 17.0 %collective-permute-start.2 = (bf16[128,1024]{1,0:T(8,128)(2,1)}, bf16[128,1024]{1,0:T(8,128)(2,1)S(1)}, u32[]{:S(2)}, u32[]{:S(2)}) collective-permute-start(bf16[128,1024]{1,0:T(8,128)(2,1)} %get-tuple-element.14), channel_id=1, source_target_pairs={{0,128},{257,385},{1,0},{256,257},{384,256},{129,1},{385,384},{128... | collective-permute-start | bytes 786440 | tf_op jit(solution)/shard_map/ppermute | solution.py:219
  104.7 17.0 %collective-permute-start.3 = (bf16[128,1024]{1,0:T(8,128)(2,1)}, bf16[128,1024]{1,0:T(8,128)(2,1)S(1)}, u32[]{:S(2)}, u32[]{:S(2)}) collective-permute-start(bf16[128,1024]{1,0:T(8,128)(2,1)} %get-tuple-element.15), channel_id=1, source_target_pairs={{0,384},{257,129},{1,128},{256,385},{384,0},{129,257},{385,256},{1... | collective-permute-start | bytes 786440 | tf_op jit(solution)/shard_map/ppermute | solution.py:219
  108.7 27.5 %collective-permute-start.4 = (bf16[128,1024]{1,0:T(8,128)(2,1)}, bf16[128,1024]{1,0:T(8,128)(2,1)S(1)}, u32[]{:S(2)}, u32[]{:S(2)}) collective-permute-start(bf16[128,1024]{1,0:T(8,128)(2,1)} %get-tuple-element.16), channel_id=1, source_target_pairs={{0,256},{257,1},{1,384},{256,129},{384,128},{129,385},{385,0},{128... | collective-permute-start | bytes 786440 | tf_op jit(solution)/shard_map/ppermute | solution.py:219
  114.7 21.4 %collective-permute-start.5 = (bf16[128,1024]{1,0:T(8,128)(2,1)}, bf16[128,1024]{1,0:T(8,128)(2,1)S(1)}, u32[]{:S(2)}, u32[]{:S(2)}) collective-permute-start(bf16[128,1024]{1,0:T(8,128)(2,1)} %get-tuple-element.17), channel_id=1, source_target_pairs={{0,0},{257,257},{1,256},{256,1},{384,384},{129,129},{385,128},{128... | collective-permute-start | bytes 786440 | tf_op jit(solution)/shard_map/ppermute | solution.py:219
  119.2 16.9 %copy-start.3 = (bf16[128,1024]{1,0:T(8,128)(2,1)}, bf16[128,1024]{1,0:T(8,128)(2,1)S(1)}, u32[]{:S(2)}) copy-start(bf16[128,1024]{1,0:T(8,128)(2,1)S(1)} %collective-permute-done.2.a_ref) | copy-start | bytes 786436
  121.7 14.5 %copy-start.4 = (bf16[128,1024]{1,0:T(8,128)(2,1)}, bf16[128,1024]{1,0:T(8,128)(2,1)S(1)}, u32[]{:S(2)}) copy-start(bf16[128,1024]{1,0:T(8,128)(2,1)S(1)} %collective-permute-done.3.b_ref) | copy-start | bytes 786436
  136.1 0.7 copy-start.5
  136.1 0.8 copy-start.6
Sparse Core Ops, SparseCore 0:
  36.6 57.8 all-gather.1

commit v8 on v7

--- a/solution.py
+++ b/solution.py
@@ -26,56 +26,68 @@
     return pairs
 
 
-def send_order():
-    order = [None] * 8
-    for (yhi, core), homes in HOMES.items():
-        order[yhi * 2 + core] = list(homes)
-        order[(yhi + 2) % 4 * 2 + 1 - core] = [(home + 2) % 4 for home in homes]
-    return jnp.array(order, jnp.int32)
-
-
-def attend_kernel(order_ref, q_ref, k_ref, v_ref, bias_ref, mask_ref, *out_refs):
-    blocks, rows, width = q_ref.shape
-    scale = 0.5 / math.sqrt(HEAD_DIM)
-    inside = mask_ref[...] > 0.0
-    for head in range(width // HEAD_DIM):
-        cols = slice(head * HEAD_DIM, (head + 1) * HEAD_DIM)
-        queries = jnp.concatenate([q_ref[order_ref[i], :, cols] for i in range(blocks)], axis=0)
-        scores = lax.dot_general(
-            queries, k_ref[:, cols], (((1,), (1,)), ((), ())), preferred_element_type=jnp.float32
-        )
-        half = scores * scale + bias_ref[head]
-        weights = jnp.where(inside, half + half * jnp.tanh(half), 0.0).astype(jnp.bfloat16)
-        sums = jnp.dot(weights, v_ref[:, cols], preferred_element_type=jnp.float32)
-        for i, out_ref in enumerate(out_refs):
-            out_ref[:, cols] = sums[i * rows : (i + 1) * rows].astype(out_ref.dtype)
-
-
-def attend(order, queries, history, bias, mask, per_step):
-    blocks, rows, full = queries.shape
-    positions = history.shape[0]
+def make_attend_kernel(pieces, blocks, with_base):
+    def kernel(*refs):
+        q_refs, refs = refs[:blocks], refs[blocks:]
+        k_refs, v_refs = refs[:pieces], refs[pieces : 2 * pieces]
+        bias_ref, mask_ref = refs[2 * pieces : 2 * pieces + 2]
+        base_refs = refs[2 * pieces + 2 : -blocks]
+        out_refs = refs[-blocks:]
+        rows = q_refs[0].shape[0]
+        scale = 0.5 / math.sqrt(HEAD_DIM)
+        inside = mask_ref[...] > 0.0
+        for head in range(bias_ref.shape[0]):
+            cols = slice(head * HEAD_DIM, (head + 1) * HEAD_DIM)
+            queries = jnp.concatenate([q_ref[:, cols] for q_ref in q_refs], axis=0)
+            keys = jnp.concatenate([k_ref[:, cols] for k_ref in k_refs], axis=0)
+            values = jnp.concatenate([v_ref[:, cols] for v_ref in v_refs], axis=0)
+            scores = lax.dot_general(
+                queries, keys, (((1,), (1,)), ((), ())), preferred_element_type=jnp.float32
+            )
+            half = scores * scale + bias_ref[head]
+            weights = jnp.where(inside, half + half * jnp.tanh(half), 0.0).astype(jnp.bfloat16)
+            sums = jnp.dot(weights, values, preferred_element_type=jnp.float32)
+            for i, out_ref in enumerate(out_refs):
+                block = sums[i * rows : (i + 1) * rows]
+                if with_base:
+                    block = block + base_refs[i][:, cols]
+                out_ref[:, cols] = block.astype(out_ref.dtype)
+
+    return kernel
+
+
+def attend(queries, history, bias, mask, per_step, out_type, base=()):
+    blocks = len(queries)
+    rows, full = queries[0].shape
+    positions = mask.shape[1]
     width = per_step * HEAD_DIM
     steps = full // width
+    spec = pl.BlockSpec((rows, width), lambda i: (0, i))
     return pl.pallas_call(
-        attend_kernel,
+        make_attend_kernel(len(history), blocks, len(base) > 0),
         grid=(steps,),
-        in_specs=[
-            pl.BlockSpec(memory_space=pltpu.SMEM),
-            pl.BlockSpec((blocks, rows, width), lambda i: (0, 0, i)),
-            pl.BlockSpec((positions, width), lambda i: (0, i)),
-            pl.BlockSpec((positions, width), lambda i: (0, i + steps)),
+        in_specs=[spec] * blocks
+        + [pl.BlockSpec((h.shape[0], width), lambda i: (0, i)) for h in history]
+        + [pl.BlockSpec((h.shape[0], width), lambda i: (0, i + steps)) for h in history]
+        + [
             pl.BlockSpec((per_step, 1, positions), lambda i: (i, 0, 0)),
             pl.BlockSpec((1, positions), lambda i: (0, 0)),
-        ],
-        out_specs=[pl.BlockSpec((rows, width), lambda i: (0, i))] * blocks,
-        out_shape=[jax.ShapeDtypeStruct((rows, full), jnp.bfloat16)] * blocks,
+        ]
+        + [spec] * len(base),
+        out_specs=[spec] * blocks,
+        out_shape=[jax.ShapeDtypeStruct((rows, full), out_type)] * blocks,
         compiler_params=pltpu.CompilerParams(vmem_limit_bytes=56 * 1024 * 1024),
         cost_estimate=pl.CostEstimate(
             flops=4 * blocks * rows * positions * full,
             bytes_accessed=4 * positions * full + 4 * blocks * rows * full,
             transcendentals=blocks * rows * positions * full // HEAD_DIM,
         ),
-    )(order, queries, history, history, bias, mask)
+    )(*queries, *history, *history, bias, mask, *base)
+
+
+def shifted(value, axis, steps):
+    count = lax.axis_size(axis)
+    return lax.ppermute(value, axis, [(i, (i + steps) % count) for i in range(count)])
 
 
 def own_kernel(q_ref, own_ref, self_bias_ref, out_ref):
@@ -181,15 +193,22 @@
     ).reshape(2 * groups, piece_len, width)
     incoming = lax.all_to_all(outgoing, ("yh0",) + GROUP, 0, 0, tiled=True)
     pieces = incoming.reshape(2 * groups * piece_len, width)
-    history = lax.all_gather(pieces, "z", tiled=True)
-
+    history = [pieces]
+    up = down = pieces
+    for _ in range(3):
+        up, down = shifted(up, "z", 1), shifted(down, "z", -1)
+        history += [up, down]
+    middle = pieces.shape[0] // 2
+    last = [shifted(up[:middle], "z", 1), shifted(down[middle:], "z", -1)]
+
+    flag = (core == 0) == (core == side)
     queries = cand_query[0]
-    own_half = lax.dynamic_slice_in_dim(queries, core * half_width, half_width, 1)
-    other_half = lax.dynamic_slice_in_dim(queries, (1 - core) * half_width, half_width, 1)
-    partner_half = swapped(other_half)
-    first = jnp.where(core == 0, own_half, partner_half)
-    second = jnp.where(core == 0, partner_half, own_half)
-    spread = lax.all_to_all(jnp.stack([first, second, second, first]), Y, 0, 0, tiled=True)
+    low, high = queries[:, :half_width], queries[:, half_width:]
+    odd, even = jnp.where(flag, high, low), jnp.where(flag, low, high)
+    spread = [
+        lax.ppermute(half, Y + ("core",), [(home, worker) for worker, home in send_pairs(step)])
+        for step, half in enumerate((odd, even, odd, even))
+    ]
 
     about = jnp.concatenate([buckets[0], lengths])
     about = jnp.where(core == side, about, swapped(about))
@@ -197,7 +216,8 @@
     own_holding = lax.dynamic_index_in_dim(holding, session, 0, keepdims=False)
     arrived = own_holding[None, :] == jnp.arange(groups, dtype=jnp.int32)[:, None]
     piece_of = jnp.sum(jnp.where(arrived, jnp.arange(slots, dtype=jnp.int32)[None, :], 0), axis=1)
-    order = jnp.arange(z_size, dtype=jnp.int32)[:, None, None, None]
+    order = (lax.axis_index("z") - jnp.array([0, 1, -1, 2, -2, 3, -3, 4], jnp.int32)) % z_size
+    order = order[:, None, None, None]
     order = order + (jnp.arange(2, dtype=jnp.int32)[None, :, None, None] + 2 * upper_y) * z_size
     place = (
         (order * slots + piece_of[None, None, :, None]) * piece_len
@@ -212,13 +232,11 @@
 
     base = own_term(queries, cand_kv[0], self_bias)
     bias, mask, base = lax.optimization_barrier((bias[:, None, :], mask, base))
-    order = send_order()[lax.axis_index(Y + ("core",))]
-    partial = attend(order, spread, history, bias, mask, 2)
-    parts = [None] * 4
-    for step in (3, 2, 1, 0):
-        parts[step] = lax.ppermute(partial[step], Y + ("core",), send_pairs(step))
-    flag = ((core == 0) == (core == side)).astype(jnp.int32)
-    return finish(flag, parts, base, cand_gate[0], norm_gain)[None]
+    cut = pieces.shape[0] * len(history)
+    sums = attend(spread, history, bias[..., :cut], mask[:, :cut], 2, jnp.float32)
+    partial = attend(spread, last, bias[..., cut:], mask[:, cut:], 4, jnp.bfloat16, sums)
+    parts = [lax.ppermute(partial[s], Y + ("core",), send_pairs(s)) for s in range(4)]
+    return finish(flag.astype(jnp.int32), parts, base, cand_gate[0], norm_gain)[None]
 
 
 def solution(mesh):

time: 147 us -> 163 us (1.11)
  starting transfers between devices: 25.6 us -> 90.6 us
  blocking collectives: 25.8 us -> 0 us
  waiting for transfers between devices: 49.5 us -> 33.5 us
  between operations: 14.3 us -> 1.25 us
  Pallas kernels: 14.4 us -> 17.5 us
  local copies, waits for them, and re-layouts: 13.1 us -> 15.9 us
    ppermute x4 -> x16, starting transfers between devices: 17 us -> 78.1 us  [the longest x8 32.3 us: shifted(): lax.ppermute(value, axis, [(i, (i + steps) % count) for i in range(count)])]
    all_to_all x1 -> x0, blocking collectives: 25.8 us -> none  [per_device(): incoming = lax.all_to_all(outgoing, ('yh0',) + GROUP, 0, 0, tiled=True)]
    all_gather x1 -> x0, waiting for transfers between devices: 20.7 us -> none  [per_device(): history = lax.all_gather(pieces, 'z', tiled=True)]
    ppermute x4 -> x16, waiting for transfers between devices: 16.9 us -> 26.7 us  [the longest x4 14.3 us: per_device(): lax.ppermute(partial[s], Y + ('core',), send_pairs(s))]
    all_to_all x1, starting transfers between devices: 3.51 us -> 10.6 us  [per_device(): incoming = lax.all_to_all(outgoing, ('yh0',) + GROUP, 0, 0, tiled=True)]
    all_to_all x1, waiting for transfers between devices: 10.5 us -> 6.78 us  [per_device(): incoming = lax.all_to_all(outgoing, ('yh0',) + GROUP, 0, 0, tiled=True)]
    pallas_call x1 -> x2, Pallas kernels: 7.74 us -> 10.9 us  [attend(): pl.pallas_call(make_attend_kernel(len(history), blocks, len(base) > 0), g...]
    ppermute x2 -> x1, starting transfers between devices: 5.06 us -> 1.92 us  [swapped(): return lax.ppermute(value, 'core', [(0, 1), (1, 0)])]
  transfers between devices with their start and end apart: 8 -> 18, of which waited for: 5 -> 4; matrix products, arithmetic and copies ran while one was open for 8% -> 7% of each run, Pallas kernels for 3% -> 7%
where the time goes in v8:
time: 163 us; the launch traced here: 162 us
  starting transfers between devices  90.6 us (56%)
  waiting for transfers between devices  33.5 us (21%)
  Pallas kernels  17.5 us (11%)
  local copies, waits for them, and re-layouts  15.9 us (10%)
  other arithmetic  2.43 us (1%)
    ppermute x8, starting transfers between devices, shifted(): lax.ppermute(value, axis, [(i, (i + steps) % count) for i in range(count)])  32.3 us
    ppermute x4, starting transfers between devices, per_device(): lax.ppermute(half, Y + ('core',), [(home, worker) for worker, home in sen...  27.4 us
    ppermute x4, starting transfers between devices, per_device(): lax.ppermute(partial[s], Y + ('core',), send_pairs(s))  18.4 us
    ppermute x4, waiting for transfers between devices, per_device(): lax.ppermute(partial[s], Y + ('core',), send_pairs(s))  14.3 us
    ppermute x8, waiting for transfers between devices, shifted(): lax.ppermute(value, axis, [(i, (i + steps) % count) for i in range(count)])  12.4 us
    pallas_call x2, Pallas kernels, attend(): pl.pallas_call(make_attend_kernel(len(history), blocks, len(base) > 0), g...  10.9 us
    all_to_all x1, starting transfers between devices, per_device(): incoming = lax.all_to_all(outgoing, ('yh0',) + GROUP, 0, 0, tiled=True)  10.6 us
    all_to_all x1, waiting for transfers between devices, per_device(): incoming = lax.all_to_all(outgoing, ('yh0',) + GROUP, 0, 0, tiled=True)  6.78 us
  transfers between devices with their start and end apart: 18, of which 4 were waited for; matrix products, arithmetic and copies ran while one was open for 7% of the time, Pallas kernels for 7%

profile of v8, /device:TPU:1, one launch (start us, length us, event | category | flops | bytes accessed | tf_op | source)
XLA Modules:
  0.0 161.7 jit_solution(11760814811156405147)
XLA Ops:
  4.0 10.6 %all-to-all-start = ((bf16[32,4,2048]{2,1,0:T(4,128)(2,1)}), bf16[32,4,2048]{2,1,0:T(4,128)(2,1)S(1)}, u32[]{:S(2)}, u32[]{:S(2)}) async-start(bf16[32,4,2048]{2,1,0:T(4,128)(2,1)} %bitcast.5), calls=%async_computation | async-start | bytes 1048576 | tf_op jit(solution)/shard_map/all_to_all | solution.py:194
  15.4 4.3 %collective-permute-start = (bf16[128,1024]{1,0:T(8,128)(2,1)}, bf16[128,1024]{1,0:T(8,128)(2,1)S(1)}, u32[]{:S(2)}, u32[]{:S(2)}) collective-permute-start(bf16[128,1024]{1,0:T(8,128)(2,1)} %get-tuple-element.32), channel_id=1, source_target_pairs={{128,0},{385,257},{0,1},{257,256},{256,384},{1,129},{384,385},{129... | collective-permute-start | bytes 786440 | tf_op jit(solution)/shard_map/ppermute | solution.py:209
  19.7 1.9 %collective-permute-start.2 = (bf16[128,1024]{1,0:T(8,128)(2,1)}, bf16[128,1024]{1,0:T(8,128)(2,1)}, u32[]{:S(2)}, u32[]{:S(2)}) collective-permute-start(bf16[128,1024]{1,0:T(8,128)(2,1)} %get-tuple-element.32), channel_id=1, source_target_pairs={{256,0},{1,257},{384,1},{129,256},{128,384},{385,129},{0,385},{257... | collective-permute-start | bytes 786440 | tf_op jit(solution)/shard_map/ppermute | solution.py:209
  24.3 6.8 %all-to-all-done = bf16[32,4,2048]{2,1,0:T(4,128)(2,1)S(1)} async-done(((bf16[32,4,2048]{2,1,0:T(4,128)(2,1)}), bf16[32,4,2048]{2,1,0:T(4,128)(2,1)S(1)}, u32[]{:S(2)}, u32[]{:S(2)}) %all-to-all-start) | async-done | bytes 524320 | tf_op jit(solution)/shard_map/all_to_all | solution.py:194
  31.2 9.3 %collective-permute-start.8 = (bf16[128,2048]{1,0:T(8,128)(2,1)S(1)}, bf16[128,2048]{1,0:T(8,128)(2,1)S(1)}, u32[]{:S(2)}, u32[]{:S(2)}) collective-permute-start(bf16[128,2048]{1,0:T(8,128)(2,1)S(1)} %reshape.165.refs_4_.refs_11_), channel_id=1, source_target_pairs={{0,112},{16,0},{32,16},{48,32},{64,48},{80,64},{96,80},{112,96},{1... | collective-permute-start | bytes 1572872 | tf_op jit(solution)/shard_map/ppermute | solution.py:90
  40.5 1.9 %collective-permute-start.4 = (bf16[128,2048]{1,0:T(8,128)(2,1)S(1)}, bf16[128,2048]{1,0:T(8,128)(2,1)S(1)}, u32[]{:S(2)}, u32[]{:S(2)}) collective-permute-start(bf16[128,2048]{1,0:T(8,128)(2,1)S(1)} %reshape.165.refs_4_.refs_11_), channel_id=1, source_target_pairs={{0,16},{16,32},{32,48},{48,64},{64,80},{80,96},{96,112},{112,0},{1... | collective-permute-start | bytes 1572872 | tf_op jit(solution)/shard_map/ppermute | solution.py:90
  42.6 6.8 %collective-permute-done.8.refs_6_.refs_13_ = bf16[128,2048]{1,0:T(8,128)(2,1)S(1)} collective-permute-done((bf16[128,2048]{1,0:T(8,128)(2,1)S(1)}, bf16[128,2048]{1,0:T(8,128)(2,1)S(1)}, u32[]{:S(2)}, u32[]{:S(2)}) %collective-permute-start.8) | collective-permute-done | bytes 524320 | tf_op jit(solution)/shard_map/ppermute | solution.py:90
  49.4 5.3 %collective-permute-start.9 = (bf16[128,2048]{1,0:T(8,128)(2,1)S(1)}, bf16[128,2048]{1,0:T(8,128)(2,1)}, u32[]{:S(2)}, u32[]{:S(2)}) collective-permute-start(bf16[128,2048]{1,0:T(8,128)(2,1)S(1)} %collective-permute-done.8.refs_6_.refs_13_), channel_id=1, source_target_pairs={{0,112},{16,0},{32,16},{48,32},{64,48},{80,64},{96,80},{112,96},{1... | collective-permute-start | bytes 1572872 | tf_op jit(solution)/shard_map/ppermute | solution.py:90
  54.9 1.9 %collective-permute-start.5 = (bf16[128,2048]{1,0:T(8,128)(2,1)S(1)}, bf16[128,2048]{1,0:T(8,128)(2,1)}, u32[]{:S(2)}, u32[]{:S(2)}) collective-permute-start(bf16[128,2048]{1,0:T(8,128)(2,1)S(1)} %collective-permute-done.4.refs_5_.refs_12_), channel_id=1, source_target_pairs={{0,16},{16,32},{32,48},{48,64},{64,80},{80,96},{96,112},{112,0},{1... | collective-permute-start | bytes 1572872 | tf_op jit(solution)/shard_map/ppermute | solution.py:90
  57.1 5.6 %collective-permute-done.9.refs_8_.refs_15_ = bf16[128,2048]{1,0:T(8,128)(2,1)} collective-permute-done((bf16[128,2048]{1,0:T(8,128)(2,1)S(1)}, bf16[128,2048]{1,0:T(8,128)(2,1)}, u32[]{:S(2)}, u32[]{:S(2)}) %collective-permute-start.9) | collective-permute-done | bytes 524320 | tf_op jit(solution)/shard_map/ppermute | solution.py:90
  62.7 5.4 %collective-permute-start.10 = (bf16[128,2048]{1,0:T(8,128)(2,1)}, bf16[128,2048]{1,0:T(8,128)(2,1)S(1)}, u32[]{:S(2)}, u32[]{:S(2)}) collective-permute-start(bf16[128,2048]{1,0:T(8,128)(2,1)} %collective-permute-done.9.refs_8_.refs_15_), channel_id=1, source_target_pairs={{0,112},{16,0},{32,16},{48,32},{64,48},{80,64},{96,80},{112,96},{1... | collective-permute-start | bytes 1572872 | tf_op jit(solution)/shard_map/ppermute | solution.py:90
  70.1 3.8 %shard_map.109.base_ref = f32[128,2048]{1,0:T(8,128)} custom-call(bf16[128,2048]{1,0:T(8,128)(2,1)} %bitcast.23, bf16[128,4096]{1,0:T(8,128)(2,1)} %bitcast.25, f32[1,16]{1,0:T(1,128)} %bitcast.32), custom_call_target="tpu_custom_call" | custom-call | tf_op jit(solution)/shard_map/pallas_call | solution.py:108
  73.9 17.6 %collective-permute-start.1 = (bf16[128,1024]{1,0:T(8,128)(2,1)}, bf16[128,1024]{1,0:T(8,128)(2,1)S(1)}, u32[]{:S(2)}, u32[]{:S(2)}) collective-permute-start(bf16[128,1024]{1,0:T(8,128)(2,1)} %get-tuple-element.31), channel_id=1, source_target_pairs={{384,0},{129,257},{128,1},{385,256},{0,384},{257,129},{256,385},{1... | collective-permute-start | bytes 786440 | tf_op jit(solution)/shard_map/ppermute | solution.py:209
  92.1 3.6 %collective-permute-start.3 = (bf16[128,1024]{1,0:T(8,128)(2,1)}, bf16[128,1024]{1,0:T(8,128)(2,1)S(1)}, u32[]{:S(2)}, u32[]{:S(2)}) collective-permute-start(bf16[128,1024]{1,0:T(8,128)(2,1)} %get-tuple-element.31), channel_id=1, source_target_pairs={{0,0},{257,257},{256,1},{1,256},{384,384},{129,129},{128,385},{385... | collective-permute-start | bytes 786440 | tf_op jit(solution)/shard_map/ppermute | solution.py:209
  96.4 6.2 %gather_fusion.1 = s32[1024]{0:T(1024)S(1)} fusion(s32[2049]{0:T(1024)S(1)} %broadcast_select_fusion.2, s32[1024]{0:T(1024)S(1)} %broadcast_clamp_fusion), kind=kCustom, calls=%fused_computation.1 | custom fusion | bytes 12288 | tf_op jit(solution)/shard_map/gather | solution.py:228
  102.7 4.6 %collective-permute-start.11 = (bf16[64,2048]{1,0:T(8,128)(2,1)S(1)}, bf16[64,2048]{1,0:T(8,128)(2,1)S(1)}, u32[]{:S(2)}, u32[]{:S(2)}) collective-permute-start(bf16[64,2048]{1,0:T(8,128)(2,1)S(1)} %slice.63), channel_id=1, source_target_pairs={{0,112},{16,0},{32,16},{48,32},{64,48},{80,64},{96,80},{112,96},{1... | collective-permute-start | bytes 786440 | tf_op jit(solution)/shard_map/ppermute | solution.py:90
  107.3 1.9 %collective-permute-start.7 = (bf16[64,2048]{1,0:T(8,128)(2,1)S(1)}, bf16[64,2048]{1,0:T(8,128)(2,1)S(1)}, u32[]{:S(2)}, u32[]{:S(2)}) collective-permute-start(bf16[64,2048]{1,0:T(8,128)(2,1)S(1)} %slice.62), channel_id=1, source_target_pairs={{0,16},{16,32},{32,48},{48,64},{64,80},{80,96},{96,112},{112,0},{1... | collective-permute-start | bytes 786440 | tf_op jit(solution)/shard_map/ppermute | solution.py:90
  113.6 7.2 %shard_map.110 = (f32[128,1024]{1,0:T(8,128)}, f32[128,1024]{1,0:T(8,128)}, f32[128,1024]{1,0:T(8,128)}, f32[128,1024]{1,0:T(8,128)}) custom-call(bf16[128,1024]{1,0:T(8,128)(2,1)} %copy-done.7, bf16[128,1024]{1,0:T(8,128)(2,1)} %copy-done.8, bf16[128,1024]{1,0:T(8,128)(2,1)} %collective-permute-done.2.refs_2_, bf16[128,1024]{1,0:T(8,128)(2,1)} %copy-done.9, ...), custom_call_target="tpu_custom_call" | custom-call | flops 1879048192 | bytes 5767168 | tf_op jit(solution)/shard_map/pallas_call | solution.py:66
  121.6 3.7 %shard_map.111 = (bf16[128,1024]{1,0:T(8,128)(2,1)}, bf16[128,1024]{1,0:T(8,128)(2,1)}, bf16[128,1024]{1,0:T(8,128)(2,1)}, bf16[128,1024]{1,0:T(8,128)(2,1)}) custom-call(bf16[128,1024]{1,0:T(8,128)(2,1)} %copy-done.7, bf16[128,1024]{1,0:T(8,128)(2,1)} %copy-done.8, bf16[128,1024]{1,0:T(8,128)(2,1)} %collective-permute-done.2.refs_2_, ...), custom_call_target="tpu_custom_call" | custom-call | flops 268435456 | bytes 2621440 | tf_op jit(solution)/shard_map/pallas_call | solution.py:66
  127.2 4.4 %collective-permute-start.14 = (bf16[128,1024]{1,0:T(8,128)(2,1)}, bf16[128,1024]{1,0:T(8,128)(2,1)S(1)}, u32[]{:S(2)}, u32[]{:S(2)}) collective-permute-start(bf16[128,1024]{1,0:T(8,128)(2,1)} %get-tuple-element.23), channel_id=1, source_target_pairs={{0,384},{257,129},{1,128},{256,385},{384,0},{129,257},{385,256},{1... | collective-permute-start | bytes 786440 | tf_op jit(solution)/shard_map/ppermute | solution.py:238
  131.6 6.0 %collective-permute-start.15 = (bf16[128,1024]{1,0:T(8,128)(2,1)}, bf16[128,1024]{1,0:T(8,128)(2,1)S(1)}, u32[]{:S(2)}, u32[]{:S(2)}) collective-permute-start(bf16[128,1024]{1,0:T(8,128)(2,1)} %get-tuple-element.24), channel_id=1, source_target_pairs={{0,256},{257,1},{1,384},{256,129},{384,128},{129,385},{385,0},{128... | collective-permute-start | bytes 786440 | tf_op jit(solution)/shard_map/ppermute | solution.py:238
  137.7 6.0 %collective-permute-start.16 = (bf16[128,1024]{1,0:T(8,128)(2,1)}, bf16[128,1024]{1,0:T(8,128)(2,1)S(1)}, u32[]{:S(2)}, u32[]{:S(2)}) collective-permute-start(bf16[128,1024]{1,0:T(8,128)(2,1)} %get-tuple-element.25), channel_id=1, source_target_pairs={{0,0},{257,257},{1,256},{256,1},{384,384},{129,129},{385,128},{128... | collective-permute-start | bytes 786440 | tf_op jit(solution)/shard_map/ppermute | solution.py:238
  143.8 14.3 %collective-permute-done.15.c_ref = bf16[128,1024]{1,0:T(8,128)(2,1)S(1)} collective-permute-done((bf16[128,1024]{1,0:T(8,128)(2,1)}, bf16[128,1024]{1,0:T(8,128)(2,1)S(1)}, u32[]{:S(2)}, u32[]{:S(2)}) %collective-permute-start.15) | collective-permute-done | bytes 262176 | tf_op jit(solution)/shard_map/ppermute | solution.py:238
  158.9 2.8 %shard_map.112 = bf16[128,2048]{1,0:T(8,128)(2,1)} custom-call(s32[1]{0:T(128)} %bitcast.flag_ref, bf16[128,1024]{1,0:T(8,128)(2,1)} %copy-done.12, bf16[128,1024]{1,0:T(8,128)(2,1)} %copy-done.13, bf16[128,1024]{1,0:T(8,128)(2,1)} %copy-done.14, bf16[128,1024]{1,0:T(8,128)(2,1)} %copy-done.15, f32[128,2048]{1,0:T(8,128)} %shard_map.109.base_ref, ...), custom_call_target="tpu_custom_call" | custom-call | tf_op jit(solution)/shard_map/pallas_call | solution.py:139
  (96 shorter events, 18.5 us)
Async XLA Ops:
  4.0 27.1 %all-to-all-start = ((bf16[32,4,2048]{2,1,0:T(4,128)(2,1)}), bf16[32,4,2048]{2,1,0:T(4,128)(2,1)S(1)}, u32[]{:S(2)}, u32[]{:S(2)}) async-start(bf16[32,4,2048]{2,1,0:T(4,128)(2,1)} %bitcast.5), calls=%async_computation | async-start | bytes 1048576 | tf_op jit(solution)/shard_map/all_to_all | solution.py:194
  15.4 91.9 %collective-permute-start = (bf16[128,1024]{1,0:T(8,128)(2,1)}, bf16[128,1024]{1,0:T(8,128)(2,1)S(1)}, u32[]{:S(2)}, u32[]{:S(2)}) collective-permute-start(bf16[128,1024]{1,0:T(8,128)(2,1)} %get-tuple-element.32), channel_id=1, source_target_pairs={{128,0},{385,257},{0,1},{257,256},{256,384},{1,129},{384,385},{129... | collective-permute-start | bytes 786440 | tf_op jit(solution)/shard_map/ppermute | solution.py:209
  19.7 92.5 %collective-permute-start.2 = (bf16[128,1024]{1,0:T(8,128)(2,1)}, bf16[128,1024]{1,0:T(8,128)(2,1)}, u32[]{:S(2)}, u32[]{:S(2)}) collective-permute-start(bf16[128,1024]{1,0:T(8,128)(2,1)} %get-tuple-element.32), channel_id=1, source_target_pairs={{256,0},{1,257},{384,1},{129,256},{128,384},{385,129},{0,385},{257... | collective-permute-start | bytes 786440 | tf_op jit(solution)/shard_map/ppermute | solution.py:209
  22.3 51.6 %collective-permute-start.12 = (s32[2049]{0:T(1024)S(1)}, s32[2049]{0:T(1024)S(1)}, u32[]{:S(2)}, u32[]{:S(2)}) collective-permute-start(s32[2049]{0:T(1024)S(1)} %pad_add_fusion), channel_id=1, source_target_pairs={{0,1},{1,0},{2,3},{3,2},{4,5},{5,4},{6,7},{7,6},{8,9},{9,8},{10,11... | collective-permute-start | bytes 24596 | tf_op jit(solution)/shard_map/ppermute | solution.py:151
  31.2 42.7 %copy-start.1 = (bf16[128,2048]{1,0:T(8,128)(2,1)}, bf16[128,2048]{1,0:T(8,128)(2,1)S(1)}, u32[]{:S(2)}) copy-start(bf16[128,2048]{1,0:T(8,128)(2,1)S(1)} %reshape.165.refs_4_.refs_11_) | copy-start | bytes 1572868
  31.2 11.3 %copy-start.19 = (s32[8]{0:T(128)S(1)}, s32[8]{0:T(128)}, u32[]{:S(2)}) copy-start(s32[8]{0:T(128)} %constant.106) | copy-start | bytes 100
  31.2 18.2 %collective-permute-start.8 = (bf16[128,2048]{1,0:T(8,128)(2,1)S(1)}, bf16[128,2048]{1,0:T(8,128)(2,1)S(1)}, u32[]{:S(2)}, u32[]{:S(2)}) collective-permute-start(bf16[128,2048]{1,0:T(8,128)(2,1)S(1)} %reshape.165.refs_4_.refs_11_), channel_id=1, source_target_pairs={{0,112},{16,0},{32,16},{48,32},{64,48},{80,64},{96,80},{112,96},{1... | collective-permute-start | bytes 1572872 | tf_op jit(solution)/shard_map/ppermute | solution.py:90
  40.5 14.3 %collective-permute-start.4 = (bf16[128,2048]{1,0:T(8,128)(2,1)S(1)}, bf16[128,2048]{1,0:T(8,128)(2,1)S(1)}, u32[]{:S(2)}, u32[]{:S(2)}) collective-permute-start(bf16[128,2048]{1,0:T(8,128)(2,1)S(1)} %reshape.165.refs_4_.refs_11_), channel_id=1, source_target_pairs={{0,16},{16,32},{32,48},{48,64},{64,80},{80,96},{96,112},{112,0},{1... | collective-permute-start | bytes 1572872 | tf_op jit(solution)/shard_map/ppermute | solution.py:90
  49.4 24.5 %copy-start.4 = (bf16[128,2048]{1,0:T(8,128)(2,1)}, bf16[128,2048]{1,0:T(8,128)(2,1)S(1)}, u32[]{:S(2)}) copy-start(bf16[128,2048]{1,0:T(8,128)(2,1)S(1)} %collective-permute-done.8.refs_6_.refs_13_) | copy-start | bytes 1572868
  49.4 13.3 %collective-permute-start.9 = (bf16[128,2048]{1,0:T(8,128)(2,1)S(1)}, bf16[128,2048]{1,0:T(8,128)(2,1)}, u32[]{:S(2)}, u32[]{:S(2)}) collective-permute-start(bf16[128,2048]{1,0:T(8,128)(2,1)S(1)} %collective-permute-done.8.refs_6_.refs_13_), channel_id=1, source_target_pairs={{0,112},{16,0},{32,16},{48,32},{64,48},{80,64},{96,80},{112,96},{1... | collective-permute-start | bytes 1572872 | tf_op jit(solution)/shard_map/ppermute | solution.py:90
  54.8 19.0 %copy-start.5 = (bf16[128,2048]{1,0:T(8,128)(2,1)}, bf16[128,2048]{1,0:T(8,128)(2,1)S(1)}, u32[]{:S(2)}) copy-start(bf16[128,2048]{1,0:T(8,128)(2,1)S(1)} %collective-permute-done.4.refs_5_.refs_12_) | copy-start | bytes 1572868
  54.9 13.3 %collective-permute-start.5 = (bf16[128,2048]{1,0:T(8,128)(2,1)S(1)}, bf16[128,2048]{1,0:T(8,128)(2,1)}, u32[]{:S(2)}, u32[]{:S(2)}) collective-permute-start(bf16[128,2048]{1,0:T(8,128)(2,1)S(1)} %collective-permute-done.4.refs_5_.refs_12_), channel_id=1, source_target_pairs={{0,16},{16,32},{32,48},{48,64},{64,80},{80,96},{96,112},{112,0},{1... | collective-permute-start | bytes 1572872 | tf_op jit(solution)/shard_map/ppermute | solution.py:90
  62.7 29.4 %collective-permute-start.10 = (bf16[128,2048]{1,0:T(8,128)(2,1)}, bf16[128,2048]{1,0:T(8,128)(2,1)S(1)}, u32[]{:S(2)}, u32[]{:S(2)}) collective-permute-start(bf16[128,2048]{1,0:T(8,128)(2,1)} %collective-permute-done.9.refs_8_.refs_15_), channel_id=1, source_target_pairs={{0,112},{16,0},{32,16},{48,32},{64,48},{80,64},{96,80},{112,96},{1... | collective-permute-start | bytes 1572872 | tf_op jit(solution)/shard_map/ppermute | solution.py:90
  68.1 34.5 %collective-permute-start.6 = (bf16[128,2048]{1,0:T(8,128)(2,1)}, bf16[128,2048]{1,0:T(8,128)(2,1)S(1)}, u32[]{:S(2)}, u32[]{:S(2)}) collective-permute-start(bf16[128,2048]{1,0:T(8,128)(2,1)} %collective-permute-done.5.refs_7_.refs_14_), channel_id=1, source_target_pairs={{0,16},{16,32},{32,48},{48,64},{64,80},{80,96},{96,112},{112,0},{1... | collective-permute-start | bytes 1572872 | tf_op jit(solution)/shard_map/ppermute | solution.py:90
  73.9 38.3 %collective-permute-start.1 = (bf16[128,1024]{1,0:T(8,128)(2,1)}, bf16[128,1024]{1,0:T(8,128)(2,1)S(1)}, u32[]{:S(2)}, u32[]{:S(2)}) collective-permute-start(bf16[128,1024]{1,0:T(8,128)(2,1)} %get-tuple-element.31), channel_id=1, source_target_pairs={{384,0},{129,257},{128,1},{385,256},{0,384},{257,129},{256,385},{1... | collective-permute-start | bytes 786440 | tf_op jit(solution)/shard_map/ppermute | solution.py:209
  92.1 20.2 %collective-permute-start.3 = (bf16[128,1024]{1,0:T(8,128)(2,1)}, bf16[128,1024]{1,0:T(8,128)(2,1)S(1)}, u32[]{:S(2)}, u32[]{:S(2)}) collective-permute-start(bf16[128,1024]{1,0:T(8,128)(2,1)} %get-tuple-element.31), channel_id=1, source_target_pairs={{0,0},{257,257},{256,1},{1,256},{384,384},{129,129},{128,385},{385... | collective-permute-start | bytes 786440 | tf_op jit(solution)/shard_map/ppermute | solution.py:209
  102.7 18.1 %collective-permute-start.11 = (bf16[64,2048]{1,0:T(8,128)(2,1)S(1)}, bf16[64,2048]{1,0:T(8,128)(2,1)S(1)}, u32[]{:S(2)}, u32[]{:S(2)}) collective-permute-start(bf16[64,2048]{1,0:T(8,128)(2,1)S(1)} %slice.63), channel_id=1, source_target_pairs={{0,112},{16,0},{32,16},{48,32},{64,48},{80,64},{96,80},{112,96},{1... | collective-permute-start | bytes 786440 | tf_op jit(solution)/shard_map/ppermute | solution.py:90
  107.3 13.5 %collective-permute-start.7 = (bf16[64,2048]{1,0:T(8,128)(2,1)S(1)}, bf16[64,2048]{1,0:T(8,128)(2,1)S(1)}, u32[]{:S(2)}, u32[]{:S(2)}) collective-permute-start(bf16[64,2048]{1,0:T(8,128)(2,1)S(1)} %slice.62), channel_id=1, source_target_pairs={{0,16},{16,32},{32,48},{48,64},{64,80},{80,96},{96,112},{112,0},{1... | collective-permute-start | bytes 786440 | tf_op jit(solution)/shard_map/ppermute | solution.py:90
  125.3 18.4 %collective-permute-start.13 = (bf16[128,1024]{1,0:T(8,128)(2,1)}, bf16[128,1024]{1,0:T(8,128)(2,1)S(1)}, u32[]{:S(2)}, u32[]{:S(2)}) collective-permute-start(bf16[128,1024]{1,0:T(8,128)(2,1)} %get-tuple-element.22), channel_id=1, source_target_pairs={{0,128},{257,385},{1,0},{256,257},{384,256},{129,1},{385,384},{128... | collective-permute-start | bytes 786440 | tf_op jit(solution)/shard_map/ppermute | solution.py:238
  127.2 16.5 %collective-permute-start.14 = (bf16[128,1024]{1,0:T(8,128)(2,1)}, bf16[128,1024]{1,0:T(8,128)(2,1)S(1)}, u32[]{:S(2)}, u32[]{:S(2)}) collective-permute-start(bf16[128,1024]{1,0:T(8,128)(2,1)} %get-tuple-element.23), channel_id=1, source_target_pairs={{0,384},{257,129},{1,128},{256,385},{384,0},{129,257},{385,256},{1... | collective-permute-start | bytes 786440 | tf_op jit(solution)/shard_map/ppermute | solution.py:238
  131.6 26.4 %collective-permute-start.15 = (bf16[128,1024]{1,0:T(8,128)(2,1)}, bf16[128,1024]{1,0:T(8,128)(2,1)S(1)}, u32[]{:S(2)}, u32[]{:S(2)}) collective-permute-start(bf16[128,1024]{1,0:T(8,128)(2,1)} %get-tuple-element.24), channel_id=1, source_target_pairs={{0,256},{257,1},{1,384},{256,129},{384,128},{129,385},{385,0},{128... | collective-permute-start | bytes 786440 | tf_op jit(solution)/shard_map/ppermute | solution.py:238
  137.7 20.4 %collective-permute-start.16 = (bf16[128,1024]{1,0:T(8,128)(2,1)}, bf16[128,1024]{1,0:T(8,128)(2,1)S(1)}, u32[]{:S(2)}, u32[]{:S(2)}) collective-permute-start(bf16[128,1024]{1,0:T(8,128)(2,1)} %get-tuple-element.25), channel_id=1, source_target_pairs={{0,0},{257,257},{1,256},{256,1},{384,384},{129,129},{385,128},{128... | collective-permute-start | bytes 786440 | tf_op jit(solution)/shard_map/ppermute | solution.py:238
  143.8 14.3 %copy-start.12 = (bf16[128,1024]{1,0:T(8,128)(2,1)}, bf16[128,1024]{1,0:T(8,128)(2,1)S(1)}, u32[]{:S(2)}) copy-start(bf16[128,1024]{1,0:T(8,128)(2,1)S(1)} %collective-permute-done.13.a_ref) | copy-start | bytes 786436
  143.8 14.3 %copy-start.13 = (bf16[128,1024]{1,0:T(8,128)(2,1)}, bf16[128,1024]{1,0:T(8,128)(2,1)S(1)}, u32[]{:S(2)}) copy-start(bf16[128,1024]{1,0:T(8,128)(2,1)S(1)} %collective-permute-done.14.b_ref) | copy-start | bytes 786436
  (14 other events, 56.5 us)

commit v9 on v8

--- a/solution.py
+++ b/solution.py
@@ -10,6 +10,7 @@
 
 HEADS = 16
 HEAD_DIM = 128
+VMEM = 62 * 1024 * 1024
 GROUP = ("x", "ylo", "core")
 LOOP = ("yh1", "yh0", "z")
 Y = ("yh1", "yh0")
@@ -76,7 +77,7 @@
         + [spec] * len(base),
         out_specs=[spec] * blocks,
         out_shape=[jax.ShapeDtypeStruct((rows, full), out_type)] * blocks,
-        compiler_params=pltpu.CompilerParams(vmem_limit_bytes=56 * 1024 * 1024),
+        compiler_params=pltpu.CompilerParams(vmem_limit_bytes=VMEM),
         cost_estimate=pl.CostEstimate(
             flops=4 * blocks * rows * positions * full,
             bytes_accessed=4 * positions * full + 4 * blocks * rows * full,
@@ -115,10 +116,11 @@
         ],
         out_specs=pl.BlockSpec((block, width), lambda i: (i, 0)),
         out_shape=jax.ShapeDtypeStruct((rows, width), jnp.float32),
+        compiler_params=pltpu.CompilerParams(vmem_limit_bytes=VMEM),
     )(queries, own, self_bias[None])
 
 
-def finish_kernel(flag_ref, a_ref, b_ref, c_ref, d_ref, base_ref, gate_ref, gain_ref, out_ref):
+def finish_kernel(flag_ref, d_ref, c_ref, b_ref, a_ref, base_ref, gate_ref, gain_ref, out_ref):
     a, b, c, d = (ref[...].astype(jnp.float32) for ref in (a_ref, b_ref, c_ref, d_ref))
     odd, even = a + c, b + d
     even_low = flag_ref[0] == 1
@@ -144,7 +146,8 @@
         + [row_spec(width), row_spec(width), pl.BlockSpec((1, width), lambda i: (0, 0))],
         out_specs=row_spec(width),
         out_shape=jax.ShapeDtypeStruct((rows, width), jnp.bfloat16),
-    )(flag[None], *parts, base, gate, gain[None])
+        compiler_params=pltpu.CompilerParams(vmem_limit_bytes=VMEM),
+    )(flag[None], *parts[::-1], base, gate, gain[None])
 
 
 def swapped(value):
@@ -193,14 +196,6 @@
     ).reshape(2 * groups, piece_len, width)
     incoming = lax.all_to_all(outgoing, ("yh0",) + GROUP, 0, 0, tiled=True)
     pieces = incoming.reshape(2 * groups * piece_len, width)
-    history = [pieces]
-    up = down = pieces
-    for _ in range(3):
-        up, down = shifted(up, "z", 1), shifted(down, "z", -1)
-        history += [up, down]
-    middle = pieces.shape[0] // 2
-    last = [shifted(up[:middle], "z", 1), shifted(down[middle:], "z", -1)]
-
     flag = (core == 0) == (core == side)
     queries = cand_query[0]
     low, high = queries[:, :half_width], queries[:, half_width:]
@@ -216,25 +211,46 @@
     own_holding = lax.dynamic_index_in_dim(holding, session, 0, keepdims=False)
     arrived = own_holding[None, :] == jnp.arange(groups, dtype=jnp.int32)[:, None]
     piece_of = jnp.sum(jnp.where(arrived, jnp.arange(slots, dtype=jnp.int32)[None, :], 0), axis=1)
-    order = (lax.axis_index("z") - jnp.array([0, 1, -1, 2, -2, 3, -3, 4], jnp.int32)) % z_size
-    order = order[:, None, None, None]
-    order = order + (jnp.arange(2, dtype=jnp.int32)[None, :, None, None] + 2 * upper_y) * z_size
-    place = (
-        (order * slots + piece_of[None, None, :, None]) * piece_len
-        + jnp.arange(piece_len, dtype=jnp.int32)[None, None, None, :]
-    ).reshape(-1)
-    mask = (place < about[-1]).astype(jnp.float32)[None, :]
-    one_hot = (
-        about[place][:, None] == jnp.arange(time_bias.shape[0], dtype=jnp.int32)[None, :]
-    ).astype(jnp.float32)
-    own_bias = lax.dynamic_slice_in_dim(time_bias, core * (HEADS // 2), HEADS // 2, 1)
-    bias = 0.5 * jnp.einsum("kn,nh->hk", one_hot, own_bias, precision=lax.Precision.HIGHEST)
-
+    near = (lax.axis_index("z") - jnp.array([0, 1, -1, 2, -2, 3, -3, 4], jnp.int32)) % z_size
+    near_hot = (near[:, None] == jnp.arange(z_size, dtype=jnp.int32)[None, :]).astype(jnp.float32)
+    half_rows = about.shape[0] // 2
+    rows = lax.dynamic_slice_in_dim(about[:-1], upper_y * half_rows, half_rows).astype(jnp.float32)
+    rows = rows.reshape(2, z_size, slots, piece_len)
+    rows = jnp.einsum("sj,yzjr->yzsr", arrived.astype(jnp.float32), rows, precision=lax.Precision.HIGHEST)
+    rows = jnp.einsum("nz,yzsr->nysr", near_hot, rows, precision=lax.Precision.HIGHEST)
+    order = near[:, None, None, None] + z_size * (
+        2 * upper_y + jnp.arange(2, dtype=jnp.int32)[None, :, None, None]
+    )
+    place = (order * slots + piece_of[None, None, :, None]) * piece_len
+    place = place + jnp.arange(piece_len, dtype=jnp.int32)[None, None, None, :]
+    own_bias = 0.5 * lax.dynamic_slice_in_dim(time_bias, core * (HEADS // 2), HEADS // 2, 1)
+
+    def bias_and_mask(part):
+        numbers = rows[part].reshape(-1, 1)
+        table = jnp.arange(time_bias.shape[0], dtype=jnp.int32).astype(jnp.float32)
+        one_hot = (jnp.abs(numbers - table[None, :]) < 0.5).astype(jnp.float32)
+        bias = jnp.einsum("kn,nh->hk", one_hot, own_bias, precision=lax.Precision.HIGHEST)
+        return bias[:, None, :], (place[part].reshape(1, -1) < about[-1]).astype(jnp.float32)
+
+    first = bias_and_mask(slice(0, 7))
+    second = bias_and_mask(slice(7, 8))
     base = own_term(queries, cand_kv[0], self_bias)
-    bias, mask, base = lax.optimization_barrier((bias[:, None, :], mask, base))
-    cut = pieces.shape[0] * len(history)
-    sums = attend(spread, history, bias[..., :cut], mask[:, :cut], 2, jnp.float32)
-    partial = attend(spread, last, bias[..., cut:], mask[:, cut:], 4, jnp.bfloat16, sums)
+    pieces, base, first, second, spread[2], spread[3] = lax.optimization_barrier(
+        (pieces, base, first, second, spread[2], spread[3])
+    )
+
+    history = [pieces]
+    up = down = pieces
+    for step in range(3):
+        if step == 2:
+            up, down, spread[0], spread[1] = lax.optimization_barrier((up, down, spread[0], spread[1]))
+        up, down = shifted(up, "z", 1), shifted(down, "z", -1)
+        history += [up, down]
+    middle = pieces.shape[0] // 2
+    last = [shifted(up[:middle], "z", 1), shifted(down[middle:], "z", -1)]
+
+    sums = attend(spread, history, *first, 2, jnp.float32)
+    partial = attend(spread, last, *second, 4, jnp.bfloat16, sums)
     parts = [lax.ppermute(partial[s], Y + ("core",), send_pairs(s)) for s in range(4)]
     return finish(flag.astype(jnp.int32), parts, base, cand_gate[0], norm_gain)[None]
 

time: 163 us -> 156 us (0.957)
  starting transfers between devices: 90.6 us -> 76.2 us
  waiting for transfers between devices: 33.5 us -> 41.8 us
  local copies, waits for them, and re-layouts: 15.9 us -> 11.8 us
    ppermute x4, waiting for transfers between devices: 0.01 us -> 10.9 us  [per_device(): lax.ppermute(half, Y + ('core',), [(home, worker) for worker, home in sen...]
    ppermute x4, starting transfers between devices: 27.4 us -> 19.1 us  [per_device(): lax.ppermute(half, Y + ('core',), [(home, worker) for worker, home in sen...]
    all_to_all x1, waiting for transfers between devices: 6.78 us -> 0.01 us  [per_device(): incoming = lax.all_to_all(outgoing, ('yh0',) + GROUP, 0, 0, tiled=True)]
    gather x1 -> x0, local copies, waits for them, and re-layouts: 6.15 us -> none  [per_device(): about[place][:, None]]
    ppermute x4, starting transfers between devices: 18.4 us -> 13.7 us  [per_device(): lax.ppermute(partial[s], Y + ('core',), send_pairs(s))]
    ppermute x8, waiting for transfers between devices: 12.4 us -> 15.3 us  [shifted(): lax.ppermute(value, axis, [(i, (i + steps) % count) for i in range(count)])]
    slice x5, local copies, waits for them, and re-layouts: 2.9 us -> 0.84 us  [the longest x1 0.58 us: bias_and_mask(): about[-1]]
    ppermute x8, starting transfers between devices: 32.3 us -> 30.6 us  [shifted(): lax.ppermute(value, axis, [(i, (i + steps) % count) for i in range(count)])]
  transfers between devices with their start and end apart: 18 -> 18, of which waited for: 4 -> 6; matrix products, arithmetic and copies ran while one was open for 7% -> 6% of each run, Pallas kernels for 7% -> 7%
where the time goes in v9:
time: 156 us; the launch traced here: 153 us
  starting transfers between devices  76.2 us (49%)
  waiting for transfers between devices  41.8 us (27%)
  Pallas kernels  17.5 us (11%)
  local copies, waits for them, and re-layouts  11.8 us (8%)
  other arithmetic  3.1 us (2%)
  matrix products  1.75 us (1%)
    ppermute x8, starting transfers between devices, shifted(): lax.ppermute(value, axis, [(i, (i + steps) % count) for i in range(count)])  30.6 us
    ppermute x4, starting transfers between devices, per_device(): lax.ppermute(half, Y + ('core',), [(home, worker) for worker, home in sen...  19.1 us
    ppermute x4, waiting for transfers between devices, per_device(): lax.ppermute(partial[s], Y + ('core',), send_pairs(s))  15.6 us
    ppermute x8, waiting for transfers between devices, shifted(): lax.ppermute(value, axis, [(i, (i + steps) % count) for i in range(count)])  15.3 us
    ppermute x4, starting transfers between devices, per_device(): lax.ppermute(partial[s], Y + ('core',), send_pairs(s))  13.7 us
    pallas_call x2, Pallas kernels, attend(): pl.pallas_call(make_attend_kernel(len(history), blocks, len(base) > 0), g...  10.9 us
    ppermute x4, waiting for transfers between devices, per_device(): lax.ppermute(half, Y + ('core',), [(home, worker) for worker, home in sen...  10.9 us
    all_to_all x1, starting transfers between devices, per_device(): incoming = lax.all_to_all(outgoing, ('yh0',) + GROUP, 0, 0, tiled=True)  10.6 us
  transfers between devices with their start and end apart: 18, of which 6 were waited for; matrix products, arithmetic and copies ran while one was open for 6% of the time, Pallas kernels for 7%

profile of v9, /device:TPU:1, one launch (start us, length us, event | category | flops | bytes accessed | tf_op | source)
XLA Modules:
  0.0 153.3 jit_solution(411999957519710902)
XLA Ops:
  4.0 10.6 %all-to-all-start = ((bf16[32,4,2048]{2,1,0:T(4,128)(2,1)}), bf16[32,4,2048]{2,1,0:T(4,128)(2,1)S(1)}, u32[]{:S(2)}, u32[]{:S(2)}) async-start(bf16[32,4,2048]{2,1,0:T(4,128)(2,1)} %bitcast.4), calls=%async_computation | async-start | bytes 1048576 | tf_op jit(solution)/shard_map/all_to_all | solution.py:197
  15.2 2.3 %collective-permute-start = (s32[2049]{0:T(1024)S(1)}, s32[2049]{0:T(1024)S(1)}, u32[]{:S(2)}, u32[]{:S(2)}) collective-permute-start(s32[2049]{0:T(1024)S(1)} %pad_add_fusion), channel_id=1, source_target_pairs={{0,1},{1,0},{2,3},{3,2},{4,5},{5,4},{6,7},{7,6},{8,9},{9,8},{10,11... | collective-permute-start | bytes 24596 | tf_op jit(solution)/shard_map/ppermute | solution.py:154
  18.3 3.2 %collective-permute-start.1 = (bf16[128,1024]{1,0:T(8,128)(2,1)}, bf16[128,1024]{1,0:T(8,128)(2,1)S(1)}, u32[]{:S(2)}, u32[]{:S(2)}) collective-permute-start(bf16[128,1024]{1,0:T(8,128)(2,1)} %get-tuple-element.46), channel_id=1, source_target_pairs={{256,0},{1,257},{384,1},{129,256},{128,384},{385,129},{0,385},{257... | collective-permute-start | bytes 786440 | tf_op jit(solution)/shard_map/ppermute | solution.py:204
  21.6 6.3 %collective-permute-start.2 = (bf16[128,1024]{1,0:T(8,128)(2,1)}, bf16[128,1024]{1,0:T(8,128)(2,1)}, u32[]{:S(2)}, u32[]{:S(2)}) collective-permute-start(bf16[128,1024]{1,0:T(8,128)(2,1)} %get-tuple-element.45), channel_id=1, source_target_pairs={{0,0},{257,257},{256,1},{1,256},{384,384},{129,129},{128,385},{385... | collective-permute-start | bytes 786440 | tf_op jit(solution)/shard_map/ppermute | solution.py:204
  29.0 3.8 %shard_map.109.base_ref = f32[128,2048]{1,0:T(8,128)} custom-call(bf16[128,2048]{1,0:T(8,128)(2,1)} %bitcast.42, bf16[128,4096]{1,0:T(8,128)(2,1)} %bitcast.44, f32[1,16]{1,0:T(1,128)} %bitcast.52), custom_call_target="tpu_custom_call" | custom-call | tf_op jit(solution)/shard_map/pallas_call | solution.py:109
  39.9 2.6 %collective-permute-start.3 = (bf16[128,2048]{1,0:T(8,128)(2,1)S(1)}, bf16[128,2048]{1,0:T(8,128)(2,1)S(1)}, u32[]{:S(2)}, u32[]{:S(2)}) collective-permute-start(bf16[128,2048]{1,0:T(8,128)(2,1)S(1)} %reshape.160.refs_4_.refs_11_), channel_id=1, source_target_pairs={{0,16},{16,32},{32,48},{48,64},{64,80},{80,96},{96,112},{112,0},{1... | collective-permute-start | bytes 1572872 | tf_op jit(solution)/shard_map/ppermute | solution.py:91
  42.5 8.6 %collective-permute-start.5 = (bf16[128,2048]{1,0:T(8,128)(2,1)S(1)}, bf16[128,2048]{1,0:T(8,128)(2,1)S(1)}, u32[]{:S(2)}, u32[]{:S(2)}) collective-permute-start(bf16[128,2048]{1,0:T(8,128)(2,1)S(1)} %reshape.160.refs_4_.refs_11_), channel_id=1, source_target_pairs={{0,112},{16,0},{32,16},{48,32},{64,48},{80,64},{96,80},{112,96},{1... | collective-permute-start | bytes 1572872 | tf_op jit(solution)/shard_map/ppermute | solution.py:91
  51.1 8.3 %collective-permute-done.3.refs_5_.refs_12_ = bf16[128,2048]{1,0:T(8,128)(2,1)S(1)} collective-permute-done((bf16[128,2048]{1,0:T(8,128)(2,1)S(1)}, bf16[128,2048]{1,0:T(8,128)(2,1)S(1)}, u32[]{:S(2)}, u32[]{:S(2)}) %collective-permute-start.3) | collective-permute-done | bytes 524320 | tf_op jit(solution)/shard_map/ppermute | solution.py:91
  61.3 4.6 %collective-permute-start.6 = (bf16[128,2048]{1,0:T(8,128)(2,1)S(1)}, bf16[128,2048]{1,0:T(8,128)(2,1)S(1)}, u32[]{:S(2)}, u32[]{:S(2)}) collective-permute-start(bf16[128,2048]{1,0:T(8,128)(2,1)S(1)} %collective-permute-done.5.refs_6_.refs_13_), channel_id=1, source_target_pairs={{0,112},{16,0},{32,16},{48,32},{64,48},{80,64},{96,80},{112,96},{1... | collective-permute-start | bytes 1572872 | tf_op jit(solution)/shard_map/ppermute | solution.py:91
  65.9 1.9 %collective-permute-start.7 = (bf16[128,1024]{1,0:T(8,128)(2,1)}, bf16[128,1024]{1,0:T(8,128)(2,1)S(1)}, u32[]{:S(2)}, u32[]{:S(2)}) collective-permute-start(bf16[128,1024]{1,0:T(8,128)(2,1)} %get-tuple-element.46), channel_id=1, source_target_pairs={{128,0},{385,257},{0,1},{257,256},{256,384},{1,129},{384,385},{129... | collective-permute-start | bytes 786440 | tf_op jit(solution)/shard_map/ppermute | solution.py:204
  67.9 7.6 %collective-permute-start.8 = (bf16[128,1024]{1,0:T(8,128)(2,1)}, bf16[128,1024]{1,0:T(8,128)(2,1)S(1)}, u32[]{:S(2)}, u32[]{:S(2)}) collective-permute-start(bf16[128,1024]{1,0:T(8,128)(2,1)} %get-tuple-element.45), channel_id=1, source_target_pairs={{384,0},{129,257},{128,1},{385,256},{0,384},{257,129},{256,385},{1... | collective-permute-start | bytes 786440 | tf_op jit(solution)/shard_map/ppermute | solution.py:204
  75.5 10.9 %collective-permute-done.8.refs_1_ = bf16[128,1024]{1,0:T(8,128)(2,1)S(1)} collective-permute-done((bf16[128,1024]{1,0:T(8,128)(2,1)}, bf16[128,1024]{1,0:T(8,128)(2,1)S(1)}, u32[]{:S(2)}, u32[]{:S(2)}) %collective-permute-start.8) | collective-permute-done | bytes 262176 | tf_op jit(solution)/shard_map/ppermute | solution.py:204
  89.0 4.6 %collective-permute-start.11 = (bf16[128,2048]{1,0:T(8,128)(2,1)S(1)}, bf16[128,2048]{1,0:T(8,128)(2,1)S(1)}, u32[]{:S(2)}, u32[]{:S(2)}) collective-permute-start(bf16[128,2048]{1,0:T(8,128)(2,1)S(1)} %collective-permute-done.6.refs_8_.refs_15_), channel_id=1, source_target_pairs={{0,112},{16,0},{32,16},{48,32},{64,48},{80,64},{96,80},{112,96},{1... | collective-permute-start | bytes 1572872 | tf_op jit(solution)/shard_map/ppermute | solution.py:91
  93.6 7.0 %collective-permute-done.9.refs_9_.refs_16_ = bf16[128,2048]{1,0:T(8,128)(2,1)S(1)} collective-permute-done((bf16[128,2048]{1,0:T(8,128)(2,1)S(1)}, bf16[128,2048]{1,0:T(8,128)(2,1)S(1)}, u32[]{:S(2)}, u32[]{:S(2)}) %collective-permute-start.9) | collective-permute-done | bytes 524320 | tf_op jit(solution)/shard_map/ppermute | solution.py:91
  101.4 1.9 %collective-permute-start.10 = (bf16[64,2048]{1,0:T(8,128)(2,1)}, bf16[64,2048]{1,0:T(8,128)(2,1)}, u32[]{:S(2)}, u32[]{:S(2)}) collective-permute-start(bf16[64,2048]{1,0:T(8,128)(2,1)} %slice.71), channel_id=1, source_target_pairs={{0,16},{16,32},{32,48},{48,64},{64,80},{80,96},{96,112},{112,0},{1... | collective-permute-start | bytes 786440 | tf_op jit(solution)/shard_map/ppermute | solution.py:91
  104.9 4.6 %collective-permute-start.12 = (bf16[64,2048]{1,0:T(8,128)(2,1)}, bf16[64,2048]{1,0:T(8,128)(2,1)}, u32[]{:S(2)}, u32[]{:S(2)}) collective-permute-start(bf16[64,2048]{1,0:T(8,128)(2,1)} %slice.72), channel_id=1, source_target_pairs={{0,112},{16,0},{32,16},{48,32},{64,48},{80,64},{96,80},{112,96},{1... | collective-permute-start | bytes 786440 | tf_op jit(solution)/shard_map/ppermute | solution.py:91
  109.5 7.2 %shard_map.110 = (f32[128,1024]{1,0:T(8,128)}, f32[128,1024]{1,0:T(8,128)}, f32[128,1024]{1,0:T(8,128)}, f32[128,1024]{1,0:T(8,128)}) custom-call(bf16[128,1024]{1,0:T(8,128)(2,1)} %copy-done.10, bf16[128,1024]{1,0:T(8,128)(2,1)} %copy-done.11, bf16[128,1024]{1,0:T(8,128)(2,1)} %copy-done.9, bf16[128,1024]{1,0:T(8,128)(2,1)} %collective-permute-done.2.refs_3_, ...), custom_call_target="tpu_custom_call" | custom-call | flops 1879048192 | bytes 5767168 | tf_op jit(solution)/shard_map/pallas_call | solution.py:67
  116.7 3.7 %shard_map.111 = (bf16[128,1024]{1,0:T(8,128)(2,1)}, bf16[128,1024]{1,0:T(8,128)(2,1)}, bf16[128,1024]{1,0:T(8,128)(2,1)}, bf16[128,1024]{1,0:T(8,128)(2,1)}) custom-call(bf16[128,1024]{1,0:T(8,128)(2,1)} %copy-done.10, bf16[128,1024]{1,0:T(8,128)(2,1)} %copy-done.11, bf16[128,1024]{1,0:T(8,128)(2,1)} %copy-done.9, ...), custom_call_target="tpu_custom_call" | custom-call | flops 268435456 | bytes 2621440 | tf_op jit(solution)/shard_map/pallas_call | solution.py:67
  120.4 4.0 %collective-permute-start.13 = (bf16[128,1024]{1,0:T(8,128)(2,1)}, bf16[128,1024]{1,0:T(8,128)(2,1)S(1)}, u32[]{:S(2)}, u32[]{:S(2)}) collective-permute-start(bf16[128,1024]{1,0:T(8,128)(2,1)} %get-tuple-element.40), channel_id=1, source_target_pairs={{0,0},{257,257},{1,256},{256,1},{384,384},{129,129},{385,128},{128... | collective-permute-start | bytes 786440 | tf_op jit(solution)/shard_map/ppermute | solution.py:254
  124.5 1.9 %collective-permute-start.14 = (bf16[128,1024]{1,0:T(8,128)(2,1)}, bf16[128,1024]{1,0:T(8,128)(2,1)S(1)}, u32[]{:S(2)}, u32[]{:S(2)}) collective-permute-start(bf16[128,1024]{1,0:T(8,128)(2,1)} %get-tuple-element.41), channel_id=1, source_target_pairs={{0,256},{257,1},{1,384},{256,129},{384,128},{129,385},{385,0},{128... | collective-permute-start | bytes 786440 | tf_op jit(solution)/shard_map/ppermute | solution.py:254
  126.4 1.9 %collective-permute-start.15 = (bf16[128,1024]{1,0:T(8,128)(2,1)}, bf16[128,1024]{1,0:T(8,128)(2,1)S(1)}, u32[]{:S(2)}, u32[]{:S(2)}) collective-permute-start(bf16[128,1024]{1,0:T(8,128)(2,1)} %get-tuple-element.42), channel_id=1, source_target_pairs={{0,384},{257,129},{1,128},{256,385},{384,0},{129,257},{385,256},{1... | collective-permute-start | bytes 786440 | tf_op jit(solution)/shard_map/ppermute | solution.py:254
  128.3 5.8 %collective-permute-start.16 = (bf16[128,1024]{1,0:T(8,128)(2,1)}, bf16[128,1024]{1,0:T(8,128)(2,1)S(1)}, u32[]{:S(2)}, u32[]{:S(2)}) collective-permute-start(bf16[128,1024]{1,0:T(8,128)(2,1)} %get-tuple-element.43), channel_id=1, source_target_pairs={{0,128},{257,385},{1,0},{256,257},{384,256},{129,1},{385,384},{128... | collective-permute-start | bytes 786440 | tf_op jit(solution)/shard_map/ppermute | solution.py:254
  134.2 13.5 %collective-permute-done.14.c_ref = bf16[128,1024]{1,0:T(8,128)(2,1)S(1)} collective-permute-done((bf16[128,1024]{1,0:T(8,128)(2,1)}, bf16[128,1024]{1,0:T(8,128)(2,1)S(1)}, u32[]{:S(2)}, u32[]{:S(2)}) %collective-permute-start.14) | collective-permute-done | bytes 262176 | tf_op jit(solution)/shard_map/ppermute | solution.py:254
  150.5 2.8 %shard_map.112 = bf16[128,2048]{1,0:T(8,128)(2,1)} custom-call(s32[1]{0:T(128)} %bitcast.flag_ref, bf16[128,1024]{1,0:T(8,128)(2,1)} %copy-done.12, bf16[128,1024]{1,0:T(8,128)(2,1)} %copy-done.13, bf16[128,1024]{1,0:T(8,128)(2,1)} %copy-done.14, bf16[128,1024]{1,0:T(8,128)(2,1)} %copy-done.15, f32[128,2048]{1,0:T(8,128)} %shard_map.109.base_ref, ...), custom_call_target="tpu_custom_call" | custom-call | tf_op jit(solution)/shard_map/pallas_call | solution.py:141
  (102 shorter events, 22.6 us)
Async XLA Ops:
  4.0 35.8 %all-to-all-start = ((bf16[32,4,2048]{2,1,0:T(4,128)(2,1)}), bf16[32,4,2048]{2,1,0:T(4,128)(2,1)S(1)}, u32[]{:S(2)}, u32[]{:S(2)}) async-start(bf16[32,4,2048]{2,1,0:T(4,128)(2,1)} %bitcast.4), calls=%async_computation | async-start | bytes 1048576 | tf_op jit(solution)/shard_map/all_to_all | solution.py:197
  15.2 17.6 %collective-permute-start = (s32[2049]{0:T(1024)S(1)}, s32[2049]{0:T(1024)S(1)}, u32[]{:S(2)}, u32[]{:S(2)}) collective-permute-start(s32[2049]{0:T(1024)S(1)} %pad_add_fusion), channel_id=1, source_target_pairs={{0,1},{1,0},{2,3},{3,2},{4,5},{5,4},{6,7},{7,6},{8,9},{9,8},{10,11... | collective-permute-start | bytes 24596 | tf_op jit(solution)/shard_map/ppermute | solution.py:154
  18.3 21.6 %collective-permute-start.1 = (bf16[128,1024]{1,0:T(8,128)(2,1)}, bf16[128,1024]{1,0:T(8,128)(2,1)S(1)}, u32[]{:S(2)}, u32[]{:S(2)}) collective-permute-start(bf16[128,1024]{1,0:T(8,128)(2,1)} %get-tuple-element.46), channel_id=1, source_target_pairs={{256,0},{1,257},{384,1},{129,256},{128,384},{385,129},{0,385},{257... | collective-permute-start | bytes 786440 | tf_op jit(solution)/shard_map/ppermute | solution.py:204
  21.6 18.4 %collective-permute-start.2 = (bf16[128,1024]{1,0:T(8,128)(2,1)}, bf16[128,1024]{1,0:T(8,128)(2,1)}, u32[]{:S(2)}, u32[]{:S(2)}) collective-permute-start(bf16[128,1024]{1,0:T(8,128)(2,1)} %get-tuple-element.45), channel_id=1, source_target_pairs={{0,0},{257,257},{256,1},{1,256},{384,384},{129,129},{128,385},{385... | collective-permute-start | bytes 786440 | tf_op jit(solution)/shard_map/ppermute | solution.py:204
  39.9 65.0 %copy-start.1 = (bf16[128,2048]{1,0:T(8,128)(2,1)}, bf16[128,2048]{1,0:T(8,128)(2,1)S(1)}, u32[]{:S(2)}) copy-start(bf16[128,2048]{1,0:T(8,128)(2,1)S(1)} %reshape.160.refs_4_.refs_11_) | copy-start | bytes 1572868
  39.9 69.6 %copy-start.9 = (bf16[128,1024]{1,0:T(8,128)(2,1)}, bf16[128,1024]{1,0:T(8,128)(2,1)S(1)}, u32[]{:S(2)}) copy-start(bf16[128,1024]{1,0:T(8,128)(2,1)S(1)} %collective-permute-done.1.refs_2_) | copy-start | bytes 786436
  39.9 19.5 %collective-permute-start.3 = (bf16[128,2048]{1,0:T(8,128)(2,1)S(1)}, bf16[128,2048]{1,0:T(8,128)(2,1)S(1)}, u32[]{:S(2)}, u32[]{:S(2)}) collective-permute-start(bf16[128,2048]{1,0:T(8,128)(2,1)S(1)} %reshape.160.refs_4_.refs_11_), channel_id=1, source_target_pairs={{0,16},{16,32},{32,48},{48,64},{64,80},{80,96},{96,112},{112,0},{1... | collective-permute-start | bytes 1572872 | tf_op jit(solution)/shard_map/ppermute | solution.py:91
  42.5 18.8 %collective-permute-start.5 = (bf16[128,2048]{1,0:T(8,128)(2,1)S(1)}, bf16[128,2048]{1,0:T(8,128)(2,1)S(1)}, u32[]{:S(2)}, u32[]{:S(2)}) collective-permute-start(bf16[128,2048]{1,0:T(8,128)(2,1)S(1)} %reshape.160.refs_4_.refs_11_), channel_id=1, source_target_pairs={{0,112},{16,0},{32,16},{48,32},{64,48},{80,64},{96,80},{112,96},{1... | collective-permute-start | bytes 1572872 | tf_op jit(solution)/shard_map/ppermute | solution.py:91
  59.4 29.6 %copy-start.4 = (bf16[128,2048]{1,0:T(8,128)(2,1)}, bf16[128,2048]{1,0:T(8,128)(2,1)S(1)}, u32[]{:S(2)}) copy-start(bf16[128,2048]{1,0:T(8,128)(2,1)S(1)} %collective-permute-done.3.refs_5_.refs_12_) | copy-start | bytes 1572868
  59.4 27.0 %collective-permute-start.4 = (bf16[128,2048]{1,0:T(8,128)(2,1)S(1)}, bf16[128,2048]{1,0:T(8,128)(2,1)S(1)}, u32[]{:S(2)}, u32[]{:S(2)}) collective-permute-start(bf16[128,2048]{1,0:T(8,128)(2,1)S(1)} %collective-permute-done.3.refs_5_.refs_12_), channel_id=1, source_target_pairs={{0,16},{16,32},{32,48},{48,64},{64,80},{80,96},{96,112},{112,0},{1... | collective-permute-start | bytes 1572872 | tf_op jit(solution)/shard_map/ppermute | solution.py:91
  61.3 32.3 %copy-start.5 = (bf16[128,2048]{1,0:T(8,128)(2,1)}, bf16[128,2048]{1,0:T(8,128)(2,1)S(1)}, u32[]{:S(2)}) copy-start(bf16[128,2048]{1,0:T(8,128)(2,1)S(1)} %collective-permute-done.5.refs_6_.refs_13_) | copy-start | bytes 1572868
  61.3 25.8 %collective-permute-start.6 = (bf16[128,2048]{1,0:T(8,128)(2,1)S(1)}, bf16[128,2048]{1,0:T(8,128)(2,1)S(1)}, u32[]{:S(2)}, u32[]{:S(2)}) collective-permute-start(bf16[128,2048]{1,0:T(8,128)(2,1)S(1)} %collective-permute-done.5.refs_6_.refs_13_), channel_id=1, source_target_pairs={{0,112},{16,0},{32,16},{48,32},{64,48},{80,64},{96,80},{112,96},{1... | collective-permute-start | bytes 1572872 | tf_op jit(solution)/shard_map/ppermute | solution.py:91
  65.9 9.6 %collective-permute-start.7 = (bf16[128,1024]{1,0:T(8,128)(2,1)}, bf16[128,1024]{1,0:T(8,128)(2,1)S(1)}, u32[]{:S(2)}, u32[]{:S(2)}) collective-permute-start(bf16[128,1024]{1,0:T(8,128)(2,1)} %get-tuple-element.46), channel_id=1, source_target_pairs={{128,0},{385,257},{0,1},{257,256},{256,384},{1,129},{384,385},{129... | collective-permute-start | bytes 786440 | tf_op jit(solution)/shard_map/ppermute | solution.py:204
  67.9 18.5 %collective-permute-start.8 = (bf16[128,1024]{1,0:T(8,128)(2,1)}, bf16[128,1024]{1,0:T(8,128)(2,1)S(1)}, u32[]{:S(2)}, u32[]{:S(2)}) collective-permute-start(bf16[128,1024]{1,0:T(8,128)(2,1)} %get-tuple-element.45), channel_id=1, source_target_pairs={{384,0},{129,257},{128,1},{385,256},{0,384},{257,129},{256,385},{1... | collective-permute-start | bytes 786440 | tf_op jit(solution)/shard_map/ppermute | solution.py:204
  87.1 17.8 %copy-start.7 = (bf16[128,2048]{1,0:T(8,128)(2,1)}, bf16[128,2048]{1,0:T(8,128)(2,1)S(1)}, u32[]{:S(2)}) copy-start(bf16[128,2048]{1,0:T(8,128)(2,1)S(1)} %collective-permute-done.6.refs_8_.refs_15_) | copy-start | bytes 1572868
  87.1 13.5 %collective-permute-start.9 = (bf16[128,2048]{1,0:T(8,128)(2,1)S(1)}, bf16[128,2048]{1,0:T(8,128)(2,1)S(1)}, u32[]{:S(2)}, u32[]{:S(2)}) collective-permute-start(bf16[128,2048]{1,0:T(8,128)(2,1)S(1)} %collective-permute-done.4.refs_7_.refs_14_), channel_id=1, source_target_pairs={{0,16},{16,32},{32,48},{48,64},{64,80},{80,96},{96,112},{112,0},{1... | collective-permute-start | bytes 1572872 | tf_op jit(solution)/shard_map/ppermute | solution.py:91
  89.0 14.3 %collective-permute-start.11 = (bf16[128,2048]{1,0:T(8,128)(2,1)S(1)}, bf16[128,2048]{1,0:T(8,128)(2,1)S(1)}, u32[]{:S(2)}, u32[]{:S(2)}) collective-permute-start(bf16[128,2048]{1,0:T(8,128)(2,1)S(1)} %collective-permute-done.6.refs_8_.refs_15_), channel_id=1, source_target_pairs={{0,112},{16,0},{32,16},{48,32},{64,48},{80,64},{96,80},{112,96},{1... | collective-permute-start | bytes 1572872 | tf_op jit(solution)/shard_map/ppermute | solution.py:91
  101.4 15.3 %collective-permute-start.10 = (bf16[64,2048]{1,0:T(8,128)(2,1)}, bf16[64,2048]{1,0:T(8,128)(2,1)}, u32[]{:S(2)}, u32[]{:S(2)}) collective-permute-start(bf16[64,2048]{1,0:T(8,128)(2,1)} %slice.71), channel_id=1, source_target_pairs={{0,16},{16,32},{32,48},{48,64},{64,80},{80,96},{96,112},{112,0},{1... | collective-permute-start | bytes 786440 | tf_op jit(solution)/shard_map/ppermute | solution.py:91
  104.9 11.8 %collective-permute-start.12 = (bf16[64,2048]{1,0:T(8,128)(2,1)}, bf16[64,2048]{1,0:T(8,128)(2,1)}, u32[]{:S(2)}, u32[]{:S(2)}) collective-permute-start(bf16[64,2048]{1,0:T(8,128)(2,1)} %slice.72), channel_id=1, source_target_pairs={{0,112},{16,0},{32,16},{48,32},{64,48},{80,64},{96,80},{112,96},{1... | collective-permute-start | bytes 786440 | tf_op jit(solution)/shard_map/ppermute | solution.py:91
  120.4 13.7 %collective-permute-start.13 = (bf16[128,1024]{1,0:T(8,128)(2,1)}, bf16[128,1024]{1,0:T(8,128)(2,1)S(1)}, u32[]{:S(2)}, u32[]{:S(2)}) collective-permute-start(bf16[128,1024]{1,0:T(8,128)(2,1)} %get-tuple-element.40), channel_id=1, source_target_pairs={{0,0},{257,257},{1,256},{256,1},{384,384},{129,129},{385,128},{128... | collective-permute-start | bytes 786440 | tf_op jit(solution)/shard_map/ppermute | solution.py:254
  124.5 23.2 %collective-permute-start.14 = (bf16[128,1024]{1,0:T(8,128)(2,1)}, bf16[128,1024]{1,0:T(8,128)(2,1)S(1)}, u32[]{:S(2)}, u32[]{:S(2)}) collective-permute-start(bf16[128,1024]{1,0:T(8,128)(2,1)} %get-tuple-element.41), channel_id=1, source_target_pairs={{0,256},{257,1},{1,384},{256,129},{384,128},{129,385},{385,0},{128... | collective-permute-start | bytes 786440 | tf_op jit(solution)/shard_map/ppermute | solution.py:254
  126.4 22.1 %collective-permute-start.15 = (bf16[128,1024]{1,0:T(8,128)(2,1)}, bf16[128,1024]{1,0:T(8,128)(2,1)S(1)}, u32[]{:S(2)}, u32[]{:S(2)}) collective-permute-start(bf16[128,1024]{1,0:T(8,128)(2,1)} %get-tuple-element.42), channel_id=1, source_target_pairs={{0,384},{257,129},{1,128},{256,385},{384,0},{129,257},{385,256},{1... | collective-permute-start | bytes 786440 | tf_op jit(solution)/shard_map/ppermute | solution.py:254
  128.3 21.5 %collective-permute-start.16 = (bf16[128,1024]{1,0:T(8,128)(2,1)}, bf16[128,1024]{1,0:T(8,128)(2,1)S(1)}, u32[]{:S(2)}, u32[]{:S(2)}) collective-permute-start(bf16[128,1024]{1,0:T(8,128)(2,1)} %get-tuple-element.43), channel_id=1, source_target_pairs={{0,128},{257,385},{1,0},{256,257},{384,256},{129,1},{385,384},{128... | collective-permute-start | bytes 786440 | tf_op jit(solution)/shard_map/ppermute | solution.py:254
  134.2 15.6 %copy-start.12 = (bf16[128,1024]{1,0:T(8,128)(2,1)}, bf16[128,1024]{1,0:T(8,128)(2,1)S(1)}, u32[]{:S(2)}) copy-start(bf16[128,1024]{1,0:T(8,128)(2,1)S(1)} %collective-permute-done.13.d_ref) | copy-start | bytes 786436
  (14 other events, 55.5 us)

commit v10 on v7

--- a/solution.py
+++ b/solution.py
@@ -34,30 +34,41 @@
     return jnp.array(order, jnp.int32)
 
 
-def attend_kernel(order_ref, q_ref, k_ref, v_ref, bias_ref, mask_ref, *out_refs):
-    blocks, rows, width = q_ref.shape
-    scale = 0.5 / math.sqrt(HEAD_DIM)
-    inside = mask_ref[...] > 0.0
-    for head in range(width // HEAD_DIM):
-        cols = slice(head * HEAD_DIM, (head + 1) * HEAD_DIM)
-        queries = jnp.concatenate([q_ref[order_ref[i], :, cols] for i in range(blocks)], axis=0)
-        scores = lax.dot_general(
-            queries, k_ref[:, cols], (((1,), (1,)), ((), ())), preferred_element_type=jnp.float32
-        )
-        half = scores * scale + bias_ref[head]
-        weights = jnp.where(inside, half + half * jnp.tanh(half), 0.0).astype(jnp.bfloat16)
-        sums = jnp.dot(weights, v_ref[:, cols], preferred_element_type=jnp.float32)
-        for i, out_ref in enumerate(out_refs):
-            out_ref[:, cols] = sums[i * rows : (i + 1) * rows].astype(out_ref.dtype)
-
-
-def attend(order, queries, history, bias, mask, per_step):
+def make_attend_kernel(blocks, with_base):
+    def kernel(order_ref, q_ref, k_ref, v_ref, bias_ref, mask_ref, *refs):
+        base_refs, out_refs = refs[:-blocks], refs[-blocks:]
+        rows = q_ref.shape[1]
+        scale = 0.5 / math.sqrt(HEAD_DIM)
+        inside = mask_ref[...] > 0.0
+        for head in range(bias_ref.shape[0]):
+            cols = slice(head * HEAD_DIM, (head + 1) * HEAD_DIM)
+            queries = jnp.concatenate([q_ref[order_ref[i], :, cols] for i in range(blocks)], axis=0)
+            scores = lax.dot_general(
+                queries,
+                k_ref[:, cols],
+                (((1,), (1,)), ((), ())),
+                preferred_element_type=jnp.float32,
+            )
+            half = scores * scale + bias_ref[head]
+            weights = jnp.where(inside, half + half * jnp.tanh(half), 0.0).astype(jnp.bfloat16)
+            sums = jnp.dot(weights, v_ref[:, cols], preferred_element_type=jnp.float32)
+            for i, out_ref in enumerate(out_refs):
+                block = sums[i * rows : (i + 1) * rows]
+                if with_base:
+                    block = block + base_refs[i][:, cols]
+                out_ref[:, cols] = block.astype(out_ref.dtype)
+
+    return kernel
+
+
+def attend(order, queries, history, bias, mask, per_step, out_type, base=()):
     blocks, rows, full = queries.shape
     positions = history.shape[0]
     width = per_step * HEAD_DIM
     steps = full // width
+    spec = pl.BlockSpec((rows, width), lambda i: (0, i))
     return pl.pallas_call(
-        attend_kernel,
+        make_attend_kernel(blocks, len(base) > 0),
         grid=(steps,),
         in_specs=[
             pl.BlockSpec(memory_space=pltpu.SMEM),
@@ -66,16 +77,17 @@
             pl.BlockSpec((positions, width), lambda i: (0, i + steps)),
             pl.BlockSpec((per_step, 1, positions), lambda i: (i, 0, 0)),
             pl.BlockSpec((1, positions), lambda i: (0, 0)),
-        ],
-        out_specs=[pl.BlockSpec((rows, width), lambda i: (0, i))] * blocks,
-        out_shape=[jax.ShapeDtypeStruct((rows, full), jnp.bfloat16)] * blocks,
+        ]
+        + [spec] * len(base),
+        out_specs=[spec] * blocks,
+        out_shape=[jax.ShapeDtypeStruct((rows, full), out_type)] * blocks,
         compiler_params=pltpu.CompilerParams(vmem_limit_bytes=56 * 1024 * 1024),
         cost_estimate=pl.CostEstimate(
             flops=4 * blocks * rows * positions * full,
             bytes_accessed=4 * positions * full + 4 * blocks * rows * full,
             transcendentals=blocks * rows * positions * full // HEAD_DIM,
         ),
-    )(order, queries, history, history, bias, mask)
+    )(order, queries, history, history, bias, mask, *base)
 
 
 def own_kernel(q_ref, own_ref, self_bias_ref, out_ref):
@@ -106,7 +118,7 @@
     )(queries, own, self_bias[None])
 
 
-def finish_kernel(flag_ref, a_ref, b_ref, c_ref, d_ref, base_ref, gate_ref, gain_ref, out_ref):
+def finish_kernel(flag_ref, d_ref, c_ref, b_ref, a_ref, base_ref, gate_ref, gain_ref, out_ref):
     a, b, c, d = (ref[...].astype(jnp.float32) for ref in (a_ref, b_ref, c_ref, d_ref))
     odd, even = a + c, b + d
     even_low = flag_ref[0] == 1
@@ -132,7 +144,8 @@
         + [row_spec(width), row_spec(width), pl.BlockSpec((1, width), lambda i: (0, 0))],
         out_specs=row_spec(width),
         out_shape=jax.ShapeDtypeStruct((rows, width), jnp.bfloat16),
-    )(flag[None], *parts, base, gate, gain[None])
+        compiler_params=pltpu.CompilerParams(vmem_limit_bytes=12 * 1024 * 1024),
+    )(flag[None], *parts[::-1], base, gate, gain[None])
 
 
 def swapped(value):
@@ -181,7 +194,8 @@
     ).reshape(2 * groups, piece_len, width)
     incoming = lax.all_to_all(outgoing, ("yh0",) + GROUP, 0, 0, tiled=True)
     pieces = incoming.reshape(2 * groups * piece_len, width)
-    history = lax.all_gather(pieces, "z", tiled=True)
+    early = 16
+    history = lax.all_gather(pieces[early:], "z", tiled=True)
 
     queries = cand_query[0]
     own_half = lax.dynamic_slice_in_dim(queries, core * half_width, half_width, 1)
@@ -197,26 +211,35 @@
     own_holding = lax.dynamic_index_in_dim(holding, session, 0, keepdims=False)
     arrived = own_holding[None, :] == jnp.arange(groups, dtype=jnp.int32)[:, None]
     piece_of = jnp.sum(jnp.where(arrived, jnp.arange(slots, dtype=jnp.int32)[None, :], 0), axis=1)
-    order = jnp.arange(z_size, dtype=jnp.int32)[:, None, None, None]
-    order = order + (jnp.arange(2, dtype=jnp.int32)[None, :, None, None] + 2 * upper_y) * z_size
-    place = (
-        (order * slots + piece_of[None, None, :, None]) * piece_len
-        + jnp.arange(piece_len, dtype=jnp.int32)[None, None, None, :]
-    ).reshape(-1)
-    mask = (place < about[-1]).astype(jnp.float32)[None, :]
-    one_hot = (
-        about[place][:, None] == jnp.arange(time_bias.shape[0], dtype=jnp.int32)[None, :]
-    ).astype(jnp.float32)
-    own_bias = lax.dynamic_slice_in_dim(time_bias, core * (HEADS // 2), HEADS // 2, 1)
-    bias = 0.5 * jnp.einsum("kn,nh->hk", one_hot, own_bias, precision=lax.Precision.HIGHEST)
-
+    half_rows = about.shape[0] // 2
+    rows = lax.dynamic_slice_in_dim(about[:-1], upper_y * half_rows, half_rows).astype(jnp.float32)
+    rows = rows.reshape(2, z_size, slots, piece_len)
+    rows = jnp.einsum("sj,yzjr->zysr", arrived.astype(jnp.float32), rows, precision=lax.Precision.HIGHEST)
+    rows = rows.reshape(z_size, -1)
+    loop = jnp.arange(z_size, dtype=jnp.int32)[:, None, None, None]
+    loop = loop + z_size * (2 * upper_y + jnp.arange(2, dtype=jnp.int32)[None, :, None, None])
+    place = (loop * slots + piece_of[None, None, :, None]) * piece_len
+    place = (place + jnp.arange(piece_len, dtype=jnp.int32)[None, None, None, :]).reshape(z_size, -1)
+    own_bias = 0.5 * lax.dynamic_slice_in_dim(time_bias, core * (HEADS // 2), HEADS // 2, 1)
+
+    def bias_and_mask(part):
+        numbers = rows[:, part].reshape(-1, 1)
+        table = jnp.arange(time_bias.shape[0], dtype=jnp.int32).astype(jnp.float32)
+        one_hot = (jnp.abs(numbers - table[None, :]) < 0.5).astype(jnp.float32)
+        bias = jnp.einsum("kn,nh->hk", one_hot, own_bias, precision=lax.Precision.HIGHEST)
+        return bias[:, None, :], (place[:, part].reshape(1, -1) < about[-1]).astype(jnp.float32)
+
+    first = bias_and_mask(slice(0, early))
+    second = bias_and_mask(slice(early, None))
     base = own_term(queries, cand_kv[0], self_bias)
-    bias, mask, base = lax.optimization_barrier((bias[:, None, :], mask, base))
     order = send_order()[lax.axis_index(Y + ("core",))]
-    partial = attend(order, spread, history, bias, mask, 2)
-    parts = [None] * 4
-    for step in (3, 2, 1, 0):
-        parts[step] = lax.ppermute(partial[step], Y + ("core",), send_pairs(step))
+    start, base, first, second, order = lax.optimization_barrier(
+        (pieces[:early], base, first, second, order)
+    )
+    early_history = lax.all_gather(start, "z", tiled=True)
+    sums = attend(order, spread, early_history, *first, 4, jnp.float32)
+    partial = attend(order, spread, history, *second, 2, jnp.bfloat16, sums)
+    parts = [lax.ppermute(partial[s], Y + ("core",), send_pairs(s)) for s in range(4)]
     flag = ((core == 0) == (core == side)).astype(jnp.int32)
     return finish(flag, parts, base, cand_gate[0], norm_gain)[None]
 

time: 147 us -> 146 us (level)
  waiting for transfers between devices: 49.5 us -> 16.1 us
  blocking collectives: 25.8 us -> 57 us
  local copies, waits for them, and re-layouts: 13.1 us -> 8.46 us
  Pallas kernels: 14.4 us -> 16.3 us
  starting transfers between devices: 25.6 us -> 27.3 us
    all_gather x0 -> x1, blocking collectives: none -> 31.1 us  [per_device(): early_history = lax.all_gather(start, 'z', tiled=True)]
    all_gather x1, waiting for transfers between devices: 20.7 us -> 0.12 us  [per_device(): history = lax.all_gather(pieces[early:], 'z', tiled=True)]
    all_to_all x1, waiting for transfers between devices: 10.5 us -> 0.01 us  [per_device(): lax.all_to_all(jnp.stack([first, second, second, first]), Y, 0, 0, tiled=...]
    gather x1 -> x0, local copies, waits for them, and re-layouts: 6.14 us -> none  [per_device(): about[place][:, None]]
    pallas_call x1 -> x2, Pallas kernels: 7.74 us -> 11 us  [attend(): pl.pallas_call(make_attend_kernel(blocks, len(base) > 0), grid=(steps,),...]
    ppermute x4, starting transfers between devices: 17 us -> 18.8 us  [per_device(): lax.ppermute(partial[s], Y + ('core',), send_pairs(s))]
  transfers between devices with their start and end apart: 8 -> 8, of which waited for: 5 -> 5; matrix products, arithmetic and copies ran while one was open for 8% -> 6% of each run, Pallas kernels for 3% -> 5%
where the time goes in v10:
time: 146 us; the launch traced here: 145 us
  blocking collectives  57 us (39%)
  starting transfers between devices  27.3 us (19%)
  Pallas kernels  16.3 us (11%)
  waiting for transfers between devices  16.1 us (11%)
  between operations  14.4 us (10%)
  local copies, waits for them, and re-layouts  8.46 us (6%)
  other arithmetic  4.12 us (3%)
  matrix products  1.56 us (1%)
    all_gather x1, blocking collectives, per_device(): early_history = lax.all_gather(start, 'z', tiled=True)  31.1 us
    all_to_all x1, blocking collectives, per_device(): incoming = lax.all_to_all(outgoing, ('yh0',) + GROUP, 0, 0, tiled=True)  25.9 us
    ppermute x4, starting transfers between devices, per_device(): lax.ppermute(partial[s], Y + ('core',), send_pairs(s))  18.8 us
    ppermute x4, waiting for transfers between devices, per_device(): lax.ppermute(partial[s], Y + ('core',), send_pairs(s))  15.9 us
    pallas_call x2, Pallas kernels, attend(): pl.pallas_call(make_attend_kernel(blocks, len(base) > 0), grid=(steps,),...  11 us
    ppermute x2, starting transfers between devices, swapped(): return lax.ppermute(value, 'core', [(0, 1), (1, 0)])  5.06 us
    pallas_call x1, Pallas kernels, own_term(): pl.pallas_call(own_kernel, grid=(rows // block,), in_specs=[pl.BlockSpec(...  3.85 us
    all_to_all x1, starting transfers between devices, per_device(): lax.all_to_all(jnp.stack([first, second, second, first]), Y, 0, 0, tiled=...  3.51 us
  transfers between devices with their start and end apart: 8, of which 5 were waited for; matrix products, arithmetic and copies ran while one was open for 6% of the time, Pallas kernels for 5%

profile of v10, /device:TPU:1, one launch (start us, length us, event | category | flops | bytes accessed | tf_op | source)
XLA Modules:
  0.0 145.2 jit_solution(12755515727556513706)
XLA Ops:
  6.5 0.7 and_select_fusion.1
  7.9 1.0 gather_fusion
  9.7 25.9 %all_to_all.10 = bf16[32,4,2048]{2,1,0:T(4,128)(2,1)S(1)} all-to-all(bf16[32,4,2048]{2,1,0:T(4,128)(2,1)S(1)} %bitcast.47), channel_id=1, replica_groups=mesh['yh1'=2,'yh0'=2,'z'=8,'x'=4,'ylo'=2,'core'=2] {'yh0','x','ylo','core'}, dimensions={0} | all-to-all | bytes 1048576 | tf_op jit(solution)/shard_map/all_to_all | solution.py:195
  35.8 0.9 slice.56
  37.4 3.1 %collective-permute-start = (s32[2049]{0:T(1024)S(1)}, s32[2049]{0:T(1024)S(1)}, u32[]{:S(2)}, u32[]{:S(2)}) collective-permute-start(s32[2049]{0:T(1024)S(1)} %pad_add_fusion), channel_id=1, source_target_pairs={{0,1},{1,0},{2,3},{3,2},{4,5},{5,4},{6,7},{7,6},{8,9},{9,8},{10,11... | collective-permute-start | bytes 24596 | tf_op jit(solution)/shard_map/ppermute | solution.py:152
  40.6 1.9 %collective-permute-start.1 = (bf16[128,1024]{1,0:T(8,128)(2,1)S(1)}, bf16[128,1024]{1,0:T(8,128)(2,1)S(1)}, u32[]{:S(2)}, u32[]{:S(2)}) collective-permute-start(bf16[128,1024]{1,0:T(8,128)(2,1)S(1)} %dynamic-slice_bitcast_fusion), channel_id=1, source_target_pairs={{0,1},{1,0},{2,3},{3,2},{4,5},{5,4},{6,7},{7,6},{8,9},{9,8},{10,11... | collective-permute-start | bytes 786440 | tf_op jit(solution)/shard_map/ppermute | solution.py:152
  42.9 1.2 fusion.20.order_ref
  44.3 3.8 %shard_map.109.base_ref = f32[128,2048]{1,0:T(8,128)} custom-call(bf16[128,2048]{1,0:T(8,128)(2,1)} %bitcast.45, bf16[128,4096]{1,0:T(8,128)(2,1)} %bitcast.48, f32[1,16]{1,0:T(1,128)} %bitcast.56), custom_call_target="tpu_custom_call" | custom-call | tf_op jit(solution)/shard_map/pallas_call | solution.py:108
  48.3 1.1 pad_maximum_fusion
  49.4 3.5 %all-to-all-start.1 = ((bf16[4,128,1024]{2,1,0:T(8,128)(2,1)}), bf16[4,128,1024]{2,1,0:T(8,128)(2,1)S(1)}, u32[]{:S(2)}, u32[]{:S(2)}) async-start(bf16[4,128,1024]{2,1,0:T(8,128)(2,1)} %pad_maximum_fusion), calls=%async_computation.1 | async-start | bytes 2097152 | tf_op jit(solution)/shard_map/all_to_all | solution.py:206
  55.3 0.7 fusion.14
  58.1 0.9 fusion.6
  59.0 31.1 %all_gather.7.k_ref.v_ref = bf16[128,2048]{1,0:T(8,128)(2,1)} all-gather(bf16[16,2048]{1,0:T(8,128)(2,1)S(1)} %slice.48), channel_id=1, replica_groups=mesh['yh1'=2,'yh0'=2,'z'=8,'x'=4,'ylo'=2,'core'=2] {'z'}, dimensions={0}, use_global_device_ids=true | all-gather | bytes 589824 | tf_op jit(solution)/shard_map/all_gather | solution.py:239
  90.1 1.0 copy-done.4
  91.1 3.5 %shard_map.110 = (f32[128,1024]{1,0:T(8,128)}, f32[128,1024]{1,0:T(8,128)}, f32[128,1024]{1,0:T(8,128)}, f32[128,1024]{1,0:T(8,128)}) custom-call(s32[4]{0:T(128)} %fusion.20.order_ref, bf16[4,128,1024]{2,1,0:T(8,128)(2,1)} %copy-done.4, bf16[128,2048]{1,0:T(8,128)(2,1)} %all_gather.7.k_ref.v_ref, bf16[128,2048]{1,0:T(8,128)(2,1)} %all_gather.7.k_ref.v_ref, ...), custom_call_target="tpu_custom_call" | custom-call | flops 268435456 | bytes 2621440 | tf_op jit(solution)/shard_map/pallas_call | solution.py:70
  94.7 7.6 %shard_map.111 = (bf16[128,1024]{1,0:T(8,128)(2,1)}, bf16[128,1024]{1,0:T(8,128)(2,1)}, bf16[128,1024]{1,0:T(8,128)(2,1)}, bf16[128,1024]{1,0:T(8,128)(2,1)}) custom-call(s32[4]{0:T(128)} %fusion.20.order_ref, bf16[4,128,1024]{2,1,0:T(8,128)(2,1)} %copy-done.4, bf16[896,2048]{1,0:T(8,128)(2,1)} %all-gather.2.cloned.1.call-done.k_ref.v_ref, ...), custom_call_target="tpu_custom_call" | custom-call | flops 1879048192 | bytes 5767168 | tf_op jit(solution)/shard_map/pallas_call | solution.py:70
  102.2 12.1 %collective-permute-start.2 = (bf16[128,1024]{1,0:T(8,128)(2,1)}, bf16[128,1024]{1,0:T(8,128)(2,1)S(1)}, u32[]{:S(2)}, u32[]{:S(2)}) collective-permute-start(bf16[128,1024]{1,0:T(8,128)(2,1)} %get-tuple-element.30), channel_id=1, source_target_pairs={{0,0},{257,257},{1,256},{256,1},{384,384},{129,129},{385,128},{128... | collective-permute-start | bytes 786440 | tf_op jit(solution)/shard_map/ppermute | solution.py:242
  114.3 1.9 %collective-permute-start.3 = (bf16[128,1024]{1,0:T(8,128)(2,1)}, bf16[128,1024]{1,0:T(8,128)(2,1)S(1)}, u32[]{:S(2)}, u32[]{:S(2)}) collective-permute-start(bf16[128,1024]{1,0:T(8,128)(2,1)} %get-tuple-element.31), channel_id=1, source_target_pairs={{0,256},{257,1},{1,384},{256,129},{384,128},{129,385},{385,0},{128... | collective-permute-start | bytes 786440 | tf_op jit(solution)/shard_map/ppermute | solution.py:242
  116.2 1.9 %collective-permute-start.4 = (bf16[128,1024]{1,0:T(8,128)(2,1)}, bf16[128,1024]{1,0:T(8,128)(2,1)S(1)}, u32[]{:S(2)}, u32[]{:S(2)}) collective-permute-start(bf16[128,1024]{1,0:T(8,128)(2,1)} %get-tuple-element.32), channel_id=1, source_target_pairs={{0,384},{257,129},{1,128},{256,385},{384,0},{129,257},{385,256},{1... | collective-permute-start | bytes 786440 | tf_op jit(solution)/shard_map/ppermute | solution.py:242
  118.2 2.9 %collective-permute-start.5 = (bf16[128,1024]{1,0:T(8,128)(2,1)}, bf16[128,1024]{1,0:T(8,128)(2,1)S(1)}, u32[]{:S(2)}, u32[]{:S(2)}) collective-permute-start(bf16[128,1024]{1,0:T(8,128)(2,1)} %get-tuple-element.33), channel_id=1, source_target_pairs={{0,128},{257,385},{1,0},{256,257},{384,256},{129,1},{385,384},{128... | collective-permute-start | bytes 786440 | tf_op jit(solution)/shard_map/ppermute | solution.py:242
  121.0 5.2 %collective-permute-done.2.d_ref = bf16[128,1024]{1,0:T(8,128)(2,1)S(1)} collective-permute-done((bf16[128,1024]{1,0:T(8,128)(2,1)}, bf16[128,1024]{1,0:T(8,128)(2,1)S(1)}, u32[]{:S(2)}, u32[]{:S(2)}) %collective-permute-start.2) | collective-permute-done | bytes 262176 | tf_op jit(solution)/shard_map/ppermute | solution.py:242
  126.2 7.7 %collective-permute-done.3.c_ref = bf16[128,1024]{1,0:T(8,128)(2,1)S(1)} collective-permute-done((bf16[128,1024]{1,0:T(8,128)(2,1)}, bf16[128,1024]{1,0:T(8,128)(2,1)S(1)}, u32[]{:S(2)}, u32[]{:S(2)}) %collective-permute-start.3) | collective-permute-done | bytes 262176 | tf_op jit(solution)/shard_map/ppermute | solution.py:242
  133.9 2.9 %collective-permute-done.4.b_ref = bf16[128,1024]{1,0:T(8,128)(2,1)S(1)} collective-permute-done((bf16[128,1024]{1,0:T(8,128)(2,1)}, bf16[128,1024]{1,0:T(8,128)(2,1)S(1)}, u32[]{:S(2)}, u32[]{:S(2)}) %collective-permute-start.4) | collective-permute-done | bytes 262176 | tf_op jit(solution)/shard_map/ppermute | solution.py:242
  137.0 1.4 shard_map.112
  (71 shorter events, 6.8 us)
Async XLA Ops:
  6.5 1.4 copy-start
  6.5 88.1 %all-gather.2.cloned.1.call-start = ((), (), s32[]{:S(2)}) async-start(), calls=%async_computation.2 | async-start | bytes 4128768 | tf_op jit(solution)/shard_map/all_gather | solution.py:198
  7.9 29.5 %copy-start.7 = (s32[1,2048]{1,0:T(1,128)S(1)}, s32[1,2048]{1,0:T(1,128)}, u32[]{:S(2)}) copy-start(s32[1,2048]{1,0:T(1,128)} %param.17) | copy-start | bytes 24580
  7.9 32.7 %copy-start.5 = (bf16[1,128,2048]{2,1,0:T(8,128)(2,1)S(1)}, bf16[1,128,2048]{2,1,0:T(8,128)(2,1)}, u32[]{:S(2)}) copy-start(bf16[1,128,2048]{2,1,0:T(8,128)(2,1)} %param.11) | copy-start | bytes 1572868
  9.7 38.4 %copy-start.6 = (bf16[1,128,2048]{2,1,0:T(8,128)(2,1)S(1)}, bf16[1,128,2048]{2,1,0:T(8,128)(2,1)}, u32[]{:S(2)}) copy-start(bf16[1,128,2048]{2,1,0:T(8,128)(2,1)} %param.11) | copy-start | bytes 1572868
  37.4 15.5 %collective-permute-start = (s32[2049]{0:T(1024)S(1)}, s32[2049]{0:T(1024)S(1)}, u32[]{:S(2)}, u32[]{:S(2)}) collective-permute-start(s32[2049]{0:T(1024)S(1)} %pad_add_fusion), channel_id=1, source_target_pairs={{0,1},{1,0},{2,3},{3,2},{4,5},{5,4},{6,7},{7,6},{8,9},{9,8},{10,11... | collective-permute-start | bytes 24596 | tf_op jit(solution)/shard_map/ppermute | solution.py:152
  40.6 7.5 %collective-permute-start.1 = (bf16[128,1024]{1,0:T(8,128)(2,1)S(1)}, bf16[128,1024]{1,0:T(8,128)(2,1)S(1)}, u32[]{:S(2)}, u32[]{:S(2)}) collective-permute-start(bf16[128,1024]{1,0:T(8,128)(2,1)S(1)} %dynamic-slice_bitcast_fusion), channel_id=1, source_target_pairs={{0,1},{1,0},{2,3},{3,2},{4,5},{5,4},{6,7},{7,6},{8,9},{9,8},{10,11... | collective-permute-start | bytes 786440 | tf_op jit(solution)/shard_map/ppermute | solution.py:152
  44.3 12.7 %copy-start.8 = (f32[128,16]{0,1:T(8,128)S(1)}, f32[128,16]{0,1:T(8,128)}, u32[]{:S(2)}) copy-start(f32[128,16]{0,1:T(8,128)} %param.18) | copy-start | bytes 24580
  49.4 40.6 %all-to-all-start.1 = ((bf16[4,128,1024]{2,1,0:T(8,128)(2,1)}), bf16[4,128,1024]{2,1,0:T(8,128)(2,1)S(1)}, u32[]{:S(2)}, u32[]{:S(2)}) async-start(bf16[4,128,1024]{2,1,0:T(8,128)(2,1)} %pad_maximum_fusion), calls=%async_computation.1 | async-start | bytes 2097152 | tf_op jit(solution)/shard_map/all_to_all | solution.py:206
  90.1 1.0 copy-start.4
  94.7 42.3 %copy-start.1 = (f32[128,2048]{1,0:T(8,128)S(1)}, f32[128,2048]{1,0:T(8,128)}, u32[]{:S(2)}) copy-start(f32[128,2048]{1,0:T(8,128)} %shard_map.109.base_ref) | copy-start | bytes 3145732
  94.7 42.3 %copy-start.2 = (bf16[1,128,2048]{2,1,0:T(8,128)(2,1)S(1)}, bf16[1,128,2048]{2,1,0:T(8,128)(2,1)}, u32[]{:S(2)}) copy-start(bf16[1,128,2048]{2,1,0:T(8,128)(2,1)} %param.13) | copy-start | bytes 1572868
  94.7 42.3 %copy-start.3 = (f32[2048]{0:T(1024)S(1)}, f32[2048]{0:T(1024)}, u32[]{:S(2)}) copy-start(f32[2048]{0:T(1024)} %param.20) | copy-start | bytes 24580
  102.2 24.0 %collective-permute-start.2 = (bf16[128,1024]{1,0:T(8,128)(2,1)}, bf16[128,1024]{1,0:T(8,128)(2,1)S(1)}, u32[]{:S(2)}, u32[]{:S(2)}) collective-permute-start(bf16[128,1024]{1,0:T(8,128)(2,1)} %get-tuple-element.30), channel_id=1, source_target_pairs={{0,0},{257,257},{1,256},{256,1},{384,384},{129,129},{385,128},{128... | collective-permute-start | bytes 786440 | tf_op jit(solution)/shard_map/ppermute | solution.py:242
  114.3 19.6 %collective-permute-start.3 = (bf16[128,1024]{1,0:T(8,128)(2,1)}, bf16[128,1024]{1,0:T(8,128)(2,1)S(1)}, u32[]{:S(2)}, u32[]{:S(2)}) collective-permute-start(bf16[128,1024]{1,0:T(8,128)(2,1)} %get-tuple-element.31), channel_id=1, source_target_pairs={{0,256},{257,1},{1,384},{256,129},{384,128},{129,385},{385,0},{128... | collective-permute-start | bytes 786440 | tf_op jit(solution)/shard_map/ppermute | solution.py:242
  116.2 20.6 %collective-permute-start.4 = (bf16[128,1024]{1,0:T(8,128)(2,1)}, bf16[128,1024]{1,0:T(8,128)(2,1)S(1)}, u32[]{:S(2)}, u32[]{:S(2)}) collective-permute-start(bf16[128,1024]{1,0:T(8,128)(2,1)} %get-tuple-element.32), channel_id=1, source_target_pairs={{0,384},{257,129},{1,128},{256,385},{384,0},{129,257},{385,256},{1... | collective-permute-start | bytes 786440 | tf_op jit(solution)/shard_map/ppermute | solution.py:242
  118.2 18.8 %collective-permute-start.5 = (bf16[128,1024]{1,0:T(8,128)(2,1)}, bf16[128,1024]{1,0:T(8,128)(2,1)S(1)}, u32[]{:S(2)}, u32[]{:S(2)}) collective-permute-start(bf16[128,1024]{1,0:T(8,128)(2,1)} %get-tuple-element.33), channel_id=1, source_target_pairs={{0,128},{257,385},{1,0},{256,257},{384,256},{129,1},{385,384},{128... | collective-permute-start | bytes 786440 | tf_op jit(solution)/shard_map/ppermute | solution.py:242
Sparse Core Ops, SparseCore 0:
  36.9 57.7 all-gather.1

commit v11 on v7

--- a/solution.py
+++ b/solution.py
@@ -10,6 +10,7 @@
 
 HEADS = 16
 HEAD_DIM = 128
+PER_STEP = 4
 GROUP = ("x", "ylo", "core")
 LOOP = ("yh1", "yh0", "z")
 Y = ("yh1", "yh0")
@@ -35,12 +36,14 @@
 
 
 def attend_kernel(order_ref, q_ref, k_ref, v_ref, bias_ref, mask_ref, *out_refs):
-    blocks, rows, width = q_ref.shape
+    rows = q_ref.shape[1]
     scale = 0.5 / math.sqrt(HEAD_DIM)
     inside = mask_ref[...] > 0.0
-    for head in range(width // HEAD_DIM):
+    for head in range(bias_ref.shape[0]):
         cols = slice(head * HEAD_DIM, (head + 1) * HEAD_DIM)
-        queries = jnp.concatenate([q_ref[order_ref[i], :, cols] for i in range(blocks)], axis=0)
+        queries = jnp.concatenate(
+            [q_ref[order_ref[i], :, cols] for i in range(len(out_refs))], axis=0
+        )
         scores = lax.dot_general(
             queries, k_ref[:, cols], (((1,), (1,)), ((), ())), preferred_element_type=jnp.float32
         )
@@ -56,6 +59,7 @@
     positions = history.shape[0]
     width = per_step * HEAD_DIM
     steps = full // width
+    count = order.shape[0]
     return pl.pallas_call(
         attend_kernel,
         grid=(steps,),
@@ -67,13 +71,13 @@
             pl.BlockSpec((per_step, 1, positions), lambda i: (i, 0, 0)),
             pl.BlockSpec((1, positions), lambda i: (0, 0)),
         ],
-        out_specs=[pl.BlockSpec((rows, width), lambda i: (0, i))] * blocks,
-        out_shape=[jax.ShapeDtypeStruct((rows, full), jnp.bfloat16)] * blocks,
+        out_specs=[pl.BlockSpec((rows, width), lambda i: (0, i))] * count,
+        out_shape=[jax.ShapeDtypeStruct((rows, full), jnp.bfloat16)] * count,
         compiler_params=pltpu.CompilerParams(vmem_limit_bytes=56 * 1024 * 1024),
         cost_estimate=pl.CostEstimate(
-            flops=4 * blocks * rows * positions * full,
-            bytes_accessed=4 * positions * full + 4 * blocks * rows * full,
-            transcendentals=blocks * rows * positions * full // HEAD_DIM,
+            flops=4 * count * rows * positions * full,
+            bytes_accessed=4 * positions * full + 4 * count * rows * full,
+            transcendentals=count * rows * positions * full // HEAD_DIM,
         ),
     )(order, queries, history, history, bias, mask)
 
@@ -106,7 +110,7 @@
     )(queries, own, self_bias[None])
 
 
-def finish_kernel(flag_ref, a_ref, b_ref, c_ref, d_ref, base_ref, gate_ref, gain_ref, out_ref):
+def finish_kernel(flag_ref, d_ref, c_ref, b_ref, a_ref, base_ref, gate_ref, gain_ref, out_ref):
     a, b, c, d = (ref[...].astype(jnp.float32) for ref in (a_ref, b_ref, c_ref, d_ref))
     odd, even = a + c, b + d
     even_low = flag_ref[0] == 1
@@ -132,7 +136,8 @@
         + [row_spec(width), row_spec(width), pl.BlockSpec((1, width), lambda i: (0, 0))],
         out_specs=row_spec(width),
         out_shape=jax.ShapeDtypeStruct((rows, width), jnp.bfloat16),
-    )(flag[None], *parts, base, gate, gain[None])
+        compiler_params=pltpu.CompilerParams(vmem_limit_bytes=12 * 1024 * 1024),
+    )(flag[None], *parts[::-1], base, gate, gain[None])
 
 
 def swapped(value):
@@ -197,26 +202,30 @@
     own_holding = lax.dynamic_index_in_dim(holding, session, 0, keepdims=False)
     arrived = own_holding[None, :] == jnp.arange(groups, dtype=jnp.int32)[:, None]
     piece_of = jnp.sum(jnp.where(arrived, jnp.arange(slots, dtype=jnp.int32)[None, :], 0), axis=1)
-    order = jnp.arange(z_size, dtype=jnp.int32)[:, None, None, None]
-    order = order + (jnp.arange(2, dtype=jnp.int32)[None, :, None, None] + 2 * upper_y) * z_size
-    place = (
-        (order * slots + piece_of[None, None, :, None]) * piece_len
-        + jnp.arange(piece_len, dtype=jnp.int32)[None, None, None, :]
-    ).reshape(-1)
-    mask = (place < about[-1]).astype(jnp.float32)[None, :]
-    one_hot = (
-        about[place][:, None] == jnp.arange(time_bias.shape[0], dtype=jnp.int32)[None, :]
-    ).astype(jnp.float32)
-    own_bias = lax.dynamic_slice_in_dim(time_bias, core * (HEADS // 2), HEADS // 2, 1)
-    bias = 0.5 * jnp.einsum("kn,nh->hk", one_hot, own_bias, precision=lax.Precision.HIGHEST)
-
+    half_rows = about.shape[0] // 2
+    rows = lax.dynamic_slice_in_dim(about[:-1], upper_y * half_rows, half_rows).astype(jnp.float32)
+    rows = rows.reshape(2, z_size, slots, piece_len)
+    rows = jnp.einsum("sj,yzjr->zysr", arrived.astype(jnp.float32), rows, precision=lax.Precision.HIGHEST)
+    rows = rows.reshape(z_size, -1)
+    loop = jnp.arange(z_size, dtype=jnp.int32)[:, None, None, None]
+    loop = loop + z_size * (2 * upper_y + jnp.arange(2, dtype=jnp.int32)[None, :, None, None])
+    place = (loop * slots + piece_of[None, None, :, None]) * piece_len
+    place = (place + jnp.arange(piece_len, dtype=jnp.int32)[None, None, None, :]).reshape(z_size, -1)
+    own_bias = 0.5 * lax.dynamic_slice_in_dim(time_bias, core * (HEADS // 2), HEADS // 2, 1)
+
+    numbers = rows.reshape(-1, 1)
+    table = jnp.arange(time_bias.shape[0], dtype=jnp.int32).astype(jnp.float32)
+    one_hot = (jnp.abs(numbers - table[None, :]) < 0.5).astype(jnp.float32)
+    bias = jnp.einsum("kn,nh->hk", one_hot, own_bias, precision=lax.Precision.HIGHEST)[:, None, :]
+    mask = (place.reshape(1, -1) < about[-1]).astype(jnp.float32)
     base = own_term(queries, cand_kv[0], self_bias)
-    bias, mask, base = lax.optimization_barrier((bias[:, None, :], mask, base))
     order = send_order()[lax.axis_index(Y + ("core",))]
-    partial = attend(order, spread, history, bias, mask, 2)
-    parts = [None] * 4
-    for step in (3, 2, 1, 0):
-        parts[step] = lax.ppermute(partial[step], Y + ("core",), send_pairs(step))
+    bias, mask, base, order = lax.optimization_barrier((bias, mask, base, order))
+    far = attend(order[2:], spread, history, bias, mask, PER_STEP)
+    *far, rest = lax.optimization_barrier((*far, order[:2]))
+    near = attend(rest, spread, history, bias, mask, PER_STEP)
+    partial = [*near, *far]
+    parts = [lax.ppermute(partial[s], Y + ("core",), send_pairs(s)) for s in range(4)]
     flag = ((core == 0) == (core == side)).astype(jnp.int32)
     return finish(flag, parts, base, cand_gate[0], norm_gain)[None]
 

time: 147 us -> 143 us (0.973)
  local copies, waits for them, and re-layouts: 13.1 us -> 6.48 us
  Pallas kernels: 14.4 us -> 16.4 us
    gather x1 -> x0, local copies, waits for them, and re-layouts: 6.14 us -> none  [per_device(): about[place][:, None]]
    all_to_all x1, waiting for transfers between devices: 10.5 us -> 16.2 us  [per_device(): lax.all_to_all(jnp.stack([first, second, second, first]), Y, 0, 0, tiled=...]
    ppermute x4, waiting for transfers between devices: 16.9 us -> 11.3 us  [per_device(): lax.ppermute(partial[s], Y + ('core',), send_pairs(s))]
    pallas_call x1 -> x2, Pallas kernels: 7.74 us -> 11.2 us  [attend(): pl.pallas_call(attend_kernel, grid=(steps,), in_specs=[pl.BlockSpec(memor...]
  transfers between devices with their start and end apart: 8 -> 8, of which waited for: 5 -> 6; matrix products, arithmetic and copies ran while one was open for 8% -> 5% of each run, Pallas kernels for 3% -> 7%
where the time goes in v11:
time: 143 us
  waiting for transfers between devices  49.5 us (35%)
  starting transfers between devices  26.1 us (18%)
  blocking collectives  25.8 us (18%)
  Pallas kernels  16.4 us (11%)
  between operations  14.3 us (10%)
  local copies, waits for them, and re-layouts  6.48 us (5%)
  other arithmetic  3.42 us (2%)
    all_to_all x1, blocking collectives, per_device(): incoming = lax.all_to_all(outgoing, ('yh0',) + GROUP, 0, 0, tiled=True)  25.8 us
    all_gather x1, waiting for transfers between devices, per_device(): history = lax.all_gather(pieces, 'z', tiled=True)  20.8 us
    ppermute x4, starting transfers between devices, per_device(): lax.ppermute(partial[s], Y + ('core',), send_pairs(s))  17.5 us
    all_to_all x1, waiting for transfers between devices, per_device(): lax.all_to_all(jnp.stack([first, second, second, first]), Y, 0, 0, tiled=...  16.2 us
    ppermute x4, waiting for transfers between devices, per_device(): lax.ppermute(partial[s], Y + ('core',), send_pairs(s))  11.3 us
    pallas_call x2, Pallas kernels, attend(): pl.pallas_call(attend_kernel, grid=(steps,), in_specs=[pl.BlockSpec(memor...  11.2 us
    ppermute x2, starting transfers between devices, swapped(): return lax.ppermute(value, 'core', [(0, 1), (1, 0)])  5.06 us
    pallas_call x1, Pallas kernels, own_term(): pl.pallas_call(own_kernel, grid=(rows // block,), in_specs=[pl.BlockSpec(...  3.81 us
  transfers between devices with their start and end apart: 8, of which 6 were waited for; matrix products, arithmetic and copies ran while one was open for 5% of the time, Pallas kernels for 7%

profile of v11, /device:TPU:1, one launch (start us, length us, event | category | flops | bytes accessed | tf_op | source)
XLA Modules:
  0.0 142.7 jit_solution(18019159475874836953)
XLA Ops:
  6.6 0.8 and_select_fusion
  8.0 1.0 gather_fusion
  9.7 25.8 %all_to_all.10 = bf16[32,4,2048]{2,1,0:T(4,128)(2,1)S(1)} all-to-all(bf16[32,4,2048]{2,1,0:T(4,128)(2,1)S(1)} %bitcast.48), channel_id=1, replica_groups=mesh['yh1'=2,'yh0'=2,'z'=8,'x'=4,'ylo'=2,'core'=2] {'yh0','x','ylo','core'}, dimensions={0} | all-to-all | bytes 1048576 | tf_op jit(solution)/shard_map/all_to_all | solution.py:187
  35.5 0.9 reshape.140
  37.1 3.1 %collective-permute-start = (s32[2049]{0:T(1024)S(1)}, s32[2049]{0:T(1024)S(1)}, u32[]{:S(2)}, u32[]{:S(2)}) collective-permute-start(s32[2049]{0:T(1024)S(1)} %pad_add_fusion), channel_id=1, source_target_pairs={{0,1},{1,0},{2,3},{3,2},{4,5},{5,4},{6,7},{7,6},{8,9},{9,8},{10,11... | collective-permute-start | bytes 24596 | tf_op jit(solution)/shard_map/ppermute | solution.py:144
  40.3 1.9 %collective-permute-start.1 = (bf16[128,1024]{1,0:T(8,128)(2,1)S(1)}, bf16[128,1024]{1,0:T(8,128)(2,1)S(1)}, u32[]{:S(2)}, u32[]{:S(2)}) collective-permute-start(bf16[128,1024]{1,0:T(8,128)(2,1)S(1)} %dynamic-slice_bitcast_fusion), channel_id=1, source_target_pairs={{0,1},{1,0},{2,3},{3,2},{4,5},{5,4},{6,7},{7,6},{8,9},{9,8},{10,11... | collective-permute-start | bytes 786440 | tf_op jit(solution)/shard_map/ppermute | solution.py:144
  42.4 1.3 collective-permute-done.1
  43.9 1.1 pad_maximum_fusion
  45.0 3.5 %all-to-all-start = ((bf16[4,128,1024]{2,1,0:T(8,128)(2,1)}), bf16[4,128,1024]{2,1,0:T(8,128)(2,1)S(1)}, u32[]{:S(2)}, u32[]{:S(2)}) async-start(bf16[4,128,1024]{2,1,0:T(8,128)(2,1)} %pad_maximum_fusion), calls=%async_computation | async-start | bytes 2097152 | tf_op jit(solution)/shard_map/all_to_all | solution.py:197
  49.3 3.8 %shard_map.109.base_ref = f32[128,2048]{1,0:T(8,128)} custom-call(bf16[128,2048]{1,0:T(8,128)(2,1)} %bitcast.46, bf16[128,4096]{1,0:T(8,128)(2,1)} %bitcast.49, f32[1,16]{1,0:T(1,128)} %bitcast.54), custom_call_target="tpu_custom_call" | custom-call | tf_op jit(solution)/shard_map/pallas_call | solution.py:100
  53.6 0.7 fusion.6
  54.4 0.7 reshape.142.mask_ref
  57.5 16.2 %all-to-all-done.q_ref = bf16[4,128,1024]{2,1,0:T(8,128)(2,1)S(1)} async-done(((bf16[4,128,1024]{2,1,0:T(8,128)(2,1)}), bf16[4,128,1024]{2,1,0:T(8,128)(2,1)S(1)}, u32[]{:S(2)}, u32[]{:S(2)}) %all-to-all-start) | async-done | bytes 1048608 | tf_op jit(solution)/shard_map/all_to_all | solution.py:197
  73.7 20.8 %all-gather.2.cloned.1.call-done.k_ref.v_ref = bf16[1024,2048]{1,0:T(8,128)(2,1)} async-done(((bf16[128,2048]{1,0:T(8,128)(2,1)}), bf16[1024,2048]{1,0:T(8,128)(2,1)}) %all-gather.2.cloned.1.call-update) | async-done | bytes 4194320 | tf_op jit(solution)/shard_map/all_gather | solution.py:189
  94.4 5.6 %shard_map.110 = (bf16[128,1024]{1,0:T(8,128)(2,1)}, bf16[128,1024]{1,0:T(8,128)(2,1)}) custom-call(s32[2]{0:T(128)} %get-tuple-element.36.order_ref, bf16[4,128,1024]{2,1,0:T(8,128)(2,1)} %copy-done.4, bf16[1024,2048]{1,0:T(8,128)(2,1)} %all-gather.2.cloned.1.call-done.k_ref.v_ref, bf16[1024,2048]{1,0:T(8,128)(2,1)} %all-gather.2.cloned.1.call-done.k_ref.v_ref, ...), custom_call_target="tpu_custom_call" | custom-call | flops 1073741824 | bytes 5242880 | tf_op jit(solution)/shard_map/pallas_call | solution.py:63
  100.0 7.8 %collective-permute-start.2 = (bf16[128,1024]{1,0:T(8,128)(2,1)}, bf16[128,1024]{1,0:T(8,128)(2,1)S(1)}, u32[]{:S(2)}, u32[]{:S(2)}) collective-permute-start(bf16[128,1024]{1,0:T(8,128)(2,1)} %get-tuple-element.21), channel_id=1, source_target_pairs={{0,0},{257,257},{1,256},{256,1},{384,384},{129,129},{385,128},{128... | collective-permute-start | bytes 786440 | tf_op jit(solution)/shard_map/ppermute | solution.py:228
  107.8 1.9 %collective-permute-start.3 = (bf16[128,1024]{1,0:T(8,128)(2,1)}, bf16[128,1024]{1,0:T(8,128)(2,1)S(1)}, u32[]{:S(2)}, u32[]{:S(2)}) collective-permute-start(bf16[128,1024]{1,0:T(8,128)(2,1)} %get-tuple-element.22), channel_id=1, source_target_pairs={{0,256},{257,1},{1,384},{256,129},{384,128},{129,385},{385,0},{128... | collective-permute-start | bytes 786440 | tf_op jit(solution)/shard_map/ppermute | solution.py:228
  109.7 5.6 %shard_map.111 = (bf16[128,1024]{1,0:T(8,128)(2,1)}, bf16[128,1024]{1,0:T(8,128)(2,1)}) custom-call(s32[2]{0:T(128)} %get-tuple-element.23.order_ref, bf16[4,128,1024]{2,1,0:T(8,128)(2,1)} %copy-done.4, bf16[1024,2048]{1,0:T(8,128)(2,1)} %all-gather.2.cloned.1.call-done.k_ref.v_ref, bf16[1024,2048]{1,0:T(8,128)(2,1)} %all-gather.2.cloned.1.call-done.k_ref.v_ref, ...), custom_call_target="tpu_custom_call" | custom-call | flops 1073741824 | bytes 5242880 | tf_op jit(solution)/shard_map/pallas_call | solution.py:63
  115.4 1.9 %collective-permute-start.4 = (bf16[128,1024]{1,0:T(8,128)(2,1)}, bf16[128,1024]{1,0:T(8,128)(2,1)S(1)}, u32[]{:S(2)}, u32[]{:S(2)}) collective-permute-start(bf16[128,1024]{1,0:T(8,128)(2,1)} %get-tuple-element.24), channel_id=1, source_target_pairs={{0,384},{257,129},{1,128},{256,385},{384,0},{129,257},{385,256},{1... | collective-permute-start | bytes 786440 | tf_op jit(solution)/shard_map/ppermute | solution.py:228
  117.3 5.9 %collective-permute-start.5 = (bf16[128,1024]{1,0:T(8,128)(2,1)}, bf16[128,1024]{1,0:T(8,128)(2,1)S(1)}, u32[]{:S(2)}, u32[]{:S(2)}) collective-permute-start(bf16[128,1024]{1,0:T(8,128)(2,1)} %get-tuple-element.25), channel_id=1, source_target_pairs={{0,128},{257,385},{1,0},{256,257},{384,256},{129,1},{385,384},{128... | collective-permute-start | bytes 786440 | tf_op jit(solution)/shard_map/ppermute | solution.py:228
  123.2 7.7 %collective-permute-done.3.c_ref = bf16[128,1024]{1,0:T(8,128)(2,1)S(1)} collective-permute-done((bf16[128,1024]{1,0:T(8,128)(2,1)}, bf16[128,1024]{1,0:T(8,128)(2,1)S(1)}, u32[]{:S(2)}, u32[]{:S(2)}) %collective-permute-start.3) | collective-permute-done | bytes 262176 | tf_op jit(solution)/shard_map/ppermute | solution.py:228
  130.9 1.6 %collective-permute-done.4.b_ref = bf16[128,1024]{1,0:T(8,128)(2,1)S(1)} collective-permute-done((bf16[128,1024]{1,0:T(8,128)(2,1)}, bf16[128,1024]{1,0:T(8,128)(2,1)S(1)}, u32[]{:S(2)}, u32[]{:S(2)}) %collective-permute-start.4) | collective-permute-done | bytes 262176 | tf_op jit(solution)/shard_map/ppermute | solution.py:228
  132.5 1.9 %collective-permute-done.5.a_ref = bf16[128,1024]{1,0:T(8,128)(2,1)S(1)} collective-permute-done((bf16[128,1024]{1,0:T(8,128)(2,1)}, bf16[128,1024]{1,0:T(8,128)(2,1)S(1)}, u32[]{:S(2)}, u32[]{:S(2)}) %collective-permute-start.5) | collective-permute-done | bytes 262176 | tf_op jit(solution)/shard_map/ppermute | solution.py:228
  134.5 1.4 shard_map.112
  (53 shorter events, 5.4 us)
Async XLA Ops:
  6.5 1.4 copy-start
  6.5 30.6 %copy-start.6 = (s32[1,2048]{1,0:T(1,128)S(1)}, s32[1,2048]{1,0:T(1,128)}, u32[]{:S(2)}) copy-start(s32[1,2048]{1,0:T(1,128)} %param.17) | copy-start | bytes 24580
  6.5 33.7 %copy-start.5 = (bf16[1,128,2048]{2,1,0:T(8,128)(2,1)S(1)}, bf16[1,128,2048]{2,1,0:T(8,128)(2,1)}, u32[]{:S(2)}) copy-start(bf16[1,128,2048]{2,1,0:T(8,128)(2,1)} %param.11) | copy-start | bytes 1572868
  6.5 87.9 %all-gather.2.cloned.1.call-start = ((), (), s32[]{:S(2)}) async-start(), calls=%async_computation.2 | async-start | bytes 4718592 | tf_op jit(solution)/shard_map/all_gather | solution.py:189
  37.1 16.0 %collective-permute-start = (s32[2049]{0:T(1024)S(1)}, s32[2049]{0:T(1024)S(1)}, u32[]{:S(2)}, u32[]{:S(2)}) collective-permute-start(s32[2049]{0:T(1024)S(1)} %pad_add_fusion), channel_id=1, source_target_pairs={{0,1},{1,0},{2,3},{3,2},{4,5},{5,4},{6,7},{7,6},{8,9},{9,8},{10,11... | collective-permute-start | bytes 24596 | tf_op jit(solution)/shard_map/ppermute | solution.py:144
  40.3 3.4 %collective-permute-start.1 = (bf16[128,1024]{1,0:T(8,128)(2,1)S(1)}, bf16[128,1024]{1,0:T(8,128)(2,1)S(1)}, u32[]{:S(2)}, u32[]{:S(2)}) collective-permute-start(bf16[128,1024]{1,0:T(8,128)(2,1)S(1)} %dynamic-slice_bitcast_fusion), channel_id=1, source_target_pairs={{0,1},{1,0},{2,3},{3,2},{4,5},{5,4},{6,7},{7,6},{8,9},{9,8},{10,11... | collective-permute-start | bytes 786440 | tf_op jit(solution)/shard_map/ppermute | solution.py:144
  42.2 13.6 %copy-start.7 = (f32[128,16]{0,1:T(8,128)S(1)}, f32[128,16]{0,1:T(8,128)}, u32[]{:S(2)}) copy-start(f32[128,16]{0,1:T(8,128)} %param.18) | copy-start | bytes 24580
  45.0 28.7 %all-to-all-start = ((bf16[4,128,1024]{2,1,0:T(8,128)(2,1)}), bf16[4,128,1024]{2,1,0:T(8,128)(2,1)S(1)}, u32[]{:S(2)}, u32[]{:S(2)}) async-start(bf16[4,128,1024]{2,1,0:T(8,128)(2,1)} %pad_maximum_fusion), calls=%async_computation | async-start | bytes 2097152 | tf_op jit(solution)/shard_map/all_to_all | solution.py:197
  73.7 20.8 %copy-start.4 = (bf16[4,128,1024]{2,1,0:T(8,128)(2,1)}, bf16[4,128,1024]{2,1,0:T(8,128)(2,1)S(1)}, u32[]{:S(2)}) copy-start(bf16[4,128,1024]{2,1,0:T(8,128)(2,1)S(1)} %all-to-all-done.q_ref) | copy-start | bytes 3145732
  100.0 34.5 %copy-start.1 = (f32[128,2048]{1,0:T(8,128)S(1)}, f32[128,2048]{1,0:T(8,128)}, u32[]{:S(2)}) copy-start(f32[128,2048]{1,0:T(8,128)} %shard_map.109.base_ref) | copy-start | bytes 3145732
  100.0 34.5 %copy-start.2 = (bf16[1,128,2048]{2,1,0:T(8,128)(2,1)S(1)}, bf16[1,128,2048]{2,1,0:T(8,128)(2,1)}, u32[]{:S(2)}) copy-start(bf16[1,128,2048]{2,1,0:T(8,128)(2,1)} %param.13) | copy-start | bytes 1572868
  100.0 34.5 %copy-start.3 = (f32[2048]{0:T(1024)S(1)}, f32[2048]{0:T(1024)}, u32[]{:S(2)}) copy-start(f32[2048]{0:T(1024)} %param.20) | copy-start | bytes 24580
  100.0 23.2 %collective-permute-start.2 = (bf16[128,1024]{1,0:T(8,128)(2,1)}, bf16[128,1024]{1,0:T(8,128)(2,1)S(1)}, u32[]{:S(2)}, u32[]{:S(2)}) collective-permute-start(bf16[128,1024]{1,0:T(8,128)(2,1)} %get-tuple-element.21), channel_id=1, source_target_pairs={{0,0},{257,257},{1,256},{256,1},{384,384},{129,129},{385,128},{128... | collective-permute-start | bytes 786440 | tf_op jit(solution)/shard_map/ppermute | solution.py:228
  107.8 23.1 %collective-permute-start.3 = (bf16[128,1024]{1,0:T(8,128)(2,1)}, bf16[128,1024]{1,0:T(8,128)(2,1)S(1)}, u32[]{:S(2)}, u32[]{:S(2)}) collective-permute-start(bf16[128,1024]{1,0:T(8,128)(2,1)} %get-tuple-element.22), channel_id=1, source_target_pairs={{0,256},{257,1},{1,384},{256,129},{384,128},{129,385},{385,0},{128... | collective-permute-start | bytes 786440 | tf_op jit(solution)/shard_map/ppermute | solution.py:228
  115.4 17.2 %collective-permute-start.4 = (bf16[128,1024]{1,0:T(8,128)(2,1)}, bf16[128,1024]{1,0:T(8,128)(2,1)S(1)}, u32[]{:S(2)}, u32[]{:S(2)}) collective-permute-start(bf16[128,1024]{1,0:T(8,128)(2,1)} %get-tuple-element.24), channel_id=1, source_target_pairs={{0,384},{257,129},{1,128},{256,385},{384,0},{129,257},{385,256},{1... | collective-permute-start | bytes 786440 | tf_op jit(solution)/shard_map/ppermute | solution.py:228
  117.3 17.2 %collective-permute-start.5 = (bf16[128,1024]{1,0:T(8,128)(2,1)}, bf16[128,1024]{1,0:T(8,128)(2,1)S(1)}, u32[]{:S(2)}, u32[]{:S(2)}) collective-permute-start(bf16[128,1024]{1,0:T(8,128)(2,1)} %get-tuple-element.25), channel_id=1, source_target_pairs={{0,128},{257,385},{1,0},{256,257},{384,256},{129,1},{385,384},{128... | collective-permute-start | bytes 786440 | tf_op jit(solution)/shard_map/ppermute | solution.py:228
Sparse Core Ops, SparseCore 0:
  36.6 57.8 all-gather.1

commit v12 on v11

--- a/solution.py
+++ b/solution.py
@@ -221,10 +221,9 @@
     base = own_term(queries, cand_kv[0], self_bias)
     order = send_order()[lax.axis_index(Y + ("core",))]
     bias, mask, base, order = lax.optimization_barrier((bias, mask, base, order))
-    far = attend(order[2:], spread, history, bias, mask, PER_STEP)
-    *far, rest = lax.optimization_barrier((*far, order[:2]))
-    near = attend(rest, spread, history, bias, mask, PER_STEP)
-    partial = [*near, *far]
+    (last,) = attend(order[3:], spread, history, bias, mask, PER_STEP)
+    last, rest = lax.optimization_barrier((last, order[:3]))
+    partial = [*attend(rest, spread, history, bias, mask, PER_STEP), last]
     parts = [lax.ppermute(partial[s], Y + ("core",), send_pairs(s)) for s in range(4)]
     flag = ((core == 0) == (core == side)).astype(jnp.int32)
     return finish(flag, parts, base, cand_gate[0], norm_gain)[None]

time: 143 us -> 147 us (1.028)
  waiting for transfers between devices: 49.5 us -> 53.4 us
    ppermute x4, waiting for transfers between devices: 11.3 us -> 15.2 us  [per_device(): lax.ppermute(partial[s], Y + ('core',), send_pairs(s))]
  transfers between devices with their start and end apart: 8 -> 8, of which waited for: 6 -> 7; matrix products, arithmetic and copies ran while one was open for 5% -> 4% of each run, Pallas kernels for 7% -> 3%
where the time goes in v12:
time: 147 us
  waiting for transfers between devices  53.4 us (36%)
  blocking collectives  25.8 us (18%)
  starting transfers between devices  25.4 us (17%)
  Pallas kernels  17.3 us (12%)
  between operations  14.4 us (10%)
  local copies, waits for them, and re-layouts  6.5 us (4%)
  other arithmetic  3.42 us (2%)
    all_to_all x1, blocking collectives, per_device(): incoming = lax.all_to_all(outgoing, ('yh0',) + GROUP, 0, 0, tiled=True)  25.8 us
    all_gather x1, waiting for transfers between devices, per_device(): history = lax.all_gather(pieces, 'z', tiled=True)  20.8 us
    ppermute x4, starting transfers between devices, per_device(): lax.ppermute(partial[s], Y + ('core',), send_pairs(s))  16.8 us
    all_to_all x1, waiting for transfers between devices, per_device(): lax.all_to_all(jnp.stack([first, second, second, first]), Y, 0, 0, tiled=...  16.1 us
    ppermute x4, waiting for transfers between devices, per_device(): lax.ppermute(partial[s], Y + ('core',), send_pairs(s))  15.2 us
    pallas_call x2, Pallas kernels, attend(): pl.pallas_call(attend_kernel, grid=(steps,), in_specs=[pl.BlockSpec(memor...  12.1 us
    ppermute x2, starting transfers between devices, swapped(): return lax.ppermute(value, 'core', [(0, 1), (1, 0)])  5.06 us
    pallas_call x1, Pallas kernels, own_term(): pl.pallas_call(own_kernel, grid=(rows // block,), in_specs=[pl.BlockSpec(...  3.82 us
  transfers between devices with their start and end apart: 8, of which 7 were waited for; matrix products, arithmetic and copies ran while one was open for 4% of the time, Pallas kernels for 3%

profile of v12, /device:TPU:1, one launch (start us, length us, event | category | flops | bytes accessed | tf_op | source)
XLA Modules:
  0.0 146.9 jit_solution(18435071596206057938)
XLA Ops:
  6.6 0.8 and_select_fusion
  8.0 1.0 gather_fusion
  9.7 25.8 %all_to_all.10 = bf16[32,4,2048]{2,1,0:T(4,128)(2,1)S(1)} all-to-all(bf16[32,4,2048]{2,1,0:T(4,128)(2,1)S(1)} %bitcast.49), channel_id=1, replica_groups=mesh['yh1'=2,'yh0'=2,'z'=8,'x'=4,'ylo'=2,'core'=2] {'yh0','x','ylo','core'}, dimensions={0} | all-to-all | bytes 1048576 | tf_op jit(solution)/shard_map/all_to_all | solution.py:187
  35.5 0.9 reshape.140
  37.1 3.1 %collective-permute-start = (s32[2049]{0:T(1024)S(1)}, s32[2049]{0:T(1024)S(1)}, u32[]{:S(2)}, u32[]{:S(2)}) collective-permute-start(s32[2049]{0:T(1024)S(1)} %pad_add_fusion), channel_id=1, source_target_pairs={{0,1},{1,0},{2,3},{3,2},{4,5},{5,4},{6,7},{7,6},{8,9},{9,8},{10,11... | collective-permute-start | bytes 24596 | tf_op jit(solution)/shard_map/ppermute | solution.py:144
  40.3 1.9 %collective-permute-start.1 = (bf16[128,1024]{1,0:T(8,128)(2,1)S(1)}, bf16[128,1024]{1,0:T(8,128)(2,1)S(1)}, u32[]{:S(2)}, u32[]{:S(2)}) collective-permute-start(bf16[128,1024]{1,0:T(8,128)(2,1)S(1)} %dynamic-slice_bitcast_fusion), channel_id=1, source_target_pairs={{0,1},{1,0},{2,3},{3,2},{4,5},{5,4},{6,7},{7,6},{8,9},{9,8},{10,11... | collective-permute-start | bytes 786440 | tf_op jit(solution)/shard_map/ppermute | solution.py:144
  42.4 1.3 collective-permute-done.1
  43.9 1.1 pad_maximum_fusion
  45.0 3.5 %all-to-all-start = ((bf16[4,128,1024]{2,1,0:T(8,128)(2,1)}), bf16[4,128,1024]{2,1,0:T(8,128)(2,1)S(1)}, u32[]{:S(2)}, u32[]{:S(2)}) async-start(bf16[4,128,1024]{2,1,0:T(8,128)(2,1)} %pad_maximum_fusion), calls=%async_computation | async-start | bytes 2097152 | tf_op jit(solution)/shard_map/all_to_all | solution.py:197
  49.3 3.8 %shard_map.109.base_ref = f32[128,2048]{1,0:T(8,128)} custom-call(bf16[128,2048]{1,0:T(8,128)(2,1)} %bitcast.47, bf16[128,4096]{1,0:T(8,128)(2,1)} %bitcast.50, f32[1,16]{1,0:T(1,128)} %bitcast.56), custom_call_target="tpu_custom_call" | custom-call | tf_op jit(solution)/shard_map/pallas_call | solution.py:100
  53.7 0.7 fusion.6
  54.4 0.7 reshape.142.mask_ref
  57.5 16.1 %all-to-all-done.q_ref = bf16[4,128,1024]{2,1,0:T(8,128)(2,1)S(1)} async-done(((bf16[4,128,1024]{2,1,0:T(8,128)(2,1)}), bf16[4,128,1024]{2,1,0:T(8,128)(2,1)S(1)}, u32[]{:S(2)}, u32[]{:S(2)}) %all-to-all-start) | async-done | bytes 1048608 | tf_op jit(solution)/shard_map/all_to_all | solution.py:197
  73.7 20.8 %all-gather.2.cloned.1.call-done.k_ref.v_ref = bf16[1024,2048]{1,0:T(8,128)(2,1)} async-done(((bf16[128,2048]{1,0:T(8,128)(2,1)}), bf16[1024,2048]{1,0:T(8,128)(2,1)}) %all-gather.2.cloned.1.call-update) | async-done | bytes 4194320 | tf_op jit(solution)/shard_map/all_gather | solution.py:189
  94.4 5.6 %shard_map.110 = bf16[128,1024]{1,0:T(8,128)(2,1)} custom-call(s32[1]{0:T(128)} %slice.26.order_ref, bf16[4,128,1024]{2,1,0:T(8,128)(2,1)} %copy-done.4, bf16[1024,2048]{1,0:T(8,128)(2,1)} %all-gather.2.cloned.1.call-done.k_ref.v_ref, bf16[1024,2048]{1,0:T(8,128)(2,1)} %all-gather.2.cloned.1.call-done.k_ref.v_ref, f32[8,1,1024]{2,1,0:T(1,128)} %broadcast_in_dim.42.bias_ref, ...), custom_call_target="tpu_custom_call" | custom-call | flops 536870912 | bytes 4718592 | tf_op jit(solution)/shard_map/pallas_call | solution.py:63
  100.0 6.6 %shard_map.111 = (bf16[128,1024]{1,0:T(8,128)(2,1)}, bf16[128,1024]{1,0:T(8,128)(2,1)}, bf16[128,1024]{1,0:T(8,128)(2,1)}) custom-call(s32[3]{0:T(128)} %bitcast.55, bf16[4,128,1024]{2,1,0:T(8,128)(2,1)} %copy-done.4, bf16[1024,2048]{1,0:T(8,128)(2,1)} %all-gather.2.cloned.1.call-done.k_ref.v_ref, ...), custom_call_target="tpu_custom_call" | custom-call | flops 1610612736 | bytes 5767168 | tf_op jit(solution)/shard_map/pallas_call | solution.py:63
  106.6 5.9 %collective-permute-start.3 = (bf16[128,1024]{1,0:T(8,128)(2,1)}, bf16[128,1024]{1,0:T(8,128)(2,1)S(1)}, u32[]{:S(2)}, u32[]{:S(2)}) collective-permute-start(bf16[128,1024]{1,0:T(8,128)(2,1)} %get-tuple-element.19), channel_id=1, source_target_pairs={{0,256},{257,1},{1,384},{256,129},{384,128},{129,385},{385,0},{128... | collective-permute-start | bytes 786440 | tf_op jit(solution)/shard_map/ppermute | solution.py:227
  112.5 3.7 %collective-permute-start.4 = (bf16[128,1024]{1,0:T(8,128)(2,1)}, bf16[128,1024]{1,0:T(8,128)(2,1)S(1)}, u32[]{:S(2)}, u32[]{:S(2)}) collective-permute-start(bf16[128,1024]{1,0:T(8,128)(2,1)} %get-tuple-element.20), channel_id=1, source_target_pairs={{0,384},{257,129},{1,128},{256,385},{384,0},{129,257},{385,256},{1... | collective-permute-start | bytes 786440 | tf_op jit(solution)/shard_map/ppermute | solution.py:227
  116.2 2.8 %collective-permute-start.5 = (bf16[128,1024]{1,0:T(8,128)(2,1)}, bf16[128,1024]{1,0:T(8,128)(2,1)S(1)}, u32[]{:S(2)}, u32[]{:S(2)}) collective-permute-start(bf16[128,1024]{1,0:T(8,128)(2,1)} %get-tuple-element.21), channel_id=1, source_target_pairs={{0,128},{257,385},{1,0},{256,257},{384,256},{129,1},{385,384},{128... | collective-permute-start | bytes 786440 | tf_op jit(solution)/shard_map/ppermute | solution.py:227
  119.0 4.5 %collective-permute-start.2 = (bf16[128,1024]{1,0:T(8,128)(2,1)S(1)}, bf16[128,1024]{1,0:T(8,128)(2,1)S(1)}, u32[]{:S(2)}, u32[]{:S(2)}) collective-permute-start(bf16[128,1024]{1,0:T(8,128)(2,1)S(1)} %copy-done.6), channel_id=1, source_target_pairs={{0,0},{257,257},{1,256},{256,1},{384,384},{129,129},{385,128},{128... | collective-permute-start | bytes 786440 | tf_op jit(solution)/shard_map/ppermute | solution.py:227
  123.5 10.7 %collective-permute-done.3.c_ref = bf16[128,1024]{1,0:T(8,128)(2,1)S(1)} collective-permute-done((bf16[128,1024]{1,0:T(8,128)(2,1)}, bf16[128,1024]{1,0:T(8,128)(2,1)S(1)}, u32[]{:S(2)}, u32[]{:S(2)}) %collective-permute-start.3) | collective-permute-done | bytes 262176 | tf_op jit(solution)/shard_map/ppermute | solution.py:227
  134.2 2.6 %collective-permute-done.4.b_ref = bf16[128,1024]{1,0:T(8,128)(2,1)S(1)} collective-permute-done((bf16[128,1024]{1,0:T(8,128)(2,1)}, bf16[128,1024]{1,0:T(8,128)(2,1)S(1)}, u32[]{:S(2)}, u32[]{:S(2)}) %collective-permute-start.4) | collective-permute-done | bytes 262176 | tf_op jit(solution)/shard_map/ppermute | solution.py:227
  136.9 1.8 %collective-permute-done.2.d_ref = bf16[128,1024]{1,0:T(8,128)(2,1)S(1)} collective-permute-done((bf16[128,1024]{1,0:T(8,128)(2,1)S(1)}, bf16[128,1024]{1,0:T(8,128)(2,1)S(1)}, u32[]{:S(2)}, u32[]{:S(2)}) %collective-permute-start.2) | collective-permute-done | bytes 262176 | tf_op jit(solution)/shard_map/ppermute | solution.py:227
  138.6 1.4 shard_map.112
  (57 shorter events, 5.5 us)
Async XLA Ops:
  6.5 1.4 copy-start
  6.5 30.5 %copy-start.7 = (s32[1,2048]{1,0:T(1,128)S(1)}, s32[1,2048]{1,0:T(1,128)}, u32[]{:S(2)}) copy-start(s32[1,2048]{1,0:T(1,128)} %param.17) | copy-start | bytes 24580
  6.5 33.7 %copy-start.5 = (bf16[1,128,2048]{2,1,0:T(8,128)(2,1)S(1)}, bf16[1,128,2048]{2,1,0:T(8,128)(2,1)}, u32[]{:S(2)}) copy-start(bf16[1,128,2048]{2,1,0:T(8,128)(2,1)} %param.11) | copy-start | bytes 1572868
  6.5 87.9 %all-gather.2.cloned.1.call-start = ((), (), s32[]{:S(2)}) async-start(), calls=%async_computation.2 | async-start | bytes 4718592 | tf_op jit(solution)/shard_map/all_gather | solution.py:189
  37.1 16.0 %collective-permute-start = (s32[2049]{0:T(1024)S(1)}, s32[2049]{0:T(1024)S(1)}, u32[]{:S(2)}, u32[]{:S(2)}) collective-permute-start(s32[2049]{0:T(1024)S(1)} %pad_add_fusion), channel_id=1, source_target_pairs={{0,1},{1,0},{2,3},{3,2},{4,5},{5,4},{6,7},{7,6},{8,9},{9,8},{10,11... | collective-permute-start | bytes 24596 | tf_op jit(solution)/shard_map/ppermute | solution.py:144
  40.3 3.4 %collective-permute-start.1 = (bf16[128,1024]{1,0:T(8,128)(2,1)S(1)}, bf16[128,1024]{1,0:T(8,128)(2,1)S(1)}, u32[]{:S(2)}, u32[]{:S(2)}) collective-permute-start(bf16[128,1024]{1,0:T(8,128)(2,1)S(1)} %dynamic-slice_bitcast_fusion), channel_id=1, source_target_pairs={{0,1},{1,0},{2,3},{3,2},{4,5},{5,4},{6,7},{7,6},{8,9},{9,8},{10,11... | collective-permute-start | bytes 786440 | tf_op jit(solution)/shard_map/ppermute | solution.py:144
  42.3 13.6 %copy-start.9 = (f32[128,16]{0,1:T(8,128)S(1)}, f32[128,16]{0,1:T(8,128)}, u32[]{:S(2)}) copy-start(f32[128,16]{0,1:T(8,128)} %param.18) | copy-start | bytes 24580
  45.0 28.7 %all-to-all-start = ((bf16[4,128,1024]{2,1,0:T(8,128)(2,1)}), bf16[4,128,1024]{2,1,0:T(8,128)(2,1)S(1)}, u32[]{:S(2)}, u32[]{:S(2)}) async-start(bf16[4,128,1024]{2,1,0:T(8,128)(2,1)} %pad_maximum_fusion), calls=%async_computation | async-start | bytes 2097152 | tf_op jit(solution)/shard_map/all_to_all | solution.py:197
  49.3 50.7 %copy-start.8 = (s32[4]{0:T(128)}, s32[4]{0:T(128)S(1)}, u32[]{:S(2)}) copy-start(s32[4]{0:T(128)S(1)} %fusion.16) | copy-start | bytes 52
  73.7 20.8 %copy-start.4 = (bf16[4,128,1024]{2,1,0:T(8,128)(2,1)}, bf16[4,128,1024]{2,1,0:T(8,128)(2,1)S(1)}, u32[]{:S(2)}) copy-start(bf16[4,128,1024]{2,1,0:T(8,128)(2,1)S(1)} %all-to-all-done.q_ref) | copy-start | bytes 3145732
  100.0 19.0 %copy-start.6 = (bf16[128,1024]{1,0:T(8,128)(2,1)S(1)}, bf16[128,1024]{1,0:T(8,128)(2,1)}, u32[]{:S(2)}) copy-start(bf16[128,1024]{1,0:T(8,128)(2,1)} %shard_map.110) | copy-start | bytes 786436
  100.0 38.6 %copy-start.1 = (f32[128,2048]{1,0:T(8,128)S(1)}, f32[128,2048]{1,0:T(8,128)}, u32[]{:S(2)}) copy-start(f32[128,2048]{1,0:T(8,128)} %shard_map.109.base_ref) | copy-start | bytes 3145732
  100.0 38.6 %copy-start.2 = (bf16[1,128,2048]{2,1,0:T(8,128)(2,1)S(1)}, bf16[1,128,2048]{2,1,0:T(8,128)(2,1)}, u32[]{:S(2)}) copy-start(bf16[1,128,2048]{2,1,0:T(8,128)(2,1)} %param.13) | copy-start | bytes 1572868
  100.0 38.6 %copy-start.3 = (f32[2048]{0:T(1024)S(1)}, f32[2048]{0:T(1024)}, u32[]{:S(2)}) copy-start(f32[2048]{0:T(1024)} %param.20) | copy-start | bytes 24580
  106.6 27.6 %collective-permute-start.3 = (bf16[128,1024]{1,0:T(8,128)(2,1)}, bf16[128,1024]{1,0:T(8,128)(2,1)S(1)}, u32[]{:S(2)}, u32[]{:S(2)}) collective-permute-start(bf16[128,1024]{1,0:T(8,128)(2,1)} %get-tuple-element.19), channel_id=1, source_target_pairs={{0,256},{257,1},{1,384},{256,129},{384,128},{129,385},{385,0},{128... | collective-permute-start | bytes 786440 | tf_op jit(solution)/shard_map/ppermute | solution.py:227
  112.5 24.3 %collective-permute-start.4 = (bf16[128,1024]{1,0:T(8,128)(2,1)}, bf16[128,1024]{1,0:T(8,128)(2,1)S(1)}, u32[]{:S(2)}, u32[]{:S(2)}) collective-permute-start(bf16[128,1024]{1,0:T(8,128)(2,1)} %get-tuple-element.20), channel_id=1, source_target_pairs={{0,384},{257,129},{1,128},{256,385},{384,0},{129,257},{385,256},{1... | collective-permute-start | bytes 786440 | tf_op jit(solution)/shard_map/ppermute | solution.py:227
  116.2 20.7 %collective-permute-start.5 = (bf16[128,1024]{1,0:T(8,128)(2,1)}, bf16[128,1024]{1,0:T(8,128)(2,1)S(1)}, u32[]{:S(2)}, u32[]{:S(2)}) collective-permute-start(bf16[128,1024]{1,0:T(8,128)(2,1)} %get-tuple-element.21), channel_id=1, source_target_pairs={{0,128},{257,385},{1,0},{256,257},{384,256},{129,1},{385,384},{128... | collective-permute-start | bytes 786440 | tf_op jit(solution)/shard_map/ppermute | solution.py:227
  119.0 19.6 %collective-permute-start.2 = (bf16[128,1024]{1,0:T(8,128)(2,1)S(1)}, bf16[128,1024]{1,0:T(8,128)(2,1)S(1)}, u32[]{:S(2)}, u32[]{:S(2)}) collective-permute-start(bf16[128,1024]{1,0:T(8,128)(2,1)S(1)} %copy-done.6), channel_id=1, source_target_pairs={{0,0},{257,257},{1,256},{256,1},{384,384},{129,129},{385,128},{128... | collective-permute-start | bytes 786440 | tf_op jit(solution)/shard_map/ppermute | solution.py:227
Sparse Core Ops, SparseCore 0:
  36.6 57.8 all-gather.1

commit v13 on v11

--- a/solution.py
+++ b/solution.py
@@ -80,6 +80,38 @@
             transcendentals=count * rows * positions * full // HEAD_DIM,
         ),
     )(order, queries, history, history, bias, mask)
+
+
+def attend_whole_kernel(order_ref, q_ref, history_ref, bias_ref, mask_ref, *out_refs):
+    rows, width = out_refs[0].shape
+    attend_kernel(
+        order_ref,
+        q_ref,
+        history_ref.at[:, :width],
+        history_ref.at[:, width:],
+        bias_ref,
+        mask_ref,
+        *out_refs,
+    )
+
+
+def attend_whole(order, queries, history, bias, mask):
+    _, rows, full = queries.shape
+    positions = history.shape[0]
+    count = order.shape[0]
+    vmem = pl.BlockSpec(memory_space=pltpu.VMEM)
+    return pl.pallas_call(
+        attend_whole_kernel,
+        in_specs=[pl.BlockSpec(memory_space=pltpu.SMEM)] + [vmem] * 4,
+        out_specs=[vmem] * count,
+        out_shape=[jax.ShapeDtypeStruct((rows, full), jnp.bfloat16)] * count,
+        compiler_params=pltpu.CompilerParams(vmem_limit_bytes=24 * 1024 * 1024),
+        cost_estimate=pl.CostEstimate(
+            flops=4 * count * rows * positions * full,
+            bytes_accessed=4 * positions * full + 4 * count * rows * full,
+            transcendentals=count * rows * positions * full // HEAD_DIM,
+        ),
+    )(order, queries, history, bias, mask)
 
 
 def own_kernel(q_ref, own_ref, self_bias_ref, out_ref):
@@ -220,10 +252,11 @@
     mask = (place.reshape(1, -1) < about[-1]).astype(jnp.float32)
     base = own_term(queries, cand_kv[0], self_bias)
     order = send_order()[lax.axis_index(Y + ("core",))]
+    near_queries = jnp.stack([spread[order[0]], spread[order[1]]])
     bias, mask, base, order = lax.optimization_barrier((bias, mask, base, order))
     far = attend(order[2:], spread, history, bias, mask, PER_STEP)
-    *far, rest = lax.optimization_barrier((*far, order[:2]))
-    near = attend(rest, spread, history, bias, mask, PER_STEP)
+    *far, rest = lax.optimization_barrier((*far, jnp.arange(2, dtype=jnp.int32)))
+    near = attend_whole(rest, near_queries, history, bias, mask)
     partial = [*near, *far]
     parts = [lax.ppermute(partial[s], Y + ("core",), send_pairs(s)) for s in range(4)]
     flag = ((core == 0) == (core == side)).astype(jnp.int32)

time: 143 us -> 142 us (level)
  waiting for transfers between devices: 49.5 us -> 44.6 us
  between operations: 14.3 us -> 18.3 us
    pallas_call x2 -> x1, Pallas kernels: 11.2 us -> 5.73 us  [attend(): pl.pallas_call(attend_kernel, grid=(steps,), in_specs=[pl.BlockSpec(memor...]
    pallas_call x0 -> x1, Pallas kernels: none -> 4.2 us  [attend_whole(): pl.pallas_call(attend_whole_kernel, in_specs=[pl.BlockSpec(memory_space=p...]
    all_to_all x1, waiting for transfers between devices: 16.2 us -> 12.9 us  [per_device(): lax.all_to_all(jnp.stack([first, second, second, first]), Y, 0, 0, tiled=...]
  transfers between devices with their start and end apart: 8 -> 8, of which waited for: 6 -> 5; matrix products, arithmetic and copies ran while one was open for 5% -> 5% of each run, Pallas kernels for 7% -> 6%
where the time goes in v13:
time: 142 us; the launch traced here: 141 us
  waiting for transfers between devices  44.6 us (31%)
  starting transfers between devices  26.1 us (18%)
  blocking collectives  25.8 us (18%)
  between operations  18.3 us (13%)
  Pallas kernels  15.2 us (11%)
  local copies, waits for them, and re-layouts  7.11 us (5%)
  other arithmetic  3.45 us (2%)
    all_to_all x1, blocking collectives, per_device(): incoming = lax.all_to_all(outgoing, ('yh0',) + GROUP, 0, 0, tiled=True)  25.8 us
    all_gather x1, waiting for transfers between devices, per_device(): history = lax.all_gather(pieces, 'z', tiled=True)  20.7 us
    ppermute x4, starting transfers between devices, per_device(): lax.ppermute(partial[s], Y + ('core',), send_pairs(s))  17.5 us
    all_to_all x1, waiting for transfers between devices, per_device(): lax.all_to_all(jnp.stack([first, second, second, first]), Y, 0, 0, tiled=...  12.9 us
    ppermute x4, waiting for transfers between devices, per_device(): lax.ppermute(partial[s], Y + ('core',), send_pairs(s))  10.9 us
    pallas_call x1, Pallas kernels, attend(): pl.pallas_call(attend_kernel, grid=(steps,), in_specs=[pl.BlockSpec(memor...  5.73 us
    ppermute x2, starting transfers between devices, swapped(): return lax.ppermute(value, 'core', [(0, 1), (1, 0)])  5.06 us
    pallas_call x1, Pallas kernels, attend_whole(): pl.pallas_call(attend_whole_kernel, in_specs=[pl.BlockSpec(memory_space=p...  4.2 us
  transfers between devices with their start and end apart: 8, of which 5 were waited for; matrix products, arithmetic and copies ran while one was open for 5% of the time, Pallas kernels for 6%

profile of v13, /device:TPU:1, one launch (start us, length us, event | category | flops | bytes accessed | tf_op | source)
XLA Modules:
  0.0 141.2 jit_solution(10193374306182971569)
XLA Ops:
  6.6 0.8 and_select_fusion
  8.0 1.0 gather_fusion
  9.7 25.8 %all_to_all.10 = bf16[32,4,2048]{2,1,0:T(4,128)(2,1)S(1)} all-to-all(bf16[32,4,2048]{2,1,0:T(4,128)(2,1)S(1)} %bitcast.50), channel_id=1, replica_groups=mesh['yh1'=2,'yh0'=2,'z'=8,'x'=4,'ylo'=2,'core'=2] {'yh0','x','ylo','core'}, dimensions={0} | all-to-all | bytes 1048576 | tf_op jit(solution)/shard_map/all_to_all | solution.py:219
  35.5 0.9 reshape.144
  37.1 3.1 %collective-permute-start = (s32[2049]{0:T(1024)S(1)}, s32[2049]{0:T(1024)S(1)}, u32[]{:S(2)}, u32[]{:S(2)}) collective-permute-start(s32[2049]{0:T(1024)S(1)} %pad_add_fusion), channel_id=1, source_target_pairs={{0,1},{1,0},{2,3},{3,2},{4,5},{5,4},{6,7},{7,6},{8,9},{9,8},{10,11... | collective-permute-start | bytes 24596 | tf_op jit(solution)/shard_map/ppermute | solution.py:176
  40.3 1.9 %collective-permute-start.1 = (bf16[128,1024]{1,0:T(8,128)(2,1)S(1)}, bf16[128,1024]{1,0:T(8,128)(2,1)S(1)}, u32[]{:S(2)}, u32[]{:S(2)}) collective-permute-start(bf16[128,1024]{1,0:T(8,128)(2,1)S(1)} %dynamic-slice_bitcast_fusion), channel_id=1, source_target_pairs={{0,1},{1,0},{2,3},{3,2},{4,5},{5,4},{6,7},{7,6},{8,9},{9,8},{10,11... | collective-permute-start | bytes 786440 | tf_op jit(solution)/shard_map/ppermute | solution.py:176
  42.3 0.7 constant_dynamic-slice_fusion.2
  43.9 1.1 pad_maximum_fusion
  45.0 3.5 %all-to-all-start = ((bf16[4,128,1024]{2,1,0:T(8,128)(2,1)}), bf16[4,128,1024]{2,1,0:T(8,128)(2,1)S(1)}, u32[]{:S(2)}, u32[]{:S(2)}) async-start(bf16[4,128,1024]{2,1,0:T(8,128)(2,1)} %pad_maximum_fusion), calls=%async_computation | async-start | bytes 2097152 | tf_op jit(solution)/shard_map/all_to_all | solution.py:229
  52.5 3.9 %shard_map.109.base_ref = f32[128,2048]{1,0:T(8,128)} custom-call(bf16[128,2048]{1,0:T(8,128)(2,1)} %bitcast.48, bf16[128,4096]{1,0:T(8,128)(2,1)} %bitcast.51, f32[1,16]{1,0:T(1,128)} %bitcast.56), custom_call_target="tpu_custom_call" | custom-call | tf_op jit(solution)/shard_map/pallas_call | solution.py:132
  56.9 0.7 fusion.6
  57.6 0.7 reshape.146.mask_ref
  59.5 0.6 broadcast_in_dim.42.bias_ref
  60.7 12.9 %all-to-all-done.q_ref = bf16[4,128,1024]{2,1,0:T(8,128)(2,1)S(1)} async-done(((bf16[4,128,1024]{2,1,0:T(8,128)(2,1)}), bf16[4,128,1024]{2,1,0:T(8,128)(2,1)S(1)}, u32[]{:S(2)}, u32[]{:S(2)}) %all-to-all-start) | async-done | bytes 1048608 | tf_op jit(solution)/shard_map/all_to_all | solution.py:229
  73.7 20.7 %all-gather.2.cloned.1.call-done.k_ref.v_ref.history_ref = bf16[1024,2048]{1,0:T(8,128)(2,1)} async-done(((bf16[128,2048]{1,0:T(8,128)(2,1)}), bf16[1024,2048]{1,0:T(8,128)(2,1)}) %all-gather.2.cloned.1.call-update) | async-done | bytes 4194320 | tf_op jit(solution)/shard_map/all_gather | solution.py:221
  94.4 5.7 %shard_map.110 = (bf16[128,1024]{1,0:T(8,128)(2,1)}, bf16[128,1024]{1,0:T(8,128)(2,1)}) custom-call(s32[2]{0:T(128)} %slice.31.order_ref, bf16[4,128,1024]{2,1,0:T(8,128)(2,1)} %copy-done.7, bf16[1024,2048]{1,0:T(8,128)(2,1)} %all-gather.2.cloned.1.call-done.k_ref.v_ref.history_ref, bf16[1024,2048]{1,0:T(8,128)(2,1)} %all-gather.2.cloned.1.call-done.k_ref.v_ref.history_ref, ...), custom_call_target="tpu_custom_call" | custom-call | flops 1073741824 | bytes 5242880 | tf_op jit(solution)/shard_map/pallas_call | solution.py:63
  100.2 7.8 %collective-permute-start.2 = (bf16[128,1024]{1,0:T(8,128)(2,1)}, bf16[128,1024]{1,0:T(8,128)(2,1)S(1)}, u32[]{:S(2)}, u32[]{:S(2)}) collective-permute-start(bf16[128,1024]{1,0:T(8,128)(2,1)} %get-tuple-element.21), channel_id=1, source_target_pairs={{0,0},{257,257},{1,256},{256,1},{384,384},{129,129},{385,128},{128... | collective-permute-start | bytes 786440 | tf_op jit(solution)/shard_map/ppermute | solution.py:261
  108.0 1.9 %collective-permute-start.3 = (bf16[128,1024]{1,0:T(8,128)(2,1)}, bf16[128,1024]{1,0:T(8,128)(2,1)S(1)}, u32[]{:S(2)}, u32[]{:S(2)}) collective-permute-start(bf16[128,1024]{1,0:T(8,128)(2,1)} %get-tuple-element.22), channel_id=1, source_target_pairs={{0,256},{257,1},{1,384},{256,129},{384,128},{129,385},{385,0},{128... | collective-permute-start | bytes 786440 | tf_op jit(solution)/shard_map/ppermute | solution.py:261
  109.9 4.2 %shard_map.111 = (bf16[128,1024]{1,0:T(8,128)(2,1)S(1)}, bf16[128,1024]{1,0:T(8,128)(2,1)}) custom-call(s32[2]{0:T(128)S(1)} %iota.36.order_ref, bf16[2,128,1024]{2,1,0:T(8,128)(2,1)S(1)} %pad_maximum_fusion.1.q_ref, bf16[1024,2048]{1,0:T(8,128)(2,1)S(1)} %copy-done.1, f32[8,1,1024]{2,1,0:T(1,128)S(1)} %copy-done.4, f32[1,1024]{1,0:T(1,128)S(1)} %copy-done.5), custom_call_target="tpu_custom_call" | custom-call | flops 1073741824 | bytes 5242880 | tf_op jit(solution)/shard_map/pallas_call | solution.py:103
  114.1 1.9 %collective-permute-start.4 = (bf16[128,1024]{1,0:T(8,128)(2,1)}, bf16[128,1024]{1,0:T(8,128)(2,1)S(1)}, u32[]{:S(2)}, u32[]{:S(2)}) collective-permute-start(bf16[128,1024]{1,0:T(8,128)(2,1)} %get-tuple-element.24), channel_id=1, source_target_pairs={{0,384},{257,129},{1,128},{256,385},{384,0},{129,257},{385,256},{1... | collective-permute-start | bytes 786440 | tf_op jit(solution)/shard_map/ppermute | solution.py:261
  116.1 5.9 %collective-permute-start.5 = (bf16[128,1024]{1,0:T(8,128)(2,1)S(1)}, bf16[128,1024]{1,0:T(8,128)(2,1)S(1)}, u32[]{:S(2)}, u32[]{:S(2)}) collective-permute-start(bf16[128,1024]{1,0:T(8,128)(2,1)S(1)} %get-tuple-element.25), channel_id=1, source_target_pairs={{0,128},{257,385},{1,0},{256,257},{384,256},{129,1},{385,384},{128... | collective-permute-start | bytes 786440 | tf_op jit(solution)/shard_map/ppermute | solution.py:261
  122.0 9.1 %collective-permute-done.3.c_ref = bf16[128,1024]{1,0:T(8,128)(2,1)S(1)} collective-permute-done((bf16[128,1024]{1,0:T(8,128)(2,1)}, bf16[128,1024]{1,0:T(8,128)(2,1)S(1)}, u32[]{:S(2)}, u32[]{:S(2)}) %collective-permute-start.3) | collective-permute-done | bytes 262176 | tf_op jit(solution)/shard_map/ppermute | solution.py:261
  131.1 1.7 %collective-permute-done.4.b_ref = bf16[128,1024]{1,0:T(8,128)(2,1)S(1)} collective-permute-done((bf16[128,1024]{1,0:T(8,128)(2,1)}, bf16[128,1024]{1,0:T(8,128)(2,1)S(1)}, u32[]{:S(2)}, u32[]{:S(2)}) %collective-permute-start.4) | collective-permute-done | bytes 262176 | tf_op jit(solution)/shard_map/ppermute | solution.py:261
  132.9 1.4 shard_map.112
  (63 shorter events, 4.9 us)
Async XLA Ops:
  6.5 1.4 %copy-start = (bf16[16,1,4,4096]{3,2,1,0:T(4,128)(2,1)S(1)}, bf16[16,1,4,4096]{3,2,1,0:T(4,128)(2,1)}, u32[]{:S(2)}) copy-start(bf16[16,1,4,4096]{3,2,1,0:T(4,128)(2,1)} %param.14) | copy-start | bytes 1572868
  6.5 30.6 %copy-start.9 = (s32[1,2048]{1,0:T(1,128)S(1)}, s32[1,2048]{1,0:T(1,128)}, u32[]{:S(2)}) copy-start(s32[1,2048]{1,0:T(1,128)} %param.17) | copy-start | bytes 24580
  6.5 33.7 %copy-start.8 = (bf16[1,128,2048]{2,1,0:T(8,128)(2,1)S(1)}, bf16[1,128,2048]{2,1,0:T(8,128)(2,1)}, u32[]{:S(2)}) copy-start(bf16[1,128,2048]{2,1,0:T(8,128)(2,1)} %param.11) | copy-start | bytes 1572868
  6.5 87.9 %all-gather.2.cloned.1.call-start = ((), (), s32[]{:S(2)}) async-start(), calls=%async_computation.2 | async-start | bytes 4718592 | tf_op jit(solution)/shard_map/all_gather | solution.py:221
  37.1 19.2 %collective-permute-start = (s32[2049]{0:T(1024)S(1)}, s32[2049]{0:T(1024)S(1)}, u32[]{:S(2)}, u32[]{:S(2)}) collective-permute-start(s32[2049]{0:T(1024)S(1)} %pad_add_fusion), channel_id=1, source_target_pairs={{0,1},{1,0},{2,3},{3,2},{4,5},{5,4},{6,7},{7,6},{8,9},{9,8},{10,11... | collective-permute-start | bytes 24596 | tf_op jit(solution)/shard_map/ppermute | solution.py:176
  40.3 3.4 %collective-permute-start.1 = (bf16[128,1024]{1,0:T(8,128)(2,1)S(1)}, bf16[128,1024]{1,0:T(8,128)(2,1)S(1)}, u32[]{:S(2)}, u32[]{:S(2)}) collective-permute-start(bf16[128,1024]{1,0:T(8,128)(2,1)S(1)} %dynamic-slice_bitcast_fusion), channel_id=1, source_target_pairs={{0,1},{1,0},{2,3},{3,2},{4,5},{5,4},{6,7},{7,6},{8,9},{9,8},{10,11... | collective-permute-start | bytes 786440 | tf_op jit(solution)/shard_map/ppermute | solution.py:176
  42.2 16.8 %copy-start.10 = (f32[128,16]{0,1:T(8,128)S(1)}, f32[128,16]{0,1:T(8,128)}, u32[]{:S(2)}) copy-start(f32[128,16]{0,1:T(8,128)} %param.18) | copy-start | bytes 24580
  45.0 28.6 %all-to-all-start = ((bf16[4,128,1024]{2,1,0:T(8,128)(2,1)}), bf16[4,128,1024]{2,1,0:T(8,128)(2,1)S(1)}, u32[]{:S(2)}, u32[]{:S(2)}) async-start(bf16[4,128,1024]{2,1,0:T(8,128)(2,1)} %pad_maximum_fusion), calls=%async_computation | async-start | bytes 2097152 | tf_op jit(solution)/shard_map/all_to_all | solution.py:229
  73.6 20.8 %copy-start.7 = (bf16[4,128,1024]{2,1,0:T(8,128)(2,1)}, bf16[4,128,1024]{2,1,0:T(8,128)(2,1)S(1)}, u32[]{:S(2)}) copy-start(bf16[4,128,1024]{2,1,0:T(8,128)(2,1)S(1)} %all-to-all-done.q_ref) | copy-start | bytes 3145732
  73.7 36.2 %copy-start.4 = (f32[8,1,1024]{2,1,0:T(1,128)S(1)}, f32[8,1,1024]{2,1,0:T(1,128)}, u32[]{:S(2)}) copy-start(f32[8,1,1024]{2,1,0:T(1,128)} %broadcast_in_dim.42.bias_ref) | copy-start | bytes 98308
  73.7 36.2 %copy-start.5 = (f32[1,1024]{1,0:T(1,128)S(1)}, f32[1,1024]{1,0:T(1,128)}, u32[]{:S(2)}) copy-start(f32[1,1024]{1,0:T(1,128)} %reshape.146.mask_ref) | copy-start | bytes 12292
  94.4 15.5 %copy-start.1 = (bf16[1024,2048]{1,0:T(8,128)(2,1)S(1)}, bf16[1024,2048]{1,0:T(8,128)(2,1)}, u32[]{:S(2)}) copy-start(bf16[1024,2048]{1,0:T(8,128)(2,1)} %all-gather.2.cloned.1.call-done.k_ref.v_ref.history_ref) | copy-start | bytes 12582916
  100.2 32.8 %copy-start.2 = (f32[128,2048]{1,0:T(8,128)S(1)}, f32[128,2048]{1,0:T(8,128)}, u32[]{:S(2)}) copy-start(f32[128,2048]{1,0:T(8,128)} %shard_map.109.base_ref) | copy-start | bytes 3145732
  100.2 32.8 %copy-start.3 = (bf16[1,128,2048]{2,1,0:T(8,128)(2,1)S(1)}, bf16[1,128,2048]{2,1,0:T(8,128)(2,1)}, u32[]{:S(2)}) copy-start(bf16[1,128,2048]{2,1,0:T(8,128)(2,1)} %param.13) | copy-start | bytes 1572868
  100.2 32.8 %copy-start.6 = (f32[2048]{0:T(1024)S(1)}, f32[2048]{0:T(1024)}, u32[]{:S(2)}) copy-start(f32[2048]{0:T(1024)} %param.20) | copy-start | bytes 24580
  100.2 21.8 %collective-permute-start.2 = (bf16[128,1024]{1,0:T(8,128)(2,1)}, bf16[128,1024]{1,0:T(8,128)(2,1)S(1)}, u32[]{:S(2)}, u32[]{:S(2)}) collective-permute-start(bf16[128,1024]{1,0:T(8,128)(2,1)} %get-tuple-element.21), channel_id=1, source_target_pairs={{0,0},{257,257},{1,256},{256,1},{384,384},{129,129},{385,128},{128... | collective-permute-start | bytes 786440 | tf_op jit(solution)/shard_map/ppermute | solution.py:261
  108.0 23.1 %collective-permute-start.3 = (bf16[128,1024]{1,0:T(8,128)(2,1)}, bf16[128,1024]{1,0:T(8,128)(2,1)S(1)}, u32[]{:S(2)}, u32[]{:S(2)}) collective-permute-start(bf16[128,1024]{1,0:T(8,128)(2,1)} %get-tuple-element.22), channel_id=1, source_target_pairs={{0,256},{257,1},{1,384},{256,129},{384,128},{129,385},{385,0},{128... | collective-permute-start | bytes 786440 | tf_op jit(solution)/shard_map/ppermute | solution.py:261
  114.1 18.7 %collective-permute-start.4 = (bf16[128,1024]{1,0:T(8,128)(2,1)}, bf16[128,1024]{1,0:T(8,128)(2,1)S(1)}, u32[]{:S(2)}, u32[]{:S(2)}) collective-permute-start(bf16[128,1024]{1,0:T(8,128)(2,1)} %get-tuple-element.24), channel_id=1, source_target_pairs={{0,384},{257,129},{1,128},{256,385},{384,0},{129,257},{385,256},{1... | collective-permute-start | bytes 786440 | tf_op jit(solution)/shard_map/ppermute | solution.py:261
  116.1 16.8 %collective-permute-start.5 = (bf16[128,1024]{1,0:T(8,128)(2,1)S(1)}, bf16[128,1024]{1,0:T(8,128)(2,1)S(1)}, u32[]{:S(2)}, u32[]{:S(2)}) collective-permute-start(bf16[128,1024]{1,0:T(8,128)(2,1)S(1)} %get-tuple-element.25), channel_id=1, source_target_pairs={{0,128},{257,385},{1,0},{256,257},{384,256},{129,1},{385,384},{128... | collective-permute-start | bytes 786440 | tf_op jit(solution)/shard_map/ppermute | solution.py:261
Sparse Core Ops, SparseCore 0:
  36.6 57.8 all-gather.1
